TPU v7x, 32 devices: a whole 2x2x4 slice. The times are simulated.
32 devices in a mesh: grp: 4 (over y, x), exp: 4 (over z), mdl: 2 (over core).
Axes of the slice: x: 2, y: 2, z: 4, core: 2. Of those that a mesh axis runs over, the one named last changes fastest.
Arguments:
- images: bfloat16 [64, 197, 768], P(('grp', 'exp')), may hold values from -6 to 6
- counts: int32 [4, 4], P('grp', 'exp'), may hold values from 1 to 4, 10 in all within a row
- routes: int32 [64, 197, 2], P(('grp', 'exp')), may hold values from 0 to 3, all different within a row
- priority: int32 [16, 788], P(('grp', 'exp')), may hold values from 0 to 787, each once within a row
- gain_one: float32 [768], replicated, may hold values from 0.25 to 1.75
- qkv_one: bfloat16 [3, 768, 768], P(None, None, 'mdl'), may hold values from -0.21875 to 0.21875
- out_one: bfloat16 [768, 768], P('mdl'), may hold values from -0.625 to 0.625
- gain_two: float32 [768], replicated, may hold values from 0.25 to 1.75
- fc_in: bfloat16 [768, 3072], P(None, 'mdl'), may hold values from -0.21875 to 0.21875
- fc_out: bfloat16 [3072, 768], P('mdl'), may hold values from -0.109375 to 0.109375
- gain_three: float32 [768], replicated, may hold values from 0.25 to 1.75
- qkv_two: bfloat16 [3, 768, 768], P(None, None, 'mdl'), may hold values from -0.21875 to 0.21875
- out_two: bfloat16 [768, 768], P('mdl'), may hold values from -0.625 to 0.625
- gain_four: float32 [768], replicated, may hold values from 0.25 to 1.75
- router: bfloat16 [768, 4], replicated, may hold values from -0.15625 to 0.15625
- expert_in: bfloat16 [4, 768, 3072], P('exp', None, 'mdl'), may hold values from -0.21875 to 0.21875
- expert_out: bfloat16 [4, 3072, 768], P('exp', 'mdl'), may hold values from -1.75 to 1.75
- cotangent: bfloat16 [64, 197, 768], P(('grp', 'exp')), may hold values from -6 to 6
Outputs:
- output: bfloat16 [64, 197, 768], P(('grp', 'exp'))
- grad_images: bfloat16 [64, 197, 768], P(('grp', 'exp'))
- grad_gain_one: float32 [768], replicated
- grad_qkv_one: float32 [3, 768, 768], P(None, None, 'mdl')
- grad_out_one: float32 [768, 768], P('mdl')
- grad_gain_two: float32 [768], replicated
- grad_fc_in: float32 [768, 3072], P(None, 'mdl')
- grad_fc_out: float32 [3072, 768], P('mdl')
- grad_gain_three: float32 [768], replicated
- grad_qkv_two: float32 [3, 768, 768], P(None, None, 'mdl')
- grad_out_two: float32 [768, 768], P('mdl')
- grad_gain_four: float32 [768], replicated
- grad_router: float32 [768, 4], replicated
- grad_expert_in: float32 [4, 768, 3072], P('exp', 'grp', 'mdl')
- grad_expert_out: float32 [4, 3072, 768], P('exp', 'mdl', 'grp')
Inputs may be any that keep to these rules, and one draw needn't show every extreme that they name: `counts`: each row sums to 10, and some device of every group holds 4 images. `routes`: the 2 experts of a token differ. `priority`: each row is a permutation of one device's token places.
All inputs are finite; a program needn't handle non-finite values.
Results may differ from a plain program's by a relative error of at most 0.029.
Values may be sent and summed in bfloat16 or wider, within the bound.
A program may use at most 192 MiB of HBM per device.

v0:
```python
import jax
import jax.numpy as jnp
from jax import lax
from jax.sharding import PartitionSpec as P

HDIM = 64
L = 197
TOPK = 2


EPSILON = 1e-06
ROOT_HALF = 0.7071067811865476
DENSITY_FACTOR = 0.3989422804014327


def gelu_slope(values):
    return (
        0.5 * (1.0 + lax.erf(values * ROOT_HALF))
        + values * jnp.exp(-0.5 * values * values) * DENSITY_FACTOR
    )


def model_sum(partial_sum):
    shares = lax.psum_scatter(
        partial_sum.astype(jnp.bfloat16), "mdl", scatter_dimension=0, tiled=True
    ).astype(jnp.float32)
    return lax.all_gather(shares.astype(jnp.bfloat16), "mdl", axis=0, tiled=True).astype(
        shares.dtype
    )


def norm_forward(residual, weight):
    center = residual - jnp.mean(residual, axis=-1, keepdims=True)
    scaled = lax.rsqrt(jnp.mean(center * center, axis=-1, keepdims=True) + EPSILON)
    normal = center * scaled
    return (normal, scaled, (normal * weight).astype(jnp.bfloat16))


def norm_backward(normal, scaled, weight, grad_normed):
    grad_normal = grad_normed * weight
    grad_weight = jnp.sum(grad_normed * normal, axis=0)
    inner_term = (
        grad_normal
        - jnp.mean(grad_normal, axis=-1, keepdims=True)
        - normal * jnp.mean(grad_normal * normal, axis=-1, keepdims=True)
    )
    return (scaled * inner_term, grad_weight)


def attention_forward(residual, weight, qkv_weight, out_weight):
    normal, scaled, normed = norm_forward(residual, weight)
    row_total = residual.shape[0]
    count_img = row_total // L
    local_heads = qkv_weight.shape[2] // HDIM
    projected = jnp.einsum(
        "rd,kdc->krc", normed, qkv_weight, preferred_element_type=jnp.float32
    ).astype(jnp.bfloat16)
    projected = projected.reshape(3, count_img, L, local_heads, HDIM)
    queries, key_rows, values = (projected[0], projected[1], projected[2])
    scores = jnp.einsum(
        "sqhd,skhd->shqk", queries, key_rows, preferred_element_type=jnp.float32
    ) * HDIM ** (-0.5)
    peak_score = jnp.max(scores, axis=-1, keepdims=True)
    exponent = jnp.exp(scores - peak_score)
    denominator = jnp.sum(exponent, axis=-1, keepdims=True)
    soft_rows = exponent / denominator
    log_total = peak_score + jnp.log(denominator)
    mixed_heads = jnp.einsum(
        "shqk,skhd->sqhd",
        soft_rows.astype(jnp.bfloat16),
        values,
        preferred_element_type=jnp.float32,
    )
    mixed_heads = mixed_heads.astype(jnp.bfloat16).reshape(row_total, local_heads * HDIM)
    branch = model_sum(jnp.dot(mixed_heads, out_weight, preferred_element_type=jnp.float32))
    kept_state = (normal, scaled, normed, queries, key_rows, values, log_total, mixed_heads)
    return (residual + branch, kept_state)


def attention_backward(grad_residual, kept_state, weight, qkv_weight, out_weight):
    normal, scaled, normed, queries, key_rows, values, log_total, mixed_heads = kept_state
    count_img, local_heads = (queries.shape[0], queries.shape[2])
    row_total = normal.shape[0]
    grad_branch = grad_residual.astype(jnp.bfloat16)
    grad_out_weight = jnp.einsum(
        "rc,rd->cd", mixed_heads, grad_branch, preferred_element_type=jnp.float32
    )
    grad_mixed = jnp.einsum(
        "rd,cd->rc", grad_branch, out_weight, preferred_element_type=jnp.float32
    )
    grad_mixed = grad_mixed.astype(jnp.bfloat16).reshape(count_img, L, local_heads, HDIM)
    scores = jnp.einsum(
        "sqhd,skhd->shqk", queries, key_rows, preferred_element_type=jnp.float32
    ) * HDIM ** (-0.5)
    soft_rows = jnp.exp(scores - log_total)
    grad_values = jnp.einsum(
        "shqk,sqhd->skhd",
        soft_rows.astype(jnp.bfloat16),
        grad_mixed,
        preferred_element_type=jnp.float32,
    )
    grad_soft = jnp.einsum(
        "sqhd,skhd->shqk", grad_mixed, values, preferred_element_type=jnp.float32
    )
    grad_scores = soft_rows * (grad_soft - jnp.sum(grad_soft * soft_rows, axis=-1, keepdims=True))
    grad_scores = grad_scores.astype(jnp.bfloat16)
    grad_queries = jnp.einsum(
        "shqk,skhd->sqhd", grad_scores, key_rows, preferred_element_type=jnp.float32
    ) * HDIM ** (-0.5)
    grad_keys = jnp.einsum(
        "shqk,sqhd->skhd", grad_scores, queries, preferred_element_type=jnp.float32
    ) * HDIM ** (-0.5)
    grad_projected = jnp.stack([grad_queries, grad_keys, grad_values]).astype(jnp.bfloat16)
    grad_projected = grad_projected.reshape(3, row_total, local_heads * HDIM)
    grad_qkv_weight = jnp.einsum(
        "rd,krc->kdc", normed, grad_projected, preferred_element_type=jnp.float32
    )
    grad_normed = model_sum(
        jnp.einsum("krc,kdc->rd", grad_projected, qkv_weight, preferred_element_type=jnp.float32)
    )
    grad_input, grad_weight = norm_backward(normal, scaled, weight, grad_normed)
    return (grad_residual + grad_input, grad_weight, grad_qkv_weight, grad_out_weight)


def feed_forward(residual, weight, in_weight, out_weight):
    normal, scaled, normed = norm_forward(residual, weight)
    hidden = jnp.dot(normed, in_weight, preferred_element_type=jnp.float32)
    active = jax.nn.gelu(hidden, approximate=False).astype(jnp.bfloat16)
    branch = model_sum(jnp.dot(active, out_weight, preferred_element_type=jnp.float32))
    return (residual + branch, (normal, scaled, normed, hidden, active))


def feed_backward(grad_residual, kept_state, weight, in_weight, out_weight):
    normal, scaled, normed, hidden, active = kept_state
    grad_branch = grad_residual.astype(jnp.bfloat16)
    grad_w_out = jnp.einsum("rf,rd->fd", active, grad_branch, preferred_element_type=jnp.float32)
    grad_active = jnp.einsum(
        "rd,fd->rf", grad_branch, out_weight, preferred_element_type=jnp.float32
    )
    grad_hidden = (grad_active * gelu_slope(hidden)).astype(jnp.bfloat16)
    grad_w_in = jnp.einsum("rd,rf->df", normed, grad_hidden, preferred_element_type=jnp.float32)
    grad_normed = model_sum(
        jnp.einsum("rf,df->rd", grad_hidden, in_weight, preferred_element_type=jnp.float32)
    )
    grad_input, grad_weight = norm_backward(normal, scaled, weight, grad_normed)
    return (grad_residual + grad_input, grad_weight, grad_w_in, grad_w_out)


def on_device(
    images,
    counts,
    routes,
    priority,
    gain_one,
    qkv_one,
    out_one,
    gain_two,
    fc_in,
    fc_out,
    gain_three,
    qkv_two,
    out_two,
    gain_four,
    router,
    expert_in,
    expert_out,
    cotangent,
):
    slot_count, length, feature_count = images.shape
    row_total = slot_count * length
    experts = router.shape[1]
    peer_count = lax.axis_size("exp")
    capacity = (25 * L * TOPK + 8 * experts - 1) // (8 * experts)
    sentinel = experts * capacity
    live_int = (jnp.arange(row_total, dtype=jnp.int32) // length < counts[0, 0]).astype(jnp.int32)
    live_rows = live_int.astype(jnp.float32)[:, None]
    residual = images.astype(jnp.float32).reshape(row_total, feature_count)
    first, state_one = attention_forward(residual, gain_one, qkv_one, out_one)
    second, state_two = feed_forward(first, gain_two, fc_in, fc_out)
    stream_three, state_three = attention_forward(second, gain_three, qkv_two, out_two)
    normal, scaled, normed = norm_forward(stream_three, gain_four)
    logits = jnp.dot(normed, router, preferred_element_type=jnp.float32)
    soft_rows = jax.nn.softmax(logits, axis=-1)
    route_rows = routes.reshape(row_total, TOPK)
    gate_values = jnp.take_along_axis(soft_rows, route_rows, axis=1)
    expert_ids = jnp.arange(experts, dtype=jnp.int32)
    picked = route_rows[:, :, None] == expert_ids[None, None, :]
    chosen = jnp.sum(picked.astype(jnp.int32), axis=1, dtype=jnp.int32) * live_int[:, None]
    priority_row = priority[0]
    inverse = (
        jnp.zeros((row_total,), jnp.int32)
        .at[priority_row]
        .set(jnp.arange(row_total, dtype=jnp.int32))
    )
    ordered = chosen[inverse]
    before = jnp.cumsum(ordered, axis=0, dtype=jnp.int32) - ordered
    rank_rows = jnp.take_along_axis(before[priority_row], route_rows, axis=1)
    kept_pairs = (rank_rows < capacity) & (live_int[:, None] > 0)
    target = jnp.where(kept_pairs, route_rows * capacity + rank_rows, sentinel)
    flat_target = jnp.transpose(target).reshape(-1)
    pair_total = TOPK * row_total
    source_flat = (
        jnp.full((sentinel,), pair_total, jnp.int32)
        .at[flat_target]
        .set(jnp.arange(pair_total, dtype=jnp.int32), mode="drop")
    )
    source_row = jnp.where(source_flat < pair_total, source_flat % row_total, row_total)
    normed_ext = jnp.concatenate([normed, jnp.zeros((1, feature_count), jnp.bfloat16)], axis=0)
    outgoing = normed_ext[source_row].reshape(experts, capacity, feature_count)
    incoming = lax.all_to_all(outgoing, "exp", split_axis=0, concat_axis=0, tiled=True).reshape(
        peer_count * capacity, feature_count
    )
    hidden = jnp.dot(incoming, expert_in[0], preferred_element_type=jnp.float32)
    active = jax.nn.gelu(hidden, approximate=False).astype(jnp.bfloat16)
    partial_rows = jnp.dot(active, expert_out[0], preferred_element_type=jnp.float32)
    summed_rows = (
        model_sum(partial_rows).astype(jnp.bfloat16).reshape(peer_count, capacity, feature_count)
    )
    returned = lax.all_to_all(summed_rows, "exp", split_axis=0, concat_axis=0, tiled=True).reshape(
        sentinel, feature_count
    )
    returned_ext = jnp.concatenate([returned, jnp.zeros((1, feature_count), jnp.bfloat16)], axis=0)
    fetched = returned_ext[target].astype(jnp.float32)
    mixture_rows = jnp.sum(gate_values[:, :, None] * fetched, axis=1)
    output = (live_rows * (stream_three + mixture_rows)).astype(jnp.bfloat16).reshape(images.shape)
    grad_out = cotangent.astype(jnp.float32).reshape(row_total, feature_count) * live_rows
    grad_gates = jnp.sum(grad_out[:, None, :] * fetched, axis=-1)
    weighted = (gate_values[:, :, None] * grad_out[:, None, :]).astype(jnp.bfloat16)
    weighted_flat = jnp.transpose(weighted, (1, 0, 2)).reshape(pair_total, feature_count)
    weighted_ext = jnp.concatenate(
        [weighted_flat, jnp.zeros((1, feature_count), jnp.bfloat16)], axis=0
    )
    grad_return = weighted_ext[source_flat].reshape(experts, capacity, feature_count)
    grad_expert_rows = lax.all_to_all(
        grad_return, "exp", split_axis=0, concat_axis=0, tiled=True
    ).reshape(peer_count * capacity, feature_count)
    grad_w_eout = jnp.einsum(
        "rd,rf->df", grad_expert_rows, active, preferred_element_type=jnp.float32
    )
    grad_active = jnp.einsum(
        "rd,fd->rf", grad_expert_rows, expert_out[0], preferred_element_type=jnp.float32
    )
    grad_hidden = (grad_active * gelu_slope(hidden)).astype(jnp.bfloat16)
    grad_w_ein = jnp.einsum("rd,rf->df", incoming, grad_hidden, preferred_element_type=jnp.float32)
    grad_partial = jnp.einsum(
        "rf,df->rd", grad_hidden, expert_in[0], preferred_element_type=jnp.float32
    )
    grad_incoming = (
        model_sum(grad_partial).astype(jnp.bfloat16).reshape(peer_count, capacity, feature_count)
    )
    grad_outgoing = lax.all_to_all(
        grad_incoming, "exp", split_axis=0, concat_axis=0, tiled=True
    ).reshape(sentinel, feature_count)
    grad_outgoing_ext = jnp.concatenate(
        [grad_outgoing, jnp.zeros((1, feature_count), jnp.bfloat16)], axis=0
    )
    grad_dispatch = jnp.sum(grad_outgoing_ext[target].astype(jnp.float32), axis=1)
    grad_soft = jnp.sum(grad_gates[:, :, None] * picked.astype(jnp.float32), axis=1)
    grad_logits = (
        soft_rows * (grad_soft - jnp.sum(grad_soft * soft_rows, axis=-1, keepdims=True))
    ).astype(jnp.bfloat16)
    grad_router = jnp.einsum("rd,re->de", normed, grad_logits, preferred_element_type=jnp.float32)
    grad_normed = grad_dispatch + jnp.einsum(
        "re,de->rd", grad_logits, router, preferred_element_type=jnp.float32
    )
    grad_norm_four, grad_gain_four = norm_backward(normal, scaled, gain_four, grad_normed)
    grad_three = grad_out + grad_norm_four
    stacked = jnp.stack([grad_w_ein, grad_w_eout])
    shared = lax.psum_scatter(
        stacked.astype(jnp.bfloat16), "grp", scatter_dimension=1, tiled=True
    ).astype(jnp.float32)
    grad_expert_in = shared[0][None]
    grad_expert_out = jnp.transpose(shared[1])[None]
    grad_two, grad_gain_three, grad_qkv_two, grad_out_two = attention_backward(
        grad_three, state_three, gain_three, qkv_two, out_two
    )
    upper_sums = (grad_gain_three, grad_qkv_two, grad_out_two, grad_gain_four, grad_router)
    grad_one, grad_gain_two, grad_fc_in, grad_fc_out = feed_backward(
        grad_two, state_two, gain_two, fc_in, fc_out
    )
    grad_input, grad_gain_one, grad_qkv_one, grad_out_one = attention_backward(
        grad_one, state_one, gain_one, qkv_one, out_one
    )
    every_sum = lax.psum(
        (
            grad_gain_one,
            grad_qkv_one,
            grad_out_one,
            grad_gain_two,
            grad_fc_in,
            grad_fc_out,
            upper_sums[0],
            upper_sums[1],
            upper_sums[2],
            upper_sums[3],
            upper_sums[4],
        ),
        ("grp", "exp"),
    )
    lower_sums = every_sum[0:6]
    upper_sums = every_sum[6:11]
    grad_images = grad_input.astype(jnp.bfloat16).reshape(images.shape)
    return (
        output,
        grad_images,
        lower_sums[0],
        lower_sums[1],
        lower_sums[2],
        lower_sums[3],
        lower_sums[4],
        lower_sums[5],
        upper_sums[0],
        upper_sums[1],
        upper_sums[2],
        upper_sums[3],
        upper_sums[4],
        grad_expert_in,
        grad_expert_out,
    )


def solution(mesh):
    placed = (
        P(("grp", "exp"), None, None),
        P("grp", "exp"),
        P(("grp", "exp"), None, None),
        P(("grp", "exp"), None),
        P(),
        P(None, None, "mdl"),
        P("mdl", None),
        P(),
        P(None, "mdl"),
        P("mdl", None),
        P(),
        P(None, None, "mdl"),
        P("mdl", None),
        P(),
        P(),
        P("exp", None, "mdl"),
        P("exp", "mdl", None),
        P(("grp", "exp"), None, None),
    )
    return jax.shard_map(
        on_device,
        mesh=mesh,
        in_specs=placed,
        out_specs=(
            P(("grp", "exp"), None, None),
            P(("grp", "exp"), None, None),
            P(),
            P(None, None, "mdl"),
            P("mdl", None),
            P(),
            P(None, "mdl"),
            P("mdl", None),
            P(),
            P(None, None, "mdl"),
            P("mdl", None),
            P(),
            P(),
            P("exp", "grp", "mdl"),
            P("exp", "mdl", "grp"),
        ),
        check_vma=False,
    )
```

profile of v0, /device:TPU:0, one launch (start us, length us, event | category | flops | bytes accessed | tf_op | source)
XLA Modules:
  0.0 1354.8 jit_solution(194358578223514602)
XLA Ops:
  49.8 5.4 fusion
  64.9 12.0 all-gather.19.cloned.1.call-done
  85.2 13.4 fusion.23
  118.7 5.7 scatter_custom_fusion
  187.1 15.1 %gather_fusion.7 = s32[1576]{0:T(1024)S(1)} fusion(s32[788,4]{1,0:T(8,128)S(1)} %gather_fusion.1, s32[1576]{0:T(1024)S(1)} %reshape.559), kind=kCustom, calls=%fused_computation.7 | custom fusion | bytes 25216 | tf_op jit(solution)/shard_map/jit(take_along_axis)/gather | solution.py:197
  209.3 8.8 scatter_custom_fusion.1
  230.1 7.2 gather_fusion.2
  247.6 41.4 %all-to-all-done = bf16[4,308,768]{2,1,0:T(8,128)(2,1)} async-done(((bf16[4,308,768]{2,1,0:T(8,128)(2,1)}), bf16[4,308,768]{2,1,0:T(8,128)(2,1)}, u32[]{:S(2)}, u32[]{:S(2)}) %all-to-all-start) | async-done | bytes 1892384 | tf_op jit(solution)/shard_map/all_to_all | solution.py:210
  291.6 20.8 %fusion.8 = (bf16[1232,1536]{1,0:T(8,128)(2,1)S(1)}, f32[1232,1536]{1,0:T(8,128)}) fusion(bf16[1232,768]{1,0:T(8,128)(2,1)} %reshape.496, bf16[1,768,1536]{2,1,0:T(8,128)(2,1)S(1)} %copy-done), kind=kOutput, calls=%fused_computation.15 | convolution fusion | flops 3029655552 | bytes 15605760 | tf_op jit(solution)/shard_map/dot_general | solution.py:213
  318.7 19.7 %gather_fusion.6 = f32[1576]{0:T(1024)S(1)} fusion(f32[788,4]{0,1:T(4,128)S(1)} %fusion.89, s32[1576]{0:T(1024)S(1)} %reshape.559), kind=kCustom, calls=%fused_computation.6 | custom fusion | bytes 25216 | tf_op jit(solution)/shard_map/jit(take_along_axis)/gather | solution.py:185
  352.7 7.8 gather_fusion.4
  363.1 48.3 %all_to_all.20 = bf16[4,308,768]{2,1,0:T(8,128)(2,1)} all-to-all(bf16[4,308,768]{2,1,0:T(8,128)(2,1)} %reshape.502), channel_id=1, replica_groups=mesh['grp'=4,'exp'=4,'mdl'=2] {'exp'}, dimensions={0} | all-to-all | bytes 3784704 | tf_op jit(solution)/shard_map/all_to_all | solution.py:234
  414.5 7.8 fusion.20
  437.3 13.0 all-gather.17.cloned.1.call-done
  452.9 26.4 %all-to-all-done.1 = bf16[4,308,768]{2,1,0:T(8,128)(2,1)} async-done(((bf16[4,308,768]{2,1,0:T(8,128)(2,1)}), bf16[4,308,768]{2,1,0:T(8,128)(2,1)}, u32[]{:S(2)}, u32[]{:S(2)}) %all-to-all-start.1) | async-done | bytes 1892384 | tf_op jit(solution)/shard_map/all_to_all | solution.py:219
  490.6 37.0 %all-to-all-done.3 = bf16[4,308,768]{2,1,0:T(8,128)(2,1)} async-done(((bf16[4,308,768]{2,1,0:T(8,128)(2,1)}), bf16[4,308,768]{2,1,0:T(8,128)(2,1)}, u32[]{:S(2)}, u32[]{:S(2)}) %all-to-all-start.3) | async-done | bytes 1892384 | tf_op jit(solution)/shard_map/all_to_all | solution.py:251
  533.1 9.2 gather_fusion.5
  542.4 9.2 gather_fusion.3
  551.6 6.4 reshape.593
  558.1 13.8 %multiply_reduce_fusion.2 = (f32[788,2]{1,0:T(8,128)S(1)}, f32[788,768]{1,0:T(8,128)}) fusion(f32[788,2,768]{2,1,0:T(2,128)} %reshape.593, f32[788,768]{1,0:T(8,128)} %get-tuple-element.165, f32[788,2]{1,0:T(8,128)S(1)} %copy.351), kind=kLoop, calls=%fused_computation.72 | loop fusion | flops 4234712 | bytes 9695552 | tf_op jit(solution)/shard_map/reduce_sum | solution.py:227
  572.2 6.6 reshape.594
  578.8 9.6 reduce_sum.292
  651.8 8.5 all-gather.25.cloned.1.call-done
  670.1 5.8 fusion.29
  694.9 6.0 fusion.42
  773.8 5.2 fusion.5
  781.3 7.4 fusion.113
  795.0 7.4 fusion.83
  835.1 82.1 %all-reduce.17 = (f32[768]{0:T(1024)}, f32[768]{0:T(1024)}, f32[768]{0:T(1024)}, f32[768]{0:T(1024)}, f32[768,4]{0,1:T(4,128)}) all-reduce(f32[768]{0:T(1024)S(1)} %get-tuple-element.111, f32[768]{0:T(1024)S(1)} %get-tuple-element.109, f32[768]{0:T(1024)S(1)} %get-tuple-element.107, ...), channel_id=1, replica_groups=mesh['grp'=4,'exp'=4,'mdl'=2] {'grp','exp'}, use_global_device_ids=true, to_apply=%region_43.44 | all-reduce | flops 6144 | bytes 49152 | tf_op jit(solution)/shard_map/psum | solution.py:284
  917.2 410.2 %all-reduce.21.cloned.1.call-done = (f32[3,768,384]{1,2,0:T(8,128)}, f32[384,768]{1,0:T(8,128)}, f32[768,1536]{1,0:T(8,128)}, f32[1536,768]{1,0:T(8,128)}, f32[3,768,384]{1,2,0:T(8,128)}, /*index=5*/f32[384,768]{1,0:T(8,128)}) async-done(((f32[3,768,384]{1,2,0:T(8,128)}, f32[384,768]{1,0:T(8,128)}, f32[768,1536]{1,0:T(8,128)}, f32[1536,768]{1,0:T(8,128)}, f32[3,768,384]{1,2,0:T(8,128)}, ...) | async-done | bytes 18874384 | tf_op jit(solution)/shard_map/psum | solution.py:284
  1332.6 5.2 copy.393
  1338.8 5.5 copy.445
  (525 shorter events, 448.8 us)
Async XLA Ops:
  7.2 284.5 %copy-start = (bf16[1,768,1536]{2,1,0:T(8,128)(2,1)S(1)}, bf16[1,768,1536]{2,1,0:T(8,128)(2,1)}, u32[]{:S(2)}) copy-start(bf16[1,768,1536]{2,1,0:T(8,128)(2,1)} %param.33) | copy-start | bytes 7077892
  7.2 69.7 %all-gather.19.cloned.1.call-start = ((), (), s32[]{:S(2)}) async-start(), calls=%async_computation.12 | async-start | bytes 1843200 | tf_op jit(solution)/shard_map/all_gather | solution.py:27
  55.2 3.3 collective-permute-start
  64.8 64.7 %all-gather.21.cloned.1.call-start = ((), (), s32[]{:S(2)}) async-start(), calls=%async_computation.13 | async-start | bytes 1843200 | tf_op jit(solution)/shard_map/all_gather | solution.py:27
  108.2 3.0 collective-permute-start.1
  117.4 100.7 %all-gather.23.cloned.1.call-start = ((), (), s32[]{:S(2)}) async-start(), calls=%async_computation.14 | async-start | bytes 1843200 | tf_op jit(solution)/shard_map/all_gather | solution.py:27
  117.6 85.2 %copy-start.60 = (s32[788,2]{0,1:T(2,128)}, s32[788,2]{0,1:T(2,128)S(1)}, u32[]{:S(2)}) copy-start(s32[788,2]{0,1:T(2,128)S(1)} %reshape.490) | copy-start | bytes 18916
  118.4 84.4 %copy-start.101 = (pred[788]{0:T(1024)(128)(4,1)}, pred[788]{0:T(1024)(128)(4,1)S(1)}, u32[]{:S(2)}) copy-start(pred[788]{0:T(1024)(128)(4,1)S(1)} %get-tuple-element.162) | copy-start | bytes 2368
  171.9 5.0 collective-permute-start.2
  240.0 49.0 %all-to-all-start = ((bf16[4,308,768]{2,1,0:T(8,128)(2,1)}), bf16[4,308,768]{2,1,0:T(8,128)(2,1)}, u32[]{:S(2)}, u32[]{:S(2)}) async-start(bf16[4,308,768]{2,1,0:T(8,128)(2,1)} %reshape.495), calls=%async_computation | async-start | bytes 3833856 | tf_op jit(solution)/shard_map/all_to_all | solution.py:210
  245.0 169.1 %reduce-scatter.16.cloned.1.call-start = ((), (), s32[]{:S(2)}) async-start(), calls=%async_computation.7 | async-start | bytes 2838528 | tf_op jit(solution)/shard_map/reduce_scatter | solution.py:24
  247.5 71.1 %copy-start.50 = (f32[788,4]{0,1:T(4,128)}, f32[788,4]{0,1:T(4,128)S(1)}, u32[]{:S(2)}) copy-start(f32[788,4]{0,1:T(4,128)S(1)} %get-tuple-element.153) | copy-start | bytes 37828
  247.5 71.1 %copy-start.68 = (f32[788]{0:T(1024)}, f32[788]{0:T(1024)S(1)}, u32[]{:S(2)}) copy-start(f32[788]{0:T(1024)S(1)} %get-tuple-element.152) | copy-start | bytes 9460
  247.6 71.1 %copy-start.76 = (f32[788]{0:T(1024)}, f32[788]{0:T(1024)S(1)}, u32[]{:S(2)}) copy-start(f32[788]{0:T(1024)S(1)} %fusion.90) | copy-start | bytes 9460
  318.6 110.0 %all-gather.15.cloned.1.call-start = ((), (), s32[]{:S(2)}) async-start(), calls=%async_computation.8 | async-start | bytes 2838528 | tf_op jit(solution)/shard_map/all_gather | solution.py:27
  414.1 23.2 %reduce-scatter.18.cloned.1.call-start = ((), (), s32[]{:S(2)}) async-start(), calls=%async_computation.9 | async-start | bytes 2838528 | tf_op jit(solution)/shard_map/reduce_scatter | solution.py:24
  431.3 48.1 %all-to-all-start.1 = ((bf16[4,308,768]{2,1,0:T(8,128)(2,1)}), bf16[4,308,768]{2,1,0:T(8,128)(2,1)}, u32[]{:S(2)}, u32[]{:S(2)}) async-start(bf16[4,308,768]{2,1,0:T(8,128)(2,1)} %reshape.497), calls=%async_computation.2 | async-start | bytes 3833856 | tf_op jit(solution)/shard_map/all_to_all | solution.py:219
  435.8 14.4 %all-gather.17.cloned.1.call-start = ((), (), s32[]{:S(2)}) async-start(), calls=%async_computation.10 | async-start | bytes 2838528 | tf_op jit(solution)/shard_map/all_gather | solution.py:27
  452.9 30.9 %copy-start.21 = (s32[1576]{0:T(1024)S(1)}, s32[1576]{0:T(1024)}, u32[]{:S(2)}) copy-start(s32[1576]{0:T(1024)} %copy-done.20) | copy-start | bytes 18916
  452.9 31.5 %copy-start.79 = (s32[788,2,1]{0,1,2:T(2,128)S(1)}, s32[788,2,1]{0,1,2:T(2,128)}, u32[]{:S(2)}) copy-start(s32[788,2,1]{0,1,2:T(2,128)} %copy-done.78) | copy-start | bytes 18916
  452.9 31.5 %copy-start.102 = (pred[788]{0:T(1024)(128)(4,1)S(1)}, pred[788]{0:T(1024)(128)(4,1)}, u32[]{:S(2)}) copy-start(pred[788]{0:T(1024)(128)(4,1)} %copy-done.101) | copy-start | bytes 2368
  452.9 31.9 %copy-start.55 = (f32[4,6,197]{2,1,0:T(8,128)S(1)}, f32[4,6,197]{2,1,0:T(8,128)}, u32[]{:S(2)}) copy-start(f32[4,6,197]{2,1,0:T(8,128)} %copy-done.54) | copy-start | bytes 56740
  452.9 32.0 %copy-start.65 = (f32[4,6,197]{2,1,0:T(8,128)S(1)}, f32[4,6,197]{2,1,0:T(8,128)}, u32[]{:S(2)}) copy-start(f32[4,6,197]{2,1,0:T(8,128)} %copy-done.64) | copy-start | bytes 56740
  479.3 48.3 %all-to-all-start.3 = ((bf16[4,308,768]{2,1,0:T(8,128)(2,1)}), bf16[4,308,768]{2,1,0:T(8,128)(2,1)}, u32[]{:S(2)}, u32[]{:S(2)}) async-start(bf16[4,308,768]{2,1,0:T(8,128)(2,1)} %reshape.504), calls=%async_computation.5 | async-start | bytes 3833856 | tf_op jit(solution)/shard_map/all_to_all | solution.py:251
  483.7 176.6 %all-gather.25.cloned.1.call-start = ((), (), s32[]{:S(2)}) async-start(), calls=%async_computation.15 | async-start | bytes 1843200 | tf_op jit(solution)/shard_map/all_gather | solution.py:27
  642.4 3.1 collective-permute-start.3
  651.8 64.3 %all-gather.27.cloned.1.call-start = ((), (), s32[]{:S(2)}) async-start(), calls=%async_computation.16 | async-start | bytes 1843200 | tf_op jit(solution)/shard_map/all_gather | solution.py:27
  685.5 3.0 collective-permute-start.4
  694.8 120.8 %reduce-scatter.20.cloned.1.call-start = ((), (), s32[]{:S(2)}) async-start(), calls=%async_computation.11 | async-start | bytes 5898240 | tf_op jit(solution)/shard_map/reduce_scatter | solution.py:269
  707.1 112.2 %all-gather.29.cloned.1.call-start = ((), (), s32[]{:S(2)}) async-start(), calls=%async_computation.17 | async-start | bytes 1843200 | tf_op jit(solution)/shard_map/all_gather | solution.py:27
  779.0 9.7 collective-permute-start.5
  795.0 532.4 %all-reduce.21.cloned.1.call-start = ((), (), s32[]{:S(2)}) async-start(), calls=%async_computation.18 | async-start | bytes 37748736 | tf_op jit(solution)/shard_map/psum | solution.py:284
  (114 other events, 615.6 us)
Sparse Core Ops, SparseCore 0:
  64.9 11.9 all-gather.18
  117.6 10.4 all-gather.20
  183.3 10.4 all-gather.22
  318.7 8.5 reduce-scatter.15
  414.2 9.3 all-gather.14
  428.7 8.5 reduce-scatter.17
  438.8 11.4 all-gather.16
  651.9 8.4 all-gather.24
  694.9 10.4 all-gather.26
  708.3 58.2 reduce-scatter.19
  795.1 10.8 all-gather.28
  813.4 513.9 all-reduce.20
where the time goes:
time: 1370 us; the launch traced here: 1350 us
  waiting for transfers between devices  553 us (40%)
  local copies, waits for them, and re-layouts  362 us (26%)
  blocking collectives  161 us (12%)
  matrix products  158 us (12%)
  other arithmetic  74.3 us (5%)
  starting transfers between devices  28.4 us (2%)
  between operations  17.7 us (1%)
    psum x1, waiting for transfers between devices, on_device(): lax.psum((grad_gain_one, grad_qkv_one, grad_out_one, grad_gain_two, grad_...  410 us
    unnamed x284, local copies, waits for them, and re-layouts  95 us
    psum x1, blocking collectives, on_device(): lax.psum((grad_gain_one, grad_qkv_one, grad_out_one, grad_gain_two, grad_...  82.1 us
    all_to_all x1, blocking collectives, on_device(): lax.all_to_all(grad_return, 'exp', split_axis=0, concat_axis=0, tiled=True)  48.3 us
    all_to_all x1, waiting for transfers between devices, on_device(): lax.all_to_all(outgoing, 'exp', split_axis=0, concat_axis=0, tiled=True)  41.4 us
    all_to_all x1, waiting for transfers between devices, on_device(): lax.all_to_all(grad_incoming, 'exp', split_axis=0, concat_axis=0, tiled=T...  37 us
    another operation x14, local copies, waits for them, and re-layouts, attention_backward(): jnp.stack([grad_queries, grad_keys, grad_values]).astype(jnp.bfloat16)  35.5 us
    all_gather x8, waiting for transfers between devices, model_sum(): lax.all_gather(shares.astype(jnp.bfloat16), 'mdl', axis=0, tiled=True)  33.6 us
  transfers between devices with their start and end apart: 21, of which 11 were waited for; matrix products, arithmetic and copies ran while one was open for 19% of the time, Pallas kernels for 0%

commit v1 on v0

v1 whole, which is shorter than its diff:
```python
import functools
import math

import jax
import jax.numpy as jnp
from jax import lax
from jax.experimental import pallas as pl
from jax.experimental.pallas import tpu as pltpu
from jax.sharding import PartitionSpec as P

HDIM = 64
L = 197
TOPK = 2
LP = (L + 15) // 16 * 16
LANES = 128
BF = jnp.bfloat16
F32 = jnp.float32
I32 = jnp.int32

EPSILON = 1e-06
ROOT_HALF = 0.7071067811865476
DENSITY_FACTOR = 0.3989422804014327
VMEM_BYTES = 60 * 1024 * 1024


def nn(a, b):
    return lax.dot_general(a, b, (((1,), (0,)), ((), ())), preferred_element_type=F32)


def nt(a, b):
    return lax.dot_general(a, b, (((1,), (1,)), ((), ())), preferred_element_type=F32)


def tn(a, b):
    return lax.dot_general(a, b, (((0,), (0,)), ((), ())), preferred_element_type=F32)


def norm_forward(v, w):
    c = v - jnp.mean(v, axis=-1, keepdims=True)
    r = lax.rsqrt(jnp.mean(c * c, axis=-1, keepdims=True) + EPSILON)
    n = c * r
    return n, r, (n * w).astype(BF)


def norm_backward(n, r, w, dh):
    dn = dh * w
    dw = jnp.sum(dh * n, axis=0, keepdims=True)
    dv = r * (dn - jnp.mean(dn, axis=-1, keepdims=True) - n * jnp.mean(dn * n, axis=-1, keepdims=True))
    return dv, dw


def whole(shape):
    return pl.BlockSpec(shape, lambda *i: (0,) * len(shape))


def call(body, out_shape, *args, grid=(), in_specs=None, out_specs=None, scratch=(), flops=0):
    if in_specs is None:
        in_specs = [whole(a.shape) for a in args]
    if out_specs is None:
        out_specs = [whole(o.shape) for o in out_shape]
    moved = sum(math.prod(a.shape) * a.dtype.itemsize for a in args)
    moved += sum(math.prod(o.shape) * jnp.dtype(o.dtype).itemsize for o in out_shape)
    return pl.pallas_call(
        body,
        grid=grid,
        in_specs=in_specs,
        out_specs=out_specs,
        out_shape=out_shape,
        scratch_shapes=list(scratch),
        cost_estimate=pl.CostEstimate(flops=int(flops), bytes_accessed=int(moved), transcendentals=0),
        compiler_params=pltpu.CompilerParams(vmem_limit_bytes=VMEM_BYTES),
    )(*args)


def out(shape, dtype):
    return jax.ShapeDtypeStruct(shape, dtype)


def head_mask(dtype):
    lane = lax.broadcasted_iota(I32, (LP, LANES), 1)
    return (lane < HDIM).astype(dtype)


def attention_forward_body(n_img, tail, *refs):
    if tail:
        x_ref, w_ref, qm, qo, om, oo, w4_ref, y_ref, h_ref, qkv_ref, p_ref, o_ref, h4_ref = refs
    else:
        x_ref, w_ref, qm, qo, om, oo, y_ref, h_ref, qkv_ref, p_ref, o_ref = refs
    d = x_ref.shape[1]
    c = qm.shape[2]
    pairs = d // LANES
    _, _, h = norm_forward(x_ref[...].astype(F32), w_ref[...])
    h_ref[...] = h
    for k in range(3):
        for half, w in ((0, qm), (1, qo)):
            at = (2 * k + half) * c
            qkv_ref[:, at : at + c] = nn(h_ref[...], w[k]).astype(BF)
    mask = head_mask(BF)
    key_ok = lax.broadcasted_iota(I32, (LP, LP), 1) < L

    def one(i, _):
        rows = pl.ds(pl.multiple_of((i // pairs) * LP, LP), LP)
        col = (i % pairs) * LANES
        q = qkv_ref[rows, pl.ds(pl.multiple_of(col, LANES), LANES)]
        ke = qkv_ref[rows, pl.ds(pl.multiple_of(d + col, LANES), LANES)]
        u = qkv_ref[rows, pl.ds(pl.multiple_of(2 * d + col, LANES), LANES)]
        o = jnp.zeros((LP, LANES), F32)
        for hh in range(2):
            mk = mask if hh == 0 else 1 - mask
            s = nt(q * mk, ke) * HDIM ** (-0.5)
            s = jnp.where(key_ok, s, -1e30)
            e = jnp.exp(s - jnp.max(s, axis=-1, keepdims=True))
            p = (e / jnp.sum(e, axis=-1, keepdims=True)).astype(BF)
            p_ref[2 * i + hh] = p
            o = o + nn(p, u * mk)
        o_ref[rows, pl.ds(pl.multiple_of(col, LANES), LANES)] = o.astype(BF)
        return 0

    lax.fori_loop(0, n_img * pairs, one, 0, unroll=2)
    y = x_ref[...].astype(F32) + nn(o_ref[:, :c], om[...]) + nn(o_ref[:, c:], oo[...])
    y_ref[...] = y
    if tail:
        _, _, h4 = norm_forward(y, w4_ref[...])
        h4_ref[...] = h4


def attention_forward(x, gain, qm, qo, om, oo, gain4=None):
    r, d = x.shape
    n_img = r // LP
    heads = d // HDIM
    shapes = [out((r, d), F32), out((r, d), BF), out((r, 3 * d), BF), out((n_img * heads, LP, LP), BF), out((r, d), BF)]
    args = [x, gain, qm, qo, om, oo]
    if gain4 is not None:
        shapes.append(out((r, d), BF))
        args.append(gain4)
    return call(
        functools.partial(attention_forward_body, n_img, gain4 is not None),
        shapes, *args, flops=2 * r * d * d * 4 + 4 * n_img * heads * LP * LP * LANES,
    )


def attention_backward_body(n_img, dy_ref, x_ref, w_ref, h_ref, qkv_ref, p_ref, o_ref, qm, qo, om, oo,
                            dx_ref, dw_ref, gm_ref, go_ref, do_ref, dqkv_ref, tr_ref):
    d = x_ref.shape[1]
    c = qm.shape[2]
    pairs = d // LANES
    da = dy_ref[...].astype(BF)
    tr_ref[...] = o_ref[...].T
    for half, (w, g) in enumerate(((om, gm_ref), (oo, go_ref))):
        gw = nn(tr_ref[half * c : (half + 1) * c, :], da).astype(BF)
        for part in range(d // c):
            g[3 * d + part * c : 3 * d + (part + 1) * c, :] = gw[:, part * c : (part + 1) * c]
        do_ref[:, half * c : (half + 1) * c] = nt(da, w[...]).astype(BF)
    mask = head_mask(BF)

    def one(i, _):
        rows = pl.ds(pl.multiple_of((i // pairs) * LP, LP), LP)
        col = (i % pairs) * LANES
        cq = pl.ds(pl.multiple_of(col, LANES), LANES)
        ck = pl.ds(pl.multiple_of(d + col, LANES), LANES)
        cu = pl.ds(pl.multiple_of(2 * d + col, LANES), LANES)
        q, ke, u, do = qkv_ref[rows, cq], qkv_ref[rows, ck], qkv_ref[rows, cu], do_ref[rows, cq]
        dq = jnp.zeros((LP, LANES), F32)
        dk = jnp.zeros((LP, LANES), F32)
        du = jnp.zeros((LP, LANES), F32)
        for hh in range(2):
            mk = mask if hh == 0 else 1 - mask
            p = p_ref[2 * i + hh]
            du = du + tn(p, do * mk)
            dp = nt(do * mk, u)
            pf = p.astype(F32)
            ds = (pf * (dp - jnp.sum(dp * pf, axis=-1, keepdims=True))).astype(BF)
            dq = dq + nn(ds, ke * mk)
            dk = dk + tn(ds, q * mk)
        dqkv_ref[rows, cq] = (dq * HDIM ** (-0.5)).astype(BF)
        dqkv_ref[rows, ck] = (dk * HDIM ** (-0.5)).astype(BF)
        dqkv_ref[rows, cu] = du.astype(BF)
        return 0

    lax.fori_loop(0, n_img * pairs, one, 0, unroll=2)
    tr_ref[...] = h_ref[...].T
    dh = jnp.zeros(x_ref.shape, F32)
    for k in range(3):
        for half, (w, g) in enumerate(((qm, gm_ref), (qo, go_ref))):
            at = (2 * k + half) * c
            g[k * d : (k + 1) * d, :] = nn(tr_ref[...], dqkv_ref[:, at : at + c]).astype(BF)
            dh = dh + nt(dqkv_ref[:, at : at + c], w[k])
    n, rr, _ = norm_forward(x_ref[...].astype(F32), w_ref[...])
    dv, dw = norm_backward(n, rr, w_ref[...], dh)
    dx_ref[...] = dy_ref[...] + dv
    dw_ref[...] = dw


def attention_backward(dy, x, gain, kept, qm, qo, om, oo):
    r, d = x.shape
    c = qm.shape[2]
    n_img = r // LP
    heads = d // HDIM
    return call(
        functools.partial(attention_backward_body, n_img),
        [out((r, d), F32), out((1, d), F32), out((3 * d + d, c), BF), out((3 * d + d, c), BF)],
        dy, x, gain, *kept, qm, qo, om, oo,
        scratch=[pltpu.VMEM((r, d), BF), pltpu.VMEM((r, 3 * d), BF), pltpu.VMEM((d, r), BF)],
        flops=4 * r * d * d * 4 + 8 * n_img * heads * LP * LP * LANES,
    )


def gelu_parts(z):
    phi = 0.5 * (1.0 + lax.erf(z * ROOT_HALF))
    return z * phi, phi + z * jnp.exp(-0.5 * z * z) * DENSITY_FACTOR


def tile_of(f):
    for t in (512, 256, 128):
        if f % t == 0:
            return t
    return f


def mlp_forward_body(x_ref, w_ref, im, io, tm, to, y_ref, h_ref, act_ref, slope_ref, acc_ref):
    step = pl.program_id(0)

    @pl.when(step == 0)
    def _():
        x = x_ref[...]
        _, _, h = norm_forward(x, w_ref[...])
        h_ref[...] = h
        acc_ref[...] = x

    for half, (wi, wo) in enumerate(((im, tm), (io, to))):
        a, s = gelu_parts(nn(h_ref[...], wi[...]))
        act = a.astype(BF)
        act_ref[half] = act
        slope_ref[half] = s.astype(BF)
        acc_ref[...] += nn(act, wo[...])

    @pl.when(step == pl.num_programs(0) - 1)
    def _():
        y_ref[...] = acc_ref[...]


def mlp_forward(x, gain, im, io, tm, to):
    r, d = x.shape
    f = im.shape[1]
    t = tile_of(f)
    col = pl.BlockSpec((d, t), lambda i: (0, i))
    row = pl.BlockSpec((t, d), lambda i: (i, 0))
    hid = pl.BlockSpec((2, r, t), lambda i: (0, 0, i))
    return call(
        mlp_forward_body,
        [out((r, d), F32), out((r, d), BF), out((2, r, f), BF), out((2, r, f), BF)],
        x, gain, im, io, tm, to, grid=(f // t,),
        in_specs=[whole((r, d)), whole((1, d)), col, col, row, row],
        out_specs=[whole((r, d)), whole((r, d)), hid, hid],
        scratch=[pltpu.VMEM((r, d), F32)], flops=8 * r * d * f,
    )


def mlp_backward_body(dy_ref, x_ref, w_ref, h_ref, act_ref, slope_ref, im, io, tm, to,
                      dx_ref, dw_ref, gim, gio, gtm, gto, da_ref, tr_ref, dh_ref):
    step = pl.program_id(0)

    @pl.when(step == 0)
    def _():
        da_ref[...] = dy_ref[...].astype(BF)
        tr_ref[...] = h_ref[...].T
        dh_ref[...] = jnp.zeros_like(dh_ref)

    for half, (wi, wo, gi, go) in enumerate(((im, tm, gim, gtm), (io, to, gio, gto))):
        dact = nt(da_ref[...], wo[...])
        dz = (dact * slope_ref[half].astype(F32)).astype(BF)
        go[...] = tn(act_ref[half], da_ref[...]).astype(BF)
        gi[...] = nn(tr_ref[...], dz).astype(BF)
        dh_ref[...] += nt(dz, wi[...])

    @pl.when(step == pl.num_programs(0) - 1)
    def _():
        n, rr, _ = norm_forward(x_ref[...], w_ref[...])
        dv, dw = norm_backward(n, rr, w_ref[...], dh_ref[...])
        dx_ref[...] = dy_ref[...] + dv
        dw_ref[...] = dw


def mlp_backward(dy, x, gain, h, act, slope, im, io, tm, to):
    r, d = x.shape
    f = im.shape[1]
    t = tile_of(f)
    col = pl.BlockSpec((d, t), lambda i: (0, i))
    row = pl.BlockSpec((t, d), lambda i: (i, 0))
    hid = pl.BlockSpec((2, r, t), lambda i: (0, 0, i))
    return call(
        mlp_backward_body,
        [out((r, d), F32), out((1, d), F32), out((d, f), BF), out((d, f), BF), out((f, d), BF), out((f, d), BF)],
        dy, x, gain, h, act, slope, im, io, tm, to, grid=(f // t,),
        in_specs=[whole((r, d)), whole((r, d)), whole((1, d)), whole((r, d)), hid, hid, col, col, row, row],
        out_specs=[whole((r, d)), whole((1, d)), col, col, row, row],
        scratch=[pltpu.VMEM((r, d), BF), pltpu.VMEM((d, r), BF), pltpu.VMEM((r, d), F32)], flops=16 * r * d * f,
    )


def routing_body(experts, capacity, half, cols_ref, rows_ref, tc_ref, tr_ref):
    n = cols_ref.shape[0]
    slots = experts * half

    def slot(rank, expert, live):
        core = (rank >= half).astype(I32)
        kept = (rank < capacity) & (live > 0)
        return jnp.where(kept, core * slots + expert * half + rank - core * half, -1)

    r0, r1, pc, lc = (cols_ref[:, i : i + 1] for i in range(4))
    s0, s1, pr, lr = (rows_ref[i : i + 1, :] for i in range(4))
    wide = lax.broadcasted_iota(I32, (n, LANES), 1)
    hot = (((wide == r0) | (wide == r1)) & (lc > 0)).astype(F32).astype(BF)
    earlier = (pr < pc).astype(F32).astype(BF)
    rank = nn(earlier, hot)
    for k, e in enumerate((r0, r1)):
        mine = jnp.sum(jnp.where(wide == e, rank, 0.0), axis=1, keepdims=True).astype(I32)
        tc_ref[:, k : k + 1] = slot(mine, e, lc)
    tall = lax.broadcasted_iota(I32, (max(experts, 8), n), 0)
    hot = (((tall == s0) | (tall == s1)) & (lr > 0)).astype(F32).astype(BF)
    earlier = (pc < pr).astype(F32).astype(BF)
    rank = nn(hot, earlier)
    for k, e in enumerate((s0, s1)):
        mine = jnp.sum(jnp.where(tall == e, rank, 0.0), axis=0, keepdims=True).astype(I32)
        tr_ref[k : k + 1, :] = slot(mine, e, lr)


def dispatch_body(ta_ref, tb_ref, a_ref, b_ref, y_ref):
    slots = y_ref.shape[0]
    n = a_ref.shape[0]
    place = lax.broadcasted_iota(I32, (slots, n), 0)
    total = None
    for t, v in ((ta_ref, a_ref), (tb_ref, b_ref)):
        hot = ((place == t[0:1, :]) | (place == t[1:2, :])).astype(F32).astype(BF)
        part = nn(hot, v[...])
        total = part if total is None else total + part
    y_ref[...] = total.astype(BF)


def dispatch(ta, tb, a, b, slots):
    return call(dispatch_body, [out((slots, a.shape[1]), BF)], ta, tb, a, b,
                flops=4 * slots * a.shape[0] * a.shape[1])[0]


def router_probs(h, router, experts):
    logits = nn(h, router)
    lane = lax.broadcasted_iota(I32, logits.shape, 1)
    logits = jnp.where(lane < experts, logits, -1e30)
    e = jnp.exp(logits - jnp.max(logits, axis=-1, keepdims=True))
    return e / jnp.sum(e, axis=-1, keepdims=True), lane


def expert_body(experts, x_ref, dy_ref, router_ref, mine_ref, im, io, tm, to,
                eout_ref, ret_ref, act_ref, dz_ref, wd_ref, acc_ref, dx_ref):
    step = pl.program_id(0)
    d = x_ref.shape[1]

    @pl.when(step == 0)
    def _():
        probs, _ = router_probs(x_ref[...], router_ref[...], experts)
        gate = jnp.sum(probs * mine_ref[...], axis=-1, keepdims=True)
        wd_ref[...] = (gate * dy_ref[...].astype(F32)).astype(BF)
        acc_ref[...] = jnp.zeros_like(acc_ref)
        dx_ref[...] = jnp.zeros_like(dx_ref)

    for half, (wi, wo) in enumerate(((im, tm), (io, to))):
        a, s = gelu_parts(nn(x_ref[...], wi[...]))
        act = a.astype(BF)
        act_ref[half] = act
        acc_ref[...] += nn(act, wo[...])
        dz = (nt(wd_ref[...], wo[...]) * s).astype(BF)
        dz_ref[half] = dz
        dx_ref[...] += nt(dz, wi[...])

    @pl.when(step == pl.num_programs(0) - 1)
    def _():
        eout = acc_ref[...].astype(BF)
        eout_ref[...] = eout
        ret_ref[:, :d] = dx_ref[...].astype(BF)
        dgate = jnp.sum(dy_ref[...].astype(F32) * eout.astype(F32), axis=-1, keepdims=True)
        high = dgate.astype(BF).astype(F32)
        lane = lax.broadcasted_iota(I32, (x_ref.shape[0], LANES), 1)
        ret_ref[:, d:] = jnp.where(lane < LANES // 2, high, dgate - high).astype(BF)


def expert_forward_backward(x, dy, router, mine, im, io, tm, to, experts):
    r, d = x.shape
    f = im.shape[1]
    t = tile_of(f) // 2
    col = pl.BlockSpec((d, t), lambda i: (0, i))
    row = pl.BlockSpec((t, d), lambda i: (i, 0))
    hid = pl.BlockSpec((2, r, t), lambda i: (0, 0, i))
    return call(
        functools.partial(expert_body, experts),
        [out((r, d), BF), out((r, d + LANES), BF), out((2, r, f), BF), out((2, r, f), BF), out((r, d), BF)],
        x, dy, router, mine, im, io, tm, to, grid=(f // t,),
        in_specs=[whole((r, d)), whole((r, d)), whole(router.shape), whole(mine.shape), col, col, row, row],
        out_specs=[whole((r, d)), whole((r, d + LANES)), hid, hid, whole((r, d))],
        scratch=[pltpu.VMEM((r, d), F32), pltpu.VMEM((r, d), F32)], flops=16 * r * d * f,
    )


def expert_weights_body(x_ref, wd_ref, act_ref, dz_ref, gm_ref, go_ref, xt_ref, wt_ref):
    @pl.when(pl.program_id(0) == 0)
    def _():
        xt_ref[...] = x_ref[...].T
        wt_ref[...] = wd_ref[...].T

    for half, g in enumerate((gm_ref, go_ref)):
        g[0] = nn(xt_ref[...], dz_ref[half]).astype(BF)
        g[1] = nn(wt_ref[...], act_ref[half]).astype(BF)


def expert_weights(x, wd, act, dz):
    r, d = x.shape
    f = act.shape[2]
    t = tile_of(f) // 2
    hid = pl.BlockSpec((2, r, t), lambda i: (0, 0, i))
    grad = pl.BlockSpec((2, d, t), lambda i: (0, 0, i))
    return call(
        expert_weights_body, [out((2, d, f), BF), out((2, d, f), BF)], x, wd, act, dz, grid=(f // t,),
        in_specs=[whole((r, d)), whole((r, d)), hid, hid], out_specs=[grad, grad],
        scratch=[pltpu.VMEM((d, r), BF), pltpu.VMEM((d, r), BF)], flops=8 * r * d * f,
    )


def merge_hots(t_ref, k, n, slots):
    lane = lax.broadcasted_iota(I32, (n, slots), 1)
    return (lane == t_ref[:, k : k + 1]).astype(F32).astype(BF)


def mixture_backward_body(experts, x_ref, w_ref, h_ref, router_ref, dy_ref, route_ref, ta_ref, tb_ref, a_ref, b_ref,
                          dx_ref, dw_ref, dr_ref):
    n, d = x_ref.shape
    slots = a_ref.shape[0]
    probs, lane = router_probs(h_ref[...], router_ref[...], experts)
    dh = jnp.zeros((n, d), F32)
    dsoft = jnp.zeros(probs.shape, F32)
    for k in range(TOPK):
        part = nn(merge_hots(ta_ref, k, n, slots), a_ref[...]) + nn(merge_hots(tb_ref, k, n, slots), b_ref[...])
        dh = dh + part[:, :d]
        dgate = part[:, d : d + 1] + part[:, d + LANES // 2 : d + LANES // 2 + 1]
        dsoft = dsoft + jnp.where(lane == route_ref[:, k : k + 1], dgate, 0.0)
    dlog = (probs * (dsoft - jnp.sum(dsoft * probs, axis=-1, keepdims=True))).astype(BF)
    dr_ref[...] = tn(h_ref[...], dlog)
    dh = dh + nt(dlog, router_ref[...])
    nrm, rr, _ = norm_forward(x_ref[...], w_ref[...])
    dv, dw = norm_backward(nrm, rr, w_ref[...], dh)
    dx_ref[...] = dy_ref[...].astype(F32) + dv
    dw_ref[...] = dw


def mixture_output_body(experts, x_ref, h_ref, router_ref, route_ref, live_ref, ta_ref, tb_ref, a_ref, b_ref, y_ref):
    n, d = x_ref.shape
    slots = a_ref.shape[0]
    probs, lane = router_probs(h_ref[...], router_ref[...], experts)
    total = x_ref[...]
    mixed = jnp.zeros((n, d), F32)
    for k in range(TOPK):
        gate = jnp.sum(jnp.where(lane == route_ref[:, k : k + 1], probs, 0.0), axis=-1, keepdims=True)
        part = nn(merge_hots(ta_ref, k, n, slots), a_ref[...]) + nn(merge_hots(tb_ref, k, n, slots), b_ref[...])
        mixed = mixed + gate * part
    y_ref[...] = (live_ref[...] * (total + mixed)).astype(BF)


def flip(axis, bit):
    size = lax.axis_size(axis)
    return [(i, i ^ bit) for i in range(size)]


def bits_of(axis):
    size = lax.axis_size(axis)
    return [1 << b for b in range(size.bit_length() - 1)]


def other_core(v):
    return lax.ppermute(v, "mdl", flip("mdl", 1))


def add16(a, b):
    return (a.astype(F32) + b.astype(F32)).astype(BF)


def halve(v, axis, bit):
    side = (lax.axis_index(axis) // bit) % 2
    n = v.shape[0] // 2
    keep = lax.dynamic_slice_in_dim(v, side * n, n)
    send = lax.dynamic_slice_in_dim(v, (1 - side) * n, n)
    return add16(keep, lax.ppermute(send, axis, flip(axis, bit)))


def double(v, axis, bit):
    side = (lax.axis_index(axis) // bit) % 2
    got = lax.ppermute(v, axis, flip(axis, bit))
    return jnp.where(side == 0, jnp.concatenate([v, got]), jnp.concatenate([got, v]))


def sum_everywhere(v):
    n = v.shape[0] // 2
    bits = bits_of("grp")
    parts = []
    for part, order in ((v[:n], bits), (v[n:], bits[::-1])):
        for bit in order:
            part = halve(part, "grp", bit)
        parts.append(part)
    size = lax.axis_size("exp")
    joined = jnp.concatenate(parts)
    rows = joined.shape[0] // size
    spread = lax.all_to_all(joined.reshape(size, rows, -1), "exp", 0, 0, tiled=True)
    mine = jnp.sum(spread.astype(F32), axis=0).astype(BF)
    joined = lax.all_gather(mine, "exp", axis=0, tiled=True)
    h = joined.shape[0] // 2
    done = []
    for part, order in ((joined[:h], bits), (joined[h:], bits[::-1])):
        for bit in order[::-1]:
            part = double(part, "grp", bit)
        done.append(part)
    return jnp.concatenate(done)


def shard_sum(v):
    bits = bits_of("grp")
    size = lax.axis_size("grp")
    two, d, f = v.shape
    n = f // 2
    done = []
    for part, order in ((v[:, :, :n], bits[::-1]), (v[:, :, n:], bits)):
        part = part.reshape((two,) + (2,) * len(bits) + (d // size, n))
        for bit in order:
            axis = len(bits) - bits.index(bit)
            side = (lax.axis_index("grp") // bit) % 2
            keep = lax.dynamic_slice_in_dim(part, side, 1, axis)
            send = lax.dynamic_slice_in_dim(part, 1 - side, 1, axis)
            part = add16(keep, lax.ppermute(send, "grp", flip("grp", bit)))
        done.append(part.reshape(two, d // size, n))
    return jnp.concatenate(done, axis=2)


def small_sum(v):
    for axis in ("mdl", "grp", "exp"):
        for bit in bits_of(axis):
            v = v + lax.ppermute(v, axis, flip(axis, bit))
    return v


def on_device(images, counts, routes, priority, gain_one, qkv_one, out_one, gain_two, fc_in, fc_out, gain_three,
              qkv_two, out_two, gain_four, router, expert_in, expert_out, cotangent):
    n_slot, length, d = images.shape
    experts = router.shape[1]
    n_mdl = lax.axis_size("mdl")
    capacity = (25 * L * TOPK + 8 * experts - 1) // (8 * experts)
    half = -(-(-(-capacity // n_mdl)) // 16) * 16
    slots = experts * half
    own_img = n_slot // n_mdl
    rows = own_img * LP
    core = lax.axis_index("mdl")

    def own(v, axis=0):
        return lax.dynamic_slice_in_dim(v, core * rows, rows, axis)

    def oth(v, axis=0):
        return lax.dynamic_slice_in_dim(v, (1 - core) * rows, rows, axis)

    def padded(v):
        return jnp.pad(v, ((0, 0), (0, LP - length), (0, 0))).reshape(n_slot * LP, -1)

    qm1, om1, im, tm, qm2, om2, em, fm = qkv_one, out_one, fc_in, fc_out, qkv_two, out_two, expert_in[0], expert_out[0]
    qo1, oo1, io, to, qo2, oo2, eo, fo = (other_core(w) for w in (qm1, om1, im, tm, qm2, om2, em, fm))
    g1, g2, g3, g4 = (g.reshape(1, d) for g in (gain_one, gain_two, gain_three, gain_four))
    router_wide = jnp.pad(router, ((0, 0), (0, LANES - experts)))
    mine = (jnp.arange(LANES, dtype=I32) == lax.axis_index("exp")).astype(F32)[None]

    img_live = (jnp.arange(n_slot, dtype=I32) < counts[0, 0]).astype(I32)
    live = jnp.pad(jnp.broadcast_to(img_live[:, None], (n_slot, length)), ((0, 0), (0, LP - length))).reshape(-1)
    x0 = own(padded(images))
    dy = padded(cotangent * img_live[:, None, None].astype(BF))
    route = padded(routes)
    prior = padded(priority.reshape(n_slot, length, 1))
    cols = jnp.concatenate([route, prior, live[:, None]], axis=1)
    slot_cols, slot_rows = call(
        functools.partial(routing_body, experts, capacity, half),
        [out((n_slot * LP, TOPK), I32), out((TOPK, n_slot * LP), I32)], cols, cols.T,
    )
    mine_rows = slot_rows - core * slots
    own_tokens_here = own(slot_cols) - core * slots
    own_tokens_there = own(slot_cols) - (1 - core) * slots
    own_tokens_there = jnp.where(own_tokens_there < slots, own_tokens_there, -1)
    peers = lax.axis_size("exp")

    def exchange(v):
        shaped = v.reshape(peers, v.shape[0] // peers, v.shape[1])
        return lax.all_to_all(shaped, "exp", 0, 0, tiled=True).reshape(v.shape)

    dy_out = dispatch(mine_rows[:, :rows], mine_rows[:, rows:], dy[:rows], dy[rows:], slots)
    dy_in = exchange(dy_out)

    x1, *kept1 = attention_forward(x0, g1, qm1, qo1, om1, oo1)
    x2, h2, act2, slope2 = mlp_forward(x1, g2, im, io, tm, to)
    x3, *kept3, h4 = attention_forward(x2, g3, qm2, qo2, om2, oo2, g4)

    h4_out = dispatch(own(mine_rows, 1), oth(mine_rows, 1), h4, other_core(h4), slots)
    h4_in = exchange(h4_out)
    eout, ret, eact, edz, ewd = expert_forward_backward(h4_in, dy_in, router_wide, mine, em, eo, fm, fo, experts)
    ret = exchange(ret)
    ret_there = other_core(ret)
    eout = exchange(eout)
    eout_there = other_core(eout)
    ge_mine, ge_other = expert_weights(h4_in, ewd, eact, edz)

    own_route = own(route)
    dx3, dg4, dr = call(
        functools.partial(mixture_backward_body, experts),
        [out((rows, d), F32), out((1, d), F32), out((d, LANES), F32)],
        x3, g4, h4, router_wide, own(dy), own_route, own_tokens_here, own_tokens_there, ret, ret_there,
        flops=8 * rows * slots * d,
    )
    [output] = call(
        functools.partial(mixture_output_body, experts), [out((rows, d), BF)],
        x3, h4, router_wide, own_route, own(live).astype(F32)[:, None], own_tokens_here, own_tokens_there, eout, eout_there,
        flops=8 * rows * slots * d,
    )
    expert_sum = shard_sum(add16(ge_mine, other_core(ge_other)))

    dx2, dg3, a2_mine, a2_other = attention_backward(dx3, x2, g3, kept3, qm2, qo2, om2, oo2)
    a2_sum = sum_everywhere(add16(a2_mine, other_core(a2_other)))
    dx1, dg2, gim, gio, gtm, gto = mlp_backward(dx2, x1, g2, h2, act2, slope2, im, io, tm, to)
    fi_sum = sum_everywhere(add16(gim, other_core(gio)))
    fo_sum = sum_everywhere(add16(gtm, other_core(gto)))
    dx0, dg1, a1_mine, a1_other = attention_backward(dx1, x0, g1, kept1, qm1, qo1, om1, oo1)
    a1_sum = sum_everywhere(add16(a1_mine, other_core(a1_other)))

    small = small_sum(jnp.concatenate([dg1, dg2, dg3, dg4, dr.T[:experts]], axis=0))

    def unpack(total):
        c = total.shape[1]
        qkv = total[: 3 * d].reshape(3, d, c).astype(F32)
        proj = jnp.concatenate([total[3 * d + i * c : 3 * d + (i + 1) * c] for i in range(d // c)], axis=1)
        return qkv, proj.astype(F32)

    def both(v):
        there = other_core(v)
        joined = jnp.where(core == 0, jnp.concatenate([v, there]), jnp.concatenate([there, v]))
        return joined.reshape(n_slot, LP, d)[:, :length]

    grad_qkv_one, grad_out_one = unpack(a1_sum)
    grad_qkv_two, grad_out_two = unpack(a2_sum)
    return (
        both(output), both(dx0.astype(BF)),
        small[0], grad_qkv_one, grad_out_one, small[1], fi_sum.astype(F32), fo_sum.astype(F32),
        small[2], grad_qkv_two, grad_out_two, small[3], small[4:].T,
        expert_sum[0].astype(F32)[None], expert_sum[1].astype(F32).T[None],
    )


def solution(mesh):
    token = P(("grp", "exp"), None, None)
    column, line = P(None, None, "mdl"), P("mdl", None)
    return jax.shard_map(
        on_device,
        mesh=mesh,
        in_specs=(token, P("grp", "exp"), token, P(("grp", "exp"), None), P(), column, line, P(), P(None, "mdl"), line,
                  P(), column, line, P(), P(), P("exp", None, "mdl"), P("exp", "mdl", None), token),
        out_specs=(token, token, P(), column, line, P(), P(None, "mdl"), line, P(), column, line, P(), P(),
                   P("exp", "grp", "mdl"), P("exp", "mdl", "grp")),
        check_vma=False,
    )
```

time: 1370 us -> 600 us (0.44)
  waiting for transfers between devices: 553 us -> 158 us
  local copies, waits for them, and re-layouts: 362 us -> 31.4 us
  matrix products: 158 us -> 0 us
  Pallas kernels: 0 us -> 154 us
  blocking collectives: 161 us -> 106 us
  starting transfers between devices: 28.4 us -> 80 us
  between operations: 17.7 us -> 2.8 us
  other arithmetic: 74.3 us -> 59.9 us
    psum x1 -> x0, waiting for transfers between devices: 410 us -> none  [on_device(): lax.psum((grad_gain_one, grad_qkv_one, grad_out_one, grad_gain_two, grad_...]
    dot_general x39 -> x0, matrix products: 158 us -> none  [the longest x1 20.8 us: on_device(): hidden = jnp.dot(incoming, expert_in[0], preferred_element_type=jnp.float32)]
    pallas_call x0 -> x13, Pallas kernels: none -> 154 us  [call(): pl.pallas_call(body, grid=grid, in_specs=in_specs, out_specs=out_specs, o...]
    ppermute x0 -> x59, waiting for transfers between devices: none -> 121 us  [the longest x16 73.7 us: halve(): return add16(keep, lax.ppermute(send, axis, flip(axis, bit)))]
    unnamed x284 -> x74, local copies, waits for them, and re-layouts: 95 us -> 10.4 us
    psum x1 -> x0, blocking collectives: 82.1 us -> none  [on_device(): lax.psum((grad_gain_one, grad_qkv_one, grad_out_one, grad_gain_two, grad_...]
    gather x16 -> x0, local copies, waits for them, and re-layouts: 75.7 us -> none  [the longest x5 22.4 us: on_device(): gate_values = jnp.take_along_axis(soft_rows, route_rows, axis=1)]
    all_gather x0 -> x4, blocking collectives: none -> 74 us  [sum_everywhere(): joined = lax.all_gather(mine, 'exp', axis=0, tiled=True)]
  transfers between devices with their start and end apart: 21 -> 66, of which waited for: 11 -> 18; matrix products, arithmetic and copies ran while one was open for 19% -> 14% of each run, Pallas kernels for 0% -> 22%
where the time goes in v1:
time: 600 us; the launch traced here: 593 us
  waiting for transfers between devices  158 us (26%)
  Pallas kernels  154 us (26%)
  blocking collectives  106 us (18%)
  starting transfers between devices  80 us (13%)
  other arithmetic  59.9 us (10%)
  local copies, waits for them, and re-layouts  31.4 us (5%)
    pallas_call x13, Pallas kernels, call(): pl.pallas_call(body, grid=grid, in_specs=in_specs, out_specs=out_specs, o...  154 us
    all_gather x4, blocking collectives, sum_everywhere(): joined = lax.all_gather(mine, 'exp', axis=0, tiled=True)  74 us
    ppermute x16, waiting for transfers between devices, halve(): return add16(keep, lax.ppermute(send, axis, flip(axis, bit)))  73.7 us
    all_to_all x3, waiting for transfers between devices, exchange(): return lax.all_to_all(shaped, 'exp', 0, 0, tiled=True).reshape(v.shape)  34.3 us
    all_to_all x1, blocking collectives, exchange(): return lax.all_to_all(shaped, 'exp', 0, 0, tiled=True).reshape(v.shape)  31.9 us
    ppermute x16, waiting for transfers between devices, double(): got = lax.ppermute(v, axis, flip(axis, bit))  30.9 us
    ppermute x16, starting transfers between devices, double(): got = lax.ppermute(v, axis, flip(axis, bit))  18.7 us
    convert_element_type x23, other arithmetic, add16(): return (a.astype(F32) + b.astype(F32)).astype(BF)  18.3 us
  transfers between devices with their start and end apart: 66, of which 18 were waited for; matrix products, arithmetic and copies ran while one was open for 14% of the time, Pallas kernels for 22%

profile of v1, /device:TPU:0, one launch (start us, length us, event | category | flops | bytes accessed | tf_op | source)
XLA Modules:
  0.0 592.7 jit_solution(695452574584386866)
XLA Ops:
  11.9 4.6 shard_map.292
  21.3 6.3 %all-to-all-start.1 = ((bf16[4,160,768]{2,1,0:T(8,128)(2,1)}), bf16[4,160,768]{2,1,0:T(8,128)(2,1)}, u32[]{:S(2)}, u32[]{:S(2)}) async-start(bf16[4,160,768]{2,1,0:T(8,128)(2,1)} %bitcast.67), calls=%async_computation.1 | async-start | bytes 1966080 | tf_op jit(solution)/shard_map/all_to_all | solution.py:592
  32.0 12.9 %shard_map.289 = (f32[416,768]{1,0:T(8,128)}, bf16[416,768]{1,0:T(8,128)(2,1)}, bf16[416,2304]{1,0:T(8,128)(2,1)}, bf16[24,208,208]{2,1,0:T(8,128)(2,1)}, bf16[416,768]{1,0:T(8,128)(2,1)}) custom-call(bf16[416,768]{1,0:T(8,128)(2,1)} %constant_dynamic-slice_fusion.26.refs_0_.x_ref, f32[1,768]{1,0:T(1,128)} %reshape.151.refs_1_.w_ref, ...), custom_call_target="tpu_custom_call" | custom-call | flops 2494562304 | bytes 11910144 | tf_op jit(solution)/shard_map/pallas_call | solution.py:63
  45.2 11.2 %shard_map.290 = (f32[416,768]{1,0:T(8,128)}, bf16[416,768]{1,0:T(8,128)(2,1)}, bf16[2,416,1536]{2,1,0:T(8,128)(2,1)}, bf16[2,416,1536]{2,1,0:T(8,128)(2,1)}) custom-call(f32[416,768]{1,0:T(8,128)} %get-tuple-element.56.x_ref, f32[1,768]{1,0:T(1,128)} %reshape.152.w_ref, bf16[768,1536]{1,0:T(8,128)(2,1)} %im.3, bf16[768,1536]{1,0:T(8,128)(2,1)} %collective-permute-done.2.io, ...), custom_call_target="tpu_custom_call" | custom-call | flops 3925868544 | bytes 17746944 | tf_op jit(solution)/shard_map/pallas_call | solution.py:63
  57.2 13.2 %shard_map.291 = (f32[416,768]{1,0:T(8,128)}, bf16[416,768]{1,0:T(8,128)(2,1)}, bf16[416,2304]{1,0:T(8,128)(2,1)}, bf16[24,208,208]{2,1,0:T(8,128)(2,1)}, bf16[4...) custom-call(f32[416,768]{1,0:T(8,128)} %get-tuple-element.57.refs_0_.x_ref, f32[1,768]{1,0:T(1,128)} %reshape.153.refs_1_.w_ref, ...), custom_call_target="tpu_custom_call" | custom-call | flops 2494562304 | bytes 13191168 | tf_op jit(solution)/shard_map/pallas_call | solution.py:63
  77.0 5.4 all-to-all-start
  83.8 23.4 %all-to-all-done = bf16[4,160,768]{2,1,0:T(8,128)(2,1)S(1)} async-done(((bf16[4,160,768]{2,1,0:T(8,128)(2,1)}), bf16[4,160,768]{2,1,0:T(8,128)(2,1)S(1)}, u32[]{:S(2)}, u32[]{:S(2)}) %all-to-all-start) | async-done | bytes 983072 | tf_op jit(solution)/shard_map/all_to_all | solution.py:592
  108.2 22.3 %shard_map.295 = (bf16[640,768]{1,0:T(8,128)(2,1)}, bf16[640,896]{1,0:T(8,128)(2,1)}, bf16[2,640,1536]{2,1,0:T(8,128)(2,1)}, bf16[2,640,1536]{2,1,0:T(8,128)(2,1)}, bf16[640,768]{1,0:T(8,128)(2,1)}) custom-call(bf16[640,768]{1,0:T(8,128)(2,1)} %bitcast.68, bf16[640,768]{1,0:T(8,128)(2,1)} %bitcast.10.dy_ref, bf16[768,128]{1,0:T(8,128)(2,1)} %pad.24.router_ref, ...), custom_call_target="tpu_custom_call" | custom-call | flops 12079595520 | bytes 22577664 | tf_op jit(solution)/shard_map/pallas_call | solution.py:63
  130.5 31.9 %all_to_all.40 = bf16[4,160,896]{2,1,0:T(8,128)(2,1)} all-to-all(bf16[4,160,896]{2,1,0:T(8,128)(2,1)} %bitcast.66), channel_id=1, replica_groups=mesh['grp'=4,'exp'=4,'mdl'=2] {'exp'}, dimensions={0} | all-to-all | bytes 2293760 | tf_op jit(solution)/shard_map/all_to_all | solution.py:592
  162.3 4.2 all-to-all-start.2
  166.6 12.2 %shard_map.301 = (bf16[2,768,1536]{2,1,0:T(8,128)(2,1)}, bf16[2,768,1536]{2,1,0:T(8,128)(2,1)}) custom-call(bf16[640,768]{1,0:T(8,128)(2,1)} %bitcast.69, bf16[640,768]{1,0:T(8,128)(2,1)} %get-tuple-element.92.wd_ref, bf16[2,640,1536]{2,1,0:T(8,128)(2,1)} %get-tuple-element.93.act_ref, bf16[2,640,1536]{2,1,0:T(8,128)(2,1)} %get-tuple-element.94.dz_ref), custom_call_target="tpu_custom_call" | custom-call | flops 6039797760 | bytes 19267584 | tf_op jit(solution)/shard_map/pallas_call | solution.py:63
  179.3 10.9 %all-to-all-done.2 = bf16[4,160,768]{2,1,0:T(8,128)(2,1)} async-done(((bf16[4,160,768]{2,1,0:T(8,128)(2,1)}), bf16[4,160,768]{2,1,0:T(8,128)(2,1)}, u32[]{:S(2)}, u32[]{:S(2)}) %all-to-all-start.2) | async-done | bytes 983072 | tf_op jit(solution)/shard_map/all_to_all | solution.py:592
  193.4 5.6 shard_map.296
  199.5 8.1 %shard_map.297 = (f32[416,768]{1,0:T(8,128)}, f32[1,768]{1,0:T(1,128)}, f32[768,128]{1,0:T(8,128)}) custom-call(f32[416,768]{1,0:T(8,128)} %get-tuple-element.58.x_ref, f32[1,768]{1,0:T(1,128)} %reshape.154.refs_6_.w_ref, bf16[416,768]{1,0:T(8,128)(2,1)} %get-tuple-element.59.a_ref.h_ref, bf16[768,128]{1,0:T(8,128)(2,1)} %pad.24.router_ref, ...), custom_call_target="tpu_custom_call" | custom-call | flops 1635778560 | bytes 6733568 | tf_op jit(solution)/shard_map/pallas_call | solution.py:63
  207.6 20.4 %shard_map.298 = (f32[416,768]{1,0:T(8,128)}, f32[1,768]{1,0:T(1,128)}, bf16[3072,384]{1,0:T(8,128)(2,1)}, bf16[3072,384]{1,0:T(8,128)(2,1)}) custom-call(f32[416,768]{1,0:T(8,128)} %get-tuple-element.64.dy_ref, f32[416,768]{1,0:T(8,128)} %get-tuple-element.57.refs_0_.x_ref, f32[1,768]{1,0:T(1,128)} %reshape.153.refs_1_.w_ref, ...), custom_call_target="tpu_custom_call" | custom-call | flops 4989124608 | bytes 18548736 | tf_op jit(solution)/shard_map/pallas_call | solution.py:63
  228.0 17.0 %shard_map.299 = (f32[416,768]{1,0:T(8,128)}, f32[1,768]{1,0:T(1,128)}, bf16[768,1536]{1,0:T(8,128)(2,1)}, bf16[768,1536]{1,0:T(8,128)(2,1)}, bf16[1536,768]{1,0:T(8,128)(2,1)}, /*index=5*/bf16[1536,768]{1,0:T(8,128)(2,1)}) custom-call(f32[416,768]{1,0:T(8,128)} %get-tuple-element.69.dy_ref, f32[416,768]{1,0:T(8,128)} %get-tuple-element.56.x_ref, ...), custom_call_target="tpu_custom_call" | custom-call | flops 7851737088 | bytes 28465152 | tf_op jit(solution)/shard_map/pallas_call | solution.py:63
  245.0 19.9 %shard_map.300 = (f32[416,768]{1,0:T(8,128)}, f32[1,768]{1,0:T(1,128)}, bf16[3072,384]{1,0:T(8,128)(2,1)}, bf16[3072,384]{1,0:T(8,128)(2,1)}) custom-call(f32[416,768]{1,0:T(8,128)} %get-tuple-element.73.dy_ref, bf16[416,768]{1,0:T(8,128)(2,1)} %constant_dynamic-slice_fusion.26.refs_0_.x_ref, f32[1,768]{1,0:T(1,128)} %reshape.151.refs_1_.w_ref, ...), custom_call_target="tpu_custom_call" | custom-call | flops 4989124608 | bytes 17909760 | tf_op jit(solution)/shard_map/pallas_call | solution.py:63
  276.2 3.8 collective-permute-done.16
  280.2 4.7 collective-permute-done.17
  294.4 3.6 add_convert_fusion
  311.9 28.5 %collective-permute-done.21 = bf16[768,384]{1,0:T(8,128)(2,1)S(1)} collective-permute-done((bf16[768,384]{1,0:T(8,128)(2,1)S(1)}, bf16[768,384]{1,0:T(8,128)(2,1)S(1)}, u32[]{:S(2)}, u32[]{:S(2)}) %collective-permute-start.21) | collective-permute-done | bytes 589856 | tf_op jit(solution)/shard_map/ppermute | solution.py:489
  343.9 21.2 %collective-permute-done.48 = bf16[768,384]{1,0:T(8,128)(2,1)S(1)} collective-permute-done((bf16[768,384]{1,0:T(8,128)(2,1)S(1)}, bf16[768,384]{1,0:T(8,128)(2,1)S(1)}, u32[]{:S(2)}, u32[]{:S(2)}) %collective-permute-start.48) | collective-permute-done | bytes 589856 | tf_op jit(solution)/shard_map/ppermute | solution.py:489
  370.1 9.7 %collective-permute-done.30 = bf16[192,1536]{1,0:T(8,128)(2,1)S(1)} collective-permute-done((bf16[192,1536]{1,0:T(8,128)(2,1)S(1)}, bf16[192,1536]{1,0:T(8,128)(2,1)S(1)}, u32[]{:S(2)}, u32[]{:S(2)}) %collective-permute-start.30) | collective-permute-done | bytes 589856 | tf_op jit(solution)/shard_map/ppermute | solution.py:489
  381.5 14.2 %collective-permute-done.37 = bf16[384,768]{1,0:T(8,128)(2,1)S(1)} collective-permute-done((bf16[384,768]{1,0:T(8,128)(2,1)S(1)}, bf16[384,768]{1,0:T(8,128)(2,1)S(1)}, u32[]{:S(2)}, u32[]{:S(2)}) %collective-permute-start.37) | collective-permute-done | bytes 589856 | tf_op jit(solution)/shard_map/ppermute | solution.py:489
  424.3 5.0 all-to-all-start.5
  445.8 20.9 %all_gather.12 = bf16[768,384]{1,0:T(8,128)(2,1)S(1)} all-gather(bf16[192,384]{1,0:T(8,128)(2,1)S(1)} %reduce_sum.48), channel_id=1, replica_groups=mesh['grp'=4,'exp'=4,'mdl'=2] {'exp'}, dimensions={0}, use_global_device_ids=true | all-gather | bytes 737280 | tf_op jit(solution)/shard_map/all_gather | solution.py:511
  471.6 16.8 %all_gather.13 = bf16[192,1536]{1,0:T(8,128)(2,1)S(1)} all-gather(bf16[48,1536]{1,0:T(8,128)(2,1)S(1)} %reduce_sum.49), channel_id=1, replica_groups=mesh['grp'=4,'exp'=4,'mdl'=2] {'exp'}, dimensions={0}, use_global_device_ids=true | all-gather | bytes 737280 | tf_op jit(solution)/shard_map/all_gather | solution.py:511
  492.9 21.0 %all_gather.14 = bf16[384,768]{1,0:T(8,128)(2,1)S(1)} all-gather(bf16[96,768]{1,0:T(8,128)(2,1)S(1)} %reduce_sum.50), channel_id=1, replica_groups=mesh['grp'=4,'exp'=4,'mdl'=2] {'exp'}, dimensions={0}, use_global_device_ids=true | all-gather | bytes 737280 | tf_op jit(solution)/shard_map/all_gather | solution.py:511
  514.2 15.3 %all_gather.15 = bf16[768,384]{1,0:T(8,128)(2,1)S(1)} all-gather(bf16[192,384]{1,0:T(8,128)(2,1)S(1)} %reduce_sum.51), channel_id=1, replica_groups=mesh['grp'=4,'exp'=4,'mdl'=2] {'exp'}, dimensions={0}, use_global_device_ids=true | all-gather | bytes 737280 | tf_op jit(solution)/shard_map/all_gather | solution.py:511
  547.4 5.4 collective-permute-done.26
  557.3 11.2 %collective-permute-done.53 = bf16[768,384]{1,0:T(8,128)(2,1)S(1)} collective-permute-done((bf16[768,384]{1,0:T(8,128)(2,1)S(1)}, bf16[768,384]{1,0:T(8,128)(2,1)S(1)}, u32[]{:S(2)}, u32[]{:S(2)}) %collective-permute-start.53) | collective-permute-done | bytes 589856 | tf_op jit(solution)/shard_map/ppermute | solution.py:494
  569.6 8.8 %collective-permute-done.51 = bf16[768,384]{1,0:T(8,128)(2,1)S(1)} collective-permute-done((bf16[768,384]{1,0:T(8,128)(2,1)S(1)}, bf16[768,384]{1,0:T(8,128)(2,1)S(1)}, u32[]{:S(2)}, u32[]{:S(2)}) %collective-permute-start.51) | collective-permute-done | bytes 589856 | tf_op jit(solution)/shard_map/ppermute | solution.py:494
  (329 shorter events, 170.3 us)
Async XLA Ops:
  0.6 44.3 %collective-permute-start.2 = (bf16[768,1536]{1,0:T(8,128)(2,1)}, bf16[768,1536]{1,0:T(8,128)(2,1)}, u32[]{:S(2)}, u32[]{:S(2)}) collective-permute-start(bf16[768,1536]{1,0:T(8,128)(2,1)} %im.3), channel_id=1, source_target_pairs={{0,1},{1,0},{2,3},{3,2},{4,5},{5,4},{6,7},{7,6},{8,9},{9,8},{10,11... | collective-permute-start | bytes 7077896 | tf_op jit(solution)/shard_map/ppermute | solution.py:477
  1.2 44.0 %collective-permute-start.3 = (bf16[1536,768]{1,0:T(8,128)(2,1)}, bf16[1536,768]{1,0:T(8,128)(2,1)}, u32[]{:S(2)}, u32[]{:S(2)}) collective-permute-start(bf16[1536,768]{1,0:T(8,128)(2,1)} %tm.3), channel_id=1, source_target_pairs={{0,1},{1,0},{2,3},{3,2},{4,5},{5,4},{6,7},{7,6},{8,9},{9,8},{10,11... | collective-permute-start | bytes 7077896 | tf_op jit(solution)/shard_map/ppermute | solution.py:477
  1.2 30.4 %collective-permute-start = (bf16[3,768,384]{2,1,0:T(8,128)(2,1)}, bf16[3,768,384]{2,1,0:T(8,128)(2,1)}, u32[]{:S(2)}, u32[]{:S(2)}) collective-permute-start(bf16[3,768,384]{2,1,0:T(8,128)(2,1)} %qm.3), channel_id=1, source_target_pairs={{0,1},{1,0},{2,3},{3,2},{4,5},{5,4},{6,7},{7,6},{8,9},{9,8},{10,11... | collective-permute-start | bytes 5308424 | tf_op jit(solution)/shard_map/ppermute | solution.py:477
  1.7 29.4 %collective-permute-start.1 = (bf16[384,768]{1,0:T(8,128)(2,1)}, bf16[384,768]{1,0:T(8,128)(2,1)}, u32[]{:S(2)}, u32[]{:S(2)}) collective-permute-start(bf16[384,768]{1,0:T(8,128)(2,1)} %om.3), channel_id=1, source_target_pairs={{0,1},{1,0},{2,3},{3,2},{4,5},{5,4},{6,7},{7,6},{8,9},{9,8},{10,11... | collective-permute-start | bytes 1769480 | tf_op jit(solution)/shard_map/ppermute | solution.py:477
  1.8 54.6 %collective-permute-start.4 = (bf16[3,768,384]{2,1,0:T(8,128)(2,1)}, bf16[3,768,384]{2,1,0:T(8,128)(2,1)}, u32[]{:S(2)}, u32[]{:S(2)}) collective-permute-start(bf16[3,768,384]{2,1,0:T(8,128)(2,1)} %qm.2), channel_id=1, source_target_pairs={{0,1},{1,0},{2,3},{3,2},{4,5},{5,4},{6,7},{7,6},{8,9},{9,8},{10,11... | collective-permute-start | bytes 5308424 | tf_op jit(solution)/shard_map/ppermute | solution.py:477
  21.3 55.6 %all-to-all-start.1 = ((bf16[4,160,768]{2,1,0:T(8,128)(2,1)}), bf16[4,160,768]{2,1,0:T(8,128)(2,1)}, u32[]{:S(2)}, u32[]{:S(2)}) async-start(bf16[4,160,768]{2,1,0:T(8,128)(2,1)} %bitcast.67), calls=%async_computation.1 | async-start | bytes 1966080 | tf_op jit(solution)/shard_map/all_to_all | solution.py:592
  31.5 24.9 %collective-permute-start.5 = (bf16[384,768]{1,0:T(8,128)(2,1)S(1)}, bf16[384,768]{1,0:T(8,128)(2,1)S(1)}, u32[]{:S(2)}, u32[]{:S(2)}) collective-permute-start(bf16[384,768]{1,0:T(8,128)(2,1)S(1)} %copy-done.29), channel_id=1, source_target_pairs={{0,1},{1,0},{2,3},{3,2},{4,5},{5,4},{6,7},{7,6},{8,9},{9,8},{10,11... | collective-permute-start | bytes 1769480 | tf_op jit(solution)/shard_map/ppermute | solution.py:477
  31.7 52.2 %collective-permute-start.7 = (bf16[768,1536]{1,0:T(8,128)(2,1)}, bf16[768,1536]{1,0:T(8,128)(2,1)}, u32[]{:S(2)}, u32[]{:S(2)}) collective-permute-start(bf16[768,1536]{1,0:T(8,128)(2,1)} %bitcast.11.im), channel_id=1, source_target_pairs={{0,1},{1,0},{2,3},{3,2},{4,5},{5,4},{6,7},{7,6},{8,9},{9,8},{10,11... | collective-permute-start | bytes 7077896 | tf_op jit(solution)/shard_map/ppermute | solution.py:477
  44.9 38.9 %collective-permute-start.8 = (bf16[1536,768]{1,0:T(8,128)(2,1)}, bf16[1536,768]{1,0:T(8,128)(2,1)}, u32[]{:S(2)}, u32[]{:S(2)}) collective-permute-start(bf16[1536,768]{1,0:T(8,128)(2,1)} %bitcast.75), channel_id=1, source_target_pairs={{0,1},{1,0},{2,3},{3,2},{4,5},{5,4},{6,7},{7,6},{8,9},{9,8},{10,11... | collective-permute-start | bytes 7077896 | tf_op jit(solution)/shard_map/ppermute | solution.py:477
  77.0 30.3 %all-to-all-start = ((bf16[4,160,768]{2,1,0:T(8,128)(2,1)}), bf16[4,160,768]{2,1,0:T(8,128)(2,1)S(1)}, u32[]{:S(2)}, u32[]{:S(2)}) async-start(bf16[4,160,768]{2,1,0:T(8,128)(2,1)} %bitcast.70), calls=%async_computation | async-start | bytes 1966080 | tf_op jit(solution)/shard_map/all_to_all | solution.py:592
  162.3 27.9 %all-to-all-start.2 = ((bf16[4,160,768]{2,1,0:T(8,128)(2,1)}), bf16[4,160,768]{2,1,0:T(8,128)(2,1)}, u32[]{:S(2)}, u32[]{:S(2)}) async-start(bf16[4,160,768]{2,1,0:T(8,128)(2,1)} %bitcast.13), calls=%async_computation.2 | async-start | bytes 1966080 | tf_op jit(solution)/shard_map/all_to_all | solution.py:592
  178.8 115.6 %collective-permute-start.54 = (bf16[2,768,1536]{2,1,0:T(8,128)(2,1)}, bf16[2,768,1536]{2,1,0:T(8,128)(2,1)}, u32[]{:S(2)}, u32[]{:S(2)}) collective-permute-start(bf16[2,768,1536]{2,1,0:T(8,128)(2,1)} %get-tuple-element.96), channel_id=1, source_target_pairs={{0,1},{1,0},{2,3},{3,2},{4,5},{5,4},{6,7},{7,6},{8,9},{9,8},{10,11... | collective-permute-start | bytes 14155784 | tf_op jit(solution)/shard_map/ppermute | solution.py:477
  199.0 87.9 %collective-permute-start.10 = (bf16[416,768]{1,0:T(8,128)(2,1)}, bf16[416,768]{1,0:T(8,128)(2,1)}, u32[]{:S(2)}, u32[]{:S(2)}) collective-permute-start(bf16[416,768]{1,0:T(8,128)(2,1)} %shard_map.296), channel_id=1, source_target_pairs={{0,1},{1,0},{2,3},{3,2},{4,5},{5,4},{6,7},{7,6},{8,9},{9,8},{10,11... | collective-permute-start | bytes 1916936 | tf_op jit(solution)/shard_map/ppermute | solution.py:477
  273.9 26.6 %collective-permute-start.18 = (bf16[3072,384]{1,0:T(8,128)(2,1)}, bf16[3072,384]{1,0:T(8,128)(2,1)S(1)}, u32[]{:S(2)}, u32[]{:S(2)}) collective-permute-start(bf16[3072,384]{1,0:T(8,128)(2,1)} %get-tuple-element.85), channel_id=1, source_target_pairs={{0,1},{1,0},{2,3},{3,2},{4,5},{5,4},{6,7},{7,6},{8,9},{9,8},{10,11... | collective-permute-start | bytes 7077896 | tf_op jit(solution)/shard_map/ppermute | solution.py:477
  298.9 103.1 %collective-permute-start.55 = (bf16[2,1,2,192,768]{4,3,0,2,1:T(8,128)(2,1)S(1)}, bf16[2,1,2,192,768]{4,3,0,2,1:T(8,128)(2,1)S(1)}, u32[]{:S(2)}, u32[]{:S(2)}) collective-permute-start(bf16[2,1,2,192,768]{4,3,0,2,1:T(8,128)(2,1)S(1)} %copy.108), channel_id=1, source_target_pairs={{0,16},{8,24},{16,0},{24,8},{1,17},{9,25},{17,1},{25,9},{2,18},{10... | collective-permute-start | bytes 3538952 | tf_op jit(solution)/shard_map/ppermute | solution.py:534
  300.5 103.4 %collective-permute-start.57 = (bf16[2,2,1,192,768]{4,3,0,2,1:T(8,128)(2,1)S(1)}, bf16[2,2,1,192,768]{4,3,0,2,1:T(8,128)(2,1)S(1)}, u32[]{:S(2)}, u32[]{:S(2)}) collective-permute-start(bf16[2,2,1,192,768]{4,3,0,2,1:T(8,128)(2,1)S(1)} %copy.110), channel_id=1, source_target_pairs={{0,8},{8,0},{16,24},{24,16},{1,9},{9,1},{17,25},{25,17},{2,10},{10... | collective-permute-start | bytes 3538952 | tf_op jit(solution)/shard_map/ppermute | solution.py:534
  303.0 37.4 %collective-permute-start.21 = (bf16[768,384]{1,0:T(8,128)(2,1)S(1)}, bf16[768,384]{1,0:T(8,128)(2,1)S(1)}, u32[]{:S(2)}, u32[]{:S(2)}) collective-permute-start(bf16[768,384]{1,0:T(8,128)(2,1)S(1)} %constant_dynamic-slice_fusion.19), channel_id=1, source_target_pairs={{0,16},{8,24},{16,0},{24,8},{1,17},{9,25},{17,1},{25,9},{2,18},{10... | collective-permute-start | bytes 1769480 | tf_op jit(solution)/shard_map/ppermute | solution.py:489
  307.0 35.1 %collective-permute-start.19 = (bf16[768,384]{1,0:T(8,128)(2,1)S(1)}, bf16[768,384]{1,0:T(8,128)(2,1)S(1)}, u32[]{:S(2)}, u32[]{:S(2)}) collective-permute-start(bf16[768,384]{1,0:T(8,128)(2,1)S(1)} %constant_dynamic-slice_fusion.21), channel_id=1, source_target_pairs={{0,8},{8,0},{16,24},{24,16},{1,9},{9,1},{17,25},{25,17},{2,10},{10... | collective-permute-start | bytes 1769480 | tf_op jit(solution)/shard_map/ppermute | solution.py:489
  309.2 59.3 %collective-permute-start.39 = (bf16[384,768]{1,0:T(8,128)(2,1)S(1)}, bf16[384,768]{1,0:T(8,128)(2,1)S(1)}, u32[]{:S(2)}, u32[]{:S(2)}) collective-permute-start(bf16[384,768]{1,0:T(8,128)(2,1)S(1)} %constant_dynamic-slice_fusion.11), channel_id=1, source_target_pairs={{0,16},{8,24},{16,0},{24,8},{1,17},{9,25},{17,1},{25,9},{2,18},{10... | collective-permute-start | bytes 1769480 | tf_op jit(solution)/shard_map/ppermute | solution.py:489
  366.8 32.7 %collective-permute-start.28 = (bf16[192,1536]{1,0:T(8,128)(2,1)S(1)}, bf16[192,1536]{1,0:T(8,128)(2,1)S(1)}, u32[]{:S(2)}, u32[]{:S(2)}) collective-permute-start(bf16[192,1536]{1,0:T(8,128)(2,1)S(1)} %constant_dynamic-slice_fusion.17), channel_id=1, source_target_pairs={{0,8},{8,0},{16,24},{24,16},{1,9},{9,1},{17,25},{25,17},{2,10},{10... | collective-permute-start | bytes 1769480 | tf_op jit(solution)/shard_map/ppermute | solution.py:489
  368.5 27.2 %collective-permute-start.37 = (bf16[384,768]{1,0:T(8,128)(2,1)S(1)}, bf16[384,768]{1,0:T(8,128)(2,1)S(1)}, u32[]{:S(2)}, u32[]{:S(2)}) collective-permute-start(bf16[384,768]{1,0:T(8,128)(2,1)S(1)} %constant_dynamic-slice_fusion.13), channel_id=1, source_target_pairs={{0,8},{8,0},{16,24},{24,16},{1,9},{9,1},{17,25},{25,17},{2,10},{10... | collective-permute-start | bytes 1769480 | tf_op jit(solution)/shard_map/ppermute | solution.py:489
  379.8 26.7 %collective-permute-start.22 = (bf16[384,384]{1,0:T(8,128)(2,1)S(1)}, bf16[384,384]{1,0:T(8,128)(2,1)S(1)}, u32[]{:S(2)}, u32[]{:S(2)}) collective-permute-start(bf16[384,384]{1,0:T(8,128)(2,1)S(1)} %constant_dynamic-slice_fusion.18), channel_id=1, source_target_pairs={{0,8},{8,0},{16,24},{24,16},{1,9},{9,1},{17,25},{25,17},{2,10},{10... | collective-permute-start | bytes 884744 | tf_op jit(solution)/shard_map/ppermute | solution.py:489
  440.5 48.0 %all-to-all-start.6 = ((bf16[4,96,768]{2,1,0:T(8,128)(2,1)}), bf16[4,96,768]{2,1,0:T(8,128)(2,1)S(1)}, u32[]{:S(2)}, u32[]{:S(2)}) async-start(bf16[4,96,768]{2,1,0:T(8,128)(2,1)} %bitcast.24), calls=%async_computation.6 | async-start | bytes 1179648 | tf_op jit(solution)/shard_map/all_to_all | solution.py:509
  466.7 68.5 %collective-permute-start.23 = (bf16[384,384]{1,0:T(8,128)(2,1)S(1)}, bf16[384,384]{1,0:T(8,128)(2,1)}, u32[]{:S(2)}, u32[]{:S(2)}) collective-permute-start(bf16[384,384]{1,0:T(8,128)(2,1)S(1)} %get-tuple-element.159), channel_id=1, source_target_pairs={{0,16},{8,24},{16,0},{24,8},{1,17},{9,25},{17,1},{25,9},{2,18},{10... | collective-permute-start | bytes 884744 | tf_op jit(solution)/shard_map/ppermute | solution.py:494
  468.7 63.6 %collective-permute-start.25 = (bf16[384,384]{1,0:T(8,128)(2,1)S(1)}, bf16[384,384]{1,0:T(8,128)(2,1)}, u32[]{:S(2)}, u32[]{:S(2)}) collective-permute-start(bf16[384,384]{1,0:T(8,128)(2,1)S(1)} %get-tuple-element.160), channel_id=1, source_target_pairs={{0,8},{8,0},{16,24},{24,16},{1,9},{9,1},{17,25},{25,17},{2,10},{10... | collective-permute-start | bytes 884744 | tf_op jit(solution)/shard_map/ppermute | solution.py:494
  488.4 25.6 %all-to-all-start.7 = ((bf16[4,192,384]{2,1,0:T(8,128)(2,1)}), bf16[4,192,384]{2,1,0:T(8,128)(2,1)S(1)}, u32[]{:S(2)}, u32[]{:S(2)}) async-start(bf16[4,192,384]{2,1,0:T(8,128)(2,1)} %bitcast.25), calls=%async_computation.7 | async-start | bytes 1179648 | tf_op jit(solution)/shard_map/all_to_all | solution.py:509
  492.0 37.5 %collective-permute-start.32 = (bf16[96,1536]{1,0:T(8,128)(2,1)S(1)}, bf16[96,1536]{1,0:T(8,128)(2,1)S(1)}, u32[]{:S(2)}, u32[]{:S(2)}) collective-permute-start(bf16[96,1536]{1,0:T(8,128)(2,1)S(1)} %get-tuple-element.157), channel_id=1, source_target_pairs={{0,16},{8,24},{16,0},{24,8},{1,17},{9,25},{17,1},{25,9},{2,18},{10... | collective-permute-start | bytes 884744 | tf_op jit(solution)/shard_map/ppermute | solution.py:494
  492.8 37.4 %collective-permute-start.34 = (bf16[96,1536]{1,0:T(8,128)(2,1)S(1)}, bf16[96,1536]{1,0:T(8,128)(2,1)S(1)}, u32[]{:S(2)}, u32[]{:S(2)}) collective-permute-start(bf16[96,1536]{1,0:T(8,128)(2,1)S(1)} %get-tuple-element.158), channel_id=1, source_target_pairs={{0,8},{8,0},{16,24},{24,16},{1,9},{9,1},{17,25},{25,17},{2,10},{10... | collective-permute-start | bytes 884744 | tf_op jit(solution)/shard_map/ppermute | solution.py:494
  539.5 44.7 %collective-permute-start.35 = (bf16[192,1536]{1,0:T(8,128)(2,1)S(1)}, bf16[192,1536]{1,0:T(8,128)(2,1)S(1)}, u32[]{:S(2)}, u32[]{:S(2)}) collective-permute-start(bf16[192,1536]{1,0:T(8,128)(2,1)S(1)} %maximum_select_fusion.13), channel_id=1, source_target_pairs={{0,16},{8,24},{16,0},{24,8},{1,17},{9,25},{17,1},{25,9},{2,18},{10... | collective-permute-start | bytes 1769480 | tf_op jit(solution)/shard_map/ppermute | solution.py:494
  544.9 39.7 %collective-permute-start.33 = (bf16[192,1536]{1,0:T(8,128)(2,1)S(1)}, bf16[192,1536]{1,0:T(8,128)(2,1)S(1)}, u32[]{:S(2)}, u32[]{:S(2)}) collective-permute-start(bf16[192,1536]{1,0:T(8,128)(2,1)S(1)} %maximum_select_fusion.12), channel_id=1, source_target_pairs={{0,8},{8,0},{16,24},{24,16},{1,9},{9,1},{17,25},{25,17},{2,10},{10... | collective-permute-start | bytes 1769480 | tf_op jit(solution)/shard_map/ppermute | solution.py:494
  552.9 32.1 %collective-permute-start.44 = (bf16[384,768]{1,0:T(8,128)(2,1)S(1)}, bf16[384,768]{1,0:T(8,128)(2,1)S(1)}, u32[]{:S(2)}, u32[]{:S(2)}) collective-permute-start(bf16[384,768]{1,0:T(8,128)(2,1)S(1)} %maximum_select_fusion.15), channel_id=1, source_target_pairs={{0,16},{8,24},{16,0},{24,8},{1,17},{9,25},{17,1},{25,9},{2,18},{10... | collective-permute-start | bytes 1769480 | tf_op jit(solution)/shard_map/ppermute | solution.py:494
  555.3 33.1 %collective-permute-start.42 = (bf16[384,768]{1,0:T(8,128)(2,1)S(1)}, bf16[384,768]{1,0:T(8,128)(2,1)S(1)}, u32[]{:S(2)}, u32[]{:S(2)}) collective-permute-start(bf16[384,768]{1,0:T(8,128)(2,1)S(1)} %maximum_select_fusion.14), channel_id=1, source_target_pairs={{0,8},{8,0},{16,24},{24,16},{1,9},{9,1},{17,25},{25,17},{2,10},{10... | collective-permute-start | bytes 1769480 | tf_op jit(solution)/shard_map/ppermute | solution.py:494
  (67 other events, 685.8 us)

commit v2 on v1

--- a/solution.py
+++ b/solution.py
@@ -21,6 +21,7 @@
 ROOT_HALF = 0.7071067811865476
 DENSITY_FACTOR = 0.3989422804014327
 VMEM_BYTES = 60 * 1024 * 1024
+MESH = pl.DeviceIdType.MESH
 
 
 def nn(a, b):
@@ -269,8 +270,11 @@
     for half, (wi, wo, gi, go) in enumerate(((im, tm, gim, gtm), (io, to, gio, gto))):
         dact = nt(da_ref[...], wo[...])
         dz = (dact * slope_ref[half].astype(F32)).astype(BF)
-        go[...] = tn(act_ref[half], da_ref[...]).astype(BF)
-        gi[...] = nn(tr_ref[...], dz).astype(BF)
+        gw = tn(act_ref[half], da_ref[...]).astype(BF)
+        t = gw.shape[0]
+        for part in range(gw.shape[1] // t):
+            go[part] = gw[:, part * t : (part + 1) * t]
+        gi[0] = nn(tr_ref[...], dz).astype(BF)
         dh_ref[...] += nt(dz, wi[...])
 
     @pl.when(step == pl.num_programs(0) - 1)
@@ -281,19 +285,21 @@
         dw_ref[...] = dw
 
 
-def mlp_backward(dy, x, gain, h, act, slope, im, io, tm, to):
+def mlp_backward(dy, x, gain, h, act, slope, im, io, tm, to, t):
     r, d = x.shape
     f = im.shape[1]
-    t = tile_of(f)
     col = pl.BlockSpec((d, t), lambda i: (0, i))
     row = pl.BlockSpec((t, d), lambda i: (i, 0))
     hid = pl.BlockSpec((2, r, t), lambda i: (0, 0, i))
+    gin = pl.BlockSpec((1, d, t), lambda i: (i, 0, 0))
+    gout = pl.BlockSpec((d // t, t, t), lambda i: (0, i, 0))
     return call(
         mlp_backward_body,
-        [out((r, d), F32), out((1, d), F32), out((d, f), BF), out((d, f), BF), out((f, d), BF), out((f, d), BF)],
+        [out((r, d), F32), out((1, d), F32), out((f // t, d, t), BF), out((f // t, d, t), BF),
+         out((d // t, f, t), BF), out((d // t, f, t), BF)],
         dy, x, gain, h, act, slope, im, io, tm, to, grid=(f // t,),
         in_specs=[whole((r, d)), whole((r, d)), whole((1, d)), whole((r, d)), hid, hid, col, col, row, row],
-        out_specs=[whole((r, d)), whole((1, d)), col, col, row, row],
+        out_specs=[whole((r, d)), whole((1, d)), gin, gin, gout, gout],
         scratch=[pltpu.VMEM((r, d), BF), pltpu.VMEM((d, r), BF), pltpu.VMEM((r, d), F32)], flops=16 * r * d * f,
     )
 
@@ -518,29 +524,204 @@
     return jnp.concatenate(done)
 
 
-def shard_sum(v):
-    bits = bits_of("grp")
-    size = lax.axis_size("grp")
-    two, d, f = v.shape
-    n = f // 2
-    done = []
-    for part, order in ((v[:, :, :n], bits[::-1]), (v[:, :, n:], bits)):
-        part = part.reshape((two,) + (2,) * len(bits) + (d // size, n))
-        for bit in order:
-            axis = len(bits) - bits.index(bit)
-            side = (lax.axis_index("grp") // bit) % 2
-            keep = lax.dynamic_slice_in_dim(part, side, 1, axis)
-            send = lax.dynamic_slice_in_dim(part, 1 - side, 1, axis)
-            part = add16(keep, lax.ppermute(send, "grp", flip("grp", bit)))
-        done.append(part.reshape(two, d // size, n))
-    return jnp.concatenate(done, axis=2)
-
-
 def small_sum(v):
     for axis in ("mdl", "grp", "exp"):
         for bit in bits_of(axis):
             v = v + lax.ppermute(v, axis, flip(axis, bit))
     return v
+
+
+def reduce_body(n_in, per, n_exp, *refs):
+    mine = refs[:n_in]
+    other = refs[n_in : 2 * n_in]
+    small_ref = refs[2 * n_in]
+    out_ref, sum_ref = refs[2 * n_in + 1 : 2 * n_in + 3]
+    (acc, got, r1, r2, zr, sm, load_sem, m_send, m_recv, x_send, x_recv, z_send, z_recv, s_send, s_recv) = refs[2 * n_in + 3 :]
+    n = n_in * per
+    rows = acc.shape[2]
+    h, q = rows // 2, rows // 4
+    t = q // n_exp
+    g = lax.axis_index("grp")
+    z = lax.axis_index("exp")
+    core = lax.axis_index("mdl")
+    bx, by = g % 2, g // 2
+    flat = {"x": g + 1 - 2 * bx, "y": g + 2 - 4 * by}
+    order = (("x", "y"), ("y", "x"))
+    bits = ((bx, by), (by, bx))
+
+    barrier = pltpu.get_barrier_semaphore()
+    others = [{"mdl": 1 - core}, {"grp": flat["x"]}, {"grp": flat["y"]}]
+    others += [{"exp": (z + o) % n_exp} for o in range(1, n_exp)]
+    for dev in others:
+        pl.semaphore_signal(barrier, inc=1, device_id=dev, device_id_type=MESH)
+    pl.semaphore_wait(barrier, len(others))
+
+    def load(c):
+        i, p = c // per, c % per
+        return pltpu.make_async_copy(mine[i].at[p], acc.at[c], load_sem.at[c])
+
+    def swap(c):
+        i, p = c // per, c % per
+        return pltpu.make_async_remote_copy(other[i].at[p], got.at[c], m_send.at[c], m_recv.at[c],
+                                            device_id={"mdl": 1 - core}, device_id_type=MESH)
+
+    for c in range(n):
+        swap(c).start()
+        load(c).start()
+
+    def swap_at(c):
+        return pltpu.make_async_remote_copy(other[0].at[0], got.at[c], m_send.at[c], m_recv.at[c],
+                                            device_id={"mdl": 1 - core}, device_id_type=MESH)
+
+    def load_at(c):
+        return pltpu.make_async_copy(mine[0].at[0], acc.at[c], load_sem.at[c])
+
+    def over(u, leg, src, dst, slot, c):
+        return pltpu.make_async_remote_copy(src, dst, x_send.at[slot, u, c], x_recv.at[slot, u, c],
+                                            device_id={"grp": flat[order[u][leg]]}, device_id_type=MESH)
+
+    def first(u, c):
+        return over(u, 0, acc.at[c, u, pl.ds(pl.multiple_of((1 - bits[u][0]) * h, h), h)], r1.at[c, u], 0, c)
+
+    def second(u, c):
+        return over(u, 1, r1.at[c, u, pl.ds(pl.multiple_of((1 - bits[u][1]) * q, q), q)], r2.at[c, u], 1, c)
+
+    def along(u, c, o):
+        return pltpu.make_async_remote_copy(
+            r2.at[c, u, pl.ds(pl.multiple_of(((z + o) % n_exp) * t, t), t)], zr.at[c, u, o - 1],
+            z_send.at[0, u, o - 1, c], z_recv.at[0, u, o - 1, c],
+            device_id={"exp": (z + o) % n_exp}, device_id_type=MESH)
+
+    def place(u):
+        return bits[u][0] * h + bits[u][1] * q
+
+    def back(u, c, o):
+        here = out_ref.at[c, u, pl.ds(pl.multiple_of(place(u) + z * t, t), t)]
+        return pltpu.make_async_remote_copy(here, here, z_send.at[1, u, o - 1, c], z_recv.at[1, u, o - 1, c],
+                                            device_id={"exp": (z + o) % n_exp}, device_id_type=MESH)
+
+    def third(u, c):
+        here = out_ref.at[c, u, pl.ds(pl.multiple_of(place(u), q), q)]
+        return over(u, 1, here, here, 2, c)
+
+    def fourth(u, c):
+        here = out_ref.at[c, u, pl.ds(pl.multiple_of(bits[u][0] * h, h), h)]
+        return over(u, 0, here, here, 3, c)
+
+    def plus(a, b):
+        return (a.astype(F32) + b.astype(F32)).astype(BF)
+
+    def s1(c):
+        load_at(c).wait()
+        swap_at(c).wait_recv()
+        for u in range(2):
+            acc[c, u] = plus(acc[c, u], got[c, u])
+            first(u, c).start()
+
+    def s2(c):
+        for u in range(2):
+            first(u, c).wait_recv()
+            keep = acc[c, u, pl.ds(pl.multiple_of(bits[u][0] * h, h), h)]
+            r1[c, u] = plus(keep, r1[c, u])
+            second(u, c).start()
+
+    def s3(c):
+        for u in range(2):
+            second(u, c).wait_recv()
+            keep = r1[c, u, pl.ds(pl.multiple_of(bits[u][1] * q, q), q)]
+            r2[c, u] = plus(keep, r2[c, u])
+            for o in range(1, n_exp):
+                along(u, c, o).start()
+
+    def s4(c):
+        for u in range(2):
+            total = r2[c, u, pl.ds(pl.multiple_of(z * t, t), t)].astype(F32)
+            for o in range(1, n_exp):
+                along(u, c, o).wait_recv()
+                total = total + zr[c, u, o - 1].astype(F32)
+            out_ref[c, u, pl.ds(pl.multiple_of(place(u) + z * t, t), t)] = total.astype(BF)
+            for o in range(1, n_exp):
+                back(u, c, o).start()
+
+    def s5(c):
+        for u in range(2):
+            for o in range(1, n_exp):
+                back(u, c, o).wait_recv()
+            third(u, c).start()
+
+    def s6(c):
+        for u in range(2):
+            third(u, c).wait_recv()
+            fourth(u, c).start()
+
+    def s7(c):
+        for u in range(2):
+            fourth(u, c).wait_recv()
+        swap_at(c).wait_send()
+        for u in range(2):
+            for make in (first, second, third, fourth):
+                make(u, c).wait_send()
+            for o in range(1, n_exp):
+                along(u, c, o).wait_send()
+                back(u, c, o).wait_send()
+
+    steps = (s1, s2, s3, s4, s5, s6, s7)
+
+    def wave(tau, _):
+        for s, step in enumerate(steps):
+            c = tau - s
+
+            @pl.when((c >= 0) & (c < n))
+            def _(step=step, c=c):
+                step(c)
+
+        return 0
+
+    lax.fori_loop(0, n + len(steps) - 1, wave, 0)
+
+    sm[0] = small_ref[...]
+    legs = [({"mdl": 1 - core}), ({"grp": flat["x"]}), ({"grp": flat["y"]})]
+    for i, dev in enumerate(legs):
+        cp = pltpu.make_async_remote_copy(sm.at[2 * i], sm.at[2 * i + 1], s_send.at[i], s_recv.at[i], device_id=dev, device_id_type=MESH)
+        cp.start()
+        cp.wait()
+        sm[2 * i + 2] = sm[2 * i] + sm[2 * i + 1]
+    base = 2 * len(legs) + 1
+    sm[pl.ds(base + z, 1)] = sm[pl.ds(base - 1, 1)]
+    cps = []
+    for o in range(1, n_exp):
+        cps.append(pltpu.make_async_remote_copy(sm.at[base - 1], sm.at[base + z], s_send.at[len(legs) + o - 1], s_recv.at[len(legs) + o - 1],
+                                                device_id={"exp": (z + o) % n_exp}, device_id_type=MESH))
+        cps[-1].start()
+    for cp in cps:
+        cp.wait()
+    total = sm[base]
+    for k in range(1, n_exp):
+        total = total + sm[base + k]
+    sum_ref[...] = total
+
+
+def reduce_all(mine, other, small, n_exp):
+    per, _, rows, c = mine[0].shape
+    n = len(mine) * per
+    h, q = rows // 2, rows // 4
+    t = q // n_exp
+    D = pltpu.SemaphoreType.DMA
+    any_ = pl.BlockSpec(memory_space=pl.ANY)
+    vm = pl.BlockSpec(memory_space=pltpu.VMEM)
+    return pl.pallas_call(
+        functools.partial(reduce_body, len(mine), per, n_exp),
+        in_specs=[any_] * (2 * len(mine)) + [vm],
+        out_specs=[vm, vm],
+        out_shape=[jax.ShapeDtypeStruct((n, 2, rows, c), BF), jax.ShapeDtypeStruct(small.shape, F32)],
+        scratch_shapes=[
+            pltpu.VMEM((n, 2, rows, c), BF), pltpu.VMEM((n, 2, rows, c), BF), pltpu.VMEM((n, 2, h, c), BF),
+            pltpu.VMEM((n, 2, q, c), BF), pltpu.VMEM((n, 2, n_exp - 1, t, c), BF), pltpu.VMEM((7 + n_exp,) + small.shape, F32),
+            D((n,)), D((n,)), D((n,)), D((4, 2, n)), D((4, 2, n)), D((2, 2, n_exp - 1, n)), D((2, 2, n_exp - 1, n)),
+            D((3 + n_exp,)), D((3 + n_exp,)),
+        ],
+        compiler_params=pltpu.CompilerParams(collective_id=0, has_side_effects=True, vmem_limit_bytes=VMEM_BYTES),
+    )(*mine, *other, small)
 
 
 def on_device(images, counts, routes, priority, gain_one, qkv_one, out_one, gain_two, fc_in, fc_out, gain_three,
@@ -552,6 +733,7 @@
     half = -(-(-(-capacity // n_mdl)) // 16) * 16
     slots = experts * half
     own_img = n_slot // n_mdl
+    f = fc_in.shape[1]
     rows = own_img * LP
     core = lax.axis_index("mdl")
 
@@ -619,34 +801,46 @@
         x3, h4, router_wide, own_route, own(live).astype(F32)[:, None], own_tokens_here, own_tokens_there, eout, eout_there,
         flops=8 * rows * slots * d,
     )
-    expert_sum = shard_sum(add16(ge_mine, other_core(ge_other)))
+    expert_sum = lax.psum_scatter(
+        add16(ge_mine, other_core(ge_other)), "grp", scatter_dimension=1, tiled=True)
 
     dx2, dg3, a2_mine, a2_other = attention_backward(dx3, x2, g3, kept3, qm2, qo2, om2, oo2)
-    a2_sum = sum_everywhere(add16(a2_mine, other_core(a2_other)))
-    dx1, dg2, gim, gio, gtm, gto = mlp_backward(dx2, x1, g2, h2, act2, slope2, im, io, tm, to)
-    fi_sum = sum_everywhere(add16(gim, other_core(gio)))
-    fo_sum = sum_everywhere(add16(gtm, other_core(gto)))
+    c = qkv_one.shape[2]
+    dx1, dg2, gim, gio, gtm, gto = mlp_backward(dx2, x1, g2, h2, act2, slope2, im, io, tm, to, c)
     dx0, dg1, a1_mine, a1_other = attention_backward(dx1, x0, g1, kept1, qm1, qo1, om1, oo1)
-    a1_sum = sum_everywhere(add16(a1_mine, other_core(a1_other)))
-
-    small = small_sum(jnp.concatenate([dg1, dg2, dg3, dg4, dr.T[:experts]], axis=0))
+    small = jnp.concatenate([dg1, dg2, dg3, dg4, dr.T[:experts]], axis=0)
+    mines, others = (a2_mine, gim, gtm, a1_mine), (a2_other, gio, gto, a1_other)
+
+    per = 2
+    unit = 4 * d // (2 * per)
+    if lax.axis_size("grp") == 4 and n_mdl == 2 and unit % (64 * peers) == 0 and f * 2 == 4 * d:
+        split = [[v.reshape(per, 2, unit, c) for v in side] for side in (mines, others)]
+        totals, small = reduce_all(*split, small, peers)
+        sums = totals.reshape(len(mines), 4 * d, c)
+    else:
+        flat = [[v.reshape(4 * d, c) for v in side] for side in (mines, others)]
+        sums = [sum_everywhere(add16(a, other_core(b))) for a, b in zip(*flat)]
+        small = small_sum(small)
 
     def unpack(total):
-        c = total.shape[1]
         qkv = total[: 3 * d].reshape(3, d, c).astype(F32)
-        proj = jnp.concatenate([total[3 * d + i * c : 3 * d + (i + 1) * c] for i in range(d // c)], axis=1)
-        return qkv, proj.astype(F32)
+        return qkv, panels(total[3 * d :].reshape(d // c, c, c))
+
+    def panels(v):
+        return jnp.concatenate([v[i] for i in range(v.shape[0])], axis=1).astype(F32)
 
     def both(v):
         there = other_core(v)
         joined = jnp.where(core == 0, jnp.concatenate([v, there]), jnp.concatenate([there, v]))
         return joined.reshape(n_slot, LP, d)[:, :length]
 
-    grad_qkv_one, grad_out_one = unpack(a1_sum)
-    grad_qkv_two, grad_out_two = unpack(a2_sum)
+    grad_qkv_two, grad_out_two = unpack(sums[0])
+    grad_fc_in = panels(sums[1].reshape(f // c, d, c))
+    grad_fc_out = panels(sums[2].reshape(d // c, f, c))
+    grad_qkv_one, grad_out_one = unpack(sums[3])
     return (
         both(output), both(dx0.astype(BF)),
-        small[0], grad_qkv_one, grad_out_one, small[1], fi_sum.astype(F32), fo_sum.astype(F32),
+        small[0], grad_qkv_one, grad_out_one, small[1], grad_fc_in, grad_fc_out,
         small[2], grad_qkv_two, grad_out_two, small[3], small[4:].T,
         expert_sum[0].astype(F32)[None], expert_sum[1].astype(F32).T[None],
     )

time: 600 us -> 520 us (0.87)
  Pallas kernels: 154 us -> 334 us
  waiting for transfers between devices: 158 us -> 57.4 us
  blocking collectives: 106 us -> 31.6 us
  starting transfers between devices: 80 us -> 19.3 us
  other arithmetic: 59.9 us -> 28.7 us
  between operations: 2.8 us -> 15.4 us
    pallas_call x0 -> x1, Pallas kernels: none -> 178 us  [reduce_all(): pl.pallas_call(functools.partial(reduce_body, len(mine), per, n_exp), in_...]
    ppermute x41 -> x0, waiting for transfers between devices: 119 us -> none  [the longest x16 73.7 us: halve(): return add16(keep, lax.ppermute(send, axis, flip(axis, bit)))]
    all_gather x4 -> x0, blocking collectives: 74 us -> none  [sum_everywhere(): joined = lax.all_gather(mine, 'exp', axis=0, tiled=True)]
    ppermute x41 -> x0, starting transfers between devices: 44.4 us -> none  [the longest x16 18.7 us: double(): got = lax.ppermute(v, axis, flip(axis, bit))]
    all_to_all x4 -> x0, starting transfers between devices: 15.5 us -> none  [sum_everywhere(): lax.all_to_all(joined.reshape(size, rows, -1), 'exp', 0, 0, tiled=True)]
    all_to_all x3, waiting for transfers between devices: 34.3 us -> 47.3 us  [exchange(): return lax.all_to_all(shaped, 'exp', 0, 0, tiled=True).reshape(v.shape)]
    convert_element_type x23 -> x1, other arithmetic: 18.3 us -> 5.76 us  [add16(): return (a.astype(F32) + b.astype(F32)).astype(BF)]
    ppermute x18 -> x14, waiting for transfers between devices: 1.98 us -> 10.1 us  [other_core(): return lax.ppermute(v, 'mdl', flip('mdl', 1))]
  transfers between devices with their start and end apart: 66 -> 18, of which waited for: 18 -> 4; matrix products, arithmetic and copies ran while one was open for 14% -> 8% of each run, Pallas kernels for 22% -> 58%
where the time goes in v2:
time: 520 us; the launch traced here: 514 us
  Pallas kernels  334 us (64%)
  waiting for transfers between devices  57.4 us (11%)
  blocking collectives  31.6 us (6%)
  other arithmetic  28.7 us (6%)
  local copies, waits for them, and re-layouts  27.6 us (5%)
  starting transfers between devices  19.3 us (4%)
  between operations  15.4 us (3%)
    pallas_call x1, Pallas kernels, reduce_all(): pl.pallas_call(functools.partial(reduce_body, len(mine), per, n_exp), in_...  178 us
    pallas_call x13, Pallas kernels, call(): pl.pallas_call(body, grid=grid, in_specs=in_specs, out_specs=out_specs, o...  156 us
    all_to_all x3, waiting for transfers between devices, exchange(): return lax.all_to_all(shaped, 'exp', 0, 0, tiled=True).reshape(v.shape)  47.3 us
    all_to_all x1, blocking collectives, exchange(): return lax.all_to_all(shaped, 'exp', 0, 0, tiled=True).reshape(v.shape)  31.6 us
    all_to_all x3, starting transfers between devices, exchange(): return lax.all_to_all(shaped, 'exp', 0, 0, tiled=True).reshape(v.shape)  15.9 us
  transfers between devices with their start and end apart: 18, of which 4 were waited for; matrix products, arithmetic and copies ran while one was open for 8% of the time, Pallas kernels for 58%

profile of v2, /device:TPU:0, one launch (start us, length us, event | category | flops | bytes accessed | tf_op | source)
XLA Modules:
  0.0 513.9 jit_solution(3030318704450447685)
XLA Ops:
  12.7 1.9 broadcast_multiply_fusion
  18.4 4.6 shard_map.292
  24.4 3.6 shard_map.294
  28.0 6.1 %all-to-all-start.1 = ((bf16[4,160,768]{2,1,0:T(8,128)(2,1)}), bf16[4,160,768]{2,1,0:T(8,128)(2,1)}, u32[]{:S(2)}, u32[]{:S(2)}) async-start(bf16[4,160,768]{2,1,0:T(8,128)(2,1)} %bitcast.87), calls=%async_computation.1 | async-start | bytes 1966080 | tf_op jit(solution)/shard_map/all_to_all | solution.py:774
  38.2 12.9 %shard_map.289 = (f32[416,768]{1,0:T(8,128)}, bf16[416,768]{1,0:T(8,128)(2,1)}, bf16[416,2304]{1,0:T(8,128)(2,1)}, bf16[24,208,208]{2,1,0:T(8,128)(2,1)}, bf16[416,768]{1,0:T(8,128)(2,1)}) custom-call(bf16[416,768]{1,0:T(8,128)(2,1)} %constant_dynamic-slice_fusion.4.refs_0_.x_ref, f32[1,768]{1,0:T(1,128)} %reshape.174.refs_1_.w_ref, ...), custom_call_target="tpu_custom_call" | custom-call | flops 2494562304 | bytes 11910144 | tf_op jit(solution)/shard_map/pallas_call | solution.py:64
  51.4 11.3 %shard_map.290 = (f32[416,768]{1,0:T(8,128)}, bf16[416,768]{1,0:T(8,128)(2,1)}, bf16[2,416,1536]{2,1,0:T(8,128)(2,1)}, bf16[2,416,1536]{2,1,0:T(8,128)(2,1)}) custom-call(f32[416,768]{1,0:T(8,128)} %get-tuple-element.58.x_ref, f32[1,768]{1,0:T(1,128)} %reshape.175.w_ref, bf16[768,1536]{1,0:T(8,128)(2,1)} %im.3, bf16[768,1536]{1,0:T(8,128)(2,1)} %collective-permute-done.2.io, ...), custom_call_target="tpu_custom_call" | custom-call | flops 3925868544 | bytes 17746944 | tf_op jit(solution)/shard_map/pallas_call | solution.py:64
  63.5 13.2 %shard_map.291 = (f32[416,768]{1,0:T(8,128)}, bf16[416,768]{1,0:T(8,128)(2,1)}, bf16[416,2304]{1,0:T(8,128)(2,1)}, bf16[24,208,208]{2,1,0:T(8,128)(2,1)}, bf16[4...) custom-call(f32[416,768]{1,0:T(8,128)} %get-tuple-element.59.refs_0_.x_ref, f32[1,768]{1,0:T(1,128)} %reshape.176.refs_1_.w_ref, ...), custom_call_target="tpu_custom_call" | custom-call | flops 2494562304 | bytes 13191168 | tf_op jit(solution)/shard_map/pallas_call | solution.py:64
  77.0 1.9 collective-permute-done.6.b_ref
  79.7 3.5 shard_map.293
  83.2 5.1 all-to-all-start
  90.0 23.2 %all-to-all-done = bf16[4,160,768]{2,1,0:T(8,128)(2,1)S(1)} async-done(((bf16[4,160,768]{2,1,0:T(8,128)(2,1)}), bf16[4,160,768]{2,1,0:T(8,128)(2,1)S(1)}, u32[]{:S(2)}, u32[]{:S(2)}) %all-to-all-start) | async-done | bytes 983072 | tf_op jit(solution)/shard_map/all_to_all | solution.py:774
  114.1 22.3 %shard_map.295 = (bf16[640,768]{1,0:T(8,128)(2,1)}, bf16[640,896]{1,0:T(8,128)(2,1)}, bf16[2,640,1536]{2,1,0:T(8,128)(2,1)}, bf16[2,640,1536]{2,1,0:T(8,128)(2,1)}, bf16[640,768]{1,0:T(8,128)(2,1)}) custom-call(bf16[640,768]{1,0:T(8,128)(2,1)} %bitcast.88, bf16[640,768]{1,0:T(8,128)(2,1)} %bitcast.10.dy_ref, bf16[768,128]{1,0:T(8,128)(2,1)} %pad.24.router_ref, ...), custom_call_target="tpu_custom_call" | custom-call | flops 12079595520 | bytes 22577664 | tf_op jit(solution)/shard_map/pallas_call | solution.py:64
  136.4 12.2 %shard_map.302 = (bf16[2,768,1536]{2,1,0:T(8,128)(2,1)}, bf16[2,768,1536]{2,1,0:T(8,128)(2,1)}) custom-call(bf16[640,768]{1,0:T(8,128)(2,1)} %bitcast.89, bf16[640,768]{1,0:T(8,128)(2,1)} %get-tuple-element.96.wd_ref, bf16[2,640,1536]{2,1,0:T(8,128)(2,1)} %get-tuple-element.97.act_ref, bf16[2,640,1536]{2,1,0:T(8,128)(2,1)} %get-tuple-element.98.dz_ref), custom_call_target="tpu_custom_call" | custom-call | flops 6039797760 | bytes 19267584 | tf_op jit(solution)/shard_map/pallas_call | solution.py:64
  148.7 8.1 %collective-permute-done.13 = bf16[2,768,1536]{2,1,0:T(8,128)(2,1)S(1)} collective-permute-done((bf16[2,768,1536]{2,1,0:T(8,128)(2,1)}, bf16[2,768,1536]{2,1,0:T(8,128)(2,1)S(1)}, u32[]{:S(2)}, u32[]{:S(2)}) %collective-permute-start.13) | collective-permute-done | bytes 4718624 | tf_op jit(solution)/shard_map/ppermute | solution.py:483
  156.8 5.8 %add_convert_fusion = bf16[2,768,1536]{2,1,0:T(8,128)(2,1)} fusion(bf16[2,768,1536]{2,1,0:T(8,128)(2,1)S(1)} %collective-permute-done.13, bf16[2,768,1536]{2,1,0:T(8,128)(2,1)} %get-tuple-element.99), kind=kLoop, calls=%fused_computation | loop fusion | flops 9437184 | bytes 14155776 | tf_op jit(solution)/shard_map/convert_element_type | solution.py:487
  163.8 31.6 %all_to_all.20 = bf16[4,160,896]{2,1,0:T(8,128)(2,1)} all-to-all(bf16[4,160,896]{2,1,0:T(8,128)(2,1)S(1)} %bitcast.86), channel_id=1, replica_groups=mesh['grp'=4,'exp'=4,'mdl'=2] {'exp'}, dimensions={0} | all-to-all | bytes 2293760 | tf_op jit(solution)/shard_map/all_to_all | solution.py:774
  195.3 4.7 all-to-all-start.2
  200.1 24.1 %all-to-all-done.2 = bf16[4,160,768]{2,1,0:T(8,128)(2,1)} async-done(((bf16[4,160,768]{2,1,0:T(8,128)(2,1)}), bf16[4,160,768]{2,1,0:T(8,128)(2,1)}, u32[]{:S(2)}, u32[]{:S(2)}) %all-to-all-start.2) | async-done | bytes 983072 | tf_op jit(solution)/shard_map/all_to_all | solution.py:774
  227.1 5.6 %shard_map.296 = bf16[416,768]{1,0:T(8,128)(2,1)} custom-call(f32[416,768]{1,0:T(8,128)} %get-tuple-element.60.x_ref, bf16[416,768]{1,0:T(8,128)(2,1)} %get-tuple-element.61.a_ref.h_ref, bf16[768,128]{1,0:T(8,128)(2,1)} %pad.24.router_ref, s32[416,2]{1,0:T(8,128)} %get-tuple-element.128.route_ref, f32[416,1]{1,0:T(8,128)} %copy.76.live_ref, ...), custom_call_target="tpu_custom_call" | custom-call | flops 1635778560 | bytes 4730240 | tf_op jit(solution)/shard_map/pallas_call | solution.py:64
  233.2 8.1 %shard_map.297 = (f32[416,768]{1,0:T(8,128)}, f32[1,768]{1,0:T(1,128)}, f32[768,128]{1,0:T(8,128)}) custom-call(f32[416,768]{1,0:T(8,128)} %get-tuple-element.60.x_ref, f32[1,768]{1,0:T(1,128)} %reshape.177.refs_6_.w_ref, bf16[416,768]{1,0:T(8,128)(2,1)} %get-tuple-element.61.a_ref.h_ref, bf16[768,128]{1,0:T(8,128)(2,1)} %pad.24.router_ref, ...), custom_call_target="tpu_custom_call" | custom-call | flops 1635778560 | bytes 6733568 | tf_op jit(solution)/shard_map/pallas_call | solution.py:64
  241.3 20.1 %shard_map.298 = (f32[416,768]{1,0:T(8,128)}, f32[1,768]{1,0:T(1,128)}, bf16[3072,384]{1,0:T(8,128)(2,1)}, bf16[3072,384]{1,0:T(8,128)(2,1)}) custom-call(f32[416,768]{1,0:T(8,128)} %get-tuple-element.66.dy_ref, f32[416,768]{1,0:T(8,128)} %get-tuple-element.59.refs_0_.x_ref, f32[1,768]{1,0:T(1,128)} %reshape.176.refs_1_.w_ref, ...), custom_call_target="tpu_custom_call" | custom-call | flops 4989124608 | bytes 18548736 | tf_op jit(solution)/shard_map/pallas_call | solution.py:64
  261.4 18.4 %shard_map.299 = (f32[416,768]{1,0:T(8,128)}, f32[1,768]{1,0:T(1,128)}, bf16[4,768,384]{2,1,0:T(8,128)(2,1)}, bf16[4,768,384]{2,1,0:T(8,128)(2,1)}, bf16[2,1536,...) custom-call(f32[416,768]{1,0:T(8,128)} %get-tuple-element.71.dy_ref, f32[416,768]{1,0:T(8,128)} %get-tuple-element.58.x_ref, ...), custom_call_target="tpu_custom_call" | custom-call | flops 7851737088 | bytes 28465152 | tf_op jit(solution)/shard_map/pallas_call | solution.py:64
  279.8 20.0 %shard_map.300 = (f32[416,768]{1,0:T(8,128)}, f32[1,768]{1,0:T(1,128)}, bf16[3072,384]{1,0:T(8,128)(2,1)}, bf16[3072,384]{1,0:T(8,128)(2,1)}) custom-call(f32[416,768]{1,0:T(8,128)} %get-tuple-element.75.dy_ref, bf16[416,768]{1,0:T(8,128)(2,1)} %constant_dynamic-slice_fusion.4.refs_0_.x_ref, f32[1,768]{1,0:T(1,128)} %reshape.174.refs_1_.w_ref, ...), custom_call_target="tpu_custom_call" | custom-call | flops 4989124608 | bytes 17909760 | tf_op jit(solution)/shard_map/pallas_call | solution.py:64
  302.2 178.3 %shard_map.301 = (bf16[8,2,768,384]{3,2,1,0:T(8,128)(2,1)}, f32[8,768]{1,0:T(8,128)}) custom-call(bf16[2,2,768,384]{3,2,1,0:T(8,128)(2,1)} %bitcast.78, bf16[2,2,768,384]{3,2,1,0:T(8,128)(2,1)} %bitcast.80, bf16[2,2,768,384]{3,2,1,0:T(8,128)(2,1)} %bitcast.82, bf16[2,2,768,384]{3,2,1,0:T(8,128)(2,1)} %bitcast.84, bf16[2,2,768,384]{3,2,1,0:T(8,128)(2,1)} %bitcast.79, ...), custom_call_target="tpu_custom_call" | custom-call | tf_op jit(solution)/shard_map/pallas_call | solution.py:712
  480.4 3.8 fusion.1
  484.6 2.0 convert.5
  486.6 2.0 convert.6
  490.7 1.9 fusion.2
  492.6 2.5 maximum_convert_fusion.1
  496.8 2.8 maximum_convert_fusion
  500.3 1.5 copy.81
  503.9 2.9 convert_bitcast_fusion
  (122 shorter events, 32.8 us)
Async XLA Ops:
  7.2 43.9 %collective-permute-start.2 = (bf16[768,1536]{1,0:T(8,128)(2,1)}, bf16[768,1536]{1,0:T(8,128)(2,1)}, u32[]{:S(2)}, u32[]{:S(2)}) collective-permute-start(bf16[768,1536]{1,0:T(8,128)(2,1)} %im.3), channel_id=1, source_target_pairs={{0,1},{1,0},{2,3},{3,2},{4,5},{5,4},{6,7},{7,6},{8,9},{9,8},{10,11... | collective-permute-start | bytes 7077896 | tf_op jit(solution)/shard_map/ppermute | solution.py:483
  7.7 43.7 %collective-permute-start.3 = (bf16[1536,768]{1,0:T(8,128)(2,1)}, bf16[1536,768]{1,0:T(8,128)(2,1)}, u32[]{:S(2)}, u32[]{:S(2)}) collective-permute-start(bf16[1536,768]{1,0:T(8,128)(2,1)} %tm.3), channel_id=1, source_target_pairs={{0,1},{1,0},{2,3},{3,2},{4,5},{5,4},{6,7},{7,6},{8,9},{9,8},{10,11... | collective-permute-start | bytes 7077896 | tf_op jit(solution)/shard_map/ppermute | solution.py:483
  7.8 30.1 %collective-permute-start = (bf16[3,768,384]{2,1,0:T(8,128)(2,1)}, bf16[3,768,384]{2,1,0:T(8,128)(2,1)}, u32[]{:S(2)}, u32[]{:S(2)}) collective-permute-start(bf16[3,768,384]{2,1,0:T(8,128)(2,1)} %qm.3), channel_id=1, source_target_pairs={{0,1},{1,0},{2,3},{3,2},{4,5},{5,4},{6,7},{7,6},{8,9},{9,8},{10,11... | collective-permute-start | bytes 5308424 | tf_op jit(solution)/shard_map/ppermute | solution.py:483
  8.2 29.4 %collective-permute-start.1 = (bf16[384,768]{1,0:T(8,128)(2,1)}, bf16[384,768]{1,0:T(8,128)(2,1)}, u32[]{:S(2)}, u32[]{:S(2)}) collective-permute-start(bf16[384,768]{1,0:T(8,128)(2,1)} %om.3), channel_id=1, source_target_pairs={{0,1},{1,0},{2,3},{3,2},{4,5},{5,4},{6,7},{7,6},{8,9},{9,8},{10,11... | collective-permute-start | bytes 1769480 | tf_op jit(solution)/shard_map/ppermute | solution.py:483
  8.3 54.4 %collective-permute-start.4 = (bf16[3,768,384]{2,1,0:T(8,128)(2,1)}, bf16[3,768,384]{2,1,0:T(8,128)(2,1)}, u32[]{:S(2)}, u32[]{:S(2)}) collective-permute-start(bf16[3,768,384]{2,1,0:T(8,128)(2,1)} %qm.2), channel_id=1, source_target_pairs={{0,1},{1,0},{2,3},{3,2},{4,5},{5,4},{6,7},{7,6},{8,9},{9,8},{10,11... | collective-permute-start | bytes 5308424 | tf_op jit(solution)/shard_map/ppermute | solution.py:483
  24.4 9.8 %copy-start.8 = (f32[768]{0:T(1024)S(1)}, f32[768]{0:T(1024)}, u32[]{:S(2)}) copy-start(f32[768]{0:T(1024)} %param.22) | copy-start | bytes 9220
  24.4 10.3 %copy-start.9 = (f32[768]{0:T(1024)S(1)}, f32[768]{0:T(1024)}, u32[]{:S(2)}) copy-start(f32[768]{0:T(1024)} %param.25) | copy-start | bytes 9220
  24.4 10.9 %copy-start.10 = (f32[768]{0:T(1024)S(1)}, f32[768]{0:T(1024)}, u32[]{:S(2)}) copy-start(f32[768]{0:T(1024)} %param.28) | copy-start | bytes 9220
  24.4 11.5 %copy-start.11 = (f32[768]{0:T(1024)S(1)}, f32[768]{0:T(1024)}, u32[]{:S(2)}) copy-start(f32[768]{0:T(1024)} %param.31) | copy-start | bytes 9220
  24.4 12.1 %copy-start = (bf16[4,197,768]{2,0,1:T(4,128)(2,1)S(1)}, bf16[4,197,768]{2,0,1:T(4,128)(2,1)}, u32[]{:S(2)}) copy-start(bf16[4,197,768]{2,0,1:T(4,128)(2,1)} %param.18) | copy-start | bytes 3631108
  28.0 55.2 %all-to-all-start.1 = ((bf16[4,160,768]{2,1,0:T(8,128)(2,1)}), bf16[4,160,768]{2,1,0:T(8,128)(2,1)}, u32[]{:S(2)}, u32[]{:S(2)}) async-start(bf16[4,160,768]{2,1,0:T(8,128)(2,1)} %bitcast.87), calls=%async_computation.1 | async-start | bytes 1966080 | tf_op jit(solution)/shard_map/all_to_all | solution.py:774
  37.7 24.9 %collective-permute-start.5 = (bf16[384,768]{1,0:T(8,128)(2,1)S(1)}, bf16[384,768]{1,0:T(8,128)(2,1)S(1)}, u32[]{:S(2)}, u32[]{:S(2)}) collective-permute-start(bf16[384,768]{1,0:T(8,128)(2,1)S(1)} %copy-done.17), channel_id=1, source_target_pairs={{0,1},{1,0},{2,3},{3,2},{4,5},{5,4},{6,7},{7,6},{8,9},{9,8},{10,11... | collective-permute-start | bytes 1769480 | tf_op jit(solution)/shard_map/ppermute | solution.py:483
  37.9 52.1 %collective-permute-start.7 = (bf16[768,1536]{1,0:T(8,128)(2,1)}, bf16[768,1536]{1,0:T(8,128)(2,1)}, u32[]{:S(2)}, u32[]{:S(2)}) collective-permute-start(bf16[768,1536]{1,0:T(8,128)(2,1)} %bitcast.11.im), channel_id=1, source_target_pairs={{0,1},{1,0},{2,3},{3,2},{4,5},{5,4},{6,7},{7,6},{8,9},{9,8},{10,11... | collective-permute-start | bytes 7077896 | tf_op jit(solution)/shard_map/ppermute | solution.py:483
  51.1 38.9 %collective-permute-start.8 = (bf16[1536,768]{1,0:T(8,128)(2,1)}, bf16[1536,768]{1,0:T(8,128)(2,1)}, u32[]{:S(2)}, u32[]{:S(2)}) collective-permute-start(bf16[1536,768]{1,0:T(8,128)(2,1)} %bitcast.96), channel_id=1, source_target_pairs={{0,1},{1,0},{2,3},{3,2},{4,5},{5,4},{6,7},{7,6},{8,9},{9,8},{10,11... | collective-permute-start | bytes 7077896 | tf_op jit(solution)/shard_map/ppermute | solution.py:483
  76.6 2.3 collective-permute-start.6
  79.7 8.8 %copy-start.7 = (bf16[768,4]{0,1:T(4,128)(2,1)S(1)}, bf16[768,4]{0,1:T(4,128)(2,1)}, u32[]{:S(2)}) copy-start(bf16[768,4]{0,1:T(4,128)(2,1)} %param.32) | copy-start | bytes 18436
  83.2 29.9 %all-to-all-start = ((bf16[4,160,768]{2,1,0:T(8,128)(2,1)}), bf16[4,160,768]{2,1,0:T(8,128)(2,1)S(1)}, u32[]{:S(2)}, u32[]{:S(2)}) async-start(bf16[4,160,768]{2,1,0:T(8,128)(2,1)} %bitcast.91), calls=%async_computation | async-start | bytes 1966080 | tf_op jit(solution)/shard_map/all_to_all | solution.py:774
  88.3 415.5 %reduce-scatter.2.cloned.1.call-start = ((), (), s32[]{:S(2)}) async-start(), calls=%async_computation.5 | async-start | bytes 5898240 | tf_op jit(solution)/shard_map/reduce_scatter | solution.py:804
  148.6 8.1 %collective-permute-start.13 = (bf16[2,768,1536]{2,1,0:T(8,128)(2,1)}, bf16[2,768,1536]{2,1,0:T(8,128)(2,1)S(1)}, u32[]{:S(2)}, u32[]{:S(2)}) collective-permute-start(bf16[2,768,1536]{2,1,0:T(8,128)(2,1)} %get-tuple-element.100), channel_id=1, source_target_pairs={{0,1},{1,0},{2,3},{3,2},{4,5},{5,4},{6,7},{7,6},{8,9},{9,8},{10,11... | collective-permute-start | bytes 14155784 | tf_op jit(solution)/shard_map/ppermute | solution.py:483
  162.5 1.3 copy-start.1
  195.3 28.8 %all-to-all-start.2 = ((bf16[4,160,768]{2,1,0:T(8,128)(2,1)}), bf16[4,160,768]{2,1,0:T(8,128)(2,1)}, u32[]{:S(2)}, u32[]{:S(2)}) async-start(bf16[4,160,768]{2,1,0:T(8,128)(2,1)} %bitcast.90), calls=%async_computation.2 | async-start | bytes 1966080 | tf_op jit(solution)/shard_map/all_to_all | solution.py:774
  200.0 33.2 %collective-permute-start.11 = (bf16[640,896]{1,0:T(8,128)(2,1)}, bf16[640,896]{1,0:T(8,128)(2,1)}, u32[]{:S(2)}, u32[]{:S(2)}) collective-permute-start(bf16[640,896]{1,0:T(8,128)(2,1)} %bitcast.18.a_ref), channel_id=1, source_target_pairs={{0,1},{1,0},{2,3},{3,2},{4,5},{5,4},{6,7},{7,6},{8,9},{9,8},{10,11... | collective-permute-start | bytes 3440648 | tf_op jit(solution)/shard_map/ppermute | solution.py:483
  224.2 3.0 collective-permute-start.9
  224.4 1.9 copy-start.5
  232.7 267.0 %collective-permute-start.10 = (bf16[416,768]{1,0:T(8,128)(2,1)}, bf16[416,768]{1,0:T(8,128)(2,1)S(1)}, u32[]{:S(2)}, u32[]{:S(2)}) collective-permute-start(bf16[416,768]{1,0:T(8,128)(2,1)} %shard_map.296), channel_id=1, source_target_pairs={{0,1},{1,0},{2,3},{3,2},{4,5},{5,4},{6,7},{7,6},{8,9},{9,8},{10,11... | collective-permute-start | bytes 1916936 | tf_op jit(solution)/shard_map/ppermute | solution.py:483
  279.8 21.5 %copy-start.4 = (f32[768,128]{1,0:T(8,128)S(1)}, f32[768,128]{1,0:T(8,128)}, u32[]{:S(2)}) copy-start(f32[768,128]{1,0:T(8,128)} %get-tuple-element.93) | copy-start | bytes 1179652
  299.8 1.7 copy-start.12
  299.8 1.7 copy-start.13
  299.8 1.7 copy-start.14
  299.8 1.7 copy-start.15
  301.4 200.3 %collective-permute-start.12 = (bf16[416,768]{1,0:T(8,128)(2,1)S(1)}, bf16[416,768]{1,0:T(8,128)(2,1)S(1)}, u32[]{:S(2)}, u32[]{:S(2)}) collective-permute-start(bf16[416,768]{1,0:T(8,128)(2,1)S(1)} %convert_element_type.85), channel_id=1, source_target_pairs={{0,1},{1,0},{2,3},{3,2},{4,5},{5,4},{6,7},{7,6},{8,9},{9,8},{10,11... | collective-permute-start | bytes 1916936 | tf_op jit(solution)/shard_map/ppermute | solution.py:483
  496.8 2.8 copy-start.3
  (5 other events, 4.8 us)
Sparse Core Ops, SparseCore 0:
  162.7 56.1 reduce-scatter.1

commit v3 on v2

--- a/solution.py
+++ b/solution.py
@@ -435,15 +435,15 @@
     return (lane == t_ref[:, k : k + 1]).astype(F32).astype(BF)
 
 
-def mixture_backward_body(experts, x_ref, w_ref, h_ref, router_ref, dy_ref, route_ref, ta_ref, tb_ref, a_ref, b_ref,
+def mixture_backward_body(experts, x_ref, w_ref, h_ref, router_ref, dy_ref, route_ref, ta_ref, tb_ref, ab_ref,
                           dx_ref, dw_ref, dr_ref):
     n, d = x_ref.shape
-    slots = a_ref.shape[0]
+    slots = ab_ref.shape[1]
     probs, lane = router_probs(h_ref[...], router_ref[...], experts)
     dh = jnp.zeros((n, d), F32)
     dsoft = jnp.zeros(probs.shape, F32)
     for k in range(TOPK):
-        part = nn(merge_hots(ta_ref, k, n, slots), a_ref[...]) + nn(merge_hots(tb_ref, k, n, slots), b_ref[...])
+        part = nn(merge_hots(ta_ref, k, n, slots), ab_ref[0]) + nn(merge_hots(tb_ref, k, n, slots), ab_ref[1])
         dh = dh + part[:, :d]
         dgate = part[:, d : d + 1] + part[:, d + LANES // 2 : d + LANES // 2 + 1]
         dsoft = dsoft + jnp.where(lane == route_ref[:, k : k + 1], dgate, 0.0)
@@ -456,15 +456,15 @@
     dw_ref[...] = dw
 
 
-def mixture_output_body(experts, x_ref, h_ref, router_ref, route_ref, live_ref, ta_ref, tb_ref, a_ref, b_ref, y_ref):
+def mixture_output_body(experts, x_ref, h_ref, router_ref, route_ref, live_ref, ta_ref, tb_ref, ab_ref, y_ref):
     n, d = x_ref.shape
-    slots = a_ref.shape[0]
+    slots = ab_ref.shape[1]
     probs, lane = router_probs(h_ref[...], router_ref[...], experts)
     total = x_ref[...]
     mixed = jnp.zeros((n, d), F32)
     for k in range(TOPK):
         gate = jnp.sum(jnp.where(lane == route_ref[:, k : k + 1], probs, 0.0), axis=-1, keepdims=True)
-        part = nn(merge_hots(ta_ref, k, n, slots), a_ref[...]) + nn(merge_hots(tb_ref, k, n, slots), b_ref[...])
+        part = nn(merge_hots(ta_ref, k, n, slots), ab_ref[0]) + nn(merge_hots(tb_ref, k, n, slots), ab_ref[1])
         mixed = mixed + gate * part
     y_ref[...] = (live_ref[...] * (total + mixed)).astype(BF)
 
@@ -724,6 +724,184 @@
     )(*mine, *other, small)
 
 
+def expert_exchange_body(experts, half, h4_ref, ta_ref, tb_ref, dyin_ref, router_ref, mine_ref, im, io, tm, to,
+                         ret_ref, eout_ref, gm_ref, go_ref,
+                         h_oth, part, xo, x, wi, wo, act, dz, wd, acc, dxa, rsend, gscr, xt, wt,
+                         w_sem, swap_sem, x_send, x_recv, r_send, r_recv, f_send, f_recv, g_sem):
+    n, d = h4_ref.shape
+    f = im.shape[1]
+    t = 256 if f % 256 == 0 else tile_of(f)
+    z = lax.axis_index("exp")
+    core = lax.axis_index("mdl")
+    partner = {"mdl": 1 - core}
+    size = experts
+    near_first = [1, 3, 2]
+
+    def there(j):
+        b0, b1 = z % 2, z // 2
+        if j & 1:
+            b0 = 1 - b0
+        if j & 2:
+            b1 = 1 - b1
+        return b0 + 2 * b1
+
+    loads = [pltpu.make_async_copy(src, dst, w_sem.at[k]) for k, (src, dst) in enumerate(
+        ((im, wi.at[0]), (io, wi.at[1]), (tm, wo.at[0]), (to, wo.at[1])))]
+    for cp in loads:
+        cp.start()
+    barrier = pltpu.get_barrier_semaphore()
+    for dev in [partner] + [{"exp": there(j)} for j in range(1, size)]:
+        pl.semaphore_signal(barrier, inc=1, device_id=dev, device_id_type=MESH)
+    pl.semaphore_wait(barrier, size)
+    swap = pltpu.make_async_remote_copy(h4_ref, h_oth, swap_sem.at[0], swap_sem.at[1], device_id=partner, device_id_type=MESH)
+    swap.start()
+
+    def hot(t_ref, e):
+        slot = lax.broadcasted_iota(I32, (half, n), 0) + e * half
+        return ((slot == t_ref[0:1, :]) | (slot == t_ref[1:2, :])).astype(F32).astype(BF)
+
+    def rows(j):
+        return slice(j * half, (j + 1) * half)
+
+    def place(e):
+        return pl.ds(pl.multiple_of(e * half, half), half)
+
+    for j in near_first + [0]:
+        part[rows(j), :] = nn(hot(ta_ref, there(j)), h4_ref[...])
+    swap.wait_recv()
+    sends = {}
+    for j in near_first + [0]:
+        block = (part[rows(j), :] + nn(hot(tb_ref, there(j)), h_oth[...])).astype(BF)
+        if j == 0:
+            x[rows(0), :] = block
+        else:
+            xo[rows(j), :] = block
+            sends[j] = pltpu.make_async_remote_copy(xo.at[rows(j)], x.at[rows(j)], x_send.at[j], x_recv.at[j],
+                                                    device_id={"exp": there(j)}, device_id_type=MESH)
+            sends[j].start()
+
+    returns, forwards = {}, {}
+
+    def forward(j):
+        here = ret_ref.at[0, place(there(j))]
+        forwards[j] = pltpu.make_async_remote_copy(here, ret_ref.at[1, place(there(j))], f_send.at[j], f_recv.at[j],
+                                                   device_id=partner, device_id_type=MESH)
+        forwards[j].start()
+
+    def run(blocks):
+        r0, r1 = blocks[0] * half, (blocks[-1] + 1) * half
+        m = r1 - r0
+        for j in blocks:
+            probs, _ = router_probs(x[rows(j), :], router_ref[...], experts)
+            gate = jnp.sum(probs * mine_ref[...], axis=-1, keepdims=True)
+            wd[rows(j), :] = (gate * dyin_ref[place(there(j)), :].astype(F32)).astype(BF)
+        acc[0:m, :] = jnp.zeros((m, d), F32)
+        dxa[0:m, :] = jnp.zeros((m, d), F32)
+
+        def tile(i, _):
+            at = pl.ds(pl.multiple_of(i * t, t), t)
+            for side in range(2):
+                a, s = gelu_parts(nn(x[r0:r1, :], wi[side, :, at]))
+                a = a.astype(BF)
+                act[side, r0:r1, at] = a
+                acc[0:m, :] += nn(a, wo[side, at, :])
+                g = (nt(wd[r0:r1, :], wo[side, at, :]) * s).astype(BF)
+                dz[side, r0:r1, at] = g
+                dxa[0:m, :] += nt(g, wi[side, :, at])
+            return 0
+
+        lax.fori_loop(0, f // t, tile, 0)
+        for b, j in enumerate(blocks):
+            here = slice(b * half, (b + 1) * half)
+            e_rows = acc[here, :].astype(BF)
+            eout_ref[place(there(j)), :] = e_rows
+            dgate = jnp.sum(dyin_ref[place(there(j)), :].astype(F32) * e_rows.astype(F32), axis=-1, keepdims=True)
+            high = dgate.astype(BF).astype(F32)
+            lane = lax.broadcasted_iota(I32, (half, LANES), 1)
+            extra = jnp.where(lane < LANES // 2, high, dgate - high).astype(BF)
+            if j == 0:
+                ret_ref[0, place(z), 0:d] = dxa[here, :].astype(BF)
+                ret_ref[0, place(z), d:] = extra
+                forward(0)
+            else:
+                rsend[rows(j), 0:d] = dxa[here, :].astype(BF)
+                rsend[rows(j), d:] = extra
+                returns[j] = pltpu.make_async_remote_copy(rsend.at[rows(j)], ret_ref.at[0, place(z)], r_send.at[j], r_recv.at[j],
+                                                          device_id={"exp": there(j)}, device_id_type=MESH)
+                returns[j].start()
+
+    for cp in loads:
+        cp.wait()
+    sends[1].wait_recv()
+    run([0, 1])
+    for j in near_first[1:]:
+        sends[j].wait_recv()
+        run([j])
+
+    xt[...] = x[...].T
+    wt[...] = wd[...].T
+
+    def stored(i, side, ref):
+        at = pl.ds(pl.multiple_of(i * t, t), t)
+        return pltpu.make_async_copy(gscr.at[side, :, :, at], ref.at[:, :, at], g_sem.at[side, i])
+
+    def weight_tile(i, _):
+        at = pl.ds(pl.multiple_of(i * t, t), t)
+        for side, ref in enumerate((gm_ref, go_ref)):
+            gscr[side, 0, :, at] = nn(xt[...], dz[side, :, at]).astype(BF)
+            gscr[side, 1, :, at] = nn(wt[...], act[side, :, at]).astype(BF)
+            stored(i, side, ref).start()
+        return 0
+
+    lax.fori_loop(0, f // t, weight_tile, 0)
+
+    def recv_return(j):
+        return pltpu.make_async_remote_copy(rsend.at[rows(j)], ret_ref.at[0, place(there(j))], r_send.at[j], r_recv.at[j],
+                                            device_id={"exp": there(j)}, device_id_type=MESH)
+
+    for j in near_first:
+        recv_return(j).wait_recv()
+        forward(j)
+
+    def drain(i, _):
+        for side, ref in enumerate((gm_ref, go_ref)):
+            stored(i, side, ref).wait()
+        return 0
+
+    lax.fori_loop(0, f // t, drain, 0)
+    swap.wait_send()
+    for j in range(size):
+        if j:
+            sends[j].wait_send()
+            returns[j].wait_send()
+        forwards[j].wait()
+
+
+def expert_exchange(h4, ta, tb, dy_in, router, mine, im, io, tm, to, experts, half):
+    n, d = h4.shape
+    f = im.shape[1]
+    s = experts * half
+    tiles = f // (256 if f % 256 == 0 else tile_of(f))
+    D, V = pltpu.SemaphoreType.DMA, pltpu.VMEM
+    any_ = pl.BlockSpec(memory_space=pl.ANY)
+    vm = pl.BlockSpec(memory_space=pltpu.VMEM)
+    return pl.pallas_call(
+        functools.partial(expert_exchange_body, experts, half),
+        in_specs=[vm] * 6 + [any_] * 4,
+        out_specs=[vm, vm, any_, any_],
+        out_shape=[out((2, s, d + LANES), BF), out((s, d), BF), out((2, d, f), BF), out((2, d, f), BF)],
+        scratch_shapes=[
+            V((n, d), BF), V((s, d), F32), V((s, d), BF), V((s, d), BF), V((2, d, f), BF), V((2, f, d), BF),
+            V((2, s, f), BF), V((2, s, f), BF), V((s, d), BF), V((2 * half, d), F32), V((2 * half, d), F32),
+            V((s, d + LANES), BF), V((2, 2, d, f), BF), V((d, s), BF), V((d, s), BF),
+            D((4,)), D((2,)), D((experts,)), D((experts,)), D((experts,)), D((experts,)), D((experts,)), D((experts,)),
+            D((2, tiles)),
+        ],
+        compiler_params=pltpu.CompilerParams(collective_id=1, has_side_effects=True, vmem_limit_bytes=VMEM_BYTES),
+        cost_estimate=pl.CostEstimate(flops=24 * s * d * f, bytes_accessed=20 * d * f, transcendentals=0),
+    )(h4, ta, tb, dy_in, router, mine, im, io, tm, to)
+
+
 def on_device(images, counts, routes, priority, gain_one, qkv_one, out_one, gain_two, fc_in, fc_out, gain_three,
               qkv_two, out_two, gain_four, router, expert_in, expert_out, cotangent):
     n_slot, length, d = images.shape
@@ -780,25 +958,24 @@
     x2, h2, act2, slope2 = mlp_forward(x1, g2, im, io, tm, to)
     x3, *kept3, h4 = attention_forward(x2, g3, qm2, qo2, om2, oo2, g4)
 
-    h4_out = dispatch(own(mine_rows, 1), oth(mine_rows, 1), h4, other_core(h4), slots)
-    h4_in = exchange(h4_out)
-    eout, ret, eact, edz, ewd = expert_forward_backward(h4_in, dy_in, router_wide, mine, em, eo, fm, fo, experts)
-    ret = exchange(ret)
-    ret_there = other_core(ret)
+    grouped = peers == 4 and experts == 4 and n_mdl == 2
+    if grouped:
+        ret, eout, ge_mine, ge_other = expert_exchange(
+            h4, own(mine_rows, 1), oth(mine_rows, 1), dy_in, router_wide, mine, em, eo, fm, fo, experts, half)
+    else:
+        h4_out = dispatch(own(mine_rows, 1), oth(mine_rows, 1), h4, other_core(h4), slots)
+        h4_in = exchange(h4_out)
+        eout, ret, eact, edz, ewd = expert_forward_backward(h4_in, dy_in, router_wide, mine, em, eo, fm, fo, experts)
+        ret = exchange(ret)
+        ret = jnp.stack([ret, other_core(ret)])
+        ge_mine, ge_other = expert_weights(h4_in, ewd, eact, edz)
     eout = exchange(eout)
-    eout_there = other_core(eout)
-    ge_mine, ge_other = expert_weights(h4_in, ewd, eact, edz)
 
     own_route = own(route)
     dx3, dg4, dr = call(
         functools.partial(mixture_backward_body, experts),
         [out((rows, d), F32), out((1, d), F32), out((d, LANES), F32)],
-        x3, g4, h4, router_wide, own(dy), own_route, own_tokens_here, own_tokens_there, ret, ret_there,
-        flops=8 * rows * slots * d,
-    )
-    [output] = call(
-        functools.partial(mixture_output_body, experts), [out((rows, d), BF)],
-        x3, h4, router_wide, own_route, own(live).astype(F32)[:, None], own_tokens_here, own_tokens_there, eout, eout_there,
+        x3, g4, h4, router_wide, own(dy), own_route, own_tokens_here, own_tokens_there, ret,
         flops=8 * rows * slots * d,
     )
     expert_sum = lax.psum_scatter(
@@ -808,6 +985,12 @@
     c = qkv_one.shape[2]
     dx1, dg2, gim, gio, gtm, gto = mlp_backward(dx2, x1, g2, h2, act2, slope2, im, io, tm, to, c)
     dx0, dg1, a1_mine, a1_other = attention_backward(dx1, x0, g1, kept1, qm1, qo1, om1, oo1)
+    eout, dx1 = lax.optimization_barrier((eout, dx1))
+    [output] = call(
+        functools.partial(mixture_output_body, experts), [out((rows, d), BF)],
+        x3, h4, router_wide, own_route, own(live).astype(F32)[:, None], own_tokens_here, own_tokens_there, jnp.stack([eout, other_core(eout)]),
+        flops=8 * rows * slots * d,
+    )
     small = jnp.concatenate([dg1, dg2, dg3, dg4, dr.T[:experts]], axis=0)
     mines, others = (a2_mine, gim, gtm, a1_mine), (a2_other, gio, gto, a1_other)
 

time: 520 us -> 473 us (0.910)
  waiting for transfers between devices: 57.4 us -> 7.8 us
  Pallas kernels: 334 us -> 366 us
  blocking collectives: 31.6 us -> 0 us
  starting transfers between devices: 19.3 us -> 13.6 us
    pallas_call x0 -> x1, Pallas kernels: none -> 66.8 us  [expert_exchange(): pl.pallas_call(functools.partial(expert_exchange_body, experts, half), in...]
    all_to_all x3 -> x2, waiting for transfers between devices: 47.3 us -> 0.01 us  [exchange(): return lax.all_to_all(shaped, 'exp', 0, 0, tiled=True).reshape(v.shape)]
    pallas_call x13 -> x10, Pallas kernels: 156 us -> 119 us  [call(): pl.pallas_call(body, grid=grid, in_specs=in_specs, out_specs=out_specs, o...]
    all_to_all x1 -> x0, blocking collectives: 31.6 us -> none  [exchange(): return lax.all_to_all(shaped, 'exp', 0, 0, tiled=True).reshape(v.shape)]
    all_to_all x3 -> x2, starting transfers between devices: 15.9 us -> 10.8 us  [exchange(): return lax.all_to_all(shaped, 'exp', 0, 0, tiled=True).reshape(v.shape)]
  transfers between devices with their start and end apart: 18 -> 15, of which waited for: 4 -> 1; matrix products, arithmetic and copies ran while one was open for 8% -> 11% of each run, Pallas kernels for 58% -> 64%
where the time goes in v3:
time: 473 us; the launch traced here: 465 us
  Pallas kernels  366 us (77%)
  other arithmetic  32.6 us (7%)
  local copies, waits for them, and re-layouts  29.7 us (6%)
  between operations  15.5 us (3%)
  starting transfers between devices  13.6 us (3%)
  waiting for transfers between devices  7.8 us (2%)
    pallas_call x1, Pallas kernels, reduce_all(): pl.pallas_call(functools.partial(reduce_body, len(mine), per, n_exp), in_...  180 us
    pallas_call x10, Pallas kernels, call(): pl.pallas_call(body, grid=grid, in_specs=in_specs, out_specs=out_specs, o...  119 us
    pallas_call x1, Pallas kernels, expert_exchange(): pl.pallas_call(functools.partial(expert_exchange_body, experts, half), in...  66.8 us
    all_to_all x2, starting transfers between devices, exchange(): return lax.all_to_all(shaped, 'exp', 0, 0, tiled=True).reshape(v.shape)  10.8 us
  transfers between devices with their start and end apart: 15, of which 1 were waited for; matrix products, arithmetic and copies ran while one was open for 11% of the time, Pallas kernels for 64%

profile of v3, /device:TPU:0, one launch (start us, length us, event | category | flops | bytes accessed | tf_op | source)
XLA Modules:
  0.0 465.2 jit_solution(6715917455352608701)
XLA Ops:
  11.6 1.9 broadcast_multiply_fusion
  14.6 1.8 pad_slice_fusion
  18.4 2.0 copy.75
  21.2 4.6 shard_map.292
  27.2 3.6 shard_map.293
  30.8 6.3 %all-to-all-start = ((bf16[4,160,768]{2,1,0:T(8,128)(2,1)}), bf16[4,160,768]{2,1,0:T(8,128)(2,1)}, u32[]{:S(2)}, u32[]{:S(2)}) async-start(bf16[4,160,768]{2,1,0:T(8,128)(2,1)} %bitcast.85), calls=%async_computation | async-start | bytes 1966080 | tf_op jit(solution)/shard_map/all_to_all | solution.py:952
  42.1 13.2 %shard_map.289 = (f32[416,768]{1,0:T(8,128)}, bf16[416,768]{1,0:T(8,128)(2,1)}, bf16[416,2304]{1,0:T(8,128)(2,1)}, bf16[24,208,208]{2,1,0:T(8,128)(2,1)}, bf16[416,768]{1,0:T(8,128)(2,1)}) custom-call(bf16[416,768]{1,0:T(8,128)(2,1)} %constant_dynamic-slice_fusion.4.refs_0_.x_ref, f32[1,768]{1,0:T(1,128)} %reshape.162.refs_1_.w_ref, ...), custom_call_target="tpu_custom_call" | custom-call | flops 2494562304 | bytes 11910144 | tf_op jit(solution)/shard_map/pallas_call | solution.py:64
  55.3 11.2 %shard_map.290 = (f32[416,768]{1,0:T(8,128)}, bf16[416,768]{1,0:T(8,128)(2,1)}, bf16[2,416,1536]{2,1,0:T(8,128)(2,1)}, bf16[2,416,1536]{2,1,0:T(8,128)(2,1)}) custom-call(f32[416,768]{1,0:T(8,128)} %get-tuple-element.56.x_ref, f32[1,768]{1,0:T(1,128)} %reshape.163.w_ref, bf16[768,1536]{1,0:T(8,128)(2,1)} %im.3, bf16[768,1536]{1,0:T(8,128)(2,1)} %collective-permute-done.2.io, ...), custom_call_target="tpu_custom_call" | custom-call | flops 3925868544 | bytes 17746944 | tf_op jit(solution)/shard_map/pallas_call | solution.py:64
  67.3 13.2 %shard_map.291 = (f32[416,768]{1,0:T(8,128)}, bf16[416,768]{1,0:T(8,128)(2,1)}, bf16[416,2304]{1,0:T(8,128)(2,1)}, bf16[24,208,208]{2,1,0:T(8,128)(2,1)}, bf16[4...) custom-call(f32[416,768]{1,0:T(8,128)} %get-tuple-element.57.refs_0_.x_ref, f32[1,768]{1,0:T(1,128)} %reshape.164.refs_1_.w_ref, ...), custom_call_target="tpu_custom_call" | custom-call | flops 2494562304 | bytes 13191168 | tf_op jit(solution)/shard_map/pallas_call | solution.py:64
  80.5 66.8 %shard_map.294 = (bf16[2,640,896]{2,1,0:T(8,128)(2,1)}, bf16[640,768]{1,0:T(8,128)(2,1)}, bf16[2,768,1536]{2,1,0:T(8,128)(2,1)}, bf16[2,768,1536]{2,1,0:T(8,128)(2,1)}) custom-call(bf16[416,768]{1,0:T(8,128)(2,1)} %get-tuple-element.59.h4_ref.h_ref, s32[2,416]{1,0:T(2,128)} %get-tuple-element.123.ta_ref, s32[2,416]{1,0:T(2,128)} %get-tuple-element.122.tb_ref, ...), custom_call_target="tpu_custom_call" | custom-call | flops 18119393280 | bytes 23592960 | tf_op jit(solution)/shard_map/pallas_call | solution.py:888
  147.7 7.7 %collective-permute-done.11 = bf16[2,768,1536]{2,1,0:T(8,128)(2,1)S(1)} collective-permute-done((bf16[2,768,1536]{2,1,0:T(8,128)(2,1)}, bf16[2,768,1536]{2,1,0:T(8,128)(2,1)S(1)}, u32[]{:S(2)}, u32[]{:S(2)}) %collective-permute-start.11) | collective-permute-done | bytes 4718624 | tf_op jit(solution)/shard_map/ppermute | solution.py:483
  155.5 5.8 %add_convert_fusion = bf16[2,768,1536]{2,1,0:T(8,128)(2,1)} fusion(bf16[2,768,1536]{2,1,0:T(8,128)(2,1)S(1)} %collective-permute-done.11, bf16[2,768,1536]{2,1,0:T(8,128)(2,1)} %get-tuple-element.95), kind=kLoop, calls=%fused_computation | loop fusion | flops 9437184 | bytes 14155776 | tf_op jit(solution)/shard_map/convert_element_type | solution.py:487
  165.6 4.5 all-to-all-start.1
  170.1 8.1 %shard_map.295 = (f32[416,768]{1,0:T(8,128)}, f32[1,768]{1,0:T(1,128)}, f32[768,128]{1,0:T(8,128)}) custom-call(f32[416,768]{1,0:T(8,128)} %get-tuple-element.58.x_ref, f32[1,768]{1,0:T(1,128)} %reshape.165.refs_6_.w_ref, bf16[416,768]{1,0:T(8,128)(2,1)} %get-tuple-element.59.h4_ref.h_ref, bf16[768,128]{1,0:T(8,128)(2,1)} %pad.24.router_ref, ...), custom_call_target="tpu_custom_call" | custom-call | flops 1635778560 | bytes 6733568 | tf_op jit(solution)/shard_map/pallas_call | solution.py:64
  178.3 20.5 %shard_map.296 = (f32[416,768]{1,0:T(8,128)}, f32[1,768]{1,0:T(1,128)}, bf16[3072,384]{1,0:T(8,128)(2,1)}, bf16[3072,384]{1,0:T(8,128)(2,1)}) custom-call(f32[416,768]{1,0:T(8,128)} %get-tuple-element.64.dy_ref, f32[416,768]{1,0:T(8,128)} %get-tuple-element.57.refs_0_.x_ref, f32[1,768]{1,0:T(1,128)} %reshape.164.refs_1_.w_ref, ...), custom_call_target="tpu_custom_call" | custom-call | flops 4989124608 | bytes 18548736 | tf_op jit(solution)/shard_map/pallas_call | solution.py:64
  198.8 18.6 %shard_map.297 = (f32[416,768]{1,0:T(8,128)}, f32[1,768]{1,0:T(1,128)}, bf16[4,768,384]{2,1,0:T(8,128)(2,1)}, bf16[4,768,384]{2,1,0:T(8,128)(2,1)}, bf16[2,1536,...) custom-call(f32[416,768]{1,0:T(8,128)} %get-tuple-element.69.dy_ref, f32[416,768]{1,0:T(8,128)} %get-tuple-element.56.x_ref, ...), custom_call_target="tpu_custom_call" | custom-call | flops 7851737088 | bytes 28465152 | tf_op jit(solution)/shard_map/pallas_call | solution.py:64
  217.4 19.9 %shard_map.299 = (f32[416,768]{1,0:T(8,128)}, f32[1,768]{1,0:T(1,128)}, bf16[3072,384]{1,0:T(8,128)(2,1)}, bf16[3072,384]{1,0:T(8,128)(2,1)}) custom-call(f32[416,768]{1,0:T(8,128)} %get-tuple-element.73.dy_ref, bf16[416,768]{1,0:T(8,128)(2,1)} %constant_dynamic-slice_fusion.4.refs_0_.x_ref, f32[1,768]{1,0:T(1,128)} %reshape.162.refs_1_.w_ref, ...), custom_call_target="tpu_custom_call" | custom-call | flops 4989124608 | bytes 17909760 | tf_op jit(solution)/shard_map/pallas_call | solution.py:64
  237.4 2.2 convert_element_type.85
  240.5 180.5 %shard_map.300 = (bf16[8,2,768,384]{3,2,1,0:T(8,128)(2,1)}, f32[8,768]{1,0:T(8,128)}) custom-call(bf16[2,2,768,384]{3,2,1,0:T(8,128)(2,1)} %bitcast.77, bf16[2,2,768,384]{3,2,1,0:T(8,128)(2,1)} %bitcast.79, bf16[2,2,768,384]{3,2,1,0:T(8,128)(2,1)} %bitcast.81, bf16[2,2,768,384]{3,2,1,0:T(8,128)(2,1)} %bitcast.83, bf16[2,2,768,384]{3,2,1,0:T(8,128)(2,1)} %bitcast.78, ...), custom_call_target="tpu_custom_call" | custom-call | tf_op jit(solution)/shard_map/pallas_call | solution.py:712
  421.0 3.9 fusion.1
  425.2 2.0 convert.5
  427.3 2.0 convert.6
  432.2 1.5 slice_bitcast_fusion.4
  433.7 1.9 fusion.2
  435.5 2.5 maximum_convert_fusion.1
  438.1 1.4 pad_maximum_fusion.ab_ref
  439.5 5.8 %shard_map.298 = bf16[416,768]{1,0:T(8,128)(2,1)} custom-call(f32[416,768]{1,0:T(8,128)} %get-tuple-element.58.x_ref, bf16[416,768]{1,0:T(8,128)(2,1)} %get-tuple-element.59.h4_ref.h_ref, bf16[768,128]{1,0:T(8,128)(2,1)} %pad.24.router_ref, s32[416,2]{1,0:T(8,128)} %constant_dynamic-slice_fusion.3.route_ref, f32[416,1]{1,0:T(8,128)} %copy.77.live_ref, ...), custom_call_target="tpu_custom_call" | custom-call | flops 1635778560 | bytes 4730240 | tf_op jit(solution)/shard_map/pallas_call | solution.py:64
  446.5 2.8 maximum_convert_fusion
  449.3 2.0 maximum_select_fusion.1
  451.4 1.5 copy.82
  453.5 1.5 copy.81
  455.0 2.9 convert_bitcast_fusion
  (122 shorter events, 25.5 us)
Async XLA Ops:
  7.2 9.3 %collective-permute-start = (bf16[3,768,384]{2,1,0:T(8,128)(2,1)}, bf16[3,768,384]{2,1,0:T(8,128)(2,1)}, u32[]{:S(2)}, u32[]{:S(2)}) collective-permute-start(bf16[3,768,384]{2,1,0:T(8,128)(2,1)} %qm.3), channel_id=1, source_target_pairs={{0,1},{1,0},{2,3},{3,2},{4,5},{5,4},{6,7},{7,6},{8,9},{9,8},{10,11... | collective-permute-start | bytes 5308424 | tf_op jit(solution)/shard_map/ppermute | solution.py:483
  7.7 34.4 %collective-permute-start.2 = (bf16[768,1536]{1,0:T(8,128)(2,1)}, bf16[768,1536]{1,0:T(8,128)(2,1)}, u32[]{:S(2)}, u32[]{:S(2)}) collective-permute-start(bf16[768,1536]{1,0:T(8,128)(2,1)} %im.3), channel_id=1, source_target_pairs={{0,1},{1,0},{2,3},{3,2},{4,5},{5,4},{6,7},{7,6},{8,9},{9,8},{10,11... | collective-permute-start | bytes 7077896 | tf_op jit(solution)/shard_map/ppermute | solution.py:483
  7.8 5.7 %collective-permute-start.1 = (bf16[384,768]{1,0:T(8,128)(2,1)}, bf16[384,768]{1,0:T(8,128)(2,1)S(1)}, u32[]{:S(2)}, u32[]{:S(2)}) collective-permute-start(bf16[384,768]{1,0:T(8,128)(2,1)} %om.3), channel_id=1, source_target_pairs={{0,1},{1,0},{2,3},{3,2},{4,5},{5,4},{6,7},{7,6},{8,9},{9,8},{10,11... | collective-permute-start | bytes 1769480 | tf_op jit(solution)/shard_map/ppermute | solution.py:483
  8.2 47.1 %collective-permute-start.3 = (bf16[1536,768]{1,0:T(8,128)(2,1)}, bf16[1536,768]{1,0:T(8,128)(2,1)}, u32[]{:S(2)}, u32[]{:S(2)}) collective-permute-start(bf16[1536,768]{1,0:T(8,128)(2,1)} %tm.3), channel_id=1, source_target_pairs={{0,1},{1,0},{2,3},{3,2},{4,5},{5,4},{6,7},{7,6},{8,9},{9,8},{10,11... | collective-permute-start | bytes 7077896 | tf_op jit(solution)/shard_map/ppermute | solution.py:483
  8.3 72.2 %collective-permute-start.6 = (bf16[768,1536]{1,0:T(8,128)(2,1)}, bf16[768,1536]{1,0:T(8,128)(2,1)}, u32[]{:S(2)}, u32[]{:S(2)}) collective-permute-start(bf16[768,1536]{1,0:T(8,128)(2,1)} %bitcast.91), channel_id=1, source_target_pairs={{0,1},{1,0},{2,3},{3,2},{4,5},{5,4},{6,7},{7,6},{8,9},{9,8},{10,11... | collective-permute-start | bytes 7077896 | tf_op jit(solution)/shard_map/ppermute | solution.py:483
  13.5 67.0 %collective-permute-start.7 = (bf16[1536,768]{1,0:T(8,128)(2,1)}, bf16[1536,768]{1,0:T(8,128)(2,1)}, u32[]{:S(2)}, u32[]{:S(2)}) collective-permute-start(bf16[1536,768]{1,0:T(8,128)(2,1)} %bitcast.10.tm), channel_id=1, source_target_pairs={{0,1},{1,0},{2,3},{3,2},{4,5},{5,4},{6,7},{7,6},{8,9},{9,8},{10,11... | collective-permute-start | bytes 7077896 | tf_op jit(solution)/shard_map/ppermute | solution.py:483
  16.4 50.0 %collective-permute-start.4 = (bf16[3,768,384]{2,1,0:T(8,128)(2,1)}, bf16[3,768,384]{2,1,0:T(8,128)(2,1)}, u32[]{:S(2)}, u32[]{:S(2)}) collective-permute-start(bf16[3,768,384]{2,1,0:T(8,128)(2,1)} %qm.2), channel_id=1, source_target_pairs={{0,1},{1,0},{2,3},{3,2},{4,5},{5,4},{6,7},{7,6},{8,9},{9,8},{10,11... | collective-permute-start | bytes 5308424 | tf_op jit(solution)/shard_map/ppermute | solution.py:483
  27.2 9.9 %copy-start.12 = (f32[768]{0:T(1024)S(1)}, f32[768]{0:T(1024)}, u32[]{:S(2)}) copy-start(f32[768]{0:T(1024)} %param.22) | copy-start | bytes 9220
  27.2 10.5 %copy-start.13 = (f32[768]{0:T(1024)S(1)}, f32[768]{0:T(1024)}, u32[]{:S(2)}) copy-start(f32[768]{0:T(1024)} %param.25) | copy-start | bytes 9220
  27.2 11.1 %copy-start.14 = (f32[768]{0:T(1024)S(1)}, f32[768]{0:T(1024)}, u32[]{:S(2)}) copy-start(f32[768]{0:T(1024)} %param.28) | copy-start | bytes 9220
  27.2 11.7 %copy-start.15 = (f32[768]{0:T(1024)S(1)}, f32[768]{0:T(1024)}, u32[]{:S(2)}) copy-start(f32[768]{0:T(1024)} %param.31) | copy-start | bytes 9220
  27.2 12.3 %copy-start.11 = (bf16[768,4]{0,1:T(4,128)(2,1)S(1)}, bf16[768,4]{0,1:T(4,128)(2,1)}, u32[]{:S(2)}) copy-start(bf16[768,4]{0,1:T(4,128)(2,1)} %param.32) | copy-start | bytes 18436
  27.2 12.4 %copy-start.4 = (bf16[4,197,768]{2,0,1:T(4,128)(2,1)S(1)}, bf16[4,197,768]{2,0,1:T(4,128)(2,1)}, u32[]{:S(2)}) copy-start(bf16[4,197,768]{2,0,1:T(4,128)(2,1)} %param.18) | copy-start | bytes 3631108
  30.8 49.7 %all-to-all-start = ((bf16[4,160,768]{2,1,0:T(8,128)(2,1)}), bf16[4,160,768]{2,1,0:T(8,128)(2,1)}, u32[]{:S(2)}, u32[]{:S(2)}) async-start(bf16[4,160,768]{2,1,0:T(8,128)(2,1)} %bitcast.85), calls=%async_computation | async-start | bytes 1966080 | tf_op jit(solution)/shard_map/all_to_all | solution.py:952
  37.1 417.9 %reduce-scatter.2.cloned.1.call-start = ((), (), s32[]{:S(2)}) async-start(), calls=%async_computation.3 | async-start | bytes 5898240 | tf_op jit(solution)/shard_map/reduce_scatter | solution.py:981
  39.8 2.3 copy-start.20
  42.1 24.4 %collective-permute-start.5 = (bf16[384,768]{1,0:T(8,128)(2,1)S(1)}, bf16[384,768]{1,0:T(8,128)(2,1)S(1)}, u32[]{:S(2)}, u32[]{:S(2)}) collective-permute-start(bf16[384,768]{1,0:T(8,128)(2,1)S(1)} %copy-done.20), channel_id=1, source_target_pairs={{0,1},{1,0},{2,3},{3,2},{4,5},{5,4},{6,7},{7,6},{8,9},{9,8},{10,11... | collective-permute-start | bytes 1769480 | tf_op jit(solution)/shard_map/ppermute | solution.py:483
  147.3 8.2 %collective-permute-start.11 = (bf16[2,768,1536]{2,1,0:T(8,128)(2,1)}, bf16[2,768,1536]{2,1,0:T(8,128)(2,1)S(1)}, u32[]{:S(2)}, u32[]{:S(2)}) collective-permute-start(bf16[2,768,1536]{2,1,0:T(8,128)(2,1)} %get-tuple-element.96), channel_id=1, source_target_pairs={{0,1},{1,0},{2,3},{3,2},{4,5},{5,4},{6,7},{7,6},{8,9},{9,8},{10,11... | collective-permute-start | bytes 14155784 | tf_op jit(solution)/shard_map/ppermute | solution.py:483
  165.6 266.6 %all-to-all-start.1 = ((bf16[4,160,768]{2,1,0:T(8,128)(2,1)}), bf16[4,160,768]{2,1,0:T(8,128)(2,1)S(1)}, u32[]{:S(2)}, u32[]{:S(2)}) async-start(bf16[4,160,768]{2,1,0:T(8,128)(2,1)} %bitcast.11), calls=%async_computation.1 | async-start | bytes 1966080 | tf_op jit(solution)/shard_map/all_to_all | solution.py:952
  217.4 22.2 %copy-start.6 = (f32[768,128]{1,0:T(8,128)S(1)}, f32[768,128]{1,0:T(8,128)}, u32[]{:S(2)}) copy-start(f32[768,128]{1,0:T(8,128)} %get-tuple-element.92) | copy-start | bytes 1179652
  237.3 2.5 copy-start.16
  237.3 2.5 copy-start.17
  237.3 2.5 copy-start.18
  237.3 2.5 copy-start.19
  239.8 209.5 %collective-permute-start.10 = (bf16[416,768]{1,0:T(8,128)(2,1)}, bf16[416,768]{1,0:T(8,128)(2,1)}, u32[]{:S(2)}, u32[]{:S(2)}) collective-permute-start(bf16[416,768]{1,0:T(8,128)(2,1)} %convert_element_type.85), channel_id=1, source_target_pairs={{0,1},{1,0},{2,3},{3,2},{4,5},{5,4},{6,7},{7,6},{8,9},{9,8},{10,11... | collective-permute-start | bytes 1916936 | tf_op jit(solution)/shard_map/ppermute | solution.py:483
  429.4 2.3 copy-start.10
  432.2 5.8 %collective-permute-start.8 = (bf16[640,768]{1,0:T(8,128)(2,1)S(1)}, bf16[640,768]{1,0:T(8,128)(2,1)S(1)}, u32[]{:S(2)}, u32[]{:S(2)}) collective-permute-start(bf16[640,768]{1,0:T(8,128)(2,1)S(1)} %bitcast.73), channel_id=1, source_target_pairs={{0,1},{1,0},{2,3},{3,2},{4,5},{5,4},{6,7},{7,6},{8,9},{9,8},{10,11... | collective-permute-start | bytes 2949128 | tf_op jit(solution)/shard_map/ppermute | solution.py:483
  439.5 6.9 %copy-start = (bf16[768,384]{1,0:T(8,128)(2,1)S(1)}, bf16[768,384]{1,0:T(8,128)(2,1)}, u32[]{:S(2)}) copy-start(bf16[768,384]{1,0:T(8,128)(2,1)} %get-tuple-element.108) | copy-start | bytes 1769476
  439.5 6.9 %copy-start.1 = (bf16[768,384]{1,0:T(8,128)(2,1)S(1)}, bf16[768,384]{1,0:T(8,128)(2,1)}, u32[]{:S(2)}) copy-start(bf16[768,384]{1,0:T(8,128)(2,1)} %get-tuple-element.109) | copy-start | bytes 1769476
  439.5 6.9 %copy-start.2 = (bf16[768,384]{1,0:T(8,128)(2,1)S(1)}, bf16[768,384]{1,0:T(8,128)(2,1)}, u32[]{:S(2)}) copy-start(bf16[768,384]{1,0:T(8,128)(2,1)} %get-tuple-element.110) | copy-start | bytes 1769476
  439.5 6.9 %copy-start.3 = (bf16[768,384]{1,0:T(8,128)(2,1)S(1)}, bf16[768,384]{1,0:T(8,128)(2,1)}, u32[]{:S(2)}) copy-start(bf16[768,384]{1,0:T(8,128)(2,1)} %get-tuple-element.111) | copy-start | bytes 1769476
  445.3 7.6 %collective-permute-start.9 = (bf16[416,768]{1,0:T(8,128)(2,1)}, bf16[416,768]{1,0:T(8,128)(2,1)S(1)}, u32[]{:S(2)}, u32[]{:S(2)}) collective-permute-start(bf16[416,768]{1,0:T(8,128)(2,1)} %shard_map.298), channel_id=1, source_target_pairs={{0,1},{1,0},{2,3},{3,2},{4,5},{5,4},{6,7},{7,6},{8,9},{9,8},{10,11... | collective-permute-start | bytes 1916936 | tf_op jit(solution)/shard_map/ppermute | solution.py:483
  (6 other events, 7.9 us)
Sparse Core Ops, SparseCore 0:
  161.5 58.0 reduce-scatter.1

commit v4 on v3

--- a/solution.py
+++ b/solution.py
@@ -13,6 +13,7 @@
 TOPK = 2
 LP = (L + 15) // 16 * 16
 LANES = 128
+LQ = (L + LANES - 1) // LANES * LANES
 BF = jnp.bfloat16
 F32 = jnp.float32
 I32 = jnp.int32
@@ -82,19 +83,69 @@
     return (lane < HDIM).astype(dtype)
 
 
-def attention_forward_body(n_img, tail, *refs):
-    if tail:
-        x_ref, w_ref, qm, qo, om, oo, w4_ref, y_ref, h_ref, qkv_ref, p_ref, o_ref, h4_ref = refs
-    else:
-        x_ref, w_ref, qm, qo, om, oo, y_ref, h_ref, qkv_ref, p_ref, o_ref = refs
+class Exchange:
+    def __init__(self, size, half, src, dst, send, recv, local):
+        self.z = lax.axis_index("exp")
+        self.size, self.half, self.src, self.dst = size, half, src, dst
+        self.send, self.recv, self.local = send, recv, local
+
+    def signal(self):
+        barrier = pltpu.get_barrier_semaphore()
+        for o in range(1, self.size):
+            pl.semaphore_signal(barrier, inc=1, device_id={"exp": (self.z + o) % self.size}, device_id_type=MESH)
+
+    def at(self, e):
+        return pl.ds(pl.multiple_of(e * self.half, self.half), self.half)
+
+    def copies(self):
+        for o in range(1, self.size):
+            to = (self.z + o) % self.size
+            yield pltpu.make_async_remote_copy(self.src.at[self.at(to)], self.dst.at[self.at(self.z)], self.send.at[o - 1],
+                                               self.recv.at[o - 1], device_id={"exp": to}, device_id_type=MESH)
+
+    def own(self):
+        return pltpu.make_async_copy(self.src.at[self.at(self.z)], self.dst.at[self.at(self.z)], self.local)
+
+    def start(self):
+        self.own().start()
+        for cp in self.copies():
+            cp.start()
+
+    def arrived(self):
+        self.own().wait()
+        for o in range(1, self.size):
+            come = (self.z + self.size - o) % self.size
+            pltpu.make_async_remote_copy(self.src.at[self.at(come)], self.dst.at[self.at(come)], self.send.at[o - 1],
+                                         self.recv.at[o - 1], device_id={"exp": come}, device_id_type=MESH).wait_recv()
+
+    def left(self):
+        for cp in self.copies():
+            cp.wait_send()
+
+
+def attention_forward_body(n_img, g_at, tail, size, half, *refs):
+    refs = list(refs)
+    x_ref, g_ref, qm, qo, om, oo = refs[:6]
+    del refs[:6]
+    src = refs.pop(0) if size else None
+    y_ref, h_ref, qkv_ref, p_ref, o_ref = refs[:5]
+    del refs[:5]
+    h4_ref = refs.pop(0) if tail is not None else None
+    if size:
+        dst, send, recv, local = refs
+        carried = Exchange(size, half, src, dst, send, recv, local)
+        carried.signal()
     d = x_ref.shape[1]
     c = qm.shape[2]
     pairs = d // LANES
-    _, _, h = norm_forward(x_ref[...].astype(F32), w_ref[...])
+    _, _, h = norm_forward(x_ref[...].astype(F32), g_ref[g_at : g_at + 1, :])
     h_ref[...] = h
+    if size:
+        pl.semaphore_wait(pltpu.get_barrier_semaphore(), size - 1)
+        carried.start()
     for k in range(3):
-        for half, w in ((0, qm), (1, qo)):
-            at = (2 * k + half) * c
+        for side, w in ((0, qm), (1, qo)):
+            at = (2 * k + side) * c
             qkv_ref[:, at : at + c] = nn(h_ref[...], w[k]).astype(BF)
     mask = head_mask(BF)
     key_ok = lax.broadcasted_iota(I32, (LP, LP), 1) < L
@@ -120,38 +171,51 @@
     lax.fori_loop(0, n_img * pairs, one, 0, unroll=2)
     y = x_ref[...].astype(F32) + nn(o_ref[:, :c], om[...]) + nn(o_ref[:, c:], oo[...])
     y_ref[...] = y
-    if tail:
-        _, _, h4 = norm_forward(y, w4_ref[...])
+    if tail is not None:
+        _, _, h4 = norm_forward(y, g_ref[tail : tail + 1, :])
         h4_ref[...] = h4
-
-
-def attention_forward(x, gain, qm, qo, om, oo, gain4=None):
+    if size:
+        carried.arrived()
+        carried.left()
+
+
+def attention_forward(x, gains, g_at, qm, qo, om, oo, tail=None, carry=None):
     r, d = x.shape
     n_img = r // LP
     heads = d // HDIM
     shapes = [out((r, d), F32), out((r, d), BF), out((r, 3 * d), BF), out((n_img * heads, LP, LP), BF), out((r, d), BF)]
-    args = [x, gain, qm, qo, om, oo]
-    if gain4 is not None:
+    args = [x, gains, qm, qo, om, oo]
+    flops = 2 * r * d * d * 4 + 4 * n_img * heads * LP * LP * LANES
+    if tail is not None:
         shapes.append(out((r, d), BF))
-        args.append(gain4)
-    return call(
-        functools.partial(attention_forward_body, n_img, gain4 is not None),
-        shapes, *args, flops=2 * r * d * d * 4 + 4 * n_img * heads * LP * LP * LANES,
-    )
-
-
-def attention_backward_body(n_img, dy_ref, x_ref, w_ref, h_ref, qkv_ref, p_ref, o_ref, qm, qo, om, oo,
-                            dx_ref, dw_ref, gm_ref, go_ref, do_ref, dqkv_ref, tr_ref):
+    if carry is None:
+        return call(functools.partial(attention_forward_body, n_img, g_at, tail, 0, 0), shapes, *args, flops=flops)
+    src, size, half = carry
+    any_ = pl.BlockSpec(memory_space=pl.ANY)
+    vm = pl.BlockSpec(memory_space=pltpu.VMEM)
+    D = pltpu.SemaphoreType.DMA
+    return pl.pallas_call(
+        functools.partial(attention_forward_body, n_img, g_at, tail, size, half),
+        in_specs=[vm] * 6 + [any_], out_specs=[vm] * len(shapes) + [any_],
+        out_shape=shapes + [out(src.shape, src.dtype)],
+        scratch_shapes=[D((size - 1,)), D((size - 1,)), D],
+        compiler_params=pltpu.CompilerParams(collective_id=2, has_side_effects=True, vmem_limit_bytes=VMEM_BYTES),
+        cost_estimate=pl.CostEstimate(flops=flops, bytes_accessed=16 * r * d * 8, transcendentals=0),
+    )(*args, src)
+
+
+def attention_backward_core(n_img, dy, x_ref, gain, h_ref, qkv_ref, p_ref, o_ref, qm, qo, om, oo,
+                            gm_ref, go_ref, do_ref, dqkv_ref, tr_ref):
     d = x_ref.shape[1]
     c = qm.shape[2]
     pairs = d // LANES
-    da = dy_ref[...].astype(BF)
+    da = dy().astype(BF)
     tr_ref[...] = o_ref[...].T
-    for half, (w, g) in enumerate(((om, gm_ref), (oo, go_ref))):
-        gw = nn(tr_ref[half * c : (half + 1) * c, :], da).astype(BF)
+    for side, (w, g) in enumerate(((om, gm_ref), (oo, go_ref))):
+        gw = nn(tr_ref[side * c : (side + 1) * c, :], da).astype(BF)
         for part in range(d // c):
             g[3 * d + part * c : 3 * d + (part + 1) * c, :] = gw[:, part * c : (part + 1) * c]
-        do_ref[:, half * c : (half + 1) * c] = nt(da, w[...]).astype(BF)
+        do_ref[:, side * c : (side + 1) * c] = nt(da, w[...]).astype(BF)
     mask = head_mask(BF)
 
     def one(i, _):
@@ -182,26 +246,39 @@
     tr_ref[...] = h_ref[...].T
     dh = jnp.zeros(x_ref.shape, F32)
     for k in range(3):
-        for half, (w, g) in enumerate(((qm, gm_ref), (qo, go_ref))):
-            at = (2 * k + half) * c
+        for side, (w, g) in enumerate(((qm, gm_ref), (qo, go_ref))):
+            at = (2 * k + side) * c
             g[k * d : (k + 1) * d, :] = nn(tr_ref[...], dqkv_ref[:, at : at + c]).astype(BF)
             dh = dh + nt(dqkv_ref[:, at : at + c], w[k])
-    n, rr, _ = norm_forward(x_ref[...].astype(F32), w_ref[...])
-    dv, dw = norm_backward(n, rr, w_ref[...], dh)
-    dx_ref[...] = dy_ref[...] + dv
+    n, rr, _ = norm_forward(x_ref[...].astype(F32), gain)
+    dv, dw = norm_backward(n, rr, gain, dh)
+    return dy() + dv, dw
+
+
+def attention_backward_body(n_img, g_at, dy_ref, x_ref, g_ref, h_ref, qkv_ref, p_ref, o_ref, qm, qo, om, oo,
+                            dx_ref, dw_ref, gm_ref, go_ref, do_ref, dqkv_ref, tr_ref):
+    dx, dw = attention_backward_core(
+        n_img, lambda: dy_ref[...], x_ref, g_ref[g_at : g_at + 1, :], h_ref, qkv_ref, p_ref, o_ref, qm, qo, om, oo,
+        gm_ref, go_ref, do_ref, dqkv_ref, tr_ref)
+    for i in range(n_img):
+        dx_ref[i] = dx[i * LP : i * LP + L].astype(BF)
     dw_ref[...] = dw
 
 
-def attention_backward(dy, x, gain, kept, qm, qo, om, oo):
+def attention_backward_scratch(r, d):
+    return [pltpu.VMEM((r, d), BF), pltpu.VMEM((r, 3 * d), BF), pltpu.VMEM((d, r), BF)]
+
+
+def attention_backward(dy, x, gains, g_at, kept, qm, qo, om, oo):
     r, d = x.shape
     c = qm.shape[2]
     n_img = r // LP
     heads = d // HDIM
     return call(
-        functools.partial(attention_backward_body, n_img),
-        [out((r, d), F32), out((1, d), F32), out((3 * d + d, c), BF), out((3 * d + d, c), BF)],
-        dy, x, gain, *kept, qm, qo, om, oo,
-        scratch=[pltpu.VMEM((r, d), BF), pltpu.VMEM((r, 3 * d), BF), pltpu.VMEM((d, r), BF)],
+        functools.partial(attention_backward_body, n_img, g_at),
+        [out((n_img, L, d), BF), out((1, d), F32), out((3 * d + d, c), BF), out((3 * d + d, c), BF)],
+        dy, x, gains, *kept, qm, qo, om, oo,
+        scratch=attention_backward_scratch(r, d),
         flops=4 * r * d * d * 4 + 8 * n_img * heads * LP * LP * LANES,
     )
 
@@ -218,13 +295,13 @@
     return f
 
 
-def mlp_forward_body(x_ref, w_ref, im, io, tm, to, y_ref, h_ref, act_ref, slope_ref, acc_ref):
+def mlp_forward_body(g_at, x_ref, g_ref, im, io, tm, to, y_ref, h_ref, act_ref, slope_ref, acc_ref):
     step = pl.program_id(0)
 
     @pl.when(step == 0)
     def _():
         x = x_ref[...]
-        _, _, h = norm_forward(x, w_ref[...])
+        _, _, h = norm_forward(x, g_ref[g_at : g_at + 1, :])
         h_ref[...] = h
         acc_ref[...] = x
 
@@ -240,7 +317,7 @@
         y_ref[...] = acc_ref[...]
 
 
-def mlp_forward(x, gain, im, io, tm, to):
+def mlp_forward(x, gains, g_at, im, io, tm, to):
     r, d = x.shape
     f = im.shape[1]
     t = tile_of(f)
@@ -248,16 +325,16 @@
     row = pl.BlockSpec((t, d), lambda i: (i, 0))
     hid = pl.BlockSpec((2, r, t), lambda i: (0, 0, i))
     return call(
-        mlp_forward_body,
+        functools.partial(mlp_forward_body, g_at),
         [out((r, d), F32), out((r, d), BF), out((2, r, f), BF), out((2, r, f), BF)],
-        x, gain, im, io, tm, to, grid=(f // t,),
-        in_specs=[whole((r, d)), whole((1, d)), col, col, row, row],
+        x, gains, im, io, tm, to, grid=(f // t,),
+        in_specs=[whole((r, d)), whole(gains.shape), col, col, row, row],
         out_specs=[whole((r, d)), whole((r, d)), hid, hid],
         scratch=[pltpu.VMEM((r, d), F32)], flops=8 * r * d * f,
     )
 
 
-def mlp_backward_body(dy_ref, x_ref, w_ref, h_ref, act_ref, slope_ref, im, io, tm, to,
+def mlp_backward_body(g_at, dy_ref, x_ref, g_ref, h_ref, act_ref, slope_ref, im, io, tm, to,
                       dx_ref, dw_ref, gim, gio, gtm, gto, da_ref, tr_ref, dh_ref):
     step = pl.program_id(0)
 
@@ -279,13 +356,14 @@
 
     @pl.when(step == pl.num_programs(0) - 1)
     def _():
-        n, rr, _ = norm_forward(x_ref[...], w_ref[...])
-        dv, dw = norm_backward(n, rr, w_ref[...], dh_ref[...])
+        gain = g_ref[g_at : g_at + 1, :]
+        n, rr, _ = norm_forward(x_ref[...], gain)
+        dv, dw = norm_backward(n, rr, gain, dh_ref[...])
         dx_ref[...] = dy_ref[...] + dv
         dw_ref[...] = dw
 
 
-def mlp_backward(dy, x, gain, h, act, slope, im, io, tm, to, t):
+def mlp_backward(dy, x, gains, g_at, h, act, slope, im, io, tm, to, t):
     r, d = x.shape
     f = im.shape[1]
     col = pl.BlockSpec((d, t), lambda i: (0, i))
@@ -294,77 +372,92 @@
     gin = pl.BlockSpec((1, d, t), lambda i: (i, 0, 0))
     gout = pl.BlockSpec((d // t, t, t), lambda i: (0, i, 0))
     return call(
-        mlp_backward_body,
+        functools.partial(mlp_backward_body, g_at),
         [out((r, d), F32), out((1, d), F32), out((f // t, d, t), BF), out((f // t, d, t), BF),
          out((d // t, f, t), BF), out((d // t, f, t), BF)],
-        dy, x, gain, h, act, slope, im, io, tm, to, grid=(f // t,),
-        in_specs=[whole((r, d)), whole((r, d)), whole((1, d)), whole((r, d)), hid, hid, col, col, row, row],
+        dy, x, gains, h, act, slope, im, io, tm, to, grid=(f // t,),
+        in_specs=[whole((r, d)), whole((r, d)), whole(gains.shape), whole((r, d)), hid, hid, col, col, row, row],
         out_specs=[whole((r, d)), whole((1, d)), gin, gin, gout, gout],
         scratch=[pltpu.VMEM((r, d), BF), pltpu.VMEM((d, r), BF), pltpu.VMEM((r, d), F32)], flops=16 * r * d * f,
     )
 
 
-def routing_body(experts, capacity, half, cols_ref, rows_ref, tc_ref, tr_ref):
-    n = cols_ref.shape[0]
+def routing_body(experts, capacity, half, rows_ref, dy_ref, tr_ref, col_ref, out_ref, tmp):
+    n_img = rows_ref.shape[0]
     slots = experts * half
-
-    def slot(rank, expert, live):
-        core = (rank >= half).astype(I32)
-        kept = (rank < capacity) & (live > 0)
-        return jnp.where(kept, core * slots + expert * half + rank - core * half, -1)
-
-    r0, r1, pc, lc = (cols_ref[:, i : i + 1] for i in range(4))
-    s0, s1, pr, lr = (rows_ref[i : i + 1, :] for i in range(4))
-    wide = lax.broadcasted_iota(I32, (n, LANES), 1)
-    hot = (((wide == r0) | (wide == r1)) & (lc > 0)).astype(F32).astype(BF)
-    earlier = (pr < pc).astype(F32).astype(BF)
-    rank = nn(earlier, hot)
-    for k, e in enumerate((r0, r1)):
-        mine = jnp.sum(jnp.where(wide == e, rank, 0.0), axis=1, keepdims=True).astype(I32)
-        tc_ref[:, k : k + 1] = slot(mine, e, lc)
-    tall = lax.broadcasted_iota(I32, (max(experts, 8), n), 0)
-    hot = (((tall == s0) | (tall == s1)) & (lr > 0)).astype(F32).astype(BF)
-    earlier = (pc < pr).astype(F32).astype(BF)
-    rank = nn(hot, earlier)
-    for k, e in enumerate((s0, s1)):
-        mine = jnp.sum(jnp.where(tall == e, rank, 0.0), axis=0, keepdims=True).astype(I32)
-        tr_ref[k : k + 1, :] = slot(mine, e, lr)
-
-
-def dispatch_body(ta_ref, tb_ref, a_ref, b_ref, y_ref):
-    slots = y_ref.shape[0]
-    n = a_ref.shape[0]
-    place = lax.broadcasted_iota(I32, (slots, n), 0)
+    core = lax.axis_index("mdl")
+    own_img = n_img // 2
+    tall = lax.broadcasted_iota(I32, (max(experts, 8), LQ), 0)
+    hots, priors = [], []
+    for i in range(n_img):
+        r = rows_ref[i]
+        live = r[3:4, :] > 0
+        hots.append((((tall == r[0:1, :]) | (tall == r[1:2, :])) & live).astype(F32).astype(BF))
+        priors.append(r.astype(F32).T[:, 2:3])
+    for i in range(n_img):
+        r = rows_ref[i]
+        rank = None
+        for k in range(n_img):
+            part = nn(hots[k], (priors[k] < r[2:3, :].astype(F32)).astype(F32).astype(BF))
+            rank = part if rank is None else rank + part
+        for k in range(TOPK):
+            e = r[k : k + 1, :]
+            mine = jnp.sum(jnp.where(tall == e, rank, 0.0), axis=0, keepdims=True).astype(I32)
+            side = (mine >= half).astype(I32)
+            slot = side * slots + e * half + mine - side * half
+            tr_ref[i, k : k + 1, :] = jnp.where((mine < capacity) & (r[3:4, :] > 0), slot, -1)
+        tr_ref[i, TOPK:, :] = jnp.full((8 - TOPK, LQ), -1, I32)
+    for i in range(own_img):
+        at = core * own_img + i
+        for k in range(TOPK):
+            t = tr_ref[at, k : k + 1, :]
+            there = t - (1 - core) * slots
+            tmp[k : k + 1, :] = t - core * slots
+            tmp[TOPK + k : TOPK + k + 1, :] = jnp.where(there < slots, there, -1)
+        tmp[4:8, :] = rows_ref[at, 0:4, :]
+        tmp[6:7, :] = rows_ref[at, 3:4, :]
+        col_ref[i * LP : (i + 1) * LP, :] = tmp[...].astype(F32).T[:LP, :].astype(I32)
     total = None
-    for t, v in ((ta_ref, a_ref), (tb_ref, b_ref)):
-        hot = ((place == t[0:1, :]) | (place == t[1:2, :])).astype(F32).astype(BF)
-        part = nn(hot, v[...])
+    for i in range(n_img):
+        part = nn(slot_hots(tr_ref[i], core * slots, slots), dy_ref[i * LP : (i + 1) * LP, :])
         total = part if total is None else total + part
+    out_ref[...] = total.astype(BF)
+
+
+def slot_hots(t, base, count):
+    place = lax.broadcasted_iota(I32, (count, LP), 0) + base
+    return ((place == t[0:1, :LP]) | (place == t[1:2, :LP])).astype(F32).astype(BF)
+
+
+def dispatch_body(experts, half, tr_ref, own_ref, oth_ref, y_ref):
+    core = lax.axis_index("mdl")
+    own_img = own_ref.shape[0] // LP
+    total = None
+    for a, v in ((core, own_ref), (1 - core, oth_ref)):
+        for i in range(own_img):
+            hot = slot_hots(tr_ref[a * own_img + i], core * experts * half, experts * half)
+            part = nn(hot, v[i * LP : (i + 1) * LP, :])
+            total = part if total is None else total + part
     y_ref[...] = total.astype(BF)
 
 
-def dispatch(ta, tb, a, b, slots):
-    return call(dispatch_body, [out((slots, a.shape[1]), BF)], ta, tb, a, b,
-                flops=4 * slots * a.shape[0] * a.shape[1])[0]
-
-
 def router_probs(h, router, experts):
-    logits = nn(h, router)
+    logits = nt(h, router)
     lane = lax.broadcasted_iota(I32, logits.shape, 1)
     logits = jnp.where(lane < experts, logits, -1e30)
     e = jnp.exp(logits - jnp.max(logits, axis=-1, keepdims=True))
     return e / jnp.sum(e, axis=-1, keepdims=True), lane
 
 
-def expert_body(experts, x_ref, dy_ref, router_ref, mine_ref, im, io, tm, to,
+def expert_body(experts, x_ref, dy_ref, router_ref, im, io, tm, to,
                 eout_ref, ret_ref, act_ref, dz_ref, wd_ref, acc_ref, dx_ref):
     step = pl.program_id(0)
     d = x_ref.shape[1]
 
     @pl.when(step == 0)
     def _():
-        probs, _ = router_probs(x_ref[...], router_ref[...], experts)
-        gate = jnp.sum(probs * mine_ref[...], axis=-1, keepdims=True)
+        probs, lane = router_probs(x_ref[...], router_ref[...], experts)
+        gate = jnp.sum(jnp.where(lane == lax.axis_index("exp"), probs, 0.0), axis=-1, keepdims=True)
         wd_ref[...] = (gate * dy_ref[...].astype(F32)).astype(BF)
         acc_ref[...] = jnp.zeros_like(acc_ref)
         dx_ref[...] = jnp.zeros_like(dx_ref)
@@ -389,7 +482,7 @@
         ret_ref[:, d:] = jnp.where(lane < LANES // 2, high, dgate - high).astype(BF)
 
 
-def expert_forward_backward(x, dy, router, mine, im, io, tm, to, experts):
+def expert_forward_backward(x, dy, router, im, io, tm, to, experts):
     r, d = x.shape
     f = im.shape[1]
     t = tile_of(f) // 2
@@ -399,8 +492,8 @@
     return call(
         functools.partial(expert_body, experts),
         [out((r, d), BF), out((r, d + LANES), BF), out((2, r, f), BF), out((2, r, f), BF), out((r, d), BF)],
-        x, dy, router, mine, im, io, tm, to, grid=(f // t,),
-        in_specs=[whole((r, d)), whole((r, d)), whole(router.shape), whole(mine.shape), col, col, row, row],
+        x, dy, router, im, io, tm, to, grid=(f // t,),
+        in_specs=[whole((r, d)), whole((r, d)), whole(router.shape), col, col, row, row],
         out_specs=[whole((r, d)), whole((r, d + LANES)), hid, hid, whole((r, d))],
         scratch=[pltpu.VMEM((r, d), F32), pltpu.VMEM((r, d), F32)], flops=16 * r * d * f,
     )
@@ -430,43 +523,111 @@
     )
 
 
-def merge_hots(t_ref, k, n, slots):
+def merge(col_ref, k, ab_ref, n):
+    slots = ab_ref.shape[1]
     lane = lax.broadcasted_iota(I32, (n, slots), 1)
-    return (lane == t_ref[:, k : k + 1]).astype(F32).astype(BF)
-
-
-def mixture_backward_body(experts, x_ref, w_ref, h_ref, router_ref, dy_ref, route_ref, ta_ref, tb_ref, ab_ref,
-                          dx_ref, dw_ref, dr_ref):
+    rows = None
+    for side in range(2):
+        hot = (lane == col_ref[:, 2 * side + k : 2 * side + k + 1]).astype(F32).astype(BF)
+        part = nn(hot, ab_ref[side])
+        rows = part if rows is None else rows + part
+    return rows
+
+
+def mixture_backward_core(experts, x_ref, gain, h_ref, router_ref, dy_ref, col_ref, ab_ref, dr_ref):
     n, d = x_ref.shape
-    slots = ab_ref.shape[1]
     probs, lane = router_probs(h_ref[...], router_ref[...], experts)
     dh = jnp.zeros((n, d), F32)
     dsoft = jnp.zeros(probs.shape, F32)
     for k in range(TOPK):
-        part = nn(merge_hots(ta_ref, k, n, slots), ab_ref[0]) + nn(merge_hots(tb_ref, k, n, slots), ab_ref[1])
+        part = merge(col_ref, k, ab_ref, n)
         dh = dh + part[:, :d]
         dgate = part[:, d : d + 1] + part[:, d + LANES // 2 : d + LANES // 2 + 1]
-        dsoft = dsoft + jnp.where(lane == route_ref[:, k : k + 1], dgate, 0.0)
+        dsoft = dsoft + jnp.where(lane == col_ref[:, 4 + k : 5 + k], dgate, 0.0)
     dlog = (probs * (dsoft - jnp.sum(dsoft * probs, axis=-1, keepdims=True))).astype(BF)
-    dr_ref[...] = tn(h_ref[...], dlog)
-    dh = dh + nt(dlog, router_ref[...])
-    nrm, rr, _ = norm_forward(x_ref[...], w_ref[...])
-    dv, dw = norm_backward(nrm, rr, w_ref[...], dh)
-    dx_ref[...] = dy_ref[...].astype(F32) + dv
-    dw_ref[...] = dw
-
-
-def mixture_output_body(experts, x_ref, h_ref, router_ref, route_ref, live_ref, ta_ref, tb_ref, ab_ref, y_ref):
+    dr_ref[...] = tn(dlog, h_ref[...])
+    dh = dh + nn(dlog, router_ref[...])
+    nrm, rr, _ = norm_forward(x_ref[...], gain)
+    dv, dw = norm_backward(nrm, rr, gain, dh)
+    return dy_ref[...].astype(F32) * col_ref[:, 6:7].astype(F32) + dv, dw
+
+
+def mixture_attention_backward_body(n_img, experts, size, half, *refs):
+    refs = list(refs)
+    x3_ref, h4_ref, router_ref, dy_ref, col_ref, ret_ref, x_ref, g_ref, h_ref, qkv_ref, p_ref, o_ref, qm, qo, om, oo = refs[:16]
+    del refs[:16]
+    src = refs.pop(0) if size else None
+    dx_ref, dw3_ref, dw4_ref, dr_ref, gm_ref, go_ref = refs[:6]
+    del refs[:6]
+    dst = refs.pop(0) if size else None
+    dx3, do_ref, dqkv_ref, tr_ref = refs[:4]
+    if size:
+        send, recv, local, f_send, f_recv = refs[4:]
+        core = lax.axis_index("mdl")
+        carried = Exchange(size, half, src, dst.at[0], send, recv, local)
+        carried.signal()
+        barrier = pltpu.get_barrier_semaphore()
+        pl.semaphore_signal(barrier, inc=1, device_id={"mdl": 1 - core}, device_id_type=MESH)
+        pl.semaphore_wait(barrier, size)
+        carried.start()
+    grad, dw4 = mixture_backward_core(experts, x3_ref, g_ref[3:4, :], h4_ref, router_ref, dy_ref, col_ref, ret_ref, dr_ref)
+    dx3[...] = grad
+    dw4_ref[...] = dw4
+    dx, dw3 = attention_backward_core(
+        n_img, lambda: dx3[...], x_ref, g_ref[2:3, :], h_ref, qkv_ref, p_ref, o_ref, qm, qo, om, oo,
+        gm_ref, go_ref, do_ref, dqkv_ref, tr_ref)
+    dx_ref[...] = dx
+    dw3_ref[...] = dw3
+    if size:
+        carried.arrived()
+        pass_on = pltpu.make_async_remote_copy(dst.at[0], dst.at[1], f_send, f_recv, device_id={"mdl": 1 - core},
+                                               device_id_type=MESH)
+        pass_on.start()
+        carried.left()
+        pass_on.wait()
+
+
+def mixture_attention_backward(experts, x3, h4, router, dy, col, ret, x, gains, kept, qm, qo, om, oo, carry=None):
+    r, d = x.shape
+    c = qm.shape[2]
+    n_img = r // LP
+    heads = d // HDIM
+    args = [x3, h4, router, dy, col, ret, x, gains, *kept, qm, qo, om, oo]
+    shapes = [out((r, d), F32), out((1, d), F32), out((1, d), F32), out(router.shape, F32),
+              out((3 * d + d, c), BF), out((3 * d + d, c), BF)]
+    scratch = [pltpu.VMEM((r, d), F32)] + attention_backward_scratch(r, d)
+    flops = 4 * r * d * d * 4 + 8 * n_img * heads * LP * LP * LANES + 8 * r * ret.shape[1] * d
+    if carry is None:
+        return call(functools.partial(mixture_attention_backward_body, n_img, experts, 0, 0), shapes, *args,
+                    scratch=scratch, flops=flops)
+    src, size, half = carry
+    any_ = pl.BlockSpec(memory_space=pl.ANY)
+    vm = pl.BlockSpec(memory_space=pltpu.VMEM)
+    D = pltpu.SemaphoreType.DMA
+    return pl.pallas_call(
+        functools.partial(mixture_attention_backward_body, n_img, experts, size, half),
+        in_specs=[vm] * len(args) + [any_], out_specs=[vm] * len(shapes) + [any_],
+        out_shape=shapes + [out((2,) + src.shape, src.dtype)],
+        scratch_shapes=scratch + [D((size - 1,)), D((size - 1,)), D, D, D],
+        compiler_params=pltpu.CompilerParams(collective_id=3, has_side_effects=True, vmem_limit_bytes=VMEM_BYTES),
+        cost_estimate=pl.CostEstimate(flops=flops, bytes_accessed=24 * r * d * 8, transcendentals=0),
+    )(*args, src)
+
+
+def mixture_output(experts, x_ref, h_ref, router_ref, col_ref, ab_ref):
     n, d = x_ref.shape
-    slots = ab_ref.shape[1]
     probs, lane = router_probs(h_ref[...], router_ref[...], experts)
-    total = x_ref[...]
     mixed = jnp.zeros((n, d), F32)
     for k in range(TOPK):
-        gate = jnp.sum(jnp.where(lane == route_ref[:, k : k + 1], probs, 0.0), axis=-1, keepdims=True)
-        part = nn(merge_hots(ta_ref, k, n, slots), ab_ref[0]) + nn(merge_hots(tb_ref, k, n, slots), ab_ref[1])
-        mixed = mixed + gate * part
-    y_ref[...] = (live_ref[...] * (total + mixed)).astype(BF)
+        gate = jnp.sum(jnp.where(lane == col_ref[:, 4 + k : 5 + k], probs, 0.0), axis=-1, keepdims=True)
+        mixed = mixed + gate * merge(col_ref, k, ab_ref, n)
+    return (col_ref[:, 6:7].astype(F32) * (x_ref[...] + mixed)).astype(BF)
+
+
+def mixture_output_body(experts, x_ref, h_ref, router_ref, col_ref, ab_ref, y_ref):
+    y = mixture_output(experts, x_ref, h_ref, router_ref, col_ref, ab_ref)
+    for i in range(y_ref.shape[0]):
+        y_ref[i] = y[i * LP : i * LP + L]
 
 
 def flip(axis, bit):
@@ -531,12 +692,16 @@
     return v
 
 
-def reduce_body(n_in, per, n_exp, *refs):
+def reduce_body(n_in, per, n_exp, experts, *refs):
     mine = refs[:n_in]
     other = refs[n_in : 2 * n_in]
-    small_ref = refs[2 * n_in]
-    out_ref, sum_ref = refs[2 * n_in + 1 : 2 * n_in + 3]
-    (acc, got, r1, r2, zr, sm, load_sem, m_send, m_recv, x_send, x_recv, z_send, z_recv, s_send, s_recv) = refs[2 * n_in + 3 :]
+    dg = refs[2 * n_in : 2 * n_in + 4]
+    dr_ref, x3_ref, h4_ref, router_ref, col_ref, ab_ref, image_ref = refs[2 * n_in + 4 : 2 * n_in + 11]
+    outs = refs[2 * n_in + 11 :]
+    qkv2, proj2, fc_in, fc_out, qkv1, proj1, sum_ref, y_ref, gx_ref = outs[:9]
+    (acc, got, r1, r2, zr, sm, y_own, load_sem, m_send, m_recv, x_send, x_recv, z_send, z_recv, s_send, s_recv,
+     i_local, i_send, i_recv) = outs[9:]
+    out_ref = got
     n = n_in * per
     rows = acc.shape[2]
     h, q = rows // 2, rows // 4
@@ -569,6 +734,22 @@
         swap(c).start()
         load(c).start()
 
+    own_img = image_ref.shape[0]
+    places = pl.ds(core * own_img, own_img)
+
+    def image_copies(k, src, dst):
+        return (pltpu.make_async_copy(src, dst.at[places], i_local.at[k]),
+                pltpu.make_async_remote_copy(src, dst.at[places], i_send.at[k], i_recv.at[k], device_id={"mdl": 1 - core},
+                                             device_id_type=MESH))
+
+    def image_come(k, src, dst):
+        there = pl.ds((1 - core) * own_img, own_img)
+        return pltpu.make_async_remote_copy(src, dst.at[there], i_send.at[k], i_recv.at[k], device_id={"mdl": 1 - core},
+                                            device_id_type=MESH)
+
+    for cp in image_copies(0, image_ref, gx_ref):
+        cp.start()
+
     def swap_at(c):
         return pltpu.make_async_remote_copy(other[0].at[0], got.at[c], m_send.at[c], m_recv.at[c],
                                             device_id={"mdl": 1 - core}, device_id_type=MESH)
@@ -665,6 +846,23 @@
                 along(u, c, o).wait_send()
                 back(u, c, o).wait_send()
 
+    def natural(c):
+        i, p = c // per, c % per
+        side = rows // 2
+        for u in range(2):
+            v = 2 * p + u
+            if i in (0, 3):
+                qkv, proj = (qkv2, proj2) if i == 0 else (qkv1, proj1)
+                if v < 3:
+                    qkv[v] = out_ref[c, u]
+                else:
+                    for k in range(2):
+                        proj[:, k * side : (k + 1) * side] = out_ref[c, u, k * side : (k + 1) * side]
+            elif i == 1:
+                fc_in[:, v * side : (v + 1) * side] = out_ref[c, u]
+            else:
+                fc_out[v % 2 * rows : (v % 2 + 1) * rows, v // 2 * side : (v // 2 + 1) * side] = out_ref[c, u]
+
     steps = (s1, s2, s3, s4, s5, s6, s7)
 
     def wave(tau, _):
@@ -677,9 +875,26 @@
 
         return 0
 
-    lax.fori_loop(0, n + len(steps) - 1, wave, 0)
-
-    sm[0] = small_ref[...]
+    first_waves = 3
+    lax.fori_loop(0, first_waves, wave, 0)
+    y = mixture_output(experts, x3_ref, h4_ref, router_ref, col_ref, ab_ref)
+    for i in range(own_img):
+        y_own[i] = y[i * LP : i * LP + L]
+    for cp in image_copies(1, y_own, y_ref):
+        cp.start()
+    lax.fori_loop(first_waves, n + len(steps) - 1, wave, 0)
+    for c in range(n):
+        natural(c)
+    for k, (src, dst) in enumerate(((image_ref, gx_ref), (y_own, y_ref))):
+        local, sent = image_copies(k, src, dst)
+        local.wait()
+        sent.wait_send()
+        image_come(k, src, dst).wait_recv()
+
+    sm[0] = jnp.zeros(sm.shape[1:], F32)
+    for k in range(4):
+        sm[0, k : k + 1, :] = dg[k][...]
+    sm[0, 4 : 4 + experts, :] = dr_ref[:experts, :]
     legs = [({"mdl": 1 - core}), ({"grp": flat["x"]}), ({"grp": flat["y"]})]
     for i, dev in enumerate(legs):
         cp = pltpu.make_async_remote_copy(sm.at[2 * i], sm.at[2 * i + 1], s_send.at[i], s_recv.at[i], device_id=dev, device_id_type=MESH)
@@ -701,33 +916,38 @@
     sum_ref[...] = total
 
 
-def reduce_all(mine, other, small, n_exp):
+def reduce_all(mine, other, dgs, dr, x3, h4, router, col, ab, image, n_exp, experts):
     per, _, rows, c = mine[0].shape
     n = len(mine) * per
+    d, f = 2 * c, 4 * c
     h, q = rows // 2, rows // 4
     t = q // n_exp
-    D = pltpu.SemaphoreType.DMA
+    small = (-(-(4 + experts) // 8) * 8, d)
+    n_img, length, _ = image.shape
+    D, V = pltpu.SemaphoreType.DMA, pltpu.VMEM
     any_ = pl.BlockSpec(memory_space=pl.ANY)
     vm = pl.BlockSpec(memory_space=pltpu.VMEM)
     return pl.pallas_call(
-        functools.partial(reduce_body, len(mine), per, n_exp),
-        in_specs=[any_] * (2 * len(mine)) + [vm],
-        out_specs=[vm, vm],
-        out_shape=[jax.ShapeDtypeStruct((n, 2, rows, c), BF), jax.ShapeDtypeStruct(small.shape, F32)],
+        functools.partial(reduce_body, len(mine), per, n_exp, experts),
+        in_specs=[any_] * (2 * len(mine)) + [vm] * 10 + [any_],
+        out_specs=[vm] * 7 + [any_] * 2,
+        out_shape=[out((3, d, c), BF), out((c, d), BF), out((d, f), BF), out((f, d), BF), out((3, d, c), BF), out((c, d), BF),
+                   out(small, F32), out((2 * n_img, length, d), BF), out((2 * n_img, length, d), BF)],
         scratch_shapes=[
-            pltpu.VMEM((n, 2, rows, c), BF), pltpu.VMEM((n, 2, rows, c), BF), pltpu.VMEM((n, 2, h, c), BF),
-            pltpu.VMEM((n, 2, q, c), BF), pltpu.VMEM((n, 2, n_exp - 1, t, c), BF), pltpu.VMEM((7 + n_exp,) + small.shape, F32),
+            V((n, 2, rows, c), BF), V((n, 2, rows, c), BF), V((n, 2, h, c), BF), V((n, 2, q, c), BF),
+            V((n, 2, n_exp - 1, t, c), BF), V((7 + n_exp,) + small, F32), V((n_img, length, d), BF),
             D((n,)), D((n,)), D((n,)), D((4, 2, n)), D((4, 2, n)), D((2, 2, n_exp - 1, n)), D((2, 2, n_exp - 1, n)),
-            D((3 + n_exp,)), D((3 + n_exp,)),
+            D((3 + n_exp,)), D((3 + n_exp,)), D((2,)), D((2,)), D((2,)),
         ],
         compiler_params=pltpu.CompilerParams(collective_id=0, has_side_effects=True, vmem_limit_bytes=VMEM_BYTES),
-    )(*mine, *other, small)
-
-
-def expert_exchange_body(experts, half, h4_ref, ta_ref, tb_ref, dyin_ref, router_ref, mine_ref, im, io, tm, to,
-                         ret_ref, eout_ref, gm_ref, go_ref,
-                         h_oth, part, xo, x, wi, wo, act, dz, wd, acc, dxa, rsend, gscr, xt, wt,
-                         w_sem, swap_sem, x_send, x_recv, r_send, r_recv, f_send, f_recv, g_sem):
+        cost_estimate=pl.CostEstimate(flops=8 * x3.shape[0] * ab.shape[1] * d, bytes_accessed=n * 8 * rows * c, transcendentals=0),
+    )(*mine, *other, *dgs, dr, x3, h4, router, col, ab, image)
+
+
+def expert_exchange_body(experts, half, h4_ref, tr_ref, dyin_ref, router_ref, im, io, tm, to,
+                         ret_ref, eout_ref, gw_ref,
+                         h_oth, part, xo, x, wi, wo, act, dz, wd, acc, dxa, rsend, gscr, ggot, xt, wt,
+                         w_sem, swap_sem, x_send, x_recv, r_send, r_recv, f_send, f_recv, g_send, g_recv, g_sem):
     n, d = h4_ref.shape
     f = im.shape[1]
     t = 256 if f % 256 == 0 else tile_of(f)
@@ -756,9 +976,15 @@
     swap = pltpu.make_async_remote_copy(h4_ref, h_oth, swap_sem.at[0], swap_sem.at[1], device_id=partner, device_id_type=MESH)
     swap.start()
 
-    def hot(t_ref, e):
-        slot = lax.broadcasted_iota(I32, (half, n), 0) + e * half
-        return ((slot == t_ref[0:1, :]) | (slot == t_ref[1:2, :])).astype(F32).astype(BF)
+    own_img = n // LP
+    base = core * size * half
+
+    def spread(side, v, j):
+        total = None
+        for i in range(own_img):
+            p = nn(slot_hots(tr_ref[side * own_img + i], base + there(j) * half, half), v[i * LP : (i + 1) * LP, :])
+            total = p if total is None else total + p
+        return total
 
     def rows(j):
         return slice(j * half, (j + 1) * half)
@@ -767,11 +993,11 @@
         return pl.ds(pl.multiple_of(e * half, half), half)
 
     for j in near_first + [0]:
-        part[rows(j), :] = nn(hot(ta_ref, there(j)), h4_ref[...])
+        part[rows(j), :] = spread(core, h4_ref, j)
     swap.wait_recv()
     sends = {}
     for j in near_first + [0]:
-        block = (part[rows(j), :] + nn(hot(tb_ref, there(j)), h_oth[...])).astype(BF)
+        block = (part[rows(j), :] + spread(1 - core, h_oth, j)).astype(BF)
         if j == 0:
             x[rows(0), :] = block
         else:
@@ -792,8 +1018,8 @@
         r0, r1 = blocks[0] * half, (blocks[-1] + 1) * half
         m = r1 - r0
         for j in blocks:
-            probs, _ = router_probs(x[rows(j), :], router_ref[...], experts)
-            gate = jnp.sum(probs * mine_ref[...], axis=-1, keepdims=True)
+            probs, lane = router_probs(x[rows(j), :], router_ref[...], experts)
+            gate = jnp.sum(jnp.where(lane == z, probs, 0.0), axis=-1, keepdims=True)
             wd[rows(j), :] = (gate * dyin_ref[place(there(j)), :].astype(F32)).astype(BF)
         acc[0:m, :] = jnp.zeros((m, d), F32)
         dxa[0:m, :] = jnp.zeros((m, d), F32)
@@ -841,19 +1067,36 @@
     xt[...] = x[...].T
     wt[...] = wd[...].T
 
-    def stored(i, side, ref):
-        at = pl.ds(pl.multiple_of(i * t, t), t)
-        return pltpu.make_async_copy(gscr.at[side, :, :, at], ref.at[:, :, at], g_sem.at[side, i])
+    tiles = f // t
+
+    def cols(i):
+        return pl.ds(pl.multiple_of(i * t, t), t)
+
+    def swapped(i):
+        return pltpu.make_async_remote_copy(gscr.at[1, :, :, cols(i)], ggot.at[:, :, cols(i)], g_send.at[i], g_recv.at[i],
+                                            device_id=partner, device_id_type=MESH)
+
+    def stored(i):
+        return pltpu.make_async_copy(gscr.at[0, :, :, cols(i)], gw_ref.at[:, :, cols(i)], g_sem.at[i])
 
     def weight_tile(i, _):
-        at = pl.ds(pl.multiple_of(i * t, t), t)
-        for side, ref in enumerate((gm_ref, go_ref)):
-            gscr[side, 0, :, at] = nn(xt[...], dz[side, :, at]).astype(BF)
-            gscr[side, 1, :, at] = nn(wt[...], act[side, :, at]).astype(BF)
-            stored(i, side, ref).start()
+        for side in (1, 0):
+            gscr[side, 0, :, cols(i)] = nn(xt[...], dz[side, :, cols(i)]).astype(BF)
+            gscr[side, 1, :, cols(i)] = nn(wt[...], act[side, :, cols(i)]).astype(BF)
+            if side == 1:
+                swapped(i).start()
         return 0
 
-    lax.fori_loop(0, f // t, weight_tile, 0)
+    lax.fori_loop(0, tiles, weight_tile, 0)
+
+    def sum_tile(i, _):
+        swapped(i).wait_recv()
+        for k in range(2):
+            gscr[0, k, :, cols(i)] = (gscr[0, k, :, cols(i)].astype(F32) + ggot[k, :, cols(i)].astype(F32)).astype(BF)
+        stored(i).start()
+        return 0
+
+    lax.fori_loop(0, tiles, sum_tile, 0)
 
     def recv_return(j):
         return pltpu.make_async_remote_copy(rsend.at[rows(j)], ret_ref.at[0, place(there(j))], r_send.at[j], r_recv.at[j],
@@ -864,11 +1107,11 @@
         forward(j)
 
     def drain(i, _):
-        for side, ref in enumerate((gm_ref, go_ref)):
-            stored(i, side, ref).wait()
+        stored(i).wait()
+        swapped(i).wait_send()
         return 0
 
-    lax.fori_loop(0, f // t, drain, 0)
+    lax.fori_loop(0, tiles, drain, 0)
     swap.wait_send()
     for j in range(size):
         if j:
@@ -877,7 +1120,7 @@
         forwards[j].wait()
 
 
-def expert_exchange(h4, ta, tb, dy_in, router, mine, im, io, tm, to, experts, half):
+def expert_exchange(h4, tr, dy_in, router, im, io, tm, to, experts, half):
     n, d = h4.shape
     f = im.shape[1]
     s = experts * half
@@ -887,19 +1130,22 @@
     vm = pl.BlockSpec(memory_space=pltpu.VMEM)
     return pl.pallas_call(
         functools.partial(expert_exchange_body, experts, half),
-        in_specs=[vm] * 6 + [any_] * 4,
-        out_specs=[vm, vm, any_, any_],
-        out_shape=[out((2, s, d + LANES), BF), out((s, d), BF), out((2, d, f), BF), out((2, d, f), BF)],
+        in_specs=[vm] * 4 + [any_] * 4,
+        out_specs=[vm, vm, any_],
+        out_shape=[out((2, s, d + LANES), BF), out((s, d), BF), out((2, d, f), BF)],
         scratch_shapes=[
             V((n, d), BF), V((s, d), F32), V((s, d), BF), V((s, d), BF), V((2, d, f), BF), V((2, f, d), BF),
             V((2, s, f), BF), V((2, s, f), BF), V((s, d), BF), V((2 * half, d), F32), V((2 * half, d), F32),
-            V((s, d + LANES), BF), V((2, 2, d, f), BF), V((d, s), BF), V((d, s), BF),
+            V((s, d + LANES), BF), V((2, 2, d, f), BF), V((2, d, f), BF), V((d, s), BF), V((d, s), BF),
             D((4,)), D((2,)), D((experts,)), D((experts,)), D((experts,)), D((experts,)), D((experts,)), D((experts,)),
-            D((2, tiles)),
+            D((tiles,)), D((tiles,)), D((tiles,)),
         ],
         compiler_params=pltpu.CompilerParams(collective_id=1, has_side_effects=True, vmem_limit_bytes=VMEM_BYTES),
         cost_estimate=pl.CostEstimate(flops=24 * s * d * f, bytes_accessed=20 * d * f, transcendentals=0),
-    )(h4, ta, tb, dy_in, router, mine, im, io, tm, to)
+    )(h4, tr, dy_in, router, im, io, tm, to)
+
+
+FUSED = True
 
 
 def on_device(images, counts, routes, priority, gain_one, qkv_one, out_one, gain_two, fc_in, fc_out, gain_three,
@@ -907,124 +1153,103 @@
     n_slot, length, d = images.shape
     experts = router.shape[1]
     n_mdl = lax.axis_size("mdl")
+    peers = lax.axis_size("exp")
     capacity = (25 * L * TOPK + 8 * experts - 1) // (8 * experts)
     half = -(-(-(-capacity // n_mdl)) // 16) * 16
     slots = experts * half
     own_img = n_slot // n_mdl
     f = fc_in.shape[1]
+    c = qkv_one.shape[2]
     rows = own_img * LP
     core = lax.axis_index("mdl")
-
-    def own(v, axis=0):
-        return lax.dynamic_slice_in_dim(v, core * rows, rows, axis)
-
-    def oth(v, axis=0):
-        return lax.dynamic_slice_in_dim(v, (1 - core) * rows, rows, axis)
+    per = 2
+    unit = 4 * d // (2 * per)
+    fused = FUSED and (lax.axis_size("grp"), peers, n_mdl) == (4, experts, 2) and peers == 4
+    fused = fused and d == 2 * c and f == 4 * c and unit % (64 * peers) == 0
+
+    def own(v):
+        return lax.dynamic_slice_in_dim(v, core * rows, rows)
 
     def padded(v):
         return jnp.pad(v, ((0, 0), (0, LP - length), (0, 0))).reshape(n_slot * LP, -1)
 
     qm1, om1, im, tm, qm2, om2, em, fm = qkv_one, out_one, fc_in, fc_out, qkv_two, out_two, expert_in[0], expert_out[0]
     qo1, oo1, io, to, qo2, oo2, eo, fo = (other_core(w) for w in (qm1, om1, im, tm, qm2, om2, em, fm))
-    g1, g2, g3, g4 = (g.reshape(1, d) for g in (gain_one, gain_two, gain_three, gain_four))
-    router_wide = jnp.pad(router, ((0, 0), (0, LANES - experts)))
-    mine = (jnp.arange(LANES, dtype=I32) == lax.axis_index("exp")).astype(F32)[None]
-
-    img_live = (jnp.arange(n_slot, dtype=I32) < counts[0, 0]).astype(I32)
-    live = jnp.pad(jnp.broadcast_to(img_live[:, None], (n_slot, length)), ((0, 0), (0, LP - length))).reshape(-1)
-    x0 = own(padded(images))
-    dy = padded(cotangent * img_live[:, None, None].astype(BF))
-    route = padded(routes)
-    prior = padded(priority.reshape(n_slot, length, 1))
-    cols = jnp.concatenate([route, prior, live[:, None]], axis=1)
-    slot_cols, slot_rows = call(
+    gains = jnp.stack([gain_one, gain_two, gain_three, gain_four])
+    router_rows = jnp.pad(router.T, ((0, LANES - experts), (0, 0)))
+
+    live = jnp.broadcast_to((jnp.arange(n_slot, dtype=I32) < counts[0, 0]).astype(I32)[:, None, None], (n_slot, 1, length))
+    lines = jnp.concatenate([jnp.transpose(routes, (0, 2, 1)), priority.reshape(n_slot, 1, length), live], axis=1)
+    lines = jnp.pad(lines, ((0, 0), (0, 4), (0, LQ - length)))
+    dy = padded(cotangent)
+    slot_rows, col, dy_out = call(
         functools.partial(routing_body, experts, capacity, half),
-        [out((n_slot * LP, TOPK), I32), out((TOPK, n_slot * LP), I32)], cols, cols.T,
+        [out((n_slot, 8, LQ), I32), out((rows, 8), I32), out((slots, d), BF)], lines, dy,
+        scratch=[pltpu.VMEM((8, LQ), I32)], flops=4 * slots * n_slot * LP * d,
     )
-    mine_rows = slot_rows - core * slots
-    own_tokens_here = own(slot_cols) - core * slots
-    own_tokens_there = own(slot_cols) - (1 - core) * slots
-    own_tokens_there = jnp.where(own_tokens_there < slots, own_tokens_there, -1)
-    peers = lax.axis_size("exp")
 
     def exchange(v):
         shaped = v.reshape(peers, v.shape[0] // peers, v.shape[1])
         return lax.all_to_all(shaped, "exp", 0, 0, tiled=True).reshape(v.shape)
 
-    dy_out = dispatch(mine_rows[:, :rows], mine_rows[:, rows:], dy[:rows], dy[rows:], slots)
-    dy_in = exchange(dy_out)
-
-    x1, *kept1 = attention_forward(x0, g1, qm1, qo1, om1, oo1)
-    x2, h2, act2, slope2 = mlp_forward(x1, g2, im, io, tm, to)
-    x3, *kept3, h4 = attention_forward(x2, g3, qm2, qo2, om2, oo2, g4)
-
-    grouped = peers == 4 and experts == 4 and n_mdl == 2
-    if grouped:
-        ret, eout, ge_mine, ge_other = expert_exchange(
-            h4, own(mine_rows, 1), oth(mine_rows, 1), dy_in, router_wide, mine, em, eo, fm, fo, experts, half)
+    x0 = own(padded(images))
+    if fused:
+        x1, *kept1, dy_in = attention_forward(x0, gains, 0, qm1, qo1, om1, oo1, carry=(dy_out, peers, half))
     else:
-        h4_out = dispatch(own(mine_rows, 1), oth(mine_rows, 1), h4, other_core(h4), slots)
+        x1, *kept1 = attention_forward(x0, gains, 0, qm1, qo1, om1, oo1)
+        dy_in = exchange(dy_out)
+    x2, h2, act2, slope2 = mlp_forward(x1, gains, 1, im, io, tm, to)
+    x3, *kept3, h4 = attention_forward(x2, gains, 2, qm2, qo2, om2, oo2, tail=3)
+
+    own_dy = own(dy)
+    second = (x2, gains, kept3, qm2, qo2, om2, oo2)
+    if fused:
+        ret, eout, ge = expert_exchange(h4, slot_rows, dy_in, router_rows, em, eo, fm, fo, experts, half)
+        dx2, dg3, dg4, dr, a2_mine, a2_other, eback = mixture_attention_backward(
+            experts, x3, h4, router_rows, own_dy, col, ret, *second, carry=(eout, peers, half))
+    else:
+        [h4_out] = call(functools.partial(dispatch_body, experts, half), [out((slots, d), BF)], slot_rows, h4, other_core(h4))
         h4_in = exchange(h4_out)
-        eout, ret, eact, edz, ewd = expert_forward_backward(h4_in, dy_in, router_wide, mine, em, eo, fm, fo, experts)
-        ret = exchange(ret)
-        ret = jnp.stack([ret, other_core(ret)])
+        eout, ret, eact, edz, ewd = expert_forward_backward(h4_in, dy_in, router_rows, em, eo, fm, fo, experts)
+        ret, eout = exchange(ret), exchange(eout)
+        ret, eback = jnp.stack([ret, other_core(ret)]), jnp.stack([eout, other_core(eout)])
         ge_mine, ge_other = expert_weights(h4_in, ewd, eact, edz)
-    eout = exchange(eout)
-
-    own_route = own(route)
-    dx3, dg4, dr = call(
-        functools.partial(mixture_backward_body, experts),
-        [out((rows, d), F32), out((1, d), F32), out((d, LANES), F32)],
-        x3, g4, h4, router_wide, own(dy), own_route, own_tokens_here, own_tokens_there, ret,
-        flops=8 * rows * slots * d,
-    )
-    expert_sum = lax.psum_scatter(
-        add16(ge_mine, other_core(ge_other)), "grp", scatter_dimension=1, tiled=True)
-
-    dx2, dg3, a2_mine, a2_other = attention_backward(dx3, x2, g3, kept3, qm2, qo2, om2, oo2)
-    c = qkv_one.shape[2]
-    dx1, dg2, gim, gio, gtm, gto = mlp_backward(dx2, x1, g2, h2, act2, slope2, im, io, tm, to, c)
-    dx0, dg1, a1_mine, a1_other = attention_backward(dx1, x0, g1, kept1, qm1, qo1, om1, oo1)
-    eout, dx1 = lax.optimization_barrier((eout, dx1))
-    [output] = call(
-        functools.partial(mixture_output_body, experts), [out((rows, d), BF)],
-        x3, h4, router_wide, own_route, own(live).astype(F32)[:, None], own_tokens_here, own_tokens_there, jnp.stack([eout, other_core(eout)]),
-        flops=8 * rows * slots * d,
-    )
-    small = jnp.concatenate([dg1, dg2, dg3, dg4, dr.T[:experts]], axis=0)
+        ge = add16(ge_mine, other_core(ge_other))
+        dx2, dg3, dg4, dr, a2_mine, a2_other = mixture_attention_backward(
+            experts, x3, h4, router_rows, own_dy, col, ret, *second)
+    expert_sum = lax.psum_scatter(ge, "grp", scatter_dimension=1, tiled=True)
+
+    dx1, dg2, gim, gio, gtm, gto = mlp_backward(dx2, x1, gains, 1, h2, act2, slope2, im, io, tm, to, c)
+    image, dg1, a1_mine, a1_other = attention_backward(dx1, x0, gains, 0, kept1, qm1, qo1, om1, oo1)
     mines, others = (a2_mine, gim, gtm, a1_mine), (a2_other, gio, gto, a1_other)
 
-    per = 2
-    unit = 4 * d // (2 * per)
-    if lax.axis_size("grp") == 4 and n_mdl == 2 and unit % (64 * peers) == 0 and f * 2 == 4 * d:
+    if fused:
         split = [[v.reshape(per, 2, unit, c) for v in side] for side in (mines, others)]
-        totals, small = reduce_all(*split, small, peers)
-        sums = totals.reshape(len(mines), 4 * d, c)
+        qkv2, proj2, fi, fo_, qkv1, proj1, small, output, grad_images = reduce_all(
+            *split, (dg1, dg2, dg3, dg4), dr, x3, h4, router_rows, col, eback, image, peers, experts)
     else:
-        flat = [[v.reshape(4 * d, c) for v in side] for side in (mines, others)]
-        sums = [sum_everywhere(add16(a, other_core(b))) for a, b in zip(*flat)]
-        small = small_sum(small)
-
-    def unpack(total):
-        qkv = total[: 3 * d].reshape(3, d, c).astype(F32)
-        return qkv, panels(total[3 * d :].reshape(d // c, c, c))
-
-    def panels(v):
-        return jnp.concatenate([v[i] for i in range(v.shape[0])], axis=1).astype(F32)
-
-    def both(v):
-        there = other_core(v)
-        joined = jnp.where(core == 0, jnp.concatenate([v, there]), jnp.concatenate([there, v]))
-        return joined.reshape(n_slot, LP, d)[:, :length]
-
-    grad_qkv_two, grad_out_two = unpack(sums[0])
-    grad_fc_in = panels(sums[1].reshape(f // c, d, c))
-    grad_fc_out = panels(sums[2].reshape(d // c, f, c))
-    grad_qkv_one, grad_out_one = unpack(sums[3])
+        sums = [sum_everywhere(add16(a.reshape(4 * d, c), other_core(b.reshape(4 * d, c)))) for a, b in zip(mines, others)]
+        small = small_sum(jnp.concatenate([dg1, dg2, dg3, dg4, dr[:experts]], axis=0))
+
+        def panels(v):
+            return jnp.concatenate([v[i] for i in range(v.shape[0])], axis=1)
+
+        (qkv2, proj2), (qkv1, proj1) = (
+            (v[: 3 * d].reshape(3, d, c), panels(v[3 * d :].reshape(d // c, c, c))) for v in (sums[0], sums[3]))
+        fi, fo_ = panels(sums[1].reshape(f // c, d, c)), panels(sums[2].reshape(d // c, f, c))
+        [own_out] = call(
+            functools.partial(mixture_output_body, experts), [out((own_img, L, d), BF)], x3, h4, router_rows, col, eback,
+            flops=8 * rows * slots * d)
+
+        def both(v):
+            there = other_core(v)
+            return jnp.where(core == 0, jnp.concatenate([v, there]), jnp.concatenate([there, v]))
+
+        output, grad_images = both(own_out), both(image)
     return (
-        both(output), both(dx0.astype(BF)),
-        small[0], grad_qkv_one, grad_out_one, small[1], grad_fc_in, grad_fc_out,
-        small[2], grad_qkv_two, grad_out_two, small[3], small[4:].T,
+        output, grad_images,
+        small[0], qkv1.astype(F32), proj1.astype(F32), small[1], fi.astype(F32), fo_.astype(F32),
+        small[2], qkv2.astype(F32), proj2.astype(F32), small[3], small[4 : 4 + experts].T,
         expert_sum[0].astype(F32)[None], expert_sum[1].astype(F32).T[None],
     )
 

time: 473 us -> 443 us (0.937)
  other arithmetic: 32.6 us -> 16.6 us
  Pallas kernels: 366 us -> 380 us
  local copies, waits for them, and re-layouts: 29.7 us -> 17.9 us
  starting transfers between devices: 13.6 us -> 2.44 us
    pallas_call x1 -> x3, Pallas kernels: 180 us -> 249 us  [the longest x1 188 us: reduce_all(): pl.pallas_call(functools.partial(reduce_body, len(mine), per, n_exp, expe...]
    pallas_call x10 -> x5, Pallas kernels: 119 us -> 66.9 us  [call(): pl.pallas_call(body, grid=grid, in_specs=in_specs, out_specs=out_specs, o...]
    slice x13 -> x0, local copies, waits for them, and re-layouts: 11.7 us -> none  [the longest x1 3.85 us: on_device(): grad_qkv_two, grad_out_two = unpack(sums[0])]
    all_to_all x2 -> x0, starting transfers between devices: 10.8 us -> none  [exchange(): return lax.all_to_all(shaped, 'exp', 0, 0, tiled=True).reshape(v.shape)]
    convert_element_type x11 -> x7, other arithmetic: 20.3 us -> 11.6 us  [the longest x1 2.82 us: on_device(): fi.astype(F32)]
    unnamed x52 -> x34, local copies, waits for them, and re-layouts: 6.51 us -> 9.53 us
  transfers between devices with their start and end apart: 15 -> 9, of which waited for: 1 -> 1; matrix products, arithmetic and copies ran while one was open for 11% -> 6% of each run, Pallas kernels for 64% -> 72%
where the time goes in v4:
time: 443 us; the launch traced here: 438 us
  Pallas kernels  380 us (86%)
  local copies, waits for them, and re-layouts  17.9 us (4%)
  other arithmetic  16.6 us (4%)
  between operations  15.1 us (3%)
  waiting for transfers between devices  5.95 us (1%)
    pallas_call x1, Pallas kernels, reduce_all(): pl.pallas_call(functools.partial(reduce_body, len(mine), per, n_exp, expe...  188 us
    pallas_call x5, Pallas kernels, call(): pl.pallas_call(body, grid=grid, in_specs=in_specs, out_specs=out_specs, o...  66.9 us
    pallas_call x1, Pallas kernels, expert_exchange(): pl.pallas_call(functools.partial(expert_exchange_body, experts, half), in...  64.9 us
    pallas_call x1, Pallas kernels, mixture_attention_backward(): pl.pallas_call(functools.partial(mixture_attention_backward_body, n_img,...  32.6 us
    pallas_call x1, Pallas kernels, attention_forward(): pl.pallas_call(functools.partial(attention_forward_body, n_img, g_at, tai...  28.1 us
    unnamed x34, local copies, waits for them, and re-layouts  9.53 us
  transfers between devices with their start and end apart: 9, of which 1 were waited for; matrix products, arithmetic and copies ran while one was open for 6% of the time, Pallas kernels for 72%

profile of v4, /device:TPU:0, one launch (start us, length us, event | category | flops | bytes accessed | tf_op | source)
XLA Modules:
  0.0 438.4 jit_solution(8332815646504613496)
XLA Ops:
  8.8 5.9 %collective-permute-done.1.refs_5_.oo = bf16[384,768]{1,0:T(8,128)(2,1)S(1)} collective-permute-done((bf16[384,768]{1,0:T(8,128)(2,1)}, bf16[384,768]{1,0:T(8,128)(2,1)S(1)}, u32[]{:S(2)}, u32[]{:S(2)}) %collective-permute-start.1) | collective-permute-done | bytes 589856 | tf_op jit(solution)/shard_map/ppermute | solution.py:644
  15.9 0.7 stack.15
  16.6 0.7 stack.16
  17.3 0.7 stack.17
  18.0 0.7 stack.18
  18.7 0.7 reduce
  19.5 0.7 pad_add_fusion
  20.9 1.4 copy.37
  23.8 1.1 pad.17.clone
  25.5 0.9 constant_dynamic-slice_fusion.1.refs_0_.x_ref
  26.4 4.2 shard_map.289
  31.0 28.1 %shard_map.290 = (f32[416,768]{1,0:T(8,128)}, bf16[416,768]{1,0:T(8,128)(2,1)}, bf16[416,2304]{1,0:T(8,128)(2,1)}, bf16[24,208,208]{2,1,0:T(8,128)(2,1)}, bf16[4...) custom-call(bf16[416,768]{1,0:T(8,128)(2,1)} %constant_dynamic-slice_fusion.1.refs_0_.x_ref, ...), custom_call_target="tpu_custom_call" | custom-call | flops 2494562304 | bytes 40894464 | tf_op jit(solution)/shard_map/pallas_call | solution.py:197
  59.1 11.2 %shard_map.291 = (f32[416,768]{1,0:T(8,128)}, bf16[416,768]{1,0:T(8,128)(2,1)}, bf16[2,416,1536]{2,1,0:T(8,128)(2,1)}, bf16[2,416,1536]{2,1,0:T(8,128)(2,1)}) custom-call(f32[416,768]{1,0:T(8,128)} %get-tuple-element.64.x_ref, f32[4,768]{1,0:T(4,128)} %pad_maximum_fusion.refs_1_.g_ref.refs_7_, bf16[768,1536]{1,0:T(8,128)(2,1)} %im.3, ...), custom_call_target="tpu_custom_call" | custom-call | flops 3925868544 | bytes 17756160 | tf_op jit(solution)/shard_map/pallas_call | solution.py:65
  70.3 0.8 copy-done.14
  71.1 13.2 %shard_map.292 = (f32[416,768]{1,0:T(8,128)}, bf16[416,768]{1,0:T(8,128)(2,1)}, bf16[416,2304]{1,0:T(8,128)(2,1)}, bf16[24,208,208]{2,1,0:T(8,128)(2,1)}, bf16[4...) custom-call(f32[416,768]{1,0:T(8,128)} %get-tuple-element.65.refs_0_.refs_6_, ...), custom_call_target="tpu_custom_call" | custom-call | flops 2494562304 | bytes 13197312 | tf_op jit(solution)/shard_map/pallas_call | solution.py:65
  84.3 64.9 %shard_map.293 = (bf16[2,640,896]{2,1,0:T(8,128)(2,1)}, bf16[640,768]{1,0:T(8,128)(2,1)}, bf16[2,768,1536]{2,1,0:T(8,128)(2,1)}) custom-call(bf16[416,768]{1,0:T(8,128)(2,1)} %get-tuple-element.67.h4_ref.refs_1_.refs_14_, s32[4,8,256]{2,1,0:T(8,128)} %get-tuple-element.69.tr_ref, bf16[640,768]{1,0:T(8,128)(2,1)} %get-tuple-element.70.dyin_ref, ...), custom_call_target="tpu_custom_call" | custom-call | flops 18119393280 | bytes 23592960 | tf_op jit(solution)/shard_map/pallas_call | solution.py:1131
  149.3 1.3 copy-done
  150.5 0.9 constant_dynamic-slice_fusion.refs_3_
  151.4 32.6 %shard_map.294 = (f32[416,768]{1,0:T(8,128)}, f32[1,768]{1,0:T(1,128)}, f32[1,768]{1,0:T(1,128)}, f32[128,768]{1,0:T(8,128)}, bf16[3072,384]{1,0:T(8,128)(2,1)},...) custom-call(f32[416,768]{1,0:T(8,128)} %get-tuple-element.66.refs_0_.refs_13_, ...), custom_call_target="tpu_custom_call" | custom-call | flops 6624903168 | bytes 61341696 | tf_op jit(solution)/shard_map/pallas_call | solution.py:607
  184.0 18.5 %shard_map.295 = (f32[416,768]{1,0:T(8,128)}, f32[1,768]{1,0:T(1,128)}, bf16[4,768,384]{2,1,0:T(8,128)(2,1)}, bf16[4,768,384]{2,1,0:T(8,128)(2,1)}, bf16[2,1536,...) custom-call(f32[416,768]{1,0:T(8,128)} %get-tuple-element.78.dy_ref, f32[416,768]{1,0:T(8,128)} %get-tuple-element.64.x_ref, ...), custom_call_target="tpu_custom_call" | custom-call | flops 7851737088 | bytes 28474368 | tf_op jit(solution)/shard_map/pallas_call | solution.py:65
  202.5 19.9 %shard_map.296 = (bf16[2,197,768]{2,1,0:T(8,128)(2,1)}, f32[1,768]{1,0:T(1,128)}, bf16[3072,384]{1,0:T(8,128)(2,1)}, bf16[3072,384]{1,0:T(8,128)(2,1)}) custom-call(f32[416,768]{1,0:T(8,128)} %get-tuple-element.84.dy_ref, bf16[416,768]{1,0:T(8,128)(2,1)} %constant_dynamic-slice_fusion.1.refs_0_.x_ref, f32[4,768]{1,0:T(4,128)} %pad_maximum_fusion.refs_1_.g_ref.refs_7_, ...), custom_call_target="tpu_custom_call" | custom-call | flops 4989124608 | bytes 17246208 | tf_op jit(solution)/shard_map/pallas_call | solution.py:65
  222.3 187.9 %shard_map.297 = (bf16[3,768,384]{2,1,0:T(8,128)(2,1)}, bf16[384,768]{1,0:T(8,128)(2,1)}, bf16[768,1536]{1,0:T(8,128)(2,1)}, bf16[1536,768]{1,0:T(8,128)(2,1)}, ...) custom-call(bf16[2,2,768,384]{3,2,1,0:T(8,128)(2,1)} %bitcast.30, ...), custom_call_target="tpu_custom_call" | custom-call | flops 1635778560 | bytes 18874368 | tf_op jit(solution)/shard_map/pallas_call | solution.py:930
  410.2 2.9 copy.35
  413.1 1.1 convert_element_type.40
  414.2 1.1 convert_element_type.44
  415.3 1.5 copy.36
  416.8 2.0 convert_element_type.39
  419.0 2.0 convert_element_type.43
  421.0 0.8 copy-done.2
  421.8 2.8 convert_element_type.41
  424.6 2.5 convert_element_type.42
  428.4 2.9 convert_bitcast_fusion
  (55 shorter events, 6.8 us)
Async XLA Ops:
  7.2 15.1 %copy-start.10 = (bf16[768,4]{0,1:T(4,128)(2,1)S(1)}, bf16[768,4]{0,1:T(4,128)(2,1)}, u32[]{:S(2)}) copy-start(bf16[768,4]{0,1:T(4,128)(2,1)} %param.32) | copy-start | bytes 18436
  7.2 421.2 %reduce-scatter.2.cloned.1.call-start = ((), (), s32[]{:S(2)}) async-start(), calls=%async_computation.1 | async-start | bytes 5898240 | tf_op jit(solution)/shard_map/reduce_scatter | solution.py:1220
  7.2 7.8 %collective-permute-start = (bf16[3,768,384]{2,1,0:T(8,128)(2,1)}, bf16[3,768,384]{2,1,0:T(8,128)(2,1)S(1)}, u32[]{:S(2)}, u32[]{:S(2)}) collective-permute-start(bf16[3,768,384]{2,1,0:T(8,128)(2,1)} %qm.1), channel_id=1, source_target_pairs={{0,1},{1,0},{2,3},{3,2},{4,5},{5,4},{6,7},{7,6},{8,9},{9,8},{10,11... | collective-permute-start | bytes 5308424 | tf_op jit(solution)/shard_map/ppermute | solution.py:644
  7.8 22.9 %collective-permute-start.2 = (bf16[768,1536]{1,0:T(8,128)(2,1)}, bf16[768,1536]{1,0:T(8,128)(2,1)}, u32[]{:S(2)}, u32[]{:S(2)}) collective-permute-start(bf16[768,1536]{1,0:T(8,128)(2,1)} %im.3), channel_id=1, source_target_pairs={{0,1},{1,0},{2,3},{3,2},{4,5},{5,4},{6,7},{7,6},{8,9},{9,8},{10,11... | collective-permute-start | bytes 7077896 | tf_op jit(solution)/shard_map/ppermute | solution.py:644
  7.8 51.3 %collective-permute-start.3 = (bf16[1536,768]{1,0:T(8,128)(2,1)}, bf16[1536,768]{1,0:T(8,128)(2,1)}, u32[]{:S(2)}, u32[]{:S(2)}) collective-permute-start(bf16[1536,768]{1,0:T(8,128)(2,1)} %tm.3), channel_id=1, source_target_pairs={{0,1},{1,0},{2,3},{3,2},{4,5},{5,4},{6,7},{7,6},{8,9},{9,8},{10,11... | collective-permute-start | bytes 7077896 | tf_op jit(solution)/shard_map/ppermute | solution.py:644
  8.3 6.4 %collective-permute-start.1 = (bf16[384,768]{1,0:T(8,128)(2,1)}, bf16[384,768]{1,0:T(8,128)(2,1)S(1)}, u32[]{:S(2)}, u32[]{:S(2)}) collective-permute-start(bf16[384,768]{1,0:T(8,128)(2,1)} %om.1), channel_id=1, source_target_pairs={{0,1},{1,0},{2,3},{3,2},{4,5},{5,4},{6,7},{7,6},{8,9},{9,8},{10,11... | collective-permute-start | bytes 1769480 | tf_op jit(solution)/shard_map/ppermute | solution.py:644
  8.3 76.0 %collective-permute-start.6 = (bf16[768,1536]{1,0:T(8,128)(2,1)}, bf16[768,1536]{1,0:T(8,128)(2,1)}, u32[]{:S(2)}, u32[]{:S(2)}) collective-permute-start(bf16[768,1536]{1,0:T(8,128)(2,1)} %bitcast.40), channel_id=1, source_target_pairs={{0,1},{1,0},{2,3},{3,2},{4,5},{5,4},{6,7},{7,6},{8,9},{9,8},{10,11... | collective-permute-start | bytes 7077896 | tf_op jit(solution)/shard_map/ppermute | solution.py:644
  14.7 7.6 %copy-start.13 = (bf16[384,768]{1,0:T(8,128)(2,1)}, bf16[384,768]{1,0:T(8,128)(2,1)S(1)}, u32[]{:S(2)}) copy-start(bf16[384,768]{1,0:T(8,128)(2,1)S(1)} %collective-permute-done.1.refs_5_.oo) | copy-start | bytes 1769476
  14.7 69.6 %collective-permute-start.7 = (bf16[1536,768]{1,0:T(8,128)(2,1)}, bf16[1536,768]{1,0:T(8,128)(2,1)}, u32[]{:S(2)}, u32[]{:S(2)}) collective-permute-start(bf16[1536,768]{1,0:T(8,128)(2,1)} %bitcast.42), channel_id=1, source_target_pairs={{0,1},{1,0},{2,3},{3,2},{4,5},{5,4},{6,7},{7,6},{8,9},{9,8},{10,11... | collective-permute-start | bytes 7077896 | tf_op jit(solution)/shard_map/ppermute | solution.py:644
  15.1 8.0 %copy-start.11 = (bf16[3,768,384]{2,1,0:T(8,128)(2,1)}, bf16[3,768,384]{2,1,0:T(8,128)(2,1)S(1)}, u32[]{:S(2)}) copy-start(bf16[3,768,384]{2,1,0:T(8,128)(2,1)S(1)} %collective-permute-done.refs_3_.qo) | copy-start | bytes 5308420
  15.1 55.2 %collective-permute-start.4 = (bf16[3,768,384]{2,1,0:T(8,128)(2,1)}, bf16[3,768,384]{2,1,0:T(8,128)(2,1)}, u32[]{:S(2)}, u32[]{:S(2)}) collective-permute-start(bf16[3,768,384]{2,1,0:T(8,128)(2,1)} %refs_12_.1), channel_id=1, source_target_pairs={{0,1},{1,0},{2,3},{3,2},{4,5},{5,4},{6,7},{7,6},{8,9},{9,8},{10,11... | collective-permute-start | bytes 5308424 | tf_op jit(solution)/shard_map/ppermute | solution.py:644
  22.3 1.4 copy-start.6
  26.4 4.2 copy-start.12
  30.6 39.6 %collective-permute-start.5 = (bf16[384,768]{1,0:T(8,128)(2,1)S(1)}, bf16[384,768]{1,0:T(8,128)(2,1)S(1)}, u32[]{:S(2)}, u32[]{:S(2)}) collective-permute-start(bf16[384,768]{1,0:T(8,128)(2,1)S(1)} %copy-done.12), channel_id=1, source_target_pairs={{0,1},{1,0},{2,3},{3,2},{4,5},{5,4},{6,7},{7,6},{8,9},{9,8},{10,11... | collective-permute-start | bytes 1769480 | tf_op jit(solution)/shard_map/ppermute | solution.py:644
  70.3 0.8 copy-start.14
  149.2 1.3 copy-start
  410.2 2.9 copy-start.8
  410.2 4.0 copy-start.7
  413.1 2.2 copy-start.5
  414.2 2.6 copy-start.4
  416.8 2.2 copy-start.3
  419.0 2.8 copy-start.2
  421.8 2.8 copy-start.1
  424.6 2.5 copy-start.9
Sparse Core Ops, SparseCore 0:
  149.4 57.5 reduce-scatter.1

commit v5 on v4

--- a/solution.py
+++ b/solution.py
@@ -83,125 +83,76 @@
     return (lane < HDIM).astype(dtype)
 
 
-class Exchange:
-    def __init__(self, size, half, src, dst, send, recv, local):
-        self.z = lax.axis_index("exp")
-        self.size, self.half, self.src, self.dst = size, half, src, dst
-        self.send, self.recv, self.local = send, recv, local
-
-    def signal(self):
-        barrier = pltpu.get_barrier_semaphore()
-        for o in range(1, self.size):
-            pl.semaphore_signal(barrier, inc=1, device_id={"exp": (self.z + o) % self.size}, device_id_type=MESH)
-
-    def at(self, e):
-        return pl.ds(pl.multiple_of(e * self.half, self.half), self.half)
-
-    def copies(self):
-        for o in range(1, self.size):
-            to = (self.z + o) % self.size
-            yield pltpu.make_async_remote_copy(self.src.at[self.at(to)], self.dst.at[self.at(self.z)], self.send.at[o - 1],
-                                               self.recv.at[o - 1], device_id={"exp": to}, device_id_type=MESH)
-
-    def own(self):
-        return pltpu.make_async_copy(self.src.at[self.at(self.z)], self.dst.at[self.at(self.z)], self.local)
-
-    def start(self):
-        self.own().start()
-        for cp in self.copies():
-            cp.start()
-
-    def arrived(self):
-        self.own().wait()
-        for o in range(1, self.size):
-            come = (self.z + self.size - o) % self.size
-            pltpu.make_async_remote_copy(self.src.at[self.at(come)], self.dst.at[self.at(come)], self.send.at[o - 1],
-                                         self.recv.at[o - 1], device_id={"exp": come}, device_id_type=MESH).wait_recv()
-
-    def left(self):
-        for cp in self.copies():
-            cp.wait_send()
-
-
-def attention_forward_body(n_img, g_at, tail, size, half, *refs):
+def beside(z, j):
+    b0, b1 = z % 2, z // 2
+    if j & 1:
+        b0 = 1 - b0
+    if j & 2:
+        b1 = 1 - b1
+    return b0 + 2 * b1
+
+
+def own_rows(ref, n):
+    if ref.shape[0] == n:
+        return ref[...]
+    return ref[pl.ds(pl.multiple_of(lax.axis_index("mdl") * n, 16), n), :]
+
+
+def attend(img, pair, d, qkv_ref, p_ref, o_ref):
+    mask = head_mask(BF)
+    key_ok = lax.broadcasted_iota(I32, (LP, LP), 1) < L
+    rows = pl.ds(pl.multiple_of(img * LP, LP), LP)
+    col = pair * LANES
+    q = qkv_ref[rows, pl.ds(pl.multiple_of(col, LANES), LANES)]
+    ke = qkv_ref[rows, pl.ds(pl.multiple_of(d + col, LANES), LANES)]
+    u = qkv_ref[rows, pl.ds(pl.multiple_of(2 * d + col, LANES), LANES)]
+    o = jnp.zeros((LP, LANES), F32)
+    for hh in range(2):
+        mk = mask if hh == 0 else 1 - mask
+        s = nt(q * mk, ke) * HDIM ** (-0.5)
+        s = jnp.where(key_ok, s, -1e30)
+        e = jnp.exp(s - jnp.max(s, axis=-1, keepdims=True))
+        p = (e / jnp.sum(e, axis=-1, keepdims=True)).astype(BF)
+        p_ref[2 * (img * (d // LANES) + pair) + hh] = p
+        o = o + nn(p, u * mk)
+    o_ref[rows, pl.ds(pl.multiple_of(col, LANES), LANES)] = o.astype(BF)
+    return 0
+
+
+def attention_forward_body(n_img, g_at, tail, *refs):
     refs = list(refs)
     x_ref, g_ref, qm, qo, om, oo = refs[:6]
     del refs[:6]
-    src = refs.pop(0) if size else None
     y_ref, h_ref, qkv_ref, p_ref, o_ref = refs[:5]
     del refs[:5]
     h4_ref = refs.pop(0) if tail is not None else None
-    if size:
-        dst, send, recv, local = refs
-        carried = Exchange(size, half, src, dst, send, recv, local)
-        carried.signal()
+    rows_all = n_img * LP
     d = x_ref.shape[1]
     c = qm.shape[2]
     pairs = d // LANES
-    _, _, h = norm_forward(x_ref[...].astype(F32), g_ref[g_at : g_at + 1, :])
+    _, _, h = norm_forward(own_rows(x_ref, rows_all).astype(F32), g_ref[g_at : g_at + 1, :])
     h_ref[...] = h
-    if size:
-        pl.semaphore_wait(pltpu.get_barrier_semaphore(), size - 1)
-        carried.start()
     for k in range(3):
         for side, w in ((0, qm), (1, qo)):
             at = (2 * k + side) * c
             qkv_ref[:, at : at + c] = nn(h_ref[...], w[k]).astype(BF)
-    mask = head_mask(BF)
-    key_ok = lax.broadcasted_iota(I32, (LP, LP), 1) < L
-
-    def one(i, _):
-        rows = pl.ds(pl.multiple_of((i // pairs) * LP, LP), LP)
-        col = (i % pairs) * LANES
-        q = qkv_ref[rows, pl.ds(pl.multiple_of(col, LANES), LANES)]
-        ke = qkv_ref[rows, pl.ds(pl.multiple_of(d + col, LANES), LANES)]
-        u = qkv_ref[rows, pl.ds(pl.multiple_of(2 * d + col, LANES), LANES)]
-        o = jnp.zeros((LP, LANES), F32)
-        for hh in range(2):
-            mk = mask if hh == 0 else 1 - mask
-            s = nt(q * mk, ke) * HDIM ** (-0.5)
-            s = jnp.where(key_ok, s, -1e30)
-            e = jnp.exp(s - jnp.max(s, axis=-1, keepdims=True))
-            p = (e / jnp.sum(e, axis=-1, keepdims=True)).astype(BF)
-            p_ref[2 * i + hh] = p
-            o = o + nn(p, u * mk)
-        o_ref[rows, pl.ds(pl.multiple_of(col, LANES), LANES)] = o.astype(BF)
-        return 0
-
-    lax.fori_loop(0, n_img * pairs, one, 0, unroll=2)
-    y = x_ref[...].astype(F32) + nn(o_ref[:, :c], om[...]) + nn(o_ref[:, c:], oo[...])
+    lax.fori_loop(0, n_img * pairs, lambda i, _: attend(i // pairs, i % pairs, d, qkv_ref, p_ref, o_ref), 0, unroll=2)
+    y = own_rows(x_ref, rows_all).astype(F32) + nn(o_ref[:, :c], om[...]) + nn(o_ref[:, c:], oo[...])
     y_ref[...] = y
     if tail is not None:
         _, _, h4 = norm_forward(y, g_ref[tail : tail + 1, :])
         h4_ref[...] = h4
-    if size:
-        carried.arrived()
-        carried.left()
-
-
-def attention_forward(x, gains, g_at, qm, qo, om, oo, tail=None, carry=None):
-    r, d = x.shape
+
+
+def attention_forward(x, r, gains, g_at, qm, qo, om, oo, tail=None):
+    d = x.shape[1]
     n_img = r // LP
     heads = d // HDIM
     shapes = [out((r, d), F32), out((r, d), BF), out((r, 3 * d), BF), out((n_img * heads, LP, LP), BF), out((r, d), BF)]
-    args = [x, gains, qm, qo, om, oo]
-    flops = 2 * r * d * d * 4 + 4 * n_img * heads * LP * LP * LANES
     if tail is not None:
         shapes.append(out((r, d), BF))
-    if carry is None:
-        return call(functools.partial(attention_forward_body, n_img, g_at, tail, 0, 0), shapes, *args, flops=flops)
-    src, size, half = carry
-    any_ = pl.BlockSpec(memory_space=pl.ANY)
-    vm = pl.BlockSpec(memory_space=pltpu.VMEM)
-    D = pltpu.SemaphoreType.DMA
-    return pl.pallas_call(
-        functools.partial(attention_forward_body, n_img, g_at, tail, size, half),
-        in_specs=[vm] * 6 + [any_], out_specs=[vm] * len(shapes) + [any_],
-        out_shape=shapes + [out(src.shape, src.dtype)],
-        scratch_shapes=[D((size - 1,)), D((size - 1,)), D],
-        compiler_params=pltpu.CompilerParams(collective_id=2, has_side_effects=True, vmem_limit_bytes=VMEM_BYTES),
-        cost_estimate=pl.CostEstimate(flops=flops, bytes_accessed=16 * r * d * 8, transcendentals=0),
-    )(*args, src)
+    return call(functools.partial(attention_forward_body, n_img, g_at, tail), shapes, x, gains, qm, qo, om, oo,
+                flops=2 * r * d * d * 4 + 4 * n_img * heads * LP * LP * LANES)
 
 
 def attention_backward_core(n_img, dy, x_ref, gain, h_ref, qkv_ref, p_ref, o_ref, qm, qo, om, oo,
@@ -244,13 +195,13 @@
 
     lax.fori_loop(0, n_img * pairs, one, 0, unroll=2)
     tr_ref[...] = h_ref[...].T
-    dh = jnp.zeros(x_ref.shape, F32)
+    dh = jnp.zeros((n_img * LP, d), F32)
     for k in range(3):
         for side, (w, g) in enumerate(((qm, gm_ref), (qo, go_ref))):
             at = (2 * k + side) * c
             g[k * d : (k + 1) * d, :] = nn(tr_ref[...], dqkv_ref[:, at : at + c]).astype(BF)
             dh = dh + nt(dqkv_ref[:, at : at + c], w[k])
-    n, rr, _ = norm_forward(x_ref[...].astype(F32), gain)
+    n, rr, _ = norm_forward(own_rows(x_ref, n_img * LP).astype(F32), gain)
     dv, dw = norm_backward(n, rr, gain, dh)
     return dy() + dv, dw
 
@@ -270,7 +221,7 @@
 
 
 def attention_backward(dy, x, gains, g_at, kept, qm, qo, om, oo):
-    r, d = x.shape
+    r, d = dy.shape
     c = qm.shape[2]
     n_img = r // LP
     heads = d // HDIM
@@ -382,7 +333,144 @@
     )
 
 
-def routing_body(experts, capacity, half, rows_ref, dy_ref, tr_ref, col_ref, out_ref, tmp):
+def forward_body(n_img, size, *refs):
+    refs = list(refs)
+
+    def take(n):
+        r = refs[:n]
+        del refs[:n]
+        return r
+
+    x_ref, g_ref = take(2)
+    own_w = take(8)
+    dy_out = take(size - 1)
+    results = take(15)
+    other_w = take(8)
+    dy_in = take(size - 1)
+    weights = take(6)
+    held = take(15)
+    load_sem, w_send, w_recv, o_sem, r_sem, d_send, d_recv = refs
+    x1, h1, qkv1, p1, o1, x2, h2, act, slope, x3, h3, qkv3, p3, o3, h4 = held
+    q1, w1, fi, fo, q3, w3 = weights
+    r = n_img * LP
+    d = x_ref.shape[1]
+    c = q1.shape[3]
+    f = fi.shape[2]
+    z = lax.axis_index("exp")
+    partner = {"mdl": 1 - lax.axis_index("mdl")}
+
+    loads = [pltpu.make_async_copy(own_w[k], weights[k].at[0], load_sem.at[k]) for k in range(6)]
+    for cp in loads:
+        cp.start()
+    barrier = pltpu.get_barrier_semaphore()
+    for dev in [partner] + [{"exp": beside(z, j)} for j in range(1, size)]:
+        pl.semaphore_signal(barrier, inc=1, device_id=dev, device_id_type=MESH)
+    pl.semaphore_wait(barrier, size)
+    swaps = [pltpu.make_async_remote_copy(own_w[k], weights[k].at[1] if k < 6 else other_w[k], w_send.at[k], w_recv.at[k],
+                                          device_id=partner, device_id_type=MESH) for k in range(8)]
+    for cp in swaps:
+        cp.start()
+    blocks = [pltpu.make_async_remote_copy(dy_out[j - 1], dy_in[j - 1], d_send.at[j - 1], d_recv.at[j - 1],
+                                           device_id={"exp": beside(z, j)}, device_id_type=MESH) for j in range(1, size)]
+    for cp in blocks:
+        cp.start()
+    keeps = [pltpu.make_async_copy(weights[k].at[1], other_w[k], o_sem.at[k]) for k in range(6)]
+    stores = [pltpu.make_async_copy(held[k], results[k], r_sem.at[k]) for k in range(15)]
+
+    def store(*at):
+        for k in at:
+            stores[k].start()
+
+    def attention(x, gain, wq, wo, kq, ko, h, qkv, p, o, y):
+        _, _, n = norm_forward(x(), gain)
+        h[...] = n
+        per_half = c // LANES
+        for side in range(2):
+            if side == 0:
+                loads[kq].wait()
+            else:
+                swaps[kq].wait_recv()
+                keeps[kq].start()
+            for k in range(3):
+                at = (2 * k + side) * c
+                qkv[:, at : at + c] = nn(h[...], wq[side, k]).astype(BF)
+            lax.fori_loop(
+                0, n_img * per_half,
+                lambda i, _, side=side: attend(i // per_half, side * per_half + i % per_half, d, qkv, p, o), 0, unroll=2)
+        loads[ko].wait()
+        swaps[ko].wait_recv()
+        keeps[ko].start()
+        y[...] = x() + nn(o[:, :c], wo[0]) + nn(o[:, c:], wo[1])
+
+    attention(lambda: own_rows(x_ref, r).astype(F32), g_ref[0:1, :], q1, w1, 0, 1, h1, qkv1, p1, o1, x1)
+    store(0, 1, 2, 3, 4)
+
+    _, _, n = norm_forward(x1[...], g_ref[1:2, :])
+    h2[...] = n
+    x2[...] = x1[...]
+    t = tile_of(f)
+    for side in range(2):
+        for k in (2, 3):
+            if side == 0:
+                loads[k].wait()
+            else:
+                swaps[k].wait_recv()
+                keeps[k].start()
+
+        def tile(i, _, side=side):
+            at = pl.ds(pl.multiple_of(i * t, t), t)
+            a, sl = gelu_parts(nn(h2[...], fi[side, :, at]))
+            a = a.astype(BF)
+            act[side, :, at] = a
+            slope[side, :, at] = sl.astype(BF)
+            x2[...] += nn(a, fo[side, at, :])
+            return 0
+
+        lax.fori_loop(0, f // t, tile, 0)
+    store(5, 6, 7, 8)
+
+    attention(lambda: x2[...], g_ref[2:3, :], q3, w3, 4, 5, h3, qkv3, p3, o3, x3)
+    store(9, 10, 11, 12, 13)
+    _, _, n = norm_forward(x3[...], g_ref[3:4, :])
+    h4[...] = n
+    store(14)
+    for cp in blocks:
+        cp.wait()
+    for cp in keeps + stores:
+        cp.wait()
+    for cp in swaps[6:]:
+        cp.wait_recv()
+    for cp in swaps:
+        cp.wait_send()
+
+
+def forward(x, gains, own_w, dy_out, r):
+    d = x.shape[1]
+    c, f = own_w[0].shape[2], own_w[2].shape[1]
+    n_img = r // LP
+    heads = d // HDIM
+    size = len(dy_out) + 1
+    half = dy_out[0].shape[0]
+    kept = [out((r, d), F32), out((r, d), BF), out((r, 3 * d), BF), out((n_img * heads, LP, LP), BF), out((r, d), BF)]
+    results = kept + [out((r, d), F32), out((r, d), BF), out((2, r, f), BF), out((2, r, f), BF)] + kept + [out((r, d), BF)]
+    shapes = results + [out(w.shape, BF) for w in own_w] + [out((half, d), BF)] * (size - 1)
+    D, V = pltpu.SemaphoreType.DMA, pltpu.VMEM
+    any_ = pl.BlockSpec(memory_space=pl.ANY)
+    vm = pl.BlockSpec(memory_space=pltpu.VMEM)
+    got = pl.pallas_call(
+        functools.partial(forward_body, n_img, size),
+        in_specs=[vm] * 2 + [any_] * (len(own_w) + size - 1), out_specs=[any_] * len(shapes), out_shape=shapes,
+        scratch_shapes=[V((2,) + w.shape, BF) for w in own_w[:6]] + [V(o.shape, o.dtype) for o in results]
+        + [D((6,)), D((8,)), D((8,)), D((6,)), D((len(results),)), D((size - 1,)), D((size - 1,))],
+        compiler_params=pltpu.CompilerParams(collective_id=2, has_side_effects=True, vmem_limit_bytes=VMEM_BYTES),
+        cost_estimate=pl.CostEstimate(flops=16 * r * d * d + 8 * r * d * f, bytes_accessed=80 * r * d, transcendentals=0),
+    )(x, gains, *own_w, *dy_out)
+    n = len(results)
+    return got[:n], got[n : n + 8], got[n + 8 :]
+
+
+def routing_body(experts, capacity, half, rows_ref, dy_ref, tr_ref, col_ref, *refs):
+    out_refs, tmp = refs[:-1], refs[-1]
     n_img = rows_ref.shape[0]
     slots = experts * half
     core = lax.axis_index("mdl")
@@ -417,11 +505,14 @@
         tmp[4:8, :] = rows_ref[at, 0:4, :]
         tmp[6:7, :] = rows_ref[at, 3:4, :]
         col_ref[i * LP : (i + 1) * LP, :] = tmp[...].astype(F32).T[:LP, :].astype(I32)
-    total = None
-    for i in range(n_img):
-        part = nn(slot_hots(tr_ref[i], core * slots, slots), dy_ref[i * LP : (i + 1) * LP, :])
-        total = part if total is None else total + part
-    out_ref[...] = total.astype(BF)
+    z = lax.axis_index("exp")
+    for j, o_ref in enumerate(out_refs):
+        at = core * slots + (beside(z, j) * half if len(out_refs) > 1 else 0)
+        total = None
+        for i in range(n_img):
+            part = nn(slot_hots(tr_ref[i], at, o_ref.shape[0]), dy_ref[i * LP : (i + 1) * LP, :])
+            total = part if total is None else total + part
+        o_ref[...] = total.astype(BF)
 
 
 def slot_hots(t, base, count):
@@ -534,6 +625,18 @@
     return rows
 
 
+def merge_blocks(col_ref, k, blocks, n):
+    rows = None
+    for side in range(2):
+        for e, ref in blocks[side]:
+            half = ref.shape[0]
+            lane = lax.broadcasted_iota(I32, (n, half), 1) + e * half
+            hot = (lane == col_ref[:, 2 * side + k : 2 * side + k + 1]).astype(F32).astype(BF)
+            part = nn(hot, ref[...])
+            rows = part if rows is None else rows + part
+    return rows
+
+
 def mixture_backward_core(experts, x_ref, gain, h_ref, router_ref, dy_ref, col_ref, ab_ref, dr_ref):
     n, d = x_ref.shape
     probs, lane = router_probs(h_ref[...], router_ref[...], experts)
@@ -549,27 +652,12 @@
     dh = dh + nn(dlog, router_ref[...])
     nrm, rr, _ = norm_forward(x_ref[...], gain)
     dv, dw = norm_backward(nrm, rr, gain, dh)
-    return dy_ref[...].astype(F32) * col_ref[:, 6:7].astype(F32) + dv, dw
-
-
-def mixture_attention_backward_body(n_img, experts, size, half, *refs):
-    refs = list(refs)
-    x3_ref, h4_ref, router_ref, dy_ref, col_ref, ret_ref, x_ref, g_ref, h_ref, qkv_ref, p_ref, o_ref, qm, qo, om, oo = refs[:16]
-    del refs[:16]
-    src = refs.pop(0) if size else None
-    dx_ref, dw3_ref, dw4_ref, dr_ref, gm_ref, go_ref = refs[:6]
-    del refs[:6]
-    dst = refs.pop(0) if size else None
-    dx3, do_ref, dqkv_ref, tr_ref = refs[:4]
-    if size:
-        send, recv, local, f_send, f_recv = refs[4:]
-        core = lax.axis_index("mdl")
-        carried = Exchange(size, half, src, dst.at[0], send, recv, local)
-        carried.signal()
-        barrier = pltpu.get_barrier_semaphore()
-        pl.semaphore_signal(barrier, inc=1, device_id={"mdl": 1 - core}, device_id_type=MESH)
-        pl.semaphore_wait(barrier, size)
-        carried.start()
+    return own_rows(dy_ref, n).astype(F32) * col_ref[:, 6:7].astype(F32) + dv, dw
+
+
+def mixture_attention_backward_body(n_img, experts, x3_ref, h4_ref, router_ref, dy_ref, col_ref, ret_ref, x_ref, g_ref, h_ref,
+                                    qkv_ref, p_ref, o_ref, qm, qo, om, oo, dx_ref, dw3_ref, dw4_ref, dr_ref, gm_ref, go_ref,
+                                    dx3, do_ref, dqkv_ref, tr_ref):
     grad, dw4 = mixture_backward_core(experts, x3_ref, g_ref[3:4, :], h4_ref, router_ref, dy_ref, col_ref, ret_ref, dr_ref)
     dx3[...] = grad
     dw4_ref[...] = dw4
@@ -578,54 +666,33 @@
         gm_ref, go_ref, do_ref, dqkv_ref, tr_ref)
     dx_ref[...] = dx
     dw3_ref[...] = dw3
-    if size:
-        carried.arrived()
-        pass_on = pltpu.make_async_remote_copy(dst.at[0], dst.at[1], f_send, f_recv, device_id={"mdl": 1 - core},
-                                               device_id_type=MESH)
-        pass_on.start()
-        carried.left()
-        pass_on.wait()
-
-
-def mixture_attention_backward(experts, x3, h4, router, dy, col, ret, x, gains, kept, qm, qo, om, oo, carry=None):
+
+
+def mixture_attention_backward(experts, x3, h4, router, dy, col, ret, x, gains, kept, qm, qo, om, oo):
     r, d = x.shape
     c = qm.shape[2]
     n_img = r // LP
     heads = d // HDIM
-    args = [x3, h4, router, dy, col, ret, x, gains, *kept, qm, qo, om, oo]
     shapes = [out((r, d), F32), out((1, d), F32), out((1, d), F32), out(router.shape, F32),
               out((3 * d + d, c), BF), out((3 * d + d, c), BF)]
-    scratch = [pltpu.VMEM((r, d), F32)] + attention_backward_scratch(r, d)
-    flops = 4 * r * d * d * 4 + 8 * n_img * heads * LP * LP * LANES + 8 * r * ret.shape[1] * d
-    if carry is None:
-        return call(functools.partial(mixture_attention_backward_body, n_img, experts, 0, 0), shapes, *args,
-                    scratch=scratch, flops=flops)
-    src, size, half = carry
-    any_ = pl.BlockSpec(memory_space=pl.ANY)
-    vm = pl.BlockSpec(memory_space=pltpu.VMEM)
-    D = pltpu.SemaphoreType.DMA
-    return pl.pallas_call(
-        functools.partial(mixture_attention_backward_body, n_img, experts, size, half),
-        in_specs=[vm] * len(args) + [any_], out_specs=[vm] * len(shapes) + [any_],
-        out_shape=shapes + [out((2,) + src.shape, src.dtype)],
-        scratch_shapes=scratch + [D((size - 1,)), D((size - 1,)), D, D, D],
-        compiler_params=pltpu.CompilerParams(collective_id=3, has_side_effects=True, vmem_limit_bytes=VMEM_BYTES),
-        cost_estimate=pl.CostEstimate(flops=flops, bytes_accessed=24 * r * d * 8, transcendentals=0),
-    )(*args, src)
-
-
-def mixture_output(experts, x_ref, h_ref, router_ref, col_ref, ab_ref):
+    return call(functools.partial(mixture_attention_backward_body, n_img, experts), shapes,
+                x3, h4, router, dy, col, ret, x, gains, *kept, qm, qo, om, oo,
+                scratch=[pltpu.VMEM((r, d), F32)] + attention_backward_scratch(r, d),
+                flops=4 * r * d * d * 4 + 8 * n_img * heads * LP * LP * LANES + 8 * r * ret.shape[1] * d)
+
+
+def mixture_output(experts, x_ref, h_ref, router_ref, col_ref, rows_of):
     n, d = x_ref.shape
     probs, lane = router_probs(h_ref[...], router_ref[...], experts)
     mixed = jnp.zeros((n, d), F32)
     for k in range(TOPK):
         gate = jnp.sum(jnp.where(lane == col_ref[:, 4 + k : 5 + k], probs, 0.0), axis=-1, keepdims=True)
-        mixed = mixed + gate * merge(col_ref, k, ab_ref, n)
+        mixed = mixed + gate * rows_of(k)
     return (col_ref[:, 6:7].astype(F32) * (x_ref[...] + mixed)).astype(BF)
 
 
 def mixture_output_body(experts, x_ref, h_ref, router_ref, col_ref, ab_ref, y_ref):
-    y = mixture_output(experts, x_ref, h_ref, router_ref, col_ref, ab_ref)
+    y = mixture_output(experts, x_ref, h_ref, router_ref, col_ref, lambda k: merge(col_ref, k, ab_ref, x_ref.shape[0]))
     for i in range(y_ref.shape[0]):
         y_ref[i] = y[i * LP : i * LP + L]
 
@@ -696,11 +763,13 @@
     mine = refs[:n_in]
     other = refs[n_in : 2 * n_in]
     dg = refs[2 * n_in : 2 * n_in + 4]
-    dr_ref, x3_ref, h4_ref, router_ref, col_ref, ab_ref, image_ref = refs[2 * n_in + 4 : 2 * n_in + 11]
-    outs = refs[2 * n_in + 11 :]
+    dr_ref, x3_ref, h4_ref, router_ref, col_ref = refs[2 * n_in + 4 : 2 * n_in + 9]
+    eouts = refs[2 * n_in + 9 : 2 * n_in + 13]
+    image_ref = refs[2 * n_in + 13]
+    outs = refs[2 * n_in + 14 :]
     qkv2, proj2, fc_in, fc_out, qkv1, proj1, sum_ref, y_ref, gx_ref = outs[:9]
-    (acc, got, r1, r2, zr, sm, y_own, load_sem, m_send, m_recv, x_send, x_recv, z_send, z_recv, s_send, s_recv,
-     i_local, i_send, i_recv) = outs[9:]
+    (acc, got, r1, r2, zr, zz, zs, sm, y_own, load_sem, m_send, m_recv, x_send, x_recv, z_send, z_recv, s_send, s_recv,
+     i_local, i_send, i_recv, e_oth, e_send, e_recv) = outs[9:]
     out_ref = got
     n = n_in * per
     rows = acc.shape[2]
@@ -750,6 +819,11 @@
     for cp in image_copies(0, image_ref, gx_ref):
         cp.start()
 
+    e_copies = [pltpu.make_async_remote_copy(eouts[j], e_oth.at[j], e_send.at[j], e_recv.at[j], device_id={"mdl": 1 - core},
+                                             device_id_type=MESH) for j in range(n_exp)]
+    for cp in e_copies:
+        cp.start()
+
     def swap_at(c):
         return pltpu.make_async_remote_copy(other[0].at[0], got.at[c], m_send.at[c], m_recv.at[c],
                                             device_id={"mdl": 1 - core}, device_id_type=MESH)
@@ -838,6 +912,87 @@
     def s7(c):
         for u in range(2):
             fourth(u, c).wait_recv()
+        for k in range(n):
+
+            @pl.when(c == k)
+            def _(k=k):
+                natural(k)
+
+    zc = 0
+    e, e2, e4 = rows // n_exp, rows // n_exp // 2, rows // n_exp // 4
+
+    def z_out(u, o):
+        return pltpu.make_async_remote_copy(
+            acc.at[zc, u, pl.ds(pl.multiple_of(((z + o) % n_exp) * e, e), e)], zz.at[u, o - 1],
+            z_send.at[0, u, o - 1, zc], z_recv.at[0, u, o - 1, zc], device_id={"exp": (z + o) % n_exp}, device_id_type=MESH)
+
+    def z_first(u):
+        return over(u, 0, zs.at[u, pl.ds(pl.multiple_of((1 - bits[u][0]) * e2, e2), e2)], r1.at[zc, u, 0:e2], 0, zc)
+
+    def z_second(u):
+        return over(u, 1, r1.at[zc, u, pl.ds(pl.multiple_of((1 - bits[u][1]) * e4, e4), e4)], r2.at[zc, u, 0:e4], 1, zc)
+
+    def z_third(u):
+        here = out_ref.at[zc, u, pl.ds(pl.multiple_of(z * e + bits[u][0] * e2 + bits[u][1] * e4, e4), e4)]
+        return over(u, 1, here, here, 2, zc)
+
+    def z_fourth(u):
+        here = out_ref.at[zc, u, pl.ds(pl.multiple_of(z * e + bits[u][0] * e2, e2), e2)]
+        return over(u, 0, here, here, 3, zc)
+
+    def z_back(u, o):
+        here = out_ref.at[zc, u, pl.ds(pl.multiple_of(z * e, e), e)]
+        return pltpu.make_async_remote_copy(here, here, z_send.at[1, u, o - 1, zc], z_recv.at[1, u, o - 1, zc],
+                                            device_id={"exp": (z + o) % n_exp}, device_id_type=MESH)
+
+    def z1():
+        load_at(zc).wait()
+        swap_at(zc).wait_recv()
+        for u in range(2):
+            acc[zc, u] = plus(acc[zc, u], got[zc, u])
+            for o in range(1, n_exp):
+                z_out(u, o).start()
+
+    def z2():
+        for u in range(2):
+            total = acc[zc, u, pl.ds(pl.multiple_of(z * e, e), e)].astype(F32)
+            for o in range(1, n_exp):
+                z_out(u, o).wait_recv()
+                total = total + zz[u, o - 1].astype(F32)
+            zs[u] = total.astype(BF)
+            z_first(u).start()
+
+    def z3():
+        for u in range(2):
+            z_first(u).wait_recv()
+            r1[zc, u, 0:e2] = plus(zs[u, pl.ds(pl.multiple_of(bits[u][0] * e2, e2), e2)], r1[zc, u, 0:e2])
+            z_second(u).start()
+
+    def z4():
+        for u in range(2):
+            z_second(u).wait_recv()
+            mine_rows = pl.ds(pl.multiple_of(z * e + bits[u][0] * e2 + bits[u][1] * e4, e4), e4)
+            out_ref[zc, u, mine_rows] = plus(r1[zc, u, pl.ds(pl.multiple_of(bits[u][1] * e4, e4), e4)], r2[zc, u, 0:e4])
+            z_third(u).start()
+
+    def z5():
+        for u in range(2):
+            z_third(u).wait_recv()
+            z_fourth(u).start()
+
+    def z6():
+        for u in range(2):
+            z_fourth(u).wait_recv()
+            for o in range(1, n_exp):
+                z_back(u, o).start()
+
+    def z7():
+        for u in range(2):
+            for o in range(1, n_exp):
+                z_back(u, o).wait_recv()
+        natural(zc)
+
+    def drain(c, _):
         swap_at(c).wait_send()
         for u in range(2):
             for make in (first, second, third, fourth):
@@ -845,6 +1000,35 @@
             for o in range(1, n_exp):
                 along(u, c, o).wait_send()
                 back(u, c, o).wait_send()
+        return 0
+
+    legs = [({"mdl": 1 - core}), ({"grp": flat["x"]}), ({"grp": flat["y"]})]
+    base = 2 * len(legs) + 1
+
+    def small_leg(i):
+        return pltpu.make_async_remote_copy(sm.at[2 * i], sm.at[2 * i + 1], s_send.at[i], s_recv.at[i], device_id=legs[i],
+                                            device_id_type=MESH)
+
+    def small_along(o):
+        return pltpu.make_async_remote_copy(sm.at[base - 1], sm.at[base + z], s_send.at[len(legs) + o - 1],
+                                            s_recv.at[len(legs) + o - 1], device_id={"exp": (z + o) % n_exp},
+                                            device_id_type=MESH)
+
+    def small_step(i):
+        if i == 0:
+            sm[0] = jnp.zeros(sm.shape[1:], F32)
+            for k in range(4):
+                sm[0, k : k + 1, :] = dg[k][...]
+            sm[0, 4 : 4 + experts, :] = dr_ref[:experts, :]
+        else:
+            small_leg(i - 1).wait()
+            sm[2 * i] = sm[2 * i - 2] + sm[2 * i - 1]
+        if i < len(legs):
+            small_leg(i).start()
+        else:
+            sm[pl.ds(base + z, 1)] = sm[pl.ds(base - 1, 1)]
+            for o in range(1, n_exp):
+                small_along(o).start()
 
     def natural(c):
         i, p = c // per, c % per
@@ -864,59 +1048,60 @@
                 fc_out[v % 2 * rows : (v % 2 + 1) * rows, v // 2 * side : (v // 2 + 1) * side] = out_ref[c, u]
 
     steps = (s1, s2, s3, s4, s5, s6, s7)
+    waves = n - 1 + len(steps) - 1
+    late = waves - 2
+    z_steps = ((0, z1), (2, z2), (3, z3), (4, z4), (5, z5), (6, z6), (late, z7))
+    small_steps = {1: 0, 3: 1, 5: 2, 7: 3}
 
     def wave(tau, _):
         for s, step in enumerate(steps):
-            c = tau - s
-
-            @pl.when((c >= 0) & (c < n))
+            c = tau - s + 1
+
+            @pl.when((c >= 1) & (c < n))
             def _(step=step, c=c):
                 step(c)
 
+        for at, step in z_steps:
+            pl.when(tau == at)(step)
+        for at, i in small_steps.items():
+            pl.when(tau == at)(functools.partial(small_step, i))
         return 0
 
-    first_waves = 3
+    first_waves = 2
     lax.fori_loop(0, first_waves, wave, 0)
-    y = mixture_output(experts, x3_ref, h4_ref, router_ref, col_ref, ab_ref)
+    for cp in e_copies:
+        cp.wait_recv()
+    blocks = [[(beside(z, j), eouts[j]) for j in range(n_exp)], [(beside(z, j), e_oth.at[j]) for j in range(n_exp)]]
+    y = mixture_output(experts, x3_ref, h4_ref, router_ref, col_ref, lambda k: merge_blocks(col_ref, k, blocks, x3_ref.shape[0]))
     for i in range(own_img):
         y_own[i] = y[i * LP : i * LP + L]
     for cp in image_copies(1, y_own, y_ref):
         cp.start()
-    lax.fori_loop(first_waves, n + len(steps) - 1, wave, 0)
-    for c in range(n):
-        natural(c)
+    lax.fori_loop(first_waves, waves, wave, 0)
+    for cp in e_copies:
+        cp.wait_send()
     for k, (src, dst) in enumerate(((image_ref, gx_ref), (y_own, y_ref))):
         local, sent = image_copies(k, src, dst)
         local.wait()
         sent.wait_send()
         image_come(k, src, dst).wait_recv()
-
-    sm[0] = jnp.zeros(sm.shape[1:], F32)
-    for k in range(4):
-        sm[0, k : k + 1, :] = dg[k][...]
-    sm[0, 4 : 4 + experts, :] = dr_ref[:experts, :]
-    legs = [({"mdl": 1 - core}), ({"grp": flat["x"]}), ({"grp": flat["y"]})]
-    for i, dev in enumerate(legs):
-        cp = pltpu.make_async_remote_copy(sm.at[2 * i], sm.at[2 * i + 1], s_send.at[i], s_recv.at[i], device_id=dev, device_id_type=MESH)
-        cp.start()
-        cp.wait()
-        sm[2 * i + 2] = sm[2 * i] + sm[2 * i + 1]
-    base = 2 * len(legs) + 1
-    sm[pl.ds(base + z, 1)] = sm[pl.ds(base - 1, 1)]
-    cps = []
+    lax.fori_loop(1, n, drain, 0)
+    swap_at(zc).wait_send()
+    for u in range(2):
+        for make in (z_first, z_second, z_third, z_fourth):
+            make(u).wait_send()
+        for o in range(1, n_exp):
+            z_out(u, o).wait_send()
+            z_back(u, o).wait_send()
     for o in range(1, n_exp):
-        cps.append(pltpu.make_async_remote_copy(sm.at[base - 1], sm.at[base + z], s_send.at[len(legs) + o - 1], s_recv.at[len(legs) + o - 1],
-                                                device_id={"exp": (z + o) % n_exp}, device_id_type=MESH))
-        cps[-1].start()
-    for cp in cps:
-        cp.wait()
+        small_along(o).wait()
     total = sm[base]
     for k in range(1, n_exp):
         total = total + sm[base + k]
     sum_ref[...] = total
 
 
-def reduce_all(mine, other, dgs, dr, x3, h4, router, col, ab, image, n_exp, experts):
+def reduce_all(mine, other, dgs, dr, x3, h4, router, col, eouts, image, n_exp, experts):
     per, _, rows, c = mine[0].shape
     n = len(mine) * per
     d, f = 2 * c, 4 * c
@@ -929,23 +1114,24 @@
     vm = pl.BlockSpec(memory_space=pltpu.VMEM)
     return pl.pallas_call(
         functools.partial(reduce_body, len(mine), per, n_exp, experts),
-        in_specs=[any_] * (2 * len(mine)) + [vm] * 10 + [any_],
+        in_specs=[any_] * (2 * len(mine)) + [vm] * 13 + [any_],
         out_specs=[vm] * 7 + [any_] * 2,
         out_shape=[out((3, d, c), BF), out((c, d), BF), out((d, f), BF), out((f, d), BF), out((3, d, c), BF), out((c, d), BF),
                    out(small, F32), out((2 * n_img, length, d), BF), out((2 * n_img, length, d), BF)],
         scratch_shapes=[
             V((n, 2, rows, c), BF), V((n, 2, rows, c), BF), V((n, 2, h, c), BF), V((n, 2, q, c), BF),
-            V((n, 2, n_exp - 1, t, c), BF), V((7 + n_exp,) + small, F32), V((n_img, length, d), BF),
+            V((n, 2, n_exp - 1, t, c), BF), V((2, n_exp - 1, rows // n_exp, c), BF), V((2, rows // n_exp, c), BF),
+            V((7 + n_exp,) + small, F32), V((n_img, length, d), BF),
             D((n,)), D((n,)), D((n,)), D((4, 2, n)), D((4, 2, n)), D((2, 2, n_exp - 1, n)), D((2, 2, n_exp - 1, n)),
-            D((3 + n_exp,)), D((3 + n_exp,)), D((2,)), D((2,)), D((2,)),
+            D((3 + n_exp,)), D((3 + n_exp,)), D((2,)), D((2,)), D((2,)), V((n_exp,) + eouts[0].shape, BF), D((n_exp,)), D((n_exp,)),
         ],
         compiler_params=pltpu.CompilerParams(collective_id=0, has_side_effects=True, vmem_limit_bytes=VMEM_BYTES),
-        cost_estimate=pl.CostEstimate(flops=8 * x3.shape[0] * ab.shape[1] * d, bytes_accessed=n * 8 * rows * c, transcendentals=0),
-    )(*mine, *other, *dgs, dr, x3, h4, router, col, ab, image)
-
-
-def expert_exchange_body(experts, half, h4_ref, tr_ref, dyin_ref, router_ref, im, io, tm, to,
-                         ret_ref, eout_ref, gw_ref,
+        cost_estimate=pl.CostEstimate(flops=8 * x3.shape[0] * x3.shape[0] * d, bytes_accessed=n * 8 * rows * c, transcendentals=0),
+    )(*mine, *other, *dgs, dr, x3, h4, router, col, *eouts, image)
+
+
+def expert_exchange_body(experts, half, h4_ref, tr_ref, dy0, dy1, dy2, dy3, router_ref, im, io, tm, to,
+                         ret_ref, e0, e1, e2, e3, gw_ref,
                          h_oth, part, xo, x, wi, wo, act, dz, wd, acc, dxa, rsend, gscr, ggot, xt, wt,
                          w_sem, swap_sem, x_send, x_recv, r_send, r_recv, f_send, f_recv, g_send, g_recv, g_sem):
     n, d = h4_ref.shape
@@ -957,13 +1143,10 @@
     size = experts
     near_first = [1, 3, 2]
 
+    out_grad, eouts = (dy0, dy1, dy2, dy3), (e0, e1, e2, e3)
+
     def there(j):
-        b0, b1 = z % 2, z // 2
-        if j & 1:
-            b0 = 1 - b0
-        if j & 2:
-            b1 = 1 - b1
-        return b0 + 2 * b1
+        return beside(z, j)
 
     loads = [pltpu.make_async_copy(src, dst, w_sem.at[k]) for k, (src, dst) in enumerate(
         ((im, wi.at[0]), (io, wi.at[1]), (tm, wo.at[0]), (to, wo.at[1])))]
@@ -1020,7 +1203,7 @@
         for j in blocks:
             probs, lane = router_probs(x[rows(j), :], router_ref[...], experts)
             gate = jnp.sum(jnp.where(lane == z, probs, 0.0), axis=-1, keepdims=True)
-            wd[rows(j), :] = (gate * dyin_ref[place(there(j)), :].astype(F32)).astype(BF)
+            wd[rows(j), :] = (gate * out_grad[j][...].astype(F32)).astype(BF)
         acc[0:m, :] = jnp.zeros((m, d), F32)
         dxa[0:m, :] = jnp.zeros((m, d), F32)
 
@@ -1040,8 +1223,8 @@
         for b, j in enumerate(blocks):
             here = slice(b * half, (b + 1) * half)
             e_rows = acc[here, :].astype(BF)
-            eout_ref[place(there(j)), :] = e_rows
-            dgate = jnp.sum(dyin_ref[place(there(j)), :].astype(F32) * e_rows.astype(F32), axis=-1, keepdims=True)
+            eouts[j][...] = e_rows
+            dgate = jnp.sum(out_grad[j][...].astype(F32) * e_rows.astype(F32), axis=-1, keepdims=True)
             high = dgate.astype(BF).astype(F32)
             lane = lax.broadcasted_iota(I32, (half, LANES), 1)
             extra = jnp.where(lane < LANES // 2, high, dgate - high).astype(BF)
@@ -1120,7 +1303,7 @@
         forwards[j].wait()
 
 
-def expert_exchange(h4, tr, dy_in, router, im, io, tm, to, experts, half):
+def expert_exchange(h4, tr, dys, router, im, io, tm, to, experts, half):
     n, d = h4.shape
     f = im.shape[1]
     s = experts * half
@@ -1130,9 +1313,9 @@
     vm = pl.BlockSpec(memory_space=pltpu.VMEM)
     return pl.pallas_call(
         functools.partial(expert_exchange_body, experts, half),
-        in_specs=[vm] * 4 + [any_] * 4,
-        out_specs=[vm, vm, any_],
-        out_shape=[out((2, s, d + LANES), BF), out((s, d), BF), out((2, d, f), BF)],
+        in_specs=[vm] * 7 + [any_] * 4,
+        out_specs=[vm] * 5 + [any_],
+        out_shape=[out((2, s, d + LANES), BF)] + [out((half, d), BF)] * 4 + [out((2, d, f), BF)],
         scratch_shapes=[
             V((n, d), BF), V((s, d), F32), V((s, d), BF), V((s, d), BF), V((2, d, f), BF), V((2, f, d), BF),
             V((2, s, f), BF), V((2, s, f), BF), V((s, d), BF), V((2 * half, d), F32), V((2 * half, d), F32),
@@ -1142,7 +1325,7 @@
         ],
         compiler_params=pltpu.CompilerParams(collective_id=1, has_side_effects=True, vmem_limit_bytes=VMEM_BYTES),
         cost_estimate=pl.CostEstimate(flops=24 * s * d * f, bytes_accessed=20 * d * f, transcendentals=0),
-    )(h4, tr, dy_in, router, im, io, tm, to)
+    )(h4, tr, *dys, router, im, io, tm, to)
 
 
 FUSED = True
@@ -1167,14 +1350,11 @@
     fused = FUSED and (lax.axis_size("grp"), peers, n_mdl) == (4, experts, 2) and peers == 4
     fused = fused and d == 2 * c and f == 4 * c and unit % (64 * peers) == 0
 
-    def own(v):
-        return lax.dynamic_slice_in_dim(v, core * rows, rows)
-
     def padded(v):
         return jnp.pad(v, ((0, 0), (0, LP - length), (0, 0))).reshape(n_slot * LP, -1)
 
-    qm1, om1, im, tm, qm2, om2, em, fm = qkv_one, out_one, fc_in, fc_out, qkv_two, out_two, expert_in[0], expert_out[0]
-    qo1, oo1, io, to, qo2, oo2, eo, fo = (other_core(w) for w in (qm1, om1, im, tm, qm2, om2, em, fm))
+    qm1, om1, im, tm, qm2, om2, em, fm = halves = (
+        qkv_one, out_one, fc_in, fc_out, qkv_two, out_two, expert_in[0], expert_out[0])
     gains = jnp.stack([gain_one, gain_two, gain_three, gain_four])
     router_rows = jnp.pad(router.T, ((0, LANES - experts), (0, 0)))
 
@@ -1182,31 +1362,36 @@
     lines = jnp.concatenate([jnp.transpose(routes, (0, 2, 1)), priority.reshape(n_slot, 1, length), live], axis=1)
     lines = jnp.pad(lines, ((0, 0), (0, 4), (0, LQ - length)))
     dy = padded(cotangent)
-    slot_rows, col, dy_out = call(
+    blocks = [(half, d)] * peers if fused else [(slots, d)]
+    slot_rows, col, *dy_out = call(
         functools.partial(routing_body, experts, capacity, half),
-        [out((n_slot, 8, LQ), I32), out((rows, 8), I32), out((slots, d), BF)], lines, dy,
+        [out((n_slot, 8, LQ), I32), out((rows, 8), I32)] + [out(b, BF) for b in blocks], lines, dy,
         scratch=[pltpu.VMEM((8, LQ), I32)], flops=4 * slots * n_slot * LP * d,
     )
+    def along_z(v):
+        return [v[0]] + [lax.ppermute(v[j], "exp", [(i, i ^ j) for i in range(peers)]) for j in range(1, peers)]
 
     def exchange(v):
         shaped = v.reshape(peers, v.shape[0] // peers, v.shape[1])
         return lax.all_to_all(shaped, "exp", 0, 0, tiled=True).reshape(v.shape)
 
-    x0 = own(padded(images))
+    x0 = padded(images)
     if fused:
-        x1, *kept1, dy_in = attention_forward(x0, gains, 0, qm1, qo1, om1, oo1, carry=(dy_out, peers, half))
+        got, (qo1, oo1, io, to, qo2, oo2, eo, fo), dy_in = forward(x0, gains, halves, dy_out[1:], rows)
+        x1, *kept1, x2, h2, act2, slope2, x3 = got[:10]
+        kept3, h4 = got[10:14], got[14]
+        dy_in = [dy_out[0], *dy_in]
     else:
-        x1, *kept1 = attention_forward(x0, gains, 0, qm1, qo1, om1, oo1)
-        dy_in = exchange(dy_out)
-    x2, h2, act2, slope2 = mlp_forward(x1, gains, 1, im, io, tm, to)
-    x3, *kept3, h4 = attention_forward(x2, gains, 2, qm2, qo2, om2, oo2, tail=3)
-
-    own_dy = own(dy)
+        qo1, oo1, io, to, qo2, oo2, eo, fo = (other_core(w) for w in halves)
+        dy_in = exchange(dy_out[0])
+        x1, *kept1 = attention_forward(x0, rows, gains, 0, qm1, qo1, om1, oo1)
+        x2, h2, act2, slope2 = mlp_forward(x1, gains, 1, im, io, tm, to)
+        x3, *kept3, h4 = attention_forward(x2, rows, gains, 2, qm2, qo2, om2, oo2, tail=3)
+
     second = (x2, gains, kept3, qm2, qo2, om2, oo2)
     if fused:
-        ret, eout, ge = expert_exchange(h4, slot_rows, dy_in, router_rows, em, eo, fm, fo, experts, half)
-        dx2, dg3, dg4, dr, a2_mine, a2_other, eback = mixture_attention_backward(
-            experts, x3, h4, router_rows, own_dy, col, ret, *second, carry=(eout, peers, half))
+        ret, *eout, ge = expert_exchange(h4, slot_rows, dy_in, router_rows, em, eo, fm, fo, experts, half)
+        eback = along_z(eout)
     else:
         [h4_out] = call(functools.partial(dispatch_body, experts, half), [out((slots, d), BF)], slot_rows, h4, other_core(h4))
         h4_in = exchange(h4_out)
@@ -1215,8 +1400,7 @@
         ret, eback = jnp.stack([ret, other_core(ret)]), jnp.stack([eout, other_core(eout)])
         ge_mine, ge_other = expert_weights(h4_in, ewd, eact, edz)
         ge = add16(ge_mine, other_core(ge_other))
-        dx2, dg3, dg4, dr, a2_mine, a2_other = mixture_attention_backward(
-            experts, x3, h4, router_rows, own_dy, col, ret, *second)
+    dx2, dg3, dg4, dr, a2_mine, a2_other = mixture_attention_backward(experts, x3, h4, router_rows, dy, col, ret, *second)
     expert_sum = lax.psum_scatter(ge, "grp", scatter_dimension=1, tiled=True)
 
     dx1, dg2, gim, gio, gtm, gto = mlp_backward(dx2, x1, gains, 1, h2, act2, slope2, im, io, tm, to, c)

time: 443 us -> 408 us (0.921)
  Pallas kernels: 380 us -> 351 us
  waiting for transfers between devices: 5.95 us -> 0.03 us
    pallas_call x2 -> x1, Pallas kernels: 60.6 us -> 39.3 us  [forward(): pl.pallas_call(functools.partial(forward_body, n_img, size), in_specs=[vm...]
    ppermute x8 -> x3, waiting for transfers between devices: 5.93 us -> 0.01 us  [along_z(): lax.ppermute(v[j], 'exp', [(i, i ^ j) for i in range(peers)])]
    pallas_call x1, Pallas kernels: 188 us -> 183 us  [reduce_all(): pl.pallas_call(functools.partial(reduce_body, len(mine), per, n_exp, expe...]
    pallas_call x1, Pallas kernels: 64.9 us -> 60.4 us  [expert_exchange(): pl.pallas_call(functools.partial(expert_exchange_body, experts, half), in...]
    pallas_call x5 -> x4, Pallas kernels: 66.9 us -> 68.2 us  [call(): pl.pallas_call(body, grid=grid, in_specs=in_specs, out_specs=out_specs, o...]
    unnamed x34 -> x36, local copies, waits for them, and re-layouts: 9.53 us -> 8.72 us
  transfers between devices with their start and end apart: 9 -> 4, of which waited for: 1 -> 0; matrix products, arithmetic and copies ran while one was open for 6% -> 4% of each run, Pallas kernels for 72% -> 61%
where the time goes in v5:
time: 408 us; the launch traced here: 404 us
  Pallas kernels  351 us (86%)
  other arithmetic  16.6 us (4%)
  local copies, waits for them, and re-layouts  16.4 us (4%)
  between operations  15.1 us (4%)
  starting transfers between devices  4.33 us (1%)
    pallas_call x1, Pallas kernels, reduce_all(): pl.pallas_call(functools.partial(reduce_body, len(mine), per, n_exp, expe...  183 us
    pallas_call x4, Pallas kernels, call(): pl.pallas_call(body, grid=grid, in_specs=in_specs, out_specs=out_specs, o...  68.2 us
    pallas_call x1, Pallas kernels, expert_exchange(): pl.pallas_call(functools.partial(expert_exchange_body, experts, half), in...  60.4 us
    pallas_call x1, Pallas kernels, forward(): pl.pallas_call(functools.partial(forward_body, n_img, size), in_specs=[vm...  39.3 us
    unnamed x36, local copies, waits for them, and re-layouts  8.72 us
  transfers between devices with their start and end apart: 4, of which 0 were waited for; matrix products, arithmetic and copies ran while one was open for 4% of the time, Pallas kernels for 61%

profile of v5, /device:TPU:0, one launch (start us, length us, event | category | flops | bytes accessed | tf_op | source)
XLA Modules:
  0.0 403.6 jit_solution(5550791900576510621)
XLA Ops:
  7.9 0.7 stack.15
  8.6 0.7 stack.16
  9.3 0.7 stack.17
  10.0 0.7 stack.18
  10.7 0.7 reduce
  11.5 0.7 pad_add_fusion
  12.8 1.4 copy.37
  14.3 0.7 pad.18.router_ref.refs_15_
  15.0 1.1 pad.15.clone
  16.2 1.1 pad.17.clone
  17.4 4.0 shard_map.289
  22.0 39.3 %shard_map.290 = (f32[416,768]{1,0:T(8,128)}, bf16[416,768]{1,0:T(8,128)(2,1)}, bf16[416,2304]{1,0:T(8,128)(2,1)}, bf16[24,208,208]{2,1,0:T(8,128)(2,1)}, bf16[4...) custom-call(bf16[832,768]{1,0:T(8,128)(2,1)} %bitcast.35, ...), custom_call_target="tpu_custom_call" | custom-call | flops 7851737088 | bytes 25559040 | tf_op jit(solution)/shard_map/pallas_call | solution.py:460
  61.3 60.4 %shard_map.291 = (bf16[2,640,896]{2,1,0:T(8,128)(2,1)}, bf16[160,768]{1,0:T(8,128)(2,1)}, bf16[160,768]{1,0:T(8,128)(2,1)}, bf16[160,768]{1,0:T(8,128)(2,1)}, bf...) custom-call(bf16[416,768]{1,0:T(8,128)(2,1)} %get-tuple-element.82.h4_ref.refs_14_, ...), custom_call_target="tpu_custom_call" | custom-call | flops 18119393280 | bytes 23592960 | tf_op jit(solution)/shard_map/pallas_call | solution.py:1314
  121.8 0.9 copy-done.15
  122.8 1.9 collective-permute-start.1
  124.7 2.4 collective-permute-start.2
  127.1 25.3 %shard_map.292 = (f32[416,768]{1,0:T(8,128)}, f32[1,768]{1,0:T(1,128)}, f32[1,768]{1,0:T(1,128)}, f32[128,768]{1,0:T(8,128)}, bf16[3072,384]{1,0:T(8,128)(2,1)}, /*index=5*/bf16[3072,384]{1,0:T(8,128)(2,1)}) custom-call(f32[416,768]{1,0:T(8,128)} %get-tuple-element.81.x3_ref.refs_13_, bf16[416,768]{1,0:T(8,128)(2,1)} %get-tuple-element.82.h4_ref.refs_14_, ...), custom_call_target="tpu_custom_call" | custom-call | flops 6624903168 | bytes 23374848 | tf_op jit(solution)/shard_map/pallas_call | solution.py:65
  152.4 18.5 %shard_map.293 = (f32[416,768]{1,0:T(8,128)}, f32[1,768]{1,0:T(1,128)}, bf16[4,768,384]{2,1,0:T(8,128)(2,1)}, bf16[4,768,384]{2,1,0:T(8,128)(2,1)}, bf16[2,1536,...) custom-call(f32[416,768]{1,0:T(8,128)} %get-tuple-element.100.dy_ref, f32[416,768]{1,0:T(8,128)} %get-tuple-element.101.x_ref, ...), custom_call_target="tpu_custom_call" | custom-call | flops 7851737088 | bytes 28474368 | tf_op jit(solution)/shard_map/pallas_call | solution.py:65
  171.0 20.3 %shard_map.294 = (bf16[2,197,768]{2,1,0:T(8,128)(2,1)}, f32[1,768]{1,0:T(1,128)}, bf16[3072,384]{1,0:T(8,128)(2,1)}, bf16[3072,384]{1,0:T(8,128)(2,1)}) custom-call(f32[416,768]{1,0:T(8,128)} %get-tuple-element.109.dy_ref, bf16[832,768]{1,0:T(8,128)(2,1)} %bitcast.36, f32[4,768]{1,0:T(4,128)} %pad_maximum_fusion.refs_1_.g_ref, ...), custom_call_target="tpu_custom_call" | custom-call | flops 4989124608 | bytes 17885184 | tf_op jit(solution)/shard_map/pallas_call | solution.py:65
  191.3 0.6 copy-done.8
  192.1 183.3 %shard_map.295 = (bf16[3,768,384]{2,1,0:T(8,128)(2,1)}, bf16[384,768]{1,0:T(8,128)(2,1)}, bf16[768,1536]{1,0:T(8,128)(2,1)}, bf16[1536,768]{1,0:T(8,128)(2,1)}, ...) custom-call(bf16[2,2,768,384]{3,2,1,0:T(8,128)(2,1)} %bitcast.27, ...), custom_call_target="tpu_custom_call" | custom-call | flops 1063256064 | bytes 18874368 | tf_op jit(solution)/shard_map/pallas_call | solution.py:1115
  375.5 2.9 copy.35
  378.3 1.1 convert_element_type.40
  379.4 1.1 convert_element_type.44
  380.5 1.5 copy.36
  382.0 2.0 convert_element_type.39
  384.2 2.0 convert_element_type.43
  386.2 0.8 copy-done.1
  387.0 2.8 convert_element_type.41
  389.9 2.5 convert_element_type.42
  392.4 0.6 slice_reduce_fusion
  393.6 2.9 convert_bitcast_fusion
  (43 shorter events, 2.7 us)
Async XLA Ops:
  7.2 7.1 %copy-start.12 = (bf16[768,4]{0,1:T(4,128)(2,1)S(1)}, bf16[768,4]{0,1:T(4,128)(2,1)}, u32[]{:S(2)}) copy-start(bf16[768,4]{0,1:T(4,128)(2,1)} %param.32) | copy-start | bytes 18436
  7.2 386.4 %reduce-scatter.2.cloned.1.call-start = ((), (), s32[]{:S(2)}) async-start(), calls=%async_computation.1 | async-start | bytes 5898240 | tf_op jit(solution)/shard_map/reduce_scatter | solution.py:1404
  14.3 1.9 copy-start.5
  121.7 0.9 copy-start.15
  121.7 1.1 copy-start.14
  121.7 2.9 copy-start.13
  122.7 68.6 %collective-permute-start = (bf16[160,768]{1,0:T(8,128)(2,1)S(1)}, bf16[160,768]{1,0:T(8,128)(2,1)S(1)}, u32[]{:S(2)}, u32[]{:S(2)}) collective-permute-start(bf16[160,768]{1,0:T(8,128)(2,1)S(1)} %copy-done.15), channel_id=1, source_target_pairs={{0,2},{2,0},{4,6},{6,4},{1,3},{3,1},{5,7},{7,5},{8,10},{10,8},{12,... | collective-permute-start | bytes 737288 | tf_op jit(solution)/shard_map/ppermute | solution.py:1372
  122.8 68.5 %collective-permute-start.1 = (bf16[160,768]{1,0:T(8,128)(2,1)S(1)}, bf16[160,768]{1,0:T(8,128)(2,1)S(1)}, u32[]{:S(2)}, u32[]{:S(2)}) collective-permute-start(bf16[160,768]{1,0:T(8,128)(2,1)S(1)} %copy-done.14), channel_id=1, source_target_pairs={{0,4},{2,6},{4,0},{6,2},{1,5},{3,7},{5,1},{7,3},{8,12},{10,14},{12... | collective-permute-start | bytes 737288 | tf_op jit(solution)/shard_map/ppermute | solution.py:1372
  124.7 66.7 %collective-permute-start.2 = (bf16[160,768]{1,0:T(8,128)(2,1)S(1)}, bf16[160,768]{1,0:T(8,128)(2,1)S(1)}, u32[]{:S(2)}, u32[]{:S(2)}) collective-permute-start(bf16[160,768]{1,0:T(8,128)(2,1)S(1)} %copy-done.13), channel_id=1, source_target_pairs={{0,6},{2,4},{4,2},{6,0},{1,7},{3,5},{5,3},{7,1},{8,14},{10,12},{12... | collective-permute-start | bytes 737288 | tf_op jit(solution)/shard_map/ppermute | solution.py:1372
  191.3 0.7 copy-start.8
  191.3 0.8 copy-start.9
  191.3 0.8 copy-start.10
  375.4 2.9 copy-start.7
  375.4 4.0 copy-start.6
  378.3 2.2 copy-start.4
  379.4 2.6 copy-start.3
  382.0 2.2 copy-start.2
  384.2 2.8 copy-start.1
  387.0 2.8 copy-start
  389.9 2.5 copy-start.11
Sparse Core Ops, SparseCore 0:
  121.9 56.1 reduce-scatter.1

commit v6 on v5

--- a/solution.py
+++ b/solution.py
@@ -90,6 +90,12 @@
     if j & 2:
         b1 = 1 - b1
     return b0 + 2 * b1
+
+
+def fill_rows(ref, at, images, first, count):
+    for i in range(count):
+        ref[at + i * LP : at + i * LP + L, :] = images[first + i].astype(ref.dtype)
+        ref[at + i * LP + L : at + (i + 1) * LP, :] = jnp.zeros((LP - L, ref.shape[1]), ref.dtype)
 
 
 def own_rows(ref, n):
@@ -341,19 +347,19 @@
         del refs[:n]
         return r
 
-    x_ref, g_ref = take(2)
+    images, g_ref = take(2)
     own_w = take(8)
     dy_out = take(size - 1)
-    results = take(15)
+    results = take(16)
     other_w = take(8)
     dy_in = take(size - 1)
     weights = take(6)
-    held = take(15)
+    held = take(16)
     load_sem, w_send, w_recv, o_sem, r_sem, d_send, d_recv = refs
-    x1, h1, qkv1, p1, o1, x2, h2, act, slope, x3, h3, qkv3, p3, o3, h4 = held
+    x1, h1, qkv1, p1, o1, x2, h2, act, slope, x3, h3, qkv3, p3, o3, h4, x0 = held
     q1, w1, fi, fo, q3, w3 = weights
     r = n_img * LP
-    d = x_ref.shape[1]
+    d = x0.shape[1]
     c = q1.shape[3]
     f = fi.shape[2]
     z = lax.axis_index("exp")
@@ -368,20 +374,20 @@
     pl.semaphore_wait(barrier, size)
     swaps = [pltpu.make_async_remote_copy(own_w[k], weights[k].at[1] if k < 6 else other_w[k], w_send.at[k], w_recv.at[k],
                                           device_id=partner, device_id_type=MESH) for k in range(8)]
-    for cp in swaps:
+    for cp in swaps[0:2]:
         cp.start()
     blocks = [pltpu.make_async_remote_copy(dy_out[j - 1], dy_in[j - 1], d_send.at[j - 1], d_recv.at[j - 1],
                                            device_id={"exp": beside(z, j)}, device_id_type=MESH) for j in range(1, size)]
     for cp in blocks:
         cp.start()
     keeps = [pltpu.make_async_copy(weights[k].at[1], other_w[k], o_sem.at[k]) for k in range(6)]
-    stores = [pltpu.make_async_copy(held[k], results[k], r_sem.at[k]) for k in range(15)]
+    stores = [pltpu.make_async_copy(held[k], results[k], r_sem.at[k]) for k in range(16)]
 
     def store(*at):
         for k in at:
             stores[k].start()
 
-    def attention(x, gain, wq, wo, kq, ko, h, qkv, p, o, y):
+    def attention(x, gain, wq, wo, kq, ko, h, qkv, p, o, y, then):
         _, _, n = norm_forward(x(), gain)
         h[...] = n
         per_half = c // LANES
@@ -391,6 +397,8 @@
             else:
                 swaps[kq].wait_recv()
                 keeps[kq].start()
+                for cp in swaps[then : then + 2]:
+                    cp.start()
             for k in range(3):
                 at = (2 * k + side) * c
                 qkv[:, at : at + c] = nn(h[...], wq[side, k]).astype(BF)
@@ -402,7 +410,9 @@
         keeps[ko].start()
         y[...] = x() + nn(o[:, :c], wo[0]) + nn(o[:, c:], wo[1])
 
-    attention(lambda: own_rows(x_ref, r).astype(F32), g_ref[0:1, :], q1, w1, 0, 1, h1, qkv1, p1, o1, x1)
+    fill_rows(x0, 0, images, lax.axis_index("mdl") * n_img, n_img)
+    store(15)
+    attention(lambda: x0[...].astype(F32), g_ref[0:1, :], q1, w1, 0, 1, h1, qkv1, p1, o1, x1, 2)
     store(0, 1, 2, 3, 4)
 
     _, _, n = norm_forward(x1[...], g_ref[1:2, :])
@@ -426,10 +436,13 @@
             x2[...] += nn(a, fo[side, at, :])
             return 0
 
+        if side == 0:
+            for cp in swaps[4:6]:
+                cp.start()
         lax.fori_loop(0, f // t, tile, 0)
     store(5, 6, 7, 8)
 
-    attention(lambda: x2[...], g_ref[2:3, :], q3, w3, 4, 5, h3, qkv3, p3, o3, x3)
+    attention(lambda: x2[...], g_ref[2:3, :], q3, w3, 4, 5, h3, qkv3, p3, o3, x3, 6)
     store(9, 10, 11, 12, 13)
     _, _, n = norm_forward(x3[...], g_ref[3:4, :])
     h4[...] = n
@@ -445,14 +458,14 @@
 
 
 def forward(x, gains, own_w, dy_out, r):
-    d = x.shape[1]
+    d = x.shape[2]
     c, f = own_w[0].shape[2], own_w[2].shape[1]
     n_img = r // LP
     heads = d // HDIM
     size = len(dy_out) + 1
     half = dy_out[0].shape[0]
     kept = [out((r, d), F32), out((r, d), BF), out((r, 3 * d), BF), out((n_img * heads, LP, LP), BF), out((r, d), BF)]
-    results = kept + [out((r, d), F32), out((r, d), BF), out((2, r, f), BF), out((2, r, f), BF)] + kept + [out((r, d), BF)]
+    results = kept + [out((r, d), F32), out((r, d), BF), out((2, r, f), BF), out((2, r, f), BF)] + kept + [out((r, d), BF), out((r, d), BF)]
     shapes = results + [out(w.shape, BF) for w in own_w] + [out((half, d), BF)] * (size - 1)
     D, V = pltpu.SemaphoreType.DMA, pltpu.VMEM
     any_ = pl.BlockSpec(memory_space=pl.ANY)
@@ -470,7 +483,8 @@
 
 
 def routing_body(experts, capacity, half, rows_ref, dy_ref, tr_ref, col_ref, *refs):
-    out_refs, tmp = refs[:-1], refs[-1]
+    out_refs, (dy_rows, tmp) = refs[:-2], refs[-2:]
+    fill_rows(dy_rows, 0, dy_ref, 0, rows_ref.shape[0])
     n_img = rows_ref.shape[0]
     slots = experts * half
     core = lax.axis_index("mdl")
@@ -510,7 +524,7 @@
         at = core * slots + (beside(z, j) * half if len(out_refs) > 1 else 0)
         total = None
         for i in range(n_img):
-            part = nn(slot_hots(tr_ref[i], at, o_ref.shape[0]), dy_ref[i * LP : (i + 1) * LP, :])
+            part = nn(slot_hots(tr_ref[i], at, o_ref.shape[0]), dy_rows[i * LP : (i + 1) * LP, :])
             total = part if total is None else total + part
         o_ref[...] = total.astype(BF)
 
@@ -637,28 +651,44 @@
     return rows
 
 
-def mixture_backward_core(experts, x_ref, gain, h_ref, router_ref, dy_ref, col_ref, ab_ref, dr_ref):
+def mixture_backward_core(experts, half, x_ref, gain, h_ref, router_ref, dy_ref, col_ref, ab_ref, dgate_ref, dr_ref, dy_rows):
     n, d = x_ref.shape
+    n_img = n // LP
+    fill_rows(dy_rows, 0, dy_ref, lax.axis_index("mdl") * n_img, n_img)
     probs, lane = router_probs(h_ref[...], router_ref[...], experts)
+    dsoft = jnp.zeros(probs.shape, F32)
     dh = jnp.zeros((n, d), F32)
-    dsoft = jnp.zeros(probs.shape, F32)
     for k in range(TOPK):
-        part = merge(col_ref, k, ab_ref, n)
-        dh = dh + part[:, :d]
-        dgate = part[:, d : d + 1] + part[:, d + LANES // 2 : d + LANES // 2 + 1]
+        dh = dh + merge(col_ref, k, ab_ref, n)
+        dgate = jnp.zeros((n, 1), F32)
+        for side in range(2):
+            t = col_ref[:, 2 * side + k : 2 * side + k + 1]
+            for e in range(experts):
+                line = dgate_ref[side, e, 0:1, :]
+                place = lax.broadcasted_iota(I32, (n, line.shape[1]), 1)
+                hit = (place + e * half == t) & (place < half)
+                dgate = dgate + jnp.sum(jnp.where(hit, line, 0.0), axis=-1, keepdims=True)
         dsoft = dsoft + jnp.where(lane == col_ref[:, 4 + k : 5 + k], dgate, 0.0)
     dlog = (probs * (dsoft - jnp.sum(dsoft * probs, axis=-1, keepdims=True))).astype(BF)
     dr_ref[...] = tn(dlog, h_ref[...])
     dh = dh + nn(dlog, router_ref[...])
     nrm, rr, _ = norm_forward(x_ref[...], gain)
     dv, dw = norm_backward(nrm, rr, gain, dh)
-    return own_rows(dy_ref, n).astype(F32) * col_ref[:, 6:7].astype(F32) + dv, dw
-
-
-def mixture_attention_backward_body(n_img, experts, x3_ref, h4_ref, router_ref, dy_ref, col_ref, ret_ref, x_ref, g_ref, h_ref,
+    return dy_rows[...].astype(F32) * col_ref[:, 6:7].astype(F32) + dv, dw
+
+
+def gate_lines(dgate):
+    half = dgate.shape[0]
+    wide = -(-half // LANES) * LANES
+    tall = jnp.concatenate([dgate, jnp.zeros((wide - half, 1), F32)], axis=0) if wide > half else dgate
+    return jnp.broadcast_to(tall, (wide, LANES)).T[0:8, :]
+
+
+def mixture_attention_backward_body(n_img, experts, half, x3_ref, h4_ref, router_ref, dy_ref, col_ref, ret_ref, dgate_ref, x_ref, g_ref, h_ref,
                                     qkv_ref, p_ref, o_ref, qm, qo, om, oo, dx_ref, dw3_ref, dw4_ref, dr_ref, gm_ref, go_ref,
-                                    dx3, do_ref, dqkv_ref, tr_ref):
-    grad, dw4 = mixture_backward_core(experts, x3_ref, g_ref[3:4, :], h4_ref, router_ref, dy_ref, col_ref, ret_ref, dr_ref)
+                                    dx3, dy_rows, do_ref, dqkv_ref, tr_ref):
+    grad, dw4 = mixture_backward_core(experts, half, x3_ref, g_ref[3:4, :], h4_ref, router_ref, dy_ref, col_ref, ret_ref, dgate_ref,
+                                      dr_ref, dy_rows)
     dx3[...] = grad
     dw4_ref[...] = dw4
     dx, dw3 = attention_backward_core(
@@ -668,17 +698,145 @@
     dw3_ref[...] = dw3
 
 
-def mixture_attention_backward(experts, x3, h4, router, dy, col, ret, x, gains, kept, qm, qo, om, oo):
+def mixture_attention_backward(experts, half, x3, h4, router, dy, col, ret, dgate, x, gains, kept, qm, qo, om, oo):
     r, d = x.shape
     c = qm.shape[2]
     n_img = r // LP
     heads = d // HDIM
     shapes = [out((r, d), F32), out((1, d), F32), out((1, d), F32), out(router.shape, F32),
               out((3 * d + d, c), BF), out((3 * d + d, c), BF)]
-    return call(functools.partial(mixture_attention_backward_body, n_img, experts), shapes,
-                x3, h4, router, dy, col, ret, x, gains, *kept, qm, qo, om, oo,
-                scratch=[pltpu.VMEM((r, d), F32)] + attention_backward_scratch(r, d),
+    return call(functools.partial(mixture_attention_backward_body, n_img, experts, half), shapes,
+                x3, h4, router, dy, col, ret, dgate, x, gains, *kept, qm, qo, om, oo,
+                scratch=[pltpu.VMEM((r, d), F32), pltpu.VMEM((r, d), BF)] + attention_backward_scratch(r, d),
                 flops=4 * r * d * d * 4 + 8 * n_img * heads * LP * LP * LANES + 8 * r * ret.shape[1] * d)
+
+
+def backward_body(n_img, experts, half, size, *refs):
+    refs = list(refs)
+
+    def take(n):
+        r = refs[:n]
+        del refs[:n]
+        return r
+
+    x3, h4, router, cotangent, col, ret, dgate, g_ref = take(8)
+    src_two, src_mlp, src_one = take(9), take(8), take(9)
+    eouts = take(size - 1)
+    dg1, dg2, dg3, dg4, dr, image = take(6)
+    out_two, out_mlp, out_one = take(2), take(4), take(2)
+    ebacks = take(size - 1)
+    attn = take(9)
+    x0, x1, h2, act, slope, fi, fo, ga, gi, go, dxs, dy_rows, do, dqkv, tr, da, dh = take(17)
+    a_sem, m_sem, b_sem, ga_sem, gi_sem, e_send, e_recv = refs
+    d = x3.shape[1]
+    f = fi.shape[2]
+    t = gi.shape[4]
+    z = lax.axis_index("exp")
+
+    def fetch(srcs, dsts, sem):
+        return [pltpu.make_async_copy(a, b, sem.at[k]) for k, (a, b) in enumerate(zip(srcs, dsts))]
+
+    two = fetch(src_two, attn, a_sem)
+    mlp = fetch(src_mlp, [x1, h2, act, slope, fi.at[0], fi.at[1], fo.at[0], fo.at[1]], m_sem)
+    one = fetch(src_one, [x0] + attn[1:], b_sem)
+    for cp in two + mlp:
+        cp.start()
+    barrier = pltpu.get_barrier_semaphore()
+    for j in range(1, size):
+        pl.semaphore_signal(barrier, inc=1, device_id={"exp": beside(z, j)}, device_id_type=MESH)
+    pl.semaphore_wait(barrier, size - 1)
+    blocks = [pltpu.make_async_remote_copy(eouts[j - 1], ebacks[j - 1], e_send.at[j - 1], e_recv.at[j - 1],
+                                           device_id={"exp": beside(z, j)}, device_id_type=MESH) for j in range(1, size)]
+    for cp in blocks:
+        cp.start()
+
+    def attention(x, gain, dst):
+        dx, dw = attention_backward_core(n_img, lambda: dxs[...], x, gain, *attn[1:], ga.at[0], ga.at[1], do, dqkv, tr)
+        leave = [pltpu.make_async_copy(ga.at[k], dst[k], ga_sem.at[k]) for k in range(2)]
+        for cp in leave:
+            cp.start()
+        return dx, dw, leave
+
+    grad, dw4 = mixture_backward_core(experts, half, x3, g_ref[3:4, :], h4, router, cotangent, col, ret, dgate, dr, dy_rows)
+    dxs[...] = grad
+    dg4[...] = dw4
+    for cp in two:
+        cp.wait()
+    dx, dw, leave = attention(attn[0], g_ref[2:3, :], out_two)
+    dxs[...] = dx
+    dg3[...] = dw
+    for cp in one:
+        cp.start()
+
+    da[...] = dxs[...].astype(BF)
+    for cp in mlp:
+        cp.wait()
+    tr[...] = h2[...].T
+    dh[...] = jnp.zeros(dh.shape, F32)
+    gone = {}
+    for i in range(f // t):
+        at = slice(i * t, (i + 1) * t)
+        slot = i % 2
+        for cp in gone.pop(slot, ()):
+            cp.wait()
+        gone[slot] = []
+        for side in range(2):
+            dz = (nt(da[...], fo[side, at, :]) * slope[side, :, at].astype(F32)).astype(BF)
+            gw = tn(act[side, :, at], da[...]).astype(BF)
+            for part in range(d // t):
+                go[slot, side, part] = gw[:, part * t : (part + 1) * t]
+            gi[slot, side, 0] = nn(tr[...], dz).astype(BF)
+            dh[...] += nt(dz, fi[side, :, at])
+            gone[slot] += [
+                pltpu.make_async_copy(gi.at[slot, side], out_mlp[side].at[i : i + 1], gi_sem.at[slot, side, 0]),
+                pltpu.make_async_copy(go.at[slot, side], out_mlp[2 + side].at[:, at], gi_sem.at[slot, side, 1])]
+            for cp in gone[slot][-2:]:
+                cp.start()
+    gain = g_ref[1:2, :]
+    n, rr, _ = norm_forward(x1[...], gain)
+    dv, dw = norm_backward(n, rr, gain, dh[...])
+    dxs[...] += dv
+    dg2[...] = dw
+
+    for cp in one + leave:
+        cp.wait()
+    dx, dw, leave = attention(x0, g_ref[0:1, :], out_one)
+    for i in range(n_img):
+        image[i] = dx[i * LP : i * LP + L].astype(BF)
+    dg1[...] = dw
+    for cp in leave + gone[0] + gone[1] + blocks:
+        cp.wait()
+
+
+def backward(experts, half, x3, h4, router, cotangent, col, ret, dgate, gains, x2, kept3, w2, x1, h2, act, slope, mlp_w, x0, kept1,
+             w1, eouts):
+    r, d = x3.shape
+    c, f = w1[0].shape[2], mlp_w[0].shape[1]
+    n_img = r // LP
+    heads = d // HDIM
+    size = len(eouts) + 1
+    t = c
+    flat = [x2, *kept3, *w2, x1, h2, act, slope, *mlp_w, x0, *kept1, *w1, *eouts]
+    near = [x3, h4, router, cotangent, col, ret, dgate, gains]
+    D, V = pltpu.SemaphoreType.DMA, pltpu.VMEM
+    any_ = pl.BlockSpec(memory_space=pl.ANY)
+    vm = pl.BlockSpec(memory_space=pltpu.VMEM)
+    shapes = [out((1, d), F32)] * 4 + [out(router.shape, F32), out((n_img, L, d), BF)]
+    shapes += [out((4 * d, c), BF)] * 2 + [out((f // t, d, t), BF)] * 2 + [out((d // t, f, t), BF)] * 2 + [out((4 * d, c), BF)] * 2
+    shapes += [out(e.shape, BF) for e in eouts]
+    like = [V(v.shape, v.dtype) for v in (x2, *kept3, *w2)]
+    got = pl.pallas_call(
+        functools.partial(backward_body, n_img, experts, half, size),
+        in_specs=[vm] * len(near) + [any_] * len(flat), out_specs=[vm] * 6 + [any_] * (len(shapes) - 6), out_shape=shapes,
+        scratch_shapes=like + [
+            V(x0.shape, x0.dtype), V((r, d), F32), V((r, d), BF), V(act.shape, BF), V(slope.shape, BF), V((2, d, f), BF),
+            V((2, f, d), BF), V((2, 4 * d, c), BF), V((2, 2, 1, d, t), BF), V((2, 2, d // t, t, t), BF), V((r, d), F32),
+            V((r, d), BF), V((r, d), BF), V((r, 3 * d), BF), V((d, r), BF), V((r, d), BF), V((r, d), F32),
+            D((9,)), D((8,)), D((9,)), D((2,)), D((2, 2, 2)), D((size - 1,)), D((size - 1,))],
+        compiler_params=pltpu.CompilerParams(collective_id=3, has_side_effects=True, vmem_limit_bytes=VMEM_BYTES),
+        cost_estimate=pl.CostEstimate(flops=32 * r * d * d + 16 * r * d * f, bytes_accessed=160 * r * d, transcendentals=0),
+    )(*near, *flat)
+    return got[:6], got[6:14], got[14:]
 
 
 def mixture_output(experts, x_ref, h_ref, router_ref, col_ref, rows_of):
@@ -1115,7 +1273,7 @@
     return pl.pallas_call(
         functools.partial(reduce_body, len(mine), per, n_exp, experts),
         in_specs=[any_] * (2 * len(mine)) + [vm] * 13 + [any_],
-        out_specs=[vm] * 7 + [any_] * 2,
+        out_specs=[vm] * 9,
         out_shape=[out((3, d, c), BF), out((c, d), BF), out((d, f), BF), out((f, d), BF), out((3, d, c), BF), out((c, d), BF),
                    out(small, F32), out((2 * n_img, length, d), BF), out((2 * n_img, length, d), BF)],
         scratch_shapes=[
@@ -1131,9 +1289,10 @@
 
 
 def expert_exchange_body(experts, half, h4_ref, tr_ref, dy0, dy1, dy2, dy3, router_ref, im, io, tm, to,
-                         ret_ref, e0, e1, e2, e3, gw_ref,
+                         ret_ref, dg_ref, e0, e1, e2, e3, gw_ref,
                          h_oth, part, xo, x, wi, wo, act, dz, wd, acc, dxa, rsend, gscr, ggot, xt, wt,
-                         w_sem, swap_sem, x_send, x_recv, r_send, r_recv, f_send, f_recv, g_send, g_recv, g_sem):
+                         w_sem, swap_sem, x_send, x_recv, r_send, r_recv, f_send, f_recv, g_send, g_recv, g_sem,
+                         dgs, l_send, l_recv, k_send, k_recv):
     n, d = h4_ref.shape
     f = im.shape[1]
     t = 256 if f % 256 == 0 else tile_of(f)
@@ -1193,9 +1352,13 @@
 
     def forward(j):
         here = ret_ref.at[0, place(there(j))]
-        forwards[j] = pltpu.make_async_remote_copy(here, ret_ref.at[1, place(there(j))], f_send.at[j], f_recv.at[j],
-                                                   device_id=partner, device_id_type=MESH)
-        forwards[j].start()
+        forwards[j] = (
+            pltpu.make_async_remote_copy(here, ret_ref.at[1, place(there(j))], f_send.at[j], f_recv.at[j],
+                                         device_id=partner, device_id_type=MESH),
+            pltpu.make_async_remote_copy(dg_ref.at[0, there(j)], dg_ref.at[1, there(j)], k_send.at[j], k_recv.at[j],
+                                         device_id=partner, device_id_type=MESH))
+        for cp in forwards[j]:
+            cp.start()
 
     def run(blocks):
         r0, r1 = blocks[0] * half, (blocks[-1] + 1) * half
@@ -1225,19 +1388,21 @@
             e_rows = acc[here, :].astype(BF)
             eouts[j][...] = e_rows
             dgate = jnp.sum(out_grad[j][...].astype(F32) * e_rows.astype(F32), axis=-1, keepdims=True)
-            high = dgate.astype(BF).astype(F32)
-            lane = lax.broadcasted_iota(I32, (half, LANES), 1)
-            extra = jnp.where(lane < LANES // 2, high, dgate - high).astype(BF)
+            lines = gate_lines(dgate)
             if j == 0:
-                ret_ref[0, place(z), 0:d] = dxa[here, :].astype(BF)
-                ret_ref[0, place(z), d:] = extra
+                ret_ref[0, place(z), :] = dxa[here, :].astype(BF)
+                dg_ref[0, pl.ds(z, 1)] = lines[None]
                 forward(0)
             else:
-                rsend[rows(j), 0:d] = dxa[here, :].astype(BF)
-                rsend[rows(j), d:] = extra
-                returns[j] = pltpu.make_async_remote_copy(rsend.at[rows(j)], ret_ref.at[0, place(z)], r_send.at[j], r_recv.at[j],
-                                                          device_id={"exp": there(j)}, device_id_type=MESH)
-                returns[j].start()
+                rsend[rows(j), :] = dxa[here, :].astype(BF)
+                dgs[j] = lines
+                returns[j] = (
+                    pltpu.make_async_remote_copy(rsend.at[rows(j)], ret_ref.at[0, place(z)], r_send.at[j], r_recv.at[j],
+                                                 device_id={"exp": there(j)}, device_id_type=MESH),
+                    pltpu.make_async_remote_copy(dgs.at[j], dg_ref.at[0, z], l_send.at[j], l_recv.at[j],
+                                                 device_id={"exp": there(j)}, device_id_type=MESH))
+                for cp in returns[j]:
+                    cp.start()
 
     for cp in loads:
         cp.wait()
@@ -1281,12 +1446,11 @@
 
     lax.fori_loop(0, tiles, sum_tile, 0)
 
-    def recv_return(j):
-        return pltpu.make_async_remote_copy(rsend.at[rows(j)], ret_ref.at[0, place(there(j))], r_send.at[j], r_recv.at[j],
-                                            device_id={"exp": there(j)}, device_id_type=MESH)
-
     for j in near_first:
-        recv_return(j).wait_recv()
+        pltpu.make_async_remote_copy(rsend.at[rows(j)], ret_ref.at[0, place(there(j))], r_send.at[j], r_recv.at[j],
+                                     device_id={"exp": there(j)}, device_id_type=MESH).wait_recv()
+        pltpu.make_async_remote_copy(dgs.at[j], dg_ref.at[0, there(j)], l_send.at[j], l_recv.at[j],
+                                     device_id={"exp": there(j)}, device_id_type=MESH).wait_recv()
         forward(j)
 
     def drain(i, _):
@@ -1299,14 +1463,17 @@
     for j in range(size):
         if j:
             sends[j].wait_send()
-            returns[j].wait_send()
-        forwards[j].wait()
+            for cp in returns[j]:
+                cp.wait_send()
+        for cp in forwards[j]:
+            cp.wait()
 
 
 def expert_exchange(h4, tr, dys, router, im, io, tm, to, experts, half):
     n, d = h4.shape
     f = im.shape[1]
     s = experts * half
+    wide = -(-half // LANES) * LANES
     tiles = f // (256 if f % 256 == 0 else tile_of(f))
     D, V = pltpu.SemaphoreType.DMA, pltpu.VMEM
     any_ = pl.BlockSpec(memory_space=pl.ANY)
@@ -1314,14 +1481,15 @@
     return pl.pallas_call(
         functools.partial(expert_exchange_body, experts, half),
         in_specs=[vm] * 7 + [any_] * 4,
-        out_specs=[vm] * 5 + [any_],
-        out_shape=[out((2, s, d + LANES), BF)] + [out((half, d), BF)] * 4 + [out((2, d, f), BF)],
+        out_specs=[vm] * 6 + [any_],
+        out_shape=[out((2, s, d), BF), out((2, experts, 8, wide), F32)] + [out((half, d), BF)] * 4 + [out((2, d, f), BF)],
         scratch_shapes=[
             V((n, d), BF), V((s, d), F32), V((s, d), BF), V((s, d), BF), V((2, d, f), BF), V((2, f, d), BF),
             V((2, s, f), BF), V((2, s, f), BF), V((s, d), BF), V((2 * half, d), F32), V((2 * half, d), F32),
-            V((s, d + LANES), BF), V((2, 2, d, f), BF), V((2, d, f), BF), V((d, s), BF), V((d, s), BF),
+            V((s, d), BF), V((2, 2, d, f), BF), V((2, d, f), BF), V((d, s), BF), V((d, s), BF),
             D((4,)), D((2,)), D((experts,)), D((experts,)), D((experts,)), D((experts,)), D((experts,)), D((experts,)),
             D((tiles,)), D((tiles,)), D((tiles,)),
+            V((experts, 8, wide), F32), D((experts,)), D((experts,)), D((experts,)), D((experts,)),
         ],
         compiler_params=pltpu.CompilerParams(collective_id=1, has_side_effects=True, vmem_limit_bytes=VMEM_BYTES),
         cost_estimate=pl.CostEstimate(flops=24 * s * d * f, bytes_accessed=20 * d * f, transcendentals=0),
@@ -1361,50 +1529,54 @@
     live = jnp.broadcast_to((jnp.arange(n_slot, dtype=I32) < counts[0, 0]).astype(I32)[:, None, None], (n_slot, 1, length))
     lines = jnp.concatenate([jnp.transpose(routes, (0, 2, 1)), priority.reshape(n_slot, 1, length), live], axis=1)
     lines = jnp.pad(lines, ((0, 0), (0, 4), (0, LQ - length)))
-    dy = padded(cotangent)
     blocks = [(half, d)] * peers if fused else [(slots, d)]
     slot_rows, col, *dy_out = call(
         functools.partial(routing_body, experts, capacity, half),
-        [out((n_slot, 8, LQ), I32), out((rows, 8), I32)] + [out(b, BF) for b in blocks], lines, dy,
-        scratch=[pltpu.VMEM((8, LQ), I32)], flops=4 * slots * n_slot * LP * d,
+        [out((n_slot, 8, LQ), I32), out((rows, 8), I32)] + [out(b, BF) for b in blocks], lines, cotangent,
+        scratch=[pltpu.VMEM((n_slot * LP, d), BF), pltpu.VMEM((8, LQ), I32)], flops=4 * slots * n_slot * LP * d,
     )
-    def along_z(v):
-        return [v[0]] + [lax.ppermute(v[j], "exp", [(i, i ^ j) for i in range(peers)]) for j in range(1, peers)]
-
     def exchange(v):
         shaped = v.reshape(peers, v.shape[0] // peers, v.shape[1])
         return lax.all_to_all(shaped, "exp", 0, 0, tiled=True).reshape(v.shape)
 
-    x0 = padded(images)
     if fused:
-        got, (qo1, oo1, io, to, qo2, oo2, eo, fo), dy_in = forward(x0, gains, halves, dy_out[1:], rows)
+        got, (qo1, oo1, io, to, qo2, oo2, eo, fo), dy_in = forward(images, gains, halves, dy_out[1:], rows)
         x1, *kept1, x2, h2, act2, slope2, x3 = got[:10]
-        kept3, h4 = got[10:14], got[14]
+        kept3, h4, x0 = got[10:14], got[14], got[15]
         dy_in = [dy_out[0], *dy_in]
     else:
+        x0 = padded(images)
         qo1, oo1, io, to, qo2, oo2, eo, fo = (other_core(w) for w in halves)
         dy_in = exchange(dy_out[0])
         x1, *kept1 = attention_forward(x0, rows, gains, 0, qm1, qo1, om1, oo1)
         x2, h2, act2, slope2 = mlp_forward(x1, gains, 1, im, io, tm, to)
         x3, *kept3, h4 = attention_forward(x2, rows, gains, 2, qm2, qo2, om2, oo2, tail=3)
 
-    second = (x2, gains, kept3, qm2, qo2, om2, oo2)
     if fused:
-        ret, *eout, ge = expert_exchange(h4, slot_rows, dy_in, router_rows, em, eo, fm, fo, experts, half)
-        eback = along_z(eout)
+        ret, dgate, *eout, ge = expert_exchange(h4, slot_rows, dy_in, router_rows, em, eo, fm, fo, experts, half)
+        (dg1, dg2, dg3, dg4, dr, image), grads, eback = backward(
+            experts, half, x3, h4, router_rows, cotangent, col, ret, dgate, gains, x2, kept3, (qm2, qo2, om2, oo2),
+            x1, h2, act2, slope2, (im, io, tm, to), x0, kept1, (qm1, qo1, om1, oo1), eout[1:])
+        a2_mine, a2_other, gim, gio, gtm, gto, a1_mine, a1_other = grads
+        eback = [eout[0], *eback]
     else:
         [h4_out] = call(functools.partial(dispatch_body, experts, half), [out((slots, d), BF)], slot_rows, h4, other_core(h4))
         h4_in = exchange(h4_out)
         eout, ret, eact, edz, ewd = expert_forward_backward(h4_in, dy_in, router_rows, em, eo, fm, fo, experts)
         ret, eout = exchange(ret), exchange(eout)
         ret, eback = jnp.stack([ret, other_core(ret)]), jnp.stack([eout, other_core(eout)])
+        dgate = ret[:, :, d].astype(F32) + ret[:, :, d + LANES // 2].astype(F32)
+        wide = -(-half // LANES) * LANES
+        dgate = jnp.pad(dgate.reshape(2, experts, 1, half), ((0, 0), (0, 0), (0, 7), (0, wide - half)))
+        ret = ret[:, :, :d]
         ge_mine, ge_other = expert_weights(h4_in, ewd, eact, edz)
         ge = add16(ge_mine, other_core(ge_other))
-    dx2, dg3, dg4, dr, a2_mine, a2_other = mixture_attention_backward(experts, x3, h4, router_rows, dy, col, ret, *second)
+        dx2, dg3, dg4, dr, a2_mine, a2_other = mixture_attention_backward(
+            experts, half, x3, h4, router_rows, cotangent, col, ret, dgate, x2, gains, kept3, qm2, qo2, om2, oo2)
+        dx1, dg2, gim, gio, gtm, gto = mlp_backward(dx2, x1, gains, 1, h2, act2, slope2, im, io, tm, to, c)
+        image, dg1, a1_mine, a1_other = attention_backward(dx1, x0, gains, 0, kept1, qm1, qo1, om1, oo1)
     expert_sum = lax.psum_scatter(ge, "grp", scatter_dimension=1, tiled=True)
 
-    dx1, dg2, gim, gio, gtm, gto = mlp_backward(dx2, x1, gains, 1, h2, act2, slope2, im, io, tm, to, c)
-    image, dg1, a1_mine, a1_other = attention_backward(dx1, x0, gains, 0, kept1, qm1, qo1, om1, oo1)
     mines, others = (a2_mine, gim, gtm, a1_mine), (a2_other, gio, gto, a1_other)
 
     if fused:

time: 408 us -> 388 us (0.951)
  Pallas kernels: 351 us -> 338 us
  starting transfers between devices: 4.33 us -> 0.04 us
    pallas_call x4 -> x1, Pallas kernels: 68.2 us -> 4.03 us  [call(): pl.pallas_call(body, grid=grid, in_specs=in_specs, out_specs=out_specs, o...]
    pallas_call x0 -> x1, Pallas kernels: none -> 54.8 us  [backward(): pl.pallas_call(functools.partial(backward_body, n_img, experts, half, siz...]
    pallas_call x1, Pallas kernels: 39.3 us -> 34.6 us  [forward(): pl.pallas_call(functools.partial(forward_body, n_img, size), in_specs=[vm...]
    ppermute x3 -> x0, starting transfers between devices: 4.29 us -> none  [along_z(): lax.ppermute(v[j], 'exp', [(i, i ^ j) for i in range(peers)])]
    unnamed x36 -> x24, local copies, waits for them, and re-layouts: 8.72 us -> 8.96 us
  transfers between devices with their start and end apart: 4 -> 1, of which waited for: 0 -> 0; matrix products, arithmetic and copies ran while one was open for 4% -> 4% of each run, Pallas kernels for 61% -> 63%
where the time goes in v6:
time: 388 us; the launch traced here: 384 us
  Pallas kernels  338 us (87%)
  other arithmetic  16.6 us (4%)
  between operations  15.3 us (4%)
  local copies, waits for them, and re-layouts  14.4 us (4%)
    pallas_call x1, Pallas kernels, reduce_all(): pl.pallas_call(functools.partial(reduce_body, len(mine), per, n_exp, expe...  185 us
    pallas_call x1, Pallas kernels, expert_exchange(): pl.pallas_call(functools.partial(expert_exchange_body, experts, half), in...  58.8 us
    pallas_call x1, Pallas kernels, backward(): pl.pallas_call(functools.partial(backward_body, n_img, experts, half, siz...  54.8 us
    pallas_call x1, Pallas kernels, forward(): pl.pallas_call(functools.partial(forward_body, n_img, size), in_specs=[vm...  34.6 us
    unnamed x24, local copies, waits for them, and re-layouts  8.96 us
  transfers between devices with their start and end apart: 1, of which 0 were waited for; matrix products, arithmetic and copies ran while one was open for 4% of the time, Pallas kernels for 63%

profile of v6, /device:TPU:0, one launch (start us, length us, event | category | flops | bytes accessed | tf_op | source)
XLA Modules:
  0.0 384.0 jit_solution(13708599542515172237)
XLA Ops:
  7.2 0.0 reduce-scatter.2.cloned.1.call-start
  8.0 0.7 stack.15
  8.7 0.7 stack.16
  9.4 0.7 stack.17
  10.1 0.7 stack.18
  10.7 0.7 reduce
  11.4 0.1 reshape.66
  11.5 0.1 broadcast_in_dim.13
  11.6 0.7 pad_add_fusion
  12.3 0.6 pad.8.rows_ref
  12.9 2.4 copy.33.dy_ref.refs_3_
  15.4 1.2 copy.34.refs_0_
  16.5 0.7 pad.9.router_ref.refs_2_.refs_15_
  17.2 4.0 %shard_map.289 = (s32[4,8,256]{2,1,0:T(8,128)}, s32[416,8]{1,0:T(8,128)}, bf16[160,768]{1,0:T(8,128)(2,1)}, bf16[160,768]{1,0:T(8,128)(2,1)}, bf16[160,768]{1,0:T(8,128)(2,1)}, /*index=5*/bf16[160,768]{1,0:T(8,128)(2,1)}) custom-call(s32[4,8,256]{2,1,0:T(8,128)} %pad.8.rows_ref, bf16[4,197,768]{2,1,0:T(8,128)(2,1)} %copy.33.dy_ref.refs_3_), custom_call_target="tpu_custom_call" | custom-call | flops 1635778560 | bytes 2272256 | tf_op jit(solution)/shard_map/pallas_call | solution.py:65
  21.3 0.6 pad_maximum_fusion.refs_1_.refs_7_
  21.9 34.6 %shard_map.290 = (f32[416,768]{1,0:T(8,128)}, bf16[416,768]{1,0:T(8,128)(2,1)}, bf16[416,2304]{1,0:T(8,128)(2,1)}, bf16[24,208,208]{2,1,0:T(8,128)(2,1)}, bf16[4...) custom-call(bf16[4,197,768]{2,1,0:T(8,128)(2,1)} %copy.34.refs_0_, ...), custom_call_target="tpu_custom_call" | custom-call | flops 7851737088 | bytes 25559040 | tf_op jit(solution)/shard_map/pallas_call | solution.py:473
  56.5 58.8 %shard_map.291 = (bf16[2,640,768]{2,1,0:T(8,128)(2,1)}, f32[2,4,8,256]{3,2,1,0:T(8,128)}, bf16[160,768]{1,0:T(8,128)(2,1)}, bf16[160,768]{1,0:T(8,128)(2,1)}, bf...) custom-call(bf16[416,768]{1,0:T(8,128)(2,1)} %get-tuple-element.85.h4_ref.refs_1_.refs_14_, ...), custom_call_target="tpu_custom_call" | custom-call | flops 18119393280 | bytes 23592960 | tf_op jit(solution)/shard_map/pallas_call | solution.py:1481
  115.3 54.8 %shard_map.292 = (f32[1,768]{1,0:T(1,128)}, f32[1,768]{1,0:T(1,128)}, f32[1,768]{1,0:T(1,128)}, f32[1,768]{1,0:T(1,128)}, f32[128,768]{1,0:T(8,128)}, /*index=5*...) custom-call(f32[416,768]{1,0:T(8,128)} %get-tuple-element.84.refs_0_, ...), custom_call_target="tpu_custom_call" | custom-call | flops 15703474176 | bytes 51118080 | tf_op jit(solution)/shard_map/pallas_call | solution.py:828
  170.1 185.4 %shard_map.293 = (bf16[3,768,384]{2,1,0:T(8,128)(2,1)}, bf16[384,768]{1,0:T(8,128)(2,1)}, bf16[768,1536]{1,0:T(8,128)(2,1)}, bf16[1536,768]{1,0:T(8,128)(2,1)}, ...) custom-call(bf16[2,2,768,384]{3,2,1,0:T(8,128)(2,1)} %bitcast.25, ...), custom_call_target="tpu_custom_call" | custom-call | flops 1063256064 | bytes 18874368 | tf_op jit(solution)/shard_map/pallas_call | solution.py:1273
  355.5 2.9 copy.36
  358.4 1.1 convert_element_type.37
  359.5 1.1 convert_element_type.41
  360.6 1.5 copy.37
  362.1 2.0 convert_element_type.36
  364.1 0.2 copy-done.2
  364.3 2.0 convert_element_type.40
  366.3 0.8 copy-done.1
  367.1 2.8 convert_element_type.38
  370.0 2.5 convert_element_type.39
  372.5 0.6 slice_reduce_fusion
  373.1 0.6 slice_bitcast_fusion.1
  373.7 2.9 convert_bitcast_fusion
  (21 shorter events, 0.1 us)
Async XLA Ops:
  7.2 8.2 %copy-start.5 = (bf16[4,197,768]{2,0,1:T(4,128)(2,1)S(1)}, bf16[4,197,768]{2,0,1:T(4,128)(2,1)}, u32[]{:S(2)}) copy-start(bf16[4,197,768]{2,0,1:T(4,128)(2,1)} %param.18) | copy-start | bytes 3631108
  7.2 366.5 %reduce-scatter.2.cloned.1.call-start = ((), (), s32[]{:S(2)}) async-start(), calls=%async_computation.1 | async-start | bytes 5898240 | tf_op jit(solution)/shard_map/reduce_scatter | solution.py:1578
  12.9 3.6 copy-start.9
  355.5 2.9 copy-start.7
  355.5 4.0 %copy-start.6 = (bf16[384,768]{1,0:T(8,128)(2,1)S(1)}, bf16[384,768]{1,0:T(8,128)(2,1)}, u32[]{:S(2)}) copy-start(bf16[384,768]{1,0:T(8,128)(2,1)} %get-tuple-element.145) | copy-start | bytes 1769476
  358.4 2.2 copy-start.4
  359.5 2.6 copy-start.3
  362.1 2.2 copy-start.2
  364.3 2.8 copy-start.1
  367.1 2.8 copy-start
  369.9 2.5 copy-start.8
Sparse Core Ops, SparseCore 0:
  115.4 55.7 reduce-scatter.1

commit v7 on v6

--- a/solution.py
+++ b/solution.py
@@ -1190,20 +1190,24 @@
 
     def natural(c):
         i, p = c // per, c % per
-        side = rows // 2
+        wide = out_ref.shape[3]
+        piece = wide // 3
         for u in range(2):
-            v = 2 * p + u
-            if i in (0, 3):
-                qkv, proj = (qkv2, proj2) if i == 0 else (qkv1, proj1)
-                if v < 3:
-                    qkv[v] = out_ref[c, u]
+            for r0 in range(0, rows, piece):
+                at = (2 * p + u) * rows + r0
+                value = out_ref[c, u, r0 : r0 + piece]
+                if i in (0, 3):
+                    qkv, proj = (qkv2, proj2) if i == 0 else (qkv1, proj1)
+                    if at < 6 * wide:
+                        k, at = divmod(at, 2 * wide)
+                        qkv[k, at : at + piece] = value
+                    else:
+                        k, at = divmod(at - 6 * wide, wide)
+                        proj[at : at + piece, k * wide : (k + 1) * wide] = value
                 else:
-                    for k in range(2):
-                        proj[:, k * side : (k + 1) * side] = out_ref[c, u, k * side : (k + 1) * side]
-            elif i == 1:
-                fc_in[:, v * side : (v + 1) * side] = out_ref[c, u]
-            else:
-                fc_out[v % 2 * rows : (v % 2 + 1) * rows, v // 2 * side : (v // 2 + 1) * side] = out_ref[c, u]
+                    to, tall = (fc_in, 2 * wide) if i == 1 else (fc_out, 4 * wide)
+                    k, at = divmod(at, tall)
+                    to[at : at + piece, k * wide : (k + 1) * wide] = value
 
     steps = (s1, s2, s3, s4, s5, s6, s7)
     waves = n - 1 + len(steps) - 1
@@ -1497,6 +1501,7 @@
 
 
 FUSED = True
+PER = 3
 
 
 def on_device(images, counts, routes, priority, gain_one, qkv_one, out_one, gain_two, fc_in, fc_out, gain_three,
@@ -1513,10 +1518,10 @@
     c = qkv_one.shape[2]
     rows = own_img * LP
     core = lax.axis_index("mdl")
-    per = 2
+    per = PER
     unit = 4 * d // (2 * per)
     fused = FUSED and (lax.axis_size("grp"), peers, n_mdl) == (4, experts, 2) and peers == 4
-    fused = fused and d == 2 * c and f == 4 * c and unit % (64 * peers) == 0
+    fused = fused and d == 2 * c and f == 4 * c and unit % (64 * peers) == 0 and c % 48 == 0
 
     def padded(v):
         return jnp.pad(v, ((0, 0), (0, LP - length), (0, 0))).reshape(n_slot * LP, -1)

time: 388 us -> 372 us (0.959)
  Pallas kernels: 338 us -> 322 us
    pallas_call x1, Pallas kernels: 185 us -> 170 us  [reduce_all(): pl.pallas_call(functools.partial(reduce_body, len(mine), per, n_exp, expe...]
  transfers between devices with their start and end apart: 1 -> 1, of which waited for: 0 -> 0; matrix products, arithmetic and copies ran while one was open for 4% -> 5% of each run, Pallas kernels for 63% -> 61%
where the time goes in v7:
time: 372 us; the launch traced here: 369 us
  Pallas kernels  322 us (87%)
  other arithmetic  16.6 us (4%)
  between operations  15.3 us (4%)
  local copies, waits for them, and re-layouts  14.4 us (4%)
    pallas_call x1, Pallas kernels, reduce_all(): pl.pallas_call(functools.partial(reduce_body, len(mine), per, n_exp, expe...  170 us
    pallas_call x1, Pallas kernels, expert_exchange(): pl.pallas_call(functools.partial(expert_exchange_body, experts, half), in...  58.8 us
    pallas_call x1, Pallas kernels, backward(): pl.pallas_call(functools.partial(backward_body, n_img, experts, half, siz...  54.8 us
    pallas_call x1, Pallas kernels, forward(): pl.pallas_call(functools.partial(forward_body, n_img, size), in_specs=[vm...  34.6 us
    unnamed x24, local copies, waits for them, and re-layouts  8.96 us
  transfers between devices with their start and end apart: 1, of which 0 were waited for; matrix products, arithmetic and copies ran while one was open for 5% of the time, Pallas kernels for 61%

profile of v7, /device:TPU:0, one launch (start us, length us, event | category | flops | bytes accessed | tf_op | source)
XLA Modules:
  0.0 368.5 jit_solution(2367565517863789924)
XLA Ops:
  7.2 0.0 reduce-scatter.2.cloned.1.call-start
  8.0 0.7 stack.15
  8.7 0.7 stack.16
  9.4 0.7 stack.17
  10.1 0.7 stack.18
  10.7 0.7 reduce
  11.4 0.1 reshape.66
  11.5 0.1 broadcast_in_dim.13
  11.6 0.7 pad_add_fusion
  12.3 0.6 pad.8.rows_ref
  12.9 2.4 copy.33.dy_ref.refs_3_
  15.4 1.2 copy.34.refs_0_
  16.5 0.7 pad.9.router_ref.refs_2_.refs_15_
  17.2 4.0 %shard_map.289 = (s32[4,8,256]{2,1,0:T(8,128)}, s32[416,8]{1,0:T(8,128)}, bf16[160,768]{1,0:T(8,128)(2,1)}, bf16[160,768]{1,0:T(8,128)(2,1)}, bf16[160,768]{1,0:T(8,128)(2,1)}, /*index=5*/bf16[160,768]{1,0:T(8,128)(2,1)}) custom-call(s32[4,8,256]{2,1,0:T(8,128)} %pad.8.rows_ref, bf16[4,197,768]{2,1,0:T(8,128)(2,1)} %copy.33.dy_ref.refs_3_), custom_call_target="tpu_custom_call" | custom-call | flops 1635778560 | bytes 2272256 | tf_op jit(solution)/shard_map/pallas_call | solution.py:65
  21.3 0.6 pad_maximum_fusion.refs_1_.refs_7_
  21.9 34.6 %shard_map.290 = (f32[416,768]{1,0:T(8,128)}, bf16[416,768]{1,0:T(8,128)(2,1)}, bf16[416,2304]{1,0:T(8,128)(2,1)}, bf16[24,208,208]{2,1,0:T(8,128)(2,1)}, bf16[4...) custom-call(bf16[4,197,768]{2,1,0:T(8,128)(2,1)} %copy.34.refs_0_, ...), custom_call_target="tpu_custom_call" | custom-call | flops 7851737088 | bytes 25559040 | tf_op jit(solution)/shard_map/pallas_call | solution.py:473
  56.5 58.8 %shard_map.291 = (bf16[2,640,768]{2,1,0:T(8,128)(2,1)}, f32[2,4,8,256]{3,2,1,0:T(8,128)}, bf16[160,768]{1,0:T(8,128)(2,1)}, bf16[160,768]{1,0:T(8,128)(2,1)}, bf...) custom-call(bf16[416,768]{1,0:T(8,128)(2,1)} %get-tuple-element.85.h4_ref.refs_1_.refs_14_, ...), custom_call_target="tpu_custom_call" | custom-call | flops 18119393280 | bytes 23592960 | tf_op jit(solution)/shard_map/pallas_call | solution.py:1485
  115.3 54.8 %shard_map.292 = (f32[1,768]{1,0:T(1,128)}, f32[1,768]{1,0:T(1,128)}, f32[1,768]{1,0:T(1,128)}, f32[1,768]{1,0:T(1,128)}, f32[128,768]{1,0:T(8,128)}, /*index=5*...) custom-call(f32[416,768]{1,0:T(8,128)} %get-tuple-element.84.refs_0_, ...), custom_call_target="tpu_custom_call" | custom-call | flops 15703474176 | bytes 51118080 | tf_op jit(solution)/shard_map/pallas_call | solution.py:828
  170.1 170.0 %shard_map.293 = (bf16[3,768,384]{2,1,0:T(8,128)(2,1)}, bf16[384,768]{1,0:T(8,128)(2,1)}, bf16[768,1536]{1,0:T(8,128)(2,1)}, bf16[1536,768]{1,0:T(8,128)(2,1)}, ...) custom-call(bf16[3,2,512,384]{3,2,1,0:T(8,128)(2,1)} %bitcast.25, ...), custom_call_target="tpu_custom_call" | custom-call | flops 1063256064 | bytes 18874368 | tf_op jit(solution)/shard_map/pallas_call | solution.py:1277
  340.1 2.9 copy.36
  343.0 1.1 convert_element_type.37
  344.1 1.1 convert_element_type.41
  345.2 1.5 copy.37
  346.7 2.0 convert_element_type.36
  348.7 0.2 copy-done.2
  348.8 2.0 convert_element_type.40
  350.9 0.8 copy-done.1
  351.7 2.8 convert_element_type.38
  354.5 2.5 convert_element_type.39
  357.1 0.6 slice_reduce_fusion
  357.7 0.6 slice_bitcast_fusion.1
  358.3 2.9 convert_bitcast_fusion
  (21 shorter events, 0.1 us)
Async XLA Ops:
  7.2 8.2 %copy-start.5 = (bf16[4,197,768]{2,0,1:T(4,128)(2,1)S(1)}, bf16[4,197,768]{2,0,1:T(4,128)(2,1)}, u32[]{:S(2)}) copy-start(bf16[4,197,768]{2,0,1:T(4,128)(2,1)} %param.18) | copy-start | bytes 3631108
  7.2 351.1 %reduce-scatter.2.cloned.1.call-start = ((), (), s32[]{:S(2)}) async-start(), calls=%async_computation.1 | async-start | bytes 5898240 | tf_op jit(solution)/shard_map/reduce_scatter | solution.py:1583
  12.9 3.6 copy-start.9
  340.1 2.9 copy-start.7
  340.1 4.0 %copy-start.6 = (bf16[384,768]{1,0:T(8,128)(2,1)S(1)}, bf16[384,768]{1,0:T(8,128)(2,1)}, u32[]{:S(2)}) copy-start(bf16[384,768]{1,0:T(8,128)(2,1)} %get-tuple-element.145) | copy-start | bytes 1769476
  343.0 2.2 copy-start.4
  344.1 2.6 copy-start.3
  346.7 2.2 copy-start.2
  348.8 2.8 copy-start.1
  351.7 2.8 copy-start
  354.5 2.5 copy-start.8
Sparse Core Ops, SparseCore 0:
  115.4 55.7 reduce-scatter.1

commit v8 on v7

--- a/solution.py
+++ b/solution.py
@@ -162,7 +162,7 @@
 
 
 def attention_backward_core(n_img, dy, x_ref, gain, h_ref, qkv_ref, p_ref, o_ref, qm, qo, om, oo,
-                            gm_ref, go_ref, do_ref, dqkv_ref, tr_ref):
+                            gm_ref, go_ref, do_ref, dqkv_ref, tr_ref, done=lambda part: None):
     d = x_ref.shape[1]
     c = qm.shape[2]
     pairs = d // LANES
@@ -173,6 +173,7 @@
         for part in range(d // c):
             g[3 * d + part * c : 3 * d + (part + 1) * c, :] = gw[:, part * c : (part + 1) * c]
         do_ref[:, side * c : (side + 1) * c] = nt(da, w[...]).astype(BF)
+    done(3)
     mask = head_mask(BF)
 
     def one(i, _):
@@ -207,6 +208,7 @@
             at = (2 * k + side) * c
             g[k * d : (k + 1) * d, :] = nn(tr_ref[...], dqkv_ref[:, at : at + c]).astype(BF)
             dh = dh + nt(dqkv_ref[:, at : at + c], w[k])
+        done(k)
     n, rr, _ = norm_forward(own_rows(x_ref, n_img * LP).astype(F32), gain)
     dv, dw = norm_backward(n, rr, gain, dh)
     return dy() + dv, dw
@@ -436,13 +438,12 @@
             x2[...] += nn(a, fo[side, at, :])
             return 0
 
-        if side == 0:
-            for cp in swaps[4:6]:
-                cp.start()
+        for cp in swaps[4 + 2 * side : 6 + 2 * side]:
+            cp.start()
         lax.fori_loop(0, f // t, tile, 0)
     store(5, 6, 7, 8)
 
-    attention(lambda: x2[...], g_ref[2:3, :], q3, w3, 4, 5, h3, qkv3, p3, o3, x3, 6)
+    attention(lambda: x2[...], g_ref[2:3, :], q3, w3, 4, 5, h3, qkv3, p3, o3, x3, 8)
     store(9, 10, 11, 12, 13)
     _, _, n = norm_forward(x3[...], g_ref[3:4, :])
     h4[...] = n
@@ -482,9 +483,20 @@
     return got[:n], got[n : n + 8], got[n + 8 :]
 
 
-def routing_body(experts, capacity, half, rows_ref, dy_ref, tr_ref, col_ref, *refs):
-    out_refs, (dy_rows, tmp) = refs[:-2], refs[-2:]
+def routing_body(experts, capacity, half, count_ref, route_ref, prior_ref, router_ref, ga, gb, gc, gd, dy_ref, tr_ref, col_ref, wide_ref,
+                 gains_ref, *refs):
+    out_refs, (dy_rows, rows_ref, tmp) = refs[:-3], refs[-3:]
+    for k, g in enumerate((ga, gb, gc, gd)):
+        gains_ref[k : k + 1, :] = g[...].reshape(1, g.shape[0])
+    wide_ref[...] = jnp.zeros(wide_ref.shape, BF)
+    wide_ref[0:experts, :] = router_ref[...]
     fill_rows(dy_rows, 0, dy_ref, 0, rows_ref.shape[0])
+    token = lax.broadcasted_iota(I32, (1, LQ), 1)
+    for i in range(rows_ref.shape[0]):
+        rows_ref[i] = jnp.zeros((8, LQ), I32)
+        rows_ref[i, 0:TOPK, 0:L] = route_ref[i]
+        rows_ref[i, 2:3, 0:L] = prior_ref[:, i * L : (i + 1) * L]
+        rows_ref[i, 3:4, :] = jnp.where(token < L, (count_ref[0, 0] > i).astype(I32), 0)
     n_img = rows_ref.shape[0]
     slots = experts * half
     core = lax.axis_index("mdl")
@@ -751,10 +763,15 @@
         cp.start()
 
     def attention(x, gain, dst):
-        dx, dw = attention_backward_core(n_img, lambda: dxs[...], x, gain, *attn[1:], ga.at[0], ga.at[1], do, dqkv, tr)
-        leave = [pltpu.make_async_copy(ga.at[k], dst[k], ga_sem.at[k]) for k in range(2)]
-        for cp in leave:
-            cp.start()
+        leave = []
+
+        def done(part):
+            at = slice(part * d, (part + 1) * d)
+            for k in range(2):
+                leave.append(pltpu.make_async_copy(ga.at[k, at], dst[k].at[at], ga_sem.at[k, part]))
+                leave[-1].start()
+
+        dx, dw = attention_backward_core(n_img, lambda: dxs[...], x, gain, *attn[1:], ga.at[0], ga.at[1], do, dqkv, tr, done)
         return dx, dw, leave
 
     grad, dw4 = mixture_backward_core(experts, half, x3, g_ref[3:4, :], h4, router, cotangent, col, ret, dgate, dr, dy_rows)
@@ -832,7 +849,7 @@
             V(x0.shape, x0.dtype), V((r, d), F32), V((r, d), BF), V(act.shape, BF), V(slope.shape, BF), V((2, d, f), BF),
             V((2, f, d), BF), V((2, 4 * d, c), BF), V((2, 2, 1, d, t), BF), V((2, 2, d // t, t, t), BF), V((r, d), F32),
             V((r, d), BF), V((r, d), BF), V((r, 3 * d), BF), V((d, r), BF), V((r, d), BF), V((r, d), F32),
-            D((9,)), D((8,)), D((9,)), D((2,)), D((2, 2, 2)), D((size - 1,)), D((size - 1,))],
+            D((9,)), D((8,)), D((9,)), D((2, 4)), D((2, 2, 2)), D((size - 1,)), D((size - 1,))],
         compiler_params=pltpu.CompilerParams(collective_id=3, has_side_effects=True, vmem_limit_bytes=VMEM_BYTES),
         cost_estimate=pl.CostEstimate(flops=32 * r * d * d + 16 * r * d * f, bytes_accessed=160 * r * d, transcendentals=0),
     )(*near, *flat)
@@ -853,6 +870,48 @@
     y = mixture_output(experts, x_ref, h_ref, router_ref, col_ref, lambda k: merge(col_ref, k, ab_ref, x_ref.shape[0]))
     for i in range(y_ref.shape[0]):
         y_ref[i] = y[i * LP : i * LP + L]
+
+
+def widen_body(pieces, n_in, n_slots, *refs):
+    src, dst = refs[:n_in], refs[n_in:-2]
+    buf, sem = refs[-2:]
+    going = []
+    for k, (i, a, o, b) in enumerate(pieces):
+        slot = k % n_slots
+        if k >= n_slots:
+            going[k - n_slots].wait()
+        value = src[i][a].astype(F32)
+        rows, cols = value.shape
+        buf[slot, 0:rows, 0:cols] = value
+        going.append(pltpu.make_async_copy(buf.at[slot, 0:rows, 0:cols], dst[o].at[b], sem.at[slot]))
+        going[k].start()
+    for cp in going[max(0, len(pieces) - n_slots) :]:
+        cp.wait()
+
+
+def widen(*vs):
+    pieces = []
+    for i, v in enumerate(vs):
+        if len(v.shape) == 3:
+            pieces += [(i, k, i, k) for k in range(v.shape[0])]
+        else:
+            n = v.shape[0]
+            step = min(n, max(16, (1 << 18) // v.shape[1] // 16 * 16))
+            while n % step:
+                step -= 16
+            pieces += [(i, slice(r, r + step), i, slice(r, r + step)) for r in range(0, n, step)]
+    rows = max(v.shape[1] if len(v.shape) == 3 else min(v.shape[0], 512) for v in vs)
+    rows = max([rows] + [a.stop - a.start for _, a, _, _ in pieces if isinstance(a, slice)])
+    cols = max(v.shape[-1] for v in vs)
+    n_slots = 4
+    any_ = pl.BlockSpec(memory_space=pl.ANY)
+    return pl.pallas_call(
+        functools.partial(widen_body, tuple(pieces), len(vs), n_slots),
+        in_specs=[pl.BlockSpec(memory_space=pltpu.VMEM)] * len(vs), out_specs=[any_] * len(vs),
+        out_shape=[out(v.shape, F32) for v in vs],
+        scratch_shapes=[pltpu.VMEM((n_slots, rows, cols), F32), pltpu.SemaphoreType.DMA((n_slots,))],
+        compiler_params=pltpu.CompilerParams(vmem_limit_bytes=34 * 1024 * 1024),
+    )(*vs)
 
 
 def flip(axis, bit):
@@ -1528,17 +1587,14 @@
 
     qm1, om1, im, tm, qm2, om2, em, fm = halves = (
         qkv_one, out_one, fc_in, fc_out, qkv_two, out_two, expert_in[0], expert_out[0])
-    gains = jnp.stack([gain_one, gain_two, gain_three, gain_four])
-    router_rows = jnp.pad(router.T, ((0, LANES - experts), (0, 0)))
-
-    live = jnp.broadcast_to((jnp.arange(n_slot, dtype=I32) < counts[0, 0]).astype(I32)[:, None, None], (n_slot, 1, length))
-    lines = jnp.concatenate([jnp.transpose(routes, (0, 2, 1)), priority.reshape(n_slot, 1, length), live], axis=1)
-    lines = jnp.pad(lines, ((0, 0), (0, 4), (0, LQ - length)))
     blocks = [(half, d)] * peers if fused else [(slots, d)]
-    slot_rows, col, *dy_out = call(
+    routing_args = (counts, jnp.transpose(routes, (0, 2, 1)), priority, router.T, gain_one, gain_two, gain_three, gain_four, cotangent)
+    slot_rows, col, router_rows, gains, *dy_out = call(
         functools.partial(routing_body, experts, capacity, half),
-        [out((n_slot, 8, LQ), I32), out((rows, 8), I32)] + [out(b, BF) for b in blocks], lines, cotangent,
-        scratch=[pltpu.VMEM((n_slot * LP, d), BF), pltpu.VMEM((8, LQ), I32)], flops=4 * slots * n_slot * LP * d,
+        [out((n_slot, 8, LQ), I32), out((rows, 8), I32), out((LANES, d), BF), out((4, d), F32)] + [out(b, BF) for b in blocks], *routing_args,
+        in_specs=[pl.BlockSpec(memory_space=pltpu.SMEM)] + [whole(v.shape) for v in routing_args[1:]],
+        scratch=[pltpu.VMEM((n_slot * LP, d), BF), pltpu.VMEM((n_slot, 8, LQ), I32), pltpu.VMEM((8, LQ), I32)],
+        flops=4 * slots * n_slot * LP * d,
     )
     def exchange(v):
         shaped = v.reshape(peers, v.shape[0] // peers, v.shape[1])
@@ -1607,11 +1663,13 @@
             return jnp.where(core == 0, jnp.concatenate([v, there]), jnp.concatenate([there, v]))
 
         output, grad_images = both(own_out), both(image)
+    shared = [v.reshape(v.shape[-2:]) for v in (expert_sum[0], expert_sum[1])]
+    wide = widen(qkv1, proj1, fi, fo_, qkv2, proj2, *shared)
     return (
         output, grad_images,
-        small[0], qkv1.astype(F32), proj1.astype(F32), small[1], fi.astype(F32), fo_.astype(F32),
-        small[2], qkv2.astype(F32), proj2.astype(F32), small[3], small[4 : 4 + experts].T,
-        expert_sum[0].astype(F32)[None], expert_sum[1].astype(F32).T[None],
+        small[0], wide[0], wide[1], small[1], wide[2], wide[3],
+        small[2], wide[4], wide[5], small[3], small[4 : 4 + experts].T,
+        wide[6][None], wide[7].T[None],
     )
 
 

time: 372 us -> 362 us (0.973)
  other arithmetic: 16.6 us -> 0 us
  Pallas kernels: 322 us -> 329 us
    convert_element_type x7 -> x0, other arithmetic: 11.6 us -> none  [the longest x1 2.82 us: on_device(): fi.astype(F32)]
    pallas_call x0 -> x1, Pallas kernels: none -> 7.49 us  [widen(): pl.pallas_call(functools.partial(widen_body, tuple(pieces), len(vs), n_sl...]
    unnamed x24 -> x22, local copies, waits for them, and re-layouts: 8.96 us -> 11.5 us
  transfers between devices with their start and end apart: 1 -> 1, of which waited for: 0 -> 0; matrix products, arithmetic and copies ran while one was open for 5% -> 2% of each run, Pallas kernels for 61% -> 62%
where the time goes in v8:
time: 362 us; the launch traced here: 358 us
  Pallas kernels  329 us (91%)
  between operations  15.3 us (4%)
  local copies, waits for them, and re-layouts  14.2 us (4%)
    pallas_call x1, Pallas kernels, reduce_all(): pl.pallas_call(functools.partial(reduce_body, len(mine), per, n_exp, expe...  170 us
    pallas_call x1, Pallas kernels, expert_exchange(): pl.pallas_call(functools.partial(expert_exchange_body, experts, half), in...  58.8 us
    pallas_call x1, Pallas kernels, backward(): pl.pallas_call(functools.partial(backward_body, n_img, experts, half, siz...  53.7 us
    pallas_call x1, Pallas kernels, forward(): pl.pallas_call(functools.partial(forward_body, n_img, size), in_specs=[vm...  34.5 us
    unnamed x22, local copies, waits for them, and re-layouts  11.5 us
    pallas_call x1, Pallas kernels, widen(): pl.pallas_call(functools.partial(widen_body, tuple(pieces), len(vs), n_sl...  7.49 us
  transfers between devices with their start and end apart: 1, of which 0 were waited for; matrix products, arithmetic and copies ran while one was open for 2% of the time, Pallas kernels for 62%

profile of v8, /device:TPU:0, one launch (start us, length us, event | category | flops | bytes accessed | tf_op | source)
XLA Modules:
  0.0 358.3 jit_solution(7159472308550982792)
XLA Ops:
  7.2 0.0 copy-start.7
  7.2 0.0 reduce-scatter.2.cloned.1.call-start
  8.0 2.4 copy.33.dy_ref.refs_3_
  10.4 0.0 copy-done.7
  10.4 1.2 copy.34.refs_0_
  11.6 4.3 %shard_map.289 = (s32[4,8,256]{2,1,0:T(8,128)}, s32[416,8]{1,0:T(8,128)}, bf16[128,768]{1,0:T(8,128)(2,1)}, f32[4,768]{1,0:T(4,128)}, bf16[160,768]{1,0:T(8,128)...) custom-call(s32[1,1]{1,0:T(1,128)S(6)} %copy.38.count_ref, ...), custom_call_target="tpu_custom_call" | custom-call | flops 1635778560 | bytes 2476276 | tf_op jit(solution)/shard_map/pallas_call | solution.py:65
  15.8 34.5 %shard_map.290 = (f32[416,768]{1,0:T(8,128)}, bf16[416,768]{1,0:T(8,128)(2,1)}, bf16[416,2304]{1,0:T(8,128)(2,1)}, bf16[24,208,208]{2,1,0:T(8,128)(2,1)}, bf16[4...) custom-call(bf16[4,197,768]{2,1,0:T(8,128)(2,1)} %copy.34.refs_0_, ...), custom_call_target="tpu_custom_call" | custom-call | flops 7851737088 | bytes 25559040 | tf_op jit(solution)/shard_map/pallas_call | solution.py:474
  50.3 58.8 %shard_map.291 = (bf16[2,640,768]{2,1,0:T(8,128)(2,1)}, f32[2,4,8,256]{3,2,1,0:T(8,128)}, bf16[160,768]{1,0:T(8,128)(2,1)}, bf16[160,768]{1,0:T(8,128)(2,1)}, bf...) custom-call(bf16[416,768]{1,0:T(8,128)(2,1)} %get-tuple-element.96.h4_ref.refs_1_.refs_14_, ...), custom_call_target="tpu_custom_call" | custom-call | flops 18119393280 | bytes 23592960 | tf_op jit(solution)/shard_map/pallas_call | solution.py:1544
  109.1 0.0 reduce-scatter.2.cloned.1.call-update
  109.1 53.7 %shard_map.292 = (f32[1,768]{1,0:T(1,128)}, f32[1,768]{1,0:T(1,128)}, f32[1,768]{1,0:T(1,128)}, f32[1,768]{1,0:T(1,128)}, f32[128,768]{1,0:T(8,128)}, /*index=5*...) custom-call(f32[416,768]{1,0:T(8,128)} %get-tuple-element.95.refs_0_, ...), custom_call_target="tpu_custom_call" | custom-call | flops 15703474176 | bytes 51118080 | tf_op jit(solution)/shard_map/pallas_call | solution.py:845
  162.8 170.0 %shard_map.293 = (bf16[3,768,384]{2,1,0:T(8,128)(2,1)}, bf16[384,768]{1,0:T(8,128)(2,1)}, bf16[768,1536]{1,0:T(8,128)(2,1)}, bf16[1536,768]{1,0:T(8,128)(2,1)}, ...) custom-call(bf16[3,2,512,384]{3,2,1,0:T(8,128)(2,1)} %bitcast.22, ...), custom_call_target="tpu_custom_call" | custom-call | flops 1063256064 | bytes 18874368 | tf_op jit(solution)/shard_map/pallas_call | solution.py:1336
  332.8 0.0 copy-start.6
  332.8 0.0 copy-start.8
  332.8 0.0 copy-start.4
  332.8 0.0 copy-start.5
  332.8 2.9 copy.36
  335.8 0.0 copy-done.6
  335.8 0.0 copy-start
  335.8 1.5 copy.37
  337.3 0.0 copy-done.8
  337.3 0.6 slice_reduce_fusion
  337.9 0.6 slice_bitcast_fusion.2
  338.5 0.0 reduce-scatter.2.cloned.1.call-done
  338.5 0.0 copy-start.1
  338.5 1.5 slice_bitcast_fusion
  340.0 0.0 copy-done.4
  340.0 0.0 copy-done.5
  340.0 0.0 copy-done
  340.0 0.5 copy-done.1
  340.5 1.5 copy-done.2
  342.0 1.5 copy-done.3
  343.5 7.5 %shard_map.294 = (f32[3,768,384]{2,1,0:T(8,128)}, f32[384,768]{1,0:T(8,128)}, f32[768,1536]{1,0:T(8,128)}, f32[1536,768]{1,0:T(8,128)}, f32[3,768,384]{2,1,0:T(8...) custom-call(bf16[3,768,384]{2,1,0:T(8,128)(2,1)S(1)} %copy-done.3, ...), custom_call_target="tpu_custom_call" | custom-call | tf_op jit(solution)/shard_map/pallas_call | solution.py:908
  (2 shorter events, 0.0 us)
Async XLA Ops:
  7.2 3.2 copy-start.7
  7.2 331.3 %reduce-scatter.2.cloned.1.call-start = ((), (), s32[]{:S(2)}) async-start(), calls=%async_computation.1 | async-start | bytes 5898240 | tf_op jit(solution)/shard_map/reduce_scatter | solution.py:1639
  332.8 3.0 copy-start.6
  332.8 4.5 %copy-start.8 = (f32[8,768]{1,0:T(8,128)S(1)}, f32[8,768]{1,0:T(8,128)}, u32[]{:S(2)}) copy-start(f32[8,768]{1,0:T(8,128)} %get-tuple-element.151) | copy-start | bytes 73732
  332.8 7.2 %copy-start.4 = (bf16[384,768]{1,0:T(8,128)(2,1)S(1)}, bf16[384,768]{1,0:T(8,128)(2,1)}, u32[]{:S(2)}) copy-start(bf16[384,768]{1,0:T(8,128)(2,1)} %get-tuple-element.157.refs_5_) | copy-start | bytes 1769476
  332.8 7.2 %copy-start.5 = (bf16[384,768]{1,0:T(8,128)(2,1)S(1)}, bf16[384,768]{1,0:T(8,128)(2,1)}, u32[]{:S(2)}) copy-start(bf16[384,768]{1,0:T(8,128)(2,1)} %get-tuple-element.153.refs_1_) | copy-start | bytes 1769476
  335.8 4.2 %copy-start = (bf16[768,1536]{1,0:T(8,128)(2,1)S(1)}, bf16[768,1536]{1,0:T(8,128)(2,1)}, u32[]{:S(2)}) copy-start(bf16[768,1536]{1,0:T(8,128)(2,1)} %get-tuple-element.154.refs_2_) | copy-start | bytes 7077892
  338.5 2.0 copy-start.1
  340.5 1.5 copy-start.2
  342.0 1.5 copy-start.3
Sparse Core Ops, SparseCore 0:
  109.3 55.9 reduce-scatter.1

commit v9 on v8

--- a/solution.py
+++ b/solution.py
@@ -889,7 +889,7 @@
         cp.wait()
 
 
-def widen(*vs):
+def widen(pair, *vs):
     pieces = []
     for i, v in enumerate(vs):
         if len(v.shape) == 3:
@@ -900,6 +900,9 @@
             while n % step:
                 step -= 16
             pieces += [(i, slice(r, r + step), i, slice(r, r + step)) for r in range(0, n, step)]
+    pieces += [(len(vs), k, len(vs) + k, slice(0, pair.shape[1])) for k in range(2)]
+    shapes = [v.shape for v in vs] + [pair.shape[1:]] * 2
+    vs = (*vs, pair)
     rows = max(v.shape[1] if len(v.shape) == 3 else min(v.shape[0], 512) for v in vs)
     rows = max([rows] + [a.stop - a.start for _, a, _, _ in pieces if isinstance(a, slice)])
     cols = max(v.shape[-1] for v in vs)
@@ -907,8 +910,8 @@
     any_ = pl.BlockSpec(memory_space=pl.ANY)
     return pl.pallas_call(
         functools.partial(widen_body, tuple(pieces), len(vs), n_slots),
-        in_specs=[pl.BlockSpec(memory_space=pltpu.VMEM)] * len(vs), out_specs=[any_] * len(vs),
-        out_shape=[out(v.shape, F32) for v in vs],
+        in_specs=[pl.BlockSpec(memory_space=pltpu.VMEM)] * len(vs), out_specs=[any_] * len(shapes),
+        out_shape=[out(v, F32) for v in shapes],
         scratch_shapes=[pltpu.VMEM((n_slots, rows, cols), F32), pltpu.SemaphoreType.DMA((n_slots,))],
         compiler_params=pltpu.CompilerParams(vmem_limit_bytes=34 * 1024 * 1024),
     )(*vs)
@@ -1269,14 +1272,14 @@
                     to[at : at + piece, k * wide : (k + 1) * wide] = value
 
     steps = (s1, s2, s3, s4, s5, s6, s7)
-    waves = n - 1 + len(steps) - 1
+    waves = n - 1 + len(steps)
     late = waves - 2
-    z_steps = ((0, z1), (2, z2), (3, z3), (4, z4), (5, z5), (6, z6), (late, z7))
+    z_steps = ((0, z1), (3, z2), (4, z3), (5, z4), (6, z5), (7, z6), (late, z7))
     small_steps = {1: 0, 3: 1, 5: 2, 7: 3}
 
     def wave(tau, _):
         for s, step in enumerate(steps):
-            c = tau - s + 1
+            c = tau - s + 1 - (s > 0)
 
             @pl.when((c >= 1) & (c < n))
             def _(step=step, c=c):
@@ -1663,8 +1666,7 @@
             return jnp.where(core == 0, jnp.concatenate([v, there]), jnp.concatenate([there, v]))
 
         output, grad_images = both(own_out), both(image)
-    shared = [v.reshape(v.shape[-2:]) for v in (expert_sum[0], expert_sum[1])]
-    wide = widen(qkv1, proj1, fi, fo_, qkv2, proj2, *shared)
+    wide = widen(expert_sum, qkv1, proj1, fi, fo_, qkv2, proj2)
     return (
         output, grad_images,
         small[0], wide[0], wide[1], small[1], wide[2], wide[3],

time: 362 us -> 360 us (level)
    unnamed x22 -> x24, local copies, waits for them, and re-layouts: 11.5 us -> 13.9 us
where the time goes in v9:
time: 360 us; the launch traced here: 357 us
  Pallas kernels  327 us (91%)
  between operations  15.3 us (4%)
  local copies, waits for them, and re-layouts  15.1 us (4%)
    pallas_call x1, Pallas kernels, reduce_all(): pl.pallas_call(functools.partial(reduce_body, len(mine), per, n_exp, expe...  168 us
    pallas_call x1, Pallas kernels, expert_exchange(): pl.pallas_call(functools.partial(expert_exchange_body, experts, half), in...  58.8 us
    pallas_call x1, Pallas kernels, backward(): pl.pallas_call(functools.partial(backward_body, n_img, experts, half, siz...  53.7 us
    pallas_call x1, Pallas kernels, forward(): pl.pallas_call(functools.partial(forward_body, n_img, size), in_specs=[vm...  34.5 us
    unnamed x24, local copies, waits for them, and re-layouts  13.9 us
    pallas_call x1, Pallas kernels, widen(): pl.pallas_call(functools.partial(widen_body, tuple(pieces), len(vs), n_sl...  7.37 us
  transfers between devices with their start and end apart: 1, of which 0 were waited for; matrix products, arithmetic and copies ran while one was open for 2% of the time, Pallas kernels for 62%

profile of v9, /device:TPU:0, one launch (start us, length us, event | category | flops | bytes accessed | tf_op | source)
XLA Modules:
  0.0 357.1 jit_solution(1108637871757433677)
XLA Ops:
  7.2 0.0 copy-start.8
  7.2 0.0 reduce-scatter.2.cloned.1.call-start
  8.0 2.4 copy.33.dy_ref.refs_3_
  10.4 0.0 copy-done.8
  10.4 1.2 copy.34.refs_0_
  11.6 4.3 %shard_map.289 = (s32[4,8,256]{2,1,0:T(8,128)}, s32[416,8]{1,0:T(8,128)}, bf16[128,768]{1,0:T(8,128)(2,1)}, f32[4,768]{1,0:T(4,128)}, bf16[160,768]{1,0:T(8,128)...) custom-call(s32[1,1]{1,0:T(1,128)S(6)} %copy.38.count_ref, ...), custom_call_target="tpu_custom_call" | custom-call | flops 1635778560 | bytes 2476276 | tf_op jit(solution)/shard_map/pallas_call | solution.py:65
  15.8 34.5 %shard_map.290 = (f32[416,768]{1,0:T(8,128)}, bf16[416,768]{1,0:T(8,128)(2,1)}, bf16[416,2304]{1,0:T(8,128)(2,1)}, bf16[24,208,208]{2,1,0:T(8,128)(2,1)}, bf16[4...) custom-call(bf16[4,197,768]{2,1,0:T(8,128)(2,1)} %copy.34.refs_0_, ...), custom_call_target="tpu_custom_call" | custom-call | flops 7851737088 | bytes 25559040 | tf_op jit(solution)/shard_map/pallas_call | solution.py:474
  50.3 58.8 %shard_map.291 = (bf16[2,640,768]{2,1,0:T(8,128)(2,1)}, f32[2,4,8,256]{3,2,1,0:T(8,128)}, bf16[160,768]{1,0:T(8,128)(2,1)}, bf16[160,768]{1,0:T(8,128)(2,1)}, bf...) custom-call(bf16[416,768]{1,0:T(8,128)(2,1)} %get-tuple-element.96.h4_ref.refs_1_.refs_14_, ...), custom_call_target="tpu_custom_call" | custom-call | flops 18119393280 | bytes 23592960 | tf_op jit(solution)/shard_map/pallas_call | solution.py:1547
  109.1 0.0 reduce-scatter.2.cloned.1.call-update
  109.1 53.7 %shard_map.292 = (f32[1,768]{1,0:T(1,128)}, f32[1,768]{1,0:T(1,128)}, f32[1,768]{1,0:T(1,128)}, f32[1,768]{1,0:T(1,128)}, f32[128,768]{1,0:T(8,128)}, /*index=5*...) custom-call(f32[416,768]{1,0:T(8,128)} %get-tuple-element.95.refs_0_, ...), custom_call_target="tpu_custom_call" | custom-call | flops 15703474176 | bytes 51118080 | tf_op jit(solution)/shard_map/pallas_call | solution.py:845
  162.8 167.9 %shard_map.293 = (bf16[3,768,384]{2,1,0:T(8,128)(2,1)}, bf16[384,768]{1,0:T(8,128)(2,1)}, bf16[768,1536]{1,0:T(8,128)(2,1)}, bf16[1536,768]{1,0:T(8,128)(2,1)}, ...) custom-call(bf16[3,2,512,384]{3,2,1,0:T(8,128)(2,1)} %bitcast.18, ...), custom_call_target="tpu_custom_call" | custom-call | flops 1063256064 | bytes 18874368 | tf_op jit(solution)/shard_map/pallas_call | solution.py:1339
  330.8 0.0 copy-start.7
  330.8 0.0 copy-start.9
  330.8 0.0 copy-start
  330.8 0.0 copy-start.5
  330.8 0.0 copy-start.6
  330.8 2.9 copy.36
  333.8 0.0 copy-done.7
  333.8 1.5 copy.37
  335.2 0.0 copy-done.9
  335.2 0.6 slice_reduce_fusion
  335.9 0.6 slice_bitcast_fusion
  336.5 0.0 reduce-scatter.2.cloned.1.call-done.refs_6_
  336.5 0.0 copy-done
  336.5 0.0 copy-done.5
  336.5 0.0 copy-done.6
  336.5 0.0 copy-start.1
  336.5 1.7 copy-done.1
  338.2 1.5 copy-done.2
  339.6 1.5 copy-done.3
  341.1 1.3 copy-done.4
  342.4 7.4 %shard_map.294 = (f32[3,768,384]{2,1,0:T(8,128)}, f32[384,768]{1,0:T(8,128)}, f32[768,1536]{1,0:T(8,128)}, f32[1536,768]{1,0:T(8,128)}, f32[3,768,384]{2,1,0:T(8...) custom-call(bf16[3,768,384]{2,1,0:T(8,128)(2,1)S(1)} %copy-done.3, ...), custom_call_target="tpu_custom_call" | custom-call | tf_op jit(solution)/shard_map/pallas_call | solution.py:911
  (3 shorter events, 0.0 us)
Async XLA Ops:
  7.2 3.2 copy-start.8
  7.2 329.3 %reduce-scatter.2.cloned.1.call-start = ((), (), s32[]{:S(2)}) async-start(), calls=%async_computation.1 | async-start | bytes 5898240 | tf_op jit(solution)/shard_map/reduce_scatter | solution.py:1642
  330.8 3.0 copy-start.7
  330.8 4.5 %copy-start.9 = (f32[8,768]{1,0:T(8,128)S(1)}, f32[8,768]{1,0:T(8,128)}, u32[]{:S(2)}) copy-start(f32[8,768]{1,0:T(8,128)} %get-tuple-element.151) | copy-start | bytes 73732
  330.8 5.7 %copy-start = (bf16[768,1536]{1,0:T(8,128)(2,1)S(1)}, bf16[768,1536]{1,0:T(8,128)(2,1)}, u32[]{:S(2)}) copy-start(bf16[768,1536]{1,0:T(8,128)(2,1)} %get-tuple-element.154.refs_2_) | copy-start | bytes 7077892
  330.8 5.7 %copy-start.5 = (bf16[384,768]{1,0:T(8,128)(2,1)S(1)}, bf16[384,768]{1,0:T(8,128)(2,1)}, u32[]{:S(2)}) copy-start(bf16[384,768]{1,0:T(8,128)(2,1)} %get-tuple-element.157.refs_5_) | copy-start | bytes 1769476
  330.8 5.7 %copy-start.6 = (bf16[384,768]{1,0:T(8,128)(2,1)S(1)}, bf16[384,768]{1,0:T(8,128)(2,1)}, u32[]{:S(2)}) copy-start(bf16[384,768]{1,0:T(8,128)(2,1)} %get-tuple-element.153.refs_1_) | copy-start | bytes 1769476
  336.5 1.7 copy-start.1
  338.2 1.5 copy-start.2
  339.6 1.5 copy-start.3
  341.1 1.3 copy-start.4
Sparse Core Ops, SparseCore 0:
  109.3 55.9 reduce-scatter.1
